TPU v7x, 512 devices: a whole 4x4x16 slice. The times are simulated.
512 devices in a mesh: gx: 64 (over x, z), gz: 8 (over y, core).
Axes of the slice: x: 4, y: 4, z: 16, core: 2. Of those that a mesh axis runs over, the one named last changes fastest.
Arguments:
- right_side: float32 [512, 512, 128], P('gx', 'gz'), may hold values from -6 to 6
- conductivity: float32 [512, 512, 128], P('gx', 'gz'), may hold values from 0.5 to 8
Outputs:
- solution_field: float32 [512, 512, 128], P('gx', 'gz')
All inputs are finite; a program needn't handle non-finite values.
Results may differ from a plain program's by a relative error of at most 0.0001.
Values sent between devices are 32-bit elements; how exact they have to be, the bound alone decides.
No kernel may reach another device: no remote copies, remote signals or barrier semaphores. Data moves between devices by JAX's collectives and lax.ppermute only.
A program may use at most 64 MiB of HBM per device.

v0:
```python
from functools import partial

import jax
import jax.numpy as jnp
from jax import lax
from jax.sharding import PartitionSpec as P

SWEEPS = 2
COARSE_ITERS = 20


def with_halo(array, sides, width):
    for axis, dim in sides:
        devices, length = (lax.axis_size(axis), array.shape[dim])
        up = [(i, (i + 1) % devices) for i in range(devices - 1)]
        down = [(j, i) for i, j in up]
        last = lax.slice_in_dim(array, length - width, length, axis=dim)
        initial = lax.slice_in_dim(array, 0, width, axis=dim)
        before = lax.ppermute(last, axis, up)
        after = lax.ppermute(initial, axis, down)
        array = jnp.concatenate([before, array, after], axis=dim)
    return array


def coefs_from_padded(padded):
    face_zero = 0.5 * (padded[:-1, 1:-1, 1:-1] + padded[1:, 1:-1, 1:-1])
    face_one = 0.5 * (padded[1:-1, :-1, 1:-1] + padded[1:-1, 1:, 1:-1])
    face_two = 0.5 * (padded[1:-1, 1:-1, :-1] + padded[1:-1, 1:-1, 1:])
    diagonal = (
        face_zero[:-1]
        + face_zero[1:]
        + face_one[:, :-1]
        + face_one[:, 1:]
        + face_two[:, :, :-1]
        + face_two[:, :, 1:]
    )
    return (face_zero, face_one, face_two, diagonal)


def operate_padded(padded, coefs, scale):
    face_zero, face_one, face_two, diagonal = coefs
    center = padded[1:-1, 1:-1, 1:-1]
    beside = face_zero[:-1] * padded[:-2, 1:-1, 1:-1] + face_zero[1:] * padded[2:, 1:-1, 1:-1]
    beside = (
        beside
        + face_one[:, :-1] * padded[1:-1, :-2, 1:-1]
        + face_one[:, 1:] * padded[1:-1, 2:, 1:-1]
    )
    beside = (
        beside
        + face_two[:, :, :-1] * padded[1:-1, 1:-1, :-2]
        + face_two[:, :, 1:] * padded[1:-1, 1:-1, 2:]
    )
    return scale * (diagonal * center - beside)


def restrict(field):
    size_a, size_b, size_c = field.shape
    return field.reshape(size_a // 2, 2, size_b // 2, 2, size_c // 2, 2).mean(axis=(1, 3, 5))


def prolong(field):
    return jnp.repeat(jnp.repeat(jnp.repeat(field, 2, 0), 2, 1), 2, 2)


def cheb_weights(count, lower, upper):
    theta = 0.5 * (upper + lower)
    delta = 0.5 * (upper - lower)
    sigma = theta / delta
    rho_prev = 1.0 / sigma
    carry_terms = [0.0]
    gain_terms = [1.0 / theta]
    for step in range(1, count):
        rho_next = 1.0 / (2.0 * sigma - rho_prev)
        carry_terms.append(rho_next * rho_prev)
        gain_terms.append(2.0 * rho_next / delta)
        rho_prev = rho_next
    return (carry_terms, gain_terms)


def extend(field, level):
    if level == 0:
        grown = with_halo(field, (("gx", 0), ("gz", 1)), 1)
    elif level < 3:
        grown = with_halo(field, (("gx", 0), ("gz", 1)), 1)
    else:
        grown = with_halo(field, (("gx", 0), ("gz", 1)), 1)
    return jnp.pad(grown, ((0, 0), (0, 0), (1, 1)))


def smooth(guess, source, coefs, scale, count, lower, upper, padder):
    carry_list, gain_list = cheb_weights(count, lower, upper)
    carry_terms = jnp.asarray(carry_list, jnp.float32)
    gain_terms = jnp.asarray(gain_list, jnp.float32)
    inverse = 1.0 / (scale * coefs[3])

    def one_step(step, state):
        current, update = state
        remainder = source - operate_padded(padder(current), coefs, scale)
        update = carry_terms[step] * update + gain_terms[step] * (inverse * remainder)
        return (current + update, update)

    result, unused = lax.fori_loop(0, count, one_step, (guess, jnp.zeros_like(guess)))
    return result


def on_device(right_side, conductivity):
    conds = [conductivity]
    for level in range(3):
        conds.append(restrict(conds[-1]))
    coefs = [coefs_from_padded(extend(conds[level], level)) for level in range(3)]
    sources = [right_side]
    guesses = []
    for level in range(3):
        scale = 0.25**level
        padder = partial(extend, level=level)
        guess = smooth(
            jnp.zeros_like(sources[level]),
            sources[level],
            coefs[level],
            scale,
            SWEEPS,
            0.25,
            2.0,
            padder,
        )
        remainder = sources[level] - operate_padded(padder(guess), coefs[level], scale)
        guesses.append(guess)
        sources.append(restrict(remainder))
    coarse_coefs = coefs_from_padded(extend(conds[3], 3))
    coarse = smooth(
        jnp.zeros_like(sources[3]),
        sources[3],
        coarse_coefs,
        0.25**3,
        COARSE_ITERS,
        0.02,
        2.0,
        partial(extend, level=3),
    )
    for level in (2, 1, 0):
        start = guesses[level] + prolong(coarse)
        coarse = smooth(
            start,
            sources[level],
            coefs[level],
            0.25**level,
            SWEEPS,
            0.25,
            2.0,
            partial(extend, level=level),
        )
    return coarse


def solution(mesh):
    return jax.shard_map(
        on_device,
        mesh=mesh,
        in_specs=(P("gx", "gz", None), P("gx", "gz", None)),
        out_specs=P("gx", "gz", None),
        check_vma=False,
    )
```

profile of v0, /device:TPU:6, one launch (start us, length us, event | category | flops | bytes accessed | tf_op | source)
XLA Modules:
  0.0 822.4 jit_solution(17366220669262013630)
XLA Ops:
  0.0 18.9 %reshape.64 = f32[4,2,32,2,64,2]{5,4,3,2,1,0:T(8,128)} reshape(f32[8,64,128]{2,1,0:T(8,128)} %param.31) | data formatting | bytes 524288 | tf_op jit(solution)/shard_map/reshape | solution.py:59
  18.9 7.0 reduce_sum.68
  35.3 9.8 %collective-permute-start.49 = (f32[1,8,16]{2,1,0:T(8,128)S(1)}, f32[1,8,16]{2,1,0:T(8,128)S(1)}, u32[]{:S(2)}, u32[]{:S(2)}) collective-permute-start(f32[1,8,16]{2,1,0:T(8,128)S(1)} %multiply_bitcast_fusion.1), channel_id=1, source_target_pairs={{8,0},{16,8},{24,16},{32,24},{40,32},{48,40},{56,48},{64,56},{72,6... | collective-permute-start | bytes 1544 | tf_op jit(solution)/shard_map/ppermute | solution.py:20
  47.0 6.0 collective-permute-start.29
  58.4 6.0 collective-permute-start.41
  73.1 6.0 collective-permute-start.33
  99.3 41.9 %while.136 = (s32[]{:T(128)}, f32[8,64,128]{2,1,0:T(8,128)S(1)}, f32[8,64,128]{2,1,0:T(8,128)S(1)}, f32[8,64,128]{2,1,0:T(8,128)S(1)}, f32[9,64,128]{2,1,0:T(8,1...) while((s32[]{:T(128)}, f32[8,64,128]{2,1,0:T(8,128)S(1)}, ...), condition=%wide.region_1.0_spmd.clone.clone, body=%wide.region_0.0_spmd.sunk.clone.clone.sunk | while | flops 2935267 | bytes 5985768 | solution.py:103
  99.3 6.3 collective-permute-start
  107.6 6.0 collective-permute-done.1
  143.9 6.0 collective-permute-start.37
  158.9 18.1 %reshape.65 = f32[4,2,32,2,64,2]{5,4,3,2,1,0:T(8,128)} reshape(f32[8,64,128]{2,1,0:T(8,128)S(1)} %fusion.114) | data formatting | bytes 524288 | tf_op jit(solution)/shard_map/reshape | solution.py:59
  177.1 7.0 reduce_sum.69
  184.1 38.7 %while.137 = (s32[]{:T(128)}, f32[4,32,64]{2,1,0:T(8,128)S(1)}, f32[4,32,64]{2,1,0:T(8,128)S(1)}, f32[4,32,64]{2,1,0:T(8,128)S(1)}, f32[5,32,64]{2,1,0:T(8,128)S...) while((s32[]{:T(128)}, f32[4,32,64]{2,1,0:T(8,128)S(1)}, ...), condition=%wide.region_5.6_spmd.clone.clone, body=%wide.region_4.5_spmd.sunk.clone.clone.sunk | while | flops 408867 | bytes 845736 | solution.py:103
  184.2 6.5 collective-permute-start.4
  192.6 5.8 collective-permute-done.5
  224.9 6.0 collective-permute-start.45
  247.1 40.8 %while.138 = (s32[]{:T(128)}, f32[2,16,32]{2,1,0:T(8,128)S(1)}, f32[2,16,32]{2,1,0:T(8,128)S(1)}, f32[2,16,32]{2,1,0:T(8,128)S(1)}, f32[3,16,32]{2,1,0:T(8,128)S...) while((s32[]{:T(128)}, f32[2,16,32]{2,1,0:T(8,128)S(1)}, ...), condition=%wide.region_9.10_spmd.clone.clone, body=%wide.region_8.9_spmd.sunk.clone.clone.sunk | while | flops 60611 | bytes 131976 | solution.py:103
  247.1 6.3 collective-permute-start.8
  255.4 5.7 collective-permute-done.9
  290.5 6.0 collective-permute-start.53
  305.0 400.7 %while.139 = (s32[]{:T(128)}, f32[1,8,16]{2,1,0:T(8,128)S(1)}, f32[1,8,16]{2,1,0:T(8,128)}, f32[1,8,16]{2,1,0:T(8,128)S(1)}, f32[2,8,16]{2,1,0:T(8,128)S(1)}, /*...) while((s32[]{:T(128)}, f32[1,8,16]{2,1,0:T(8,128)S(1)}, ...), condition=%wide.region_15.16_spmd.clone.clone, body=%wide.region_14.15_spmd.sunk.clone.clone.sunk | while | flops 10259 | bytes 22072 | solution.py:103
  305.0 6.3 collective-permute-start.12
  705.8 39.8 %while.140 = (s32[]{:T(128)}, f32[2,16,32]{2,1,0:T(8,128)S(1)}, f32[2,16,32]{2,1,0:T(8,128)S(1)}, f32[2,16,32]{2,1,0:T(8,128)S(1)}, f32[3,16,32]{2,1,0:T(8,128)S...) while((s32[]{:T(128)}, f32[2,16,32]{2,1,0:T(8,128)S(1)}, ...), condition=%wide.region_17.18_spmd.clone.clone, body=%wide.region_16.17_spmd.sunk.clone.clone.sunk | while | flops 45187 | bytes 192391 | solution.py:103
  707.8 6.0 collective-permute-start.17
  727.5 6.0 collective-permute-start.17
  736.2 5.4 collective-permute-start.19
  745.9 36.5 %while.141 = (s32[]{:T(128)}, f32[4,32,64]{2,1,0:T(8,128)S(1)}, f32[4,32,64]{2,1,0:T(8,128)S(1)}, f32[4,32,64]{2,1,0:T(8,128)S(1)}, f32[5,32,64]{2,1,0:T(8,128)S...) while((s32[]{:T(128)}, f32[4,32,64]{2,1,0:T(8,128)S(1)}, ...), condition=%wide.region_19.20_spmd.clone.clone, body=%wide.region_18.19_spmd.sunk.clone.clone.sunk | while | flops 312515 | bytes 1037223 | solution.py:103
  747.9 6.0 collective-permute-start.21
  766.1 6.0 collective-permute-start.21
  784.1 37.7 %while.142 = (s32[]{:T(128)}, f32[8,64,128]{2,1,0:T(8,128)S(1)}, f32[8,64,128]{2,1,0:T(8,128)S(1)}, f32[8,64,128]{2,1,0:T(8,128)S(1)}, f32[9,64,128]{2,1,0:T(8,1...) while((s32[]{:T(128)}, f32[8,64,128]{2,1,0:T(8,128)S(1)}, ...), condition=%wide.region_21.22_spmd.clone.clone, body=%wide.region_20.21_spmd.sunk.clone.clone.sunk | while | flops 2259267 | bytes 6651367 | solution.py:103
  786.0 6.0 collective-permute-start.25
  804.9 6.0 collective-permute-start.25
  (660 shorter events, 637.7 us)
Async XLA Ops:
  31.5 23.7 %collective-permute-start.48 = (f32[1,8,16]{2,1,0:T(8,128)S(1)}, f32[1,8,16]{2,1,0:T(8,128)S(1)}, u32[]{:S(2)}, u32[]{:S(2)}) collective-permute-start(f32[1,8,16]{2,1,0:T(8,128)S(1)} %multiply_bitcast_fusion.1), channel_id=1, source_target_pairs={{0,8},{8,16},{16,24},{24,32},{32,40},{40,48},{48,56},{56,64},{64,7... | collective-permute-start | bytes 1544 | tf_op jit(solution)/shard_map/ppermute | solution.py:19
  35.3 19.8 %collective-permute-start.49 = (f32[1,8,16]{2,1,0:T(8,128)S(1)}, f32[1,8,16]{2,1,0:T(8,128)S(1)}, u32[]{:S(2)}, u32[]{:S(2)}) collective-permute-start(f32[1,8,16]{2,1,0:T(8,128)S(1)} %multiply_bitcast_fusion.1), channel_id=1, source_target_pairs={{8,0},{16,8},{24,16},{32,24},{40,32},{48,40},{56,48},{64,56},{72,6... | collective-permute-start | bytes 1544 | tf_op jit(solution)/shard_map/ppermute | solution.py:20
  45.1 46.0 %collective-permute-start.28 = (f32[1,64,128]{2,1,0:T(8,128)S(1)}, f32[1,64,128]{2,1,0:T(8,128)S(1)}, u32[]{:S(2)}, u32[]{:S(2)}) collective-permute-start(f32[1,64,128]{2,1,0:T(8,128)S(1)} %get-tuple-element.2511), channel_id=1, source_target_pairs={{0,8},{8,16},{16,24},{24,32},{32,40},{40,48},{48,56},{56,64},{64,7... | collective-permute-start | bytes 98312 | tf_op jit(solution)/shard_map/ppermute | solution.py:19
  47.0 44.1 %collective-permute-start.29 = (f32[1,64,128]{2,1,0:T(8,128)S(1)}, f32[1,64,128]{2,1,0:T(8,128)S(1)}, u32[]{:S(2)}, u32[]{:S(2)}) collective-permute-start(f32[1,64,128]{2,1,0:T(8,128)S(1)} %get-tuple-element.2510), channel_id=1, source_target_pairs={{8,0},{16,8},{24,16},{32,24},{40,32},{48,40},{56,48},{64,56},{72,6... | collective-permute-start | bytes 98312 | tf_op jit(solution)/shard_map/ppermute | solution.py:20
  53.2 11.4 %collective-permute-start.40 = (f32[1,16,32]{2,1,0:T(8,128)S(1)}, f32[1,16,32]{2,1,0:T(8,128)S(1)}, u32[]{:S(2)}, u32[]{:S(2)}) collective-permute-start(f32[1,16,32]{2,1,0:T(8,128)S(1)} %get-tuple-element.2528), channel_id=1, source_target_pairs={{0,8},{8,16},{16,24},{24,32},{32,40},{40,48},{48,56},{56,64},{64,7... | collective-permute-start | bytes 6152 | tf_op jit(solution)/shard_map/ppermute | solution.py:19
  69.8 9.3 %collective-permute-start.43 = (f32[4,1,32]{2,1,0:T(1,128)S(1)}, f32[4,1,32]{2,1,0:T(1,128)S(1)}, u32[]{:S(2)}, u32[]{:S(2)}) collective-permute-start(f32[4,1,32]{2,1,0:T(1,128)S(1)} %get-tuple-element.2523), channel_id=1, source_target_pairs={{1,0},{2,1},{3,2},{4,3},{5,4},{6,5},{7,6},{9,8},{10,9},{11,10},{12... | collective-permute-start | bytes 1544 | tf_op jit(solution)/shard_map/ppermute | solution.py:20
  141.2 8.7 %collective-permute-start.36 = (f32[1,64,128]{2,1,0:T(8,128)S(1)}, f32[1,64,128]{2,1,0:T(8,128)S(1)}, u32[]{:S(2)}, u32[]{:S(2)}) collective-permute-start(f32[1,64,128]{2,1,0:T(8,128)S(1)} %get-tuple-element.2509), channel_id=1, source_target_pairs={{0,8},{8,16},{16,24},{24,32},{32,40},{40,48},{48,56},{56,64},{64,7... | collective-permute-start | bytes 98312 | tf_op jit(solution)/shard_map/ppermute | solution.py:19
  184.2 8.4 %collective-permute-start.4 = (f32[1,32,64]{2,1,0:T(8,128)S(1)}, f32[1,32,64]{2,1,0:T(8,128)S(1)}, u32[]{:S(2)}, u32[]{:S(2)}) collective-permute-start(f32[1,32,64]{2,1,0:T(8,128)S(1)} %get-tuple-element.2918), channel_id=1, source_target_pairs={{8,0},{16,8},{24,16},{32,24},{40,32},{48,40},{56,48},{64,56},{72,6... | collective-permute-start | bytes 24584 | tf_op jit(solution)/shard_map/while/body/eval_jaxpr/ppermute | solution.py:20
  247.1 8.3 %collective-permute-start.8 = (f32[1,16,32]{2,1,0:T(8,128)S(1)}, f32[1,16,32]{2,1,0:T(8,128)S(1)}, u32[]{:S(2)}, u32[]{:S(2)}) collective-permute-start(f32[1,16,32]{2,1,0:T(8,128)S(1)} %get-tuple-element.2933), channel_id=1, source_target_pairs={{8,0},{16,8},{24,16},{32,24},{40,32},{48,40},{56,48},{64,56},{72,6... | collective-permute-start | bytes 6152 | tf_op jit(solution)/shard_map/while/body/eval_jaxpr/ppermute | solution.py:20
  287.9 8.7 %collective-permute-start.52 = (f32[1,16,32]{2,1,0:T(8,128)S(1)}, f32[1,16,32]{2,1,0:T(8,128)S(1)}, u32[]{:S(2)}, u32[]{:S(2)}) collective-permute-start(f32[1,16,32]{2,1,0:T(8,128)S(1)} %get-tuple-element.2525), channel_id=1, source_target_pairs={{0,8},{8,16},{16,24},{24,32},{32,40},{40,48},{48,56},{56,64},{64,7... | collective-permute-start | bytes 6152 | tf_op jit(solution)/shard_map/ppermute | solution.py:19
  305.0 10.8 %collective-permute-start.12 = (f32[1,8,16]{2,1,0:T(8,128)S(1)}, f32[1,8,16]{2,1,0:T(8,128)S(1)}, u32[]{:S(2)}, u32[]{:S(2)}) collective-permute-start(f32[1,8,16]{2,1,0:T(8,128)S(1)} %broadcast_select_fusion.11), channel_id=1, source_target_pairs={{8,0},{16,8},{24,16},{32,24},{40,32},{48,40},{56,48},{64,56},{72,6... | collective-permute-start | bytes 1544 | tf_op jit(solution)/shard_map/while/body/eval_jaxpr/ppermute | solution.py:20
  326.5 8.4 %collective-permute-start.12 = (f32[1,8,16]{2,1,0:T(8,128)S(1)}, f32[1,8,16]{2,1,0:T(8,128)S(1)}, u32[]{:S(2)}, u32[]{:S(2)}) collective-permute-start(f32[1,8,16]{2,1,0:T(8,128)S(1)} %broadcast_select_fusion.11), channel_id=1, source_target_pairs={{8,0},{16,8},{24,16},{32,24},{40,32},{48,40},{56,48},{64,56},{72,6... | collective-permute-start | bytes 1544 | tf_op jit(solution)/shard_map/while/body/eval_jaxpr/ppermute | solution.py:20
  345.7 8.4 %collective-permute-start.12 = (f32[1,8,16]{2,1,0:T(8,128)S(1)}, f32[1,8,16]{2,1,0:T(8,128)S(1)}, u32[]{:S(2)}, u32[]{:S(2)}) collective-permute-start(f32[1,8,16]{2,1,0:T(8,128)S(1)} %broadcast_select_fusion.11), channel_id=1, source_target_pairs={{8,0},{16,8},{24,16},{32,24},{40,32},{48,40},{56,48},{64,56},{72,6... | collective-permute-start | bytes 1544 | tf_op jit(solution)/shard_map/while/body/eval_jaxpr/ppermute | solution.py:20
  365.4 8.4 %collective-permute-start.12 = (f32[1,8,16]{2,1,0:T(8,128)S(1)}, f32[1,8,16]{2,1,0:T(8,128)S(1)}, u32[]{:S(2)}, u32[]{:S(2)}) collective-permute-start(f32[1,8,16]{2,1,0:T(8,128)S(1)} %broadcast_select_fusion.11), channel_id=1, source_target_pairs={{8,0},{16,8},{24,16},{32,24},{40,32},{48,40},{56,48},{64,56},{72,6... | collective-permute-start | bytes 1544 | tf_op jit(solution)/shard_map/while/body/eval_jaxpr/ppermute | solution.py:20
  385.4 8.4 %collective-permute-start.12 = (f32[1,8,16]{2,1,0:T(8,128)S(1)}, f32[1,8,16]{2,1,0:T(8,128)S(1)}, u32[]{:S(2)}, u32[]{:S(2)}) collective-permute-start(f32[1,8,16]{2,1,0:T(8,128)S(1)} %broadcast_select_fusion.11), channel_id=1, source_target_pairs={{8,0},{16,8},{24,16},{32,24},{40,32},{48,40},{56,48},{64,56},{72,6... | collective-permute-start | bytes 1544 | tf_op jit(solution)/shard_map/while/body/eval_jaxpr/ppermute | solution.py:20
  405.5 8.4 %collective-permute-start.12 = (f32[1,8,16]{2,1,0:T(8,128)S(1)}, f32[1,8,16]{2,1,0:T(8,128)S(1)}, u32[]{:S(2)}, u32[]{:S(2)}) collective-permute-start(f32[1,8,16]{2,1,0:T(8,128)S(1)} %broadcast_select_fusion.11), channel_id=1, source_target_pairs={{8,0},{16,8},{24,16},{32,24},{40,32},{48,40},{56,48},{64,56},{72,6... | collective-permute-start | bytes 1544 | tf_op jit(solution)/shard_map/while/body/eval_jaxpr/ppermute | solution.py:20
  425.5 8.4 %collective-permute-start.12 = (f32[1,8,16]{2,1,0:T(8,128)S(1)}, f32[1,8,16]{2,1,0:T(8,128)S(1)}, u32[]{:S(2)}, u32[]{:S(2)}) collective-permute-start(f32[1,8,16]{2,1,0:T(8,128)S(1)} %broadcast_select_fusion.11), channel_id=1, source_target_pairs={{8,0},{16,8},{24,16},{32,24},{40,32},{48,40},{56,48},{64,56},{72,6... | collective-permute-start | bytes 1544 | tf_op jit(solution)/shard_map/while/body/eval_jaxpr/ppermute | solution.py:20
  445.5 8.4 %collective-permute-start.12 = (f32[1,8,16]{2,1,0:T(8,128)S(1)}, f32[1,8,16]{2,1,0:T(8,128)S(1)}, u32[]{:S(2)}, u32[]{:S(2)}) collective-permute-start(f32[1,8,16]{2,1,0:T(8,128)S(1)} %broadcast_select_fusion.11), channel_id=1, source_target_pairs={{8,0},{16,8},{24,16},{32,24},{40,32},{48,40},{56,48},{64,56},{72,6... | collective-permute-start | bytes 1544 | tf_op jit(solution)/shard_map/while/body/eval_jaxpr/ppermute | solution.py:20
  465.5 8.4 %collective-permute-start.12 = (f32[1,8,16]{2,1,0:T(8,128)S(1)}, f32[1,8,16]{2,1,0:T(8,128)S(1)}, u32[]{:S(2)}, u32[]{:S(2)}) collective-permute-start(f32[1,8,16]{2,1,0:T(8,128)S(1)} %broadcast_select_fusion.11), channel_id=1, source_target_pairs={{8,0},{16,8},{24,16},{32,24},{40,32},{48,40},{56,48},{64,56},{72,6... | collective-permute-start | bytes 1544 | tf_op jit(solution)/shard_map/while/body/eval_jaxpr/ppermute | solution.py:20
  485.5 8.4 %collective-permute-start.12 = (f32[1,8,16]{2,1,0:T(8,128)S(1)}, f32[1,8,16]{2,1,0:T(8,128)S(1)}, u32[]{:S(2)}, u32[]{:S(2)}) collective-permute-start(f32[1,8,16]{2,1,0:T(8,128)S(1)} %broadcast_select_fusion.11), channel_id=1, source_target_pairs={{8,0},{16,8},{24,16},{32,24},{40,32},{48,40},{56,48},{64,56},{72,6... | collective-permute-start | bytes 1544 | tf_op jit(solution)/shard_map/while/body/eval_jaxpr/ppermute | solution.py:20
  505.5 8.4 %collective-permute-start.12 = (f32[1,8,16]{2,1,0:T(8,128)S(1)}, f32[1,8,16]{2,1,0:T(8,128)S(1)}, u32[]{:S(2)}, u32[]{:S(2)}) collective-permute-start(f32[1,8,16]{2,1,0:T(8,128)S(1)} %broadcast_select_fusion.11), channel_id=1, source_target_pairs={{8,0},{16,8},{24,16},{32,24},{40,32},{48,40},{56,48},{64,56},{72,6... | collective-permute-start | bytes 1544 | tf_op jit(solution)/shard_map/while/body/eval_jaxpr/ppermute | solution.py:20
  525.5 8.4 %collective-permute-start.12 = (f32[1,8,16]{2,1,0:T(8,128)S(1)}, f32[1,8,16]{2,1,0:T(8,128)S(1)}, u32[]{:S(2)}, u32[]{:S(2)}) collective-permute-start(f32[1,8,16]{2,1,0:T(8,128)S(1)} %broadcast_select_fusion.11), channel_id=1, source_target_pairs={{8,0},{16,8},{24,16},{32,24},{40,32},{48,40},{56,48},{64,56},{72,6... | collective-permute-start | bytes 1544 | tf_op jit(solution)/shard_map/while/body/eval_jaxpr/ppermute | solution.py:20
  545.5 8.4 %collective-permute-start.12 = (f32[1,8,16]{2,1,0:T(8,128)S(1)}, f32[1,8,16]{2,1,0:T(8,128)S(1)}, u32[]{:S(2)}, u32[]{:S(2)}) collective-permute-start(f32[1,8,16]{2,1,0:T(8,128)S(1)} %broadcast_select_fusion.11), channel_id=1, source_target_pairs={{8,0},{16,8},{24,16},{32,24},{40,32},{48,40},{56,48},{64,56},{72,6... | collective-permute-start | bytes 1544 | tf_op jit(solution)/shard_map/while/body/eval_jaxpr/ppermute | solution.py:20
  565.6 8.4 %collective-permute-start.12 = (f32[1,8,16]{2,1,0:T(8,128)S(1)}, f32[1,8,16]{2,1,0:T(8,128)S(1)}, u32[]{:S(2)}, u32[]{:S(2)}) collective-permute-start(f32[1,8,16]{2,1,0:T(8,128)S(1)} %broadcast_select_fusion.11), channel_id=1, source_target_pairs={{8,0},{16,8},{24,16},{32,24},{40,32},{48,40},{56,48},{64,56},{72,6... | collective-permute-start | bytes 1544 | tf_op jit(solution)/shard_map/while/body/eval_jaxpr/ppermute | solution.py:20
  585.6 8.4 %collective-permute-start.12 = (f32[1,8,16]{2,1,0:T(8,128)S(1)}, f32[1,8,16]{2,1,0:T(8,128)S(1)}, u32[]{:S(2)}, u32[]{:S(2)}) collective-permute-start(f32[1,8,16]{2,1,0:T(8,128)S(1)} %broadcast_select_fusion.11), channel_id=1, source_target_pairs={{8,0},{16,8},{24,16},{32,24},{40,32},{48,40},{56,48},{64,56},{72,6... | collective-permute-start | bytes 1544 | tf_op jit(solution)/shard_map/while/body/eval_jaxpr/ppermute | solution.py:20
  605.6 8.4 %collective-permute-start.12 = (f32[1,8,16]{2,1,0:T(8,128)S(1)}, f32[1,8,16]{2,1,0:T(8,128)S(1)}, u32[]{:S(2)}, u32[]{:S(2)}) collective-permute-start(f32[1,8,16]{2,1,0:T(8,128)S(1)} %broadcast_select_fusion.11), channel_id=1, source_target_pairs={{8,0},{16,8},{24,16},{32,24},{40,32},{48,40},{56,48},{64,56},{72,6... | collective-permute-start | bytes 1544 | tf_op jit(solution)/shard_map/while/body/eval_jaxpr/ppermute | solution.py:20
  625.6 8.4 %collective-permute-start.12 = (f32[1,8,16]{2,1,0:T(8,128)S(1)}, f32[1,8,16]{2,1,0:T(8,128)S(1)}, u32[]{:S(2)}, u32[]{:S(2)}) collective-permute-start(f32[1,8,16]{2,1,0:T(8,128)S(1)} %broadcast_select_fusion.11), channel_id=1, source_target_pairs={{8,0},{16,8},{24,16},{32,24},{40,32},{48,40},{56,48},{64,56},{72,6... | collective-permute-start | bytes 1544 | tf_op jit(solution)/shard_map/while/body/eval_jaxpr/ppermute | solution.py:20
  645.6 8.4 %collective-permute-start.12 = (f32[1,8,16]{2,1,0:T(8,128)S(1)}, f32[1,8,16]{2,1,0:T(8,128)S(1)}, u32[]{:S(2)}, u32[]{:S(2)}) collective-permute-start(f32[1,8,16]{2,1,0:T(8,128)S(1)} %broadcast_select_fusion.11), channel_id=1, source_target_pairs={{8,0},{16,8},{24,16},{32,24},{40,32},{48,40},{56,48},{64,56},{72,6... | collective-permute-start | bytes 1544 | tf_op jit(solution)/shard_map/while/body/eval_jaxpr/ppermute | solution.py:20
  665.6 8.4 %collective-permute-start.12 = (f32[1,8,16]{2,1,0:T(8,128)S(1)}, f32[1,8,16]{2,1,0:T(8,128)S(1)}, u32[]{:S(2)}, u32[]{:S(2)}) collective-permute-start(f32[1,8,16]{2,1,0:T(8,128)S(1)} %broadcast_select_fusion.11), channel_id=1, source_target_pairs={{8,0},{16,8},{24,16},{32,24},{40,32},{48,40},{56,48},{64,56},{72,6... | collective-permute-start | bytes 1544 | tf_op jit(solution)/shard_map/while/body/eval_jaxpr/ppermute | solution.py:20
  685.6 8.4 %collective-permute-start.12 = (f32[1,8,16]{2,1,0:T(8,128)S(1)}, f32[1,8,16]{2,1,0:T(8,128)S(1)}, u32[]{:S(2)}, u32[]{:S(2)}) collective-permute-start(f32[1,8,16]{2,1,0:T(8,128)S(1)} %broadcast_select_fusion.11), channel_id=1, source_target_pairs={{8,0},{16,8},{24,16},{32,24},{40,32},{48,40},{56,48},{64,56},{72,6... | collective-permute-start | bytes 1544 | tf_op jit(solution)/shard_map/while/body/eval_jaxpr/ppermute | solution.py:20
  715.1 8.9 %collective-permute-start.18 = (f32[4,1,32]{2,1,0:T(1,128)S(1)}, f32[4,1,32]{2,1,0:T(1,128)S(1)}, u32[]{:S(2)}, u32[]{:S(2)}) collective-permute-start(f32[4,1,32]{2,1,0:T(1,128)S(1)} %get-tuple-element.2963), channel_id=1, source_target_pairs={{1,0},{2,1},{3,2},{4,3},{5,4},{6,5},{7,6},{9,8},{10,9},{11,10},{12... | collective-permute-start | bytes 1544 | tf_op jit(solution)/shard_map/while/body/eval_jaxpr/ppermute | solution.py:20
  734.9 9.2 %collective-permute-start.18 = (f32[4,1,32]{2,1,0:T(1,128)S(1)}, f32[4,1,32]{2,1,0:T(1,128)S(1)}, u32[]{:S(2)}, u32[]{:S(2)}) collective-permute-start(f32[4,1,32]{2,1,0:T(1,128)S(1)} %get-tuple-element.2963), channel_id=1, source_target_pairs={{1,0},{2,1},{3,2},{4,3},{5,4},{6,5},{7,6},{9,8},{10,9},{11,10},{12... | collective-permute-start | bytes 1544 | tf_op jit(solution)/shard_map/while/body/eval_jaxpr/ppermute | solution.py:20
  (150 other events, 1751.0 us)
where the time goes:
time: 833 us; the launch traced here: 822 us
  starting transfers between devices  463 us (56%)
  waiting for transfers between devices  134 us (16%)
  local copies, waits for them, and re-layouts  126 us (15%)
  other arithmetic  97 us (12%)
    ppermute x78, starting transfers between devices, with_halo(): after = lax.ppermute(initial, axis, down)  234 us
    ppermute x78, starting transfers between devices, with_halo(): before = lax.ppermute(last, axis, up)  228 us
    ppermute x78, waiting for transfers between devices, with_halo(): before = lax.ppermute(last, axis, up)  105 us
    add x32, other arithmetic, one_step(): return (current + update, update)  69.4 us
    reshape x3, local copies, waits for them, and re-layouts, restrict(): field.reshape(size_a // 2, 2, size_b // 2, 2, size_c // 2, 2)  40.5 us
    dynamic_slice x32, local copies, waits for them, and re-layouts, one_step(): carry_terms[step] * update + gain_terms[step] * (inverse * remainder)  39.3 us
    dynamic_slice x32, local copies, waits for them, and re-layouts, one_step(): gain_terms[step] * (inverse * remainder)  38.6 us
    ppermute x78, waiting for transfers between devices, with_halo(): after = lax.ppermute(initial, axis, down)  29.1 us
  transfers between devices with their start and end apart: 156, of which 62 were waited for; matrix products, arithmetic and copies ran while one was open for 10% of the time, Pallas kernels for 0%

commit v1 on v0

v1 whole, which is shorter than its diff:
```python
import functools

import jax
import jax.numpy as jnp
from jax import lax
from jax.experimental import pallas as pl
from jax.experimental.pallas import tpu as pltpu
from jax.sharding import PartitionSpec as P

COARSE_ITERS = 20
LANES = 128
ROW = 16
VMEM_LIMIT = 48 * 1024 * 1024


def cheb_weights(count, lower, upper):
    theta = 0.5 * (upper + lower)
    delta = 0.5 * (upper - lower)
    sigma = theta / delta
    rho_prev = 1.0 / sigma
    carry_terms = [0.0]
    gain_terms = [1.0 / theta]
    for step in range(1, count):
        rho_next = 1.0 / (2.0 * sigma - rho_prev)
        carry_terms.append(rho_next * rho_prev)
        gain_terms.append(2.0 * rho_next / delta)
        rho_prev = rho_next
    return (carry_terms, gain_terms)


(_, CARRY), (GAIN_FIRST, GAIN) = cheb_weights(2, 0.25, 2.0)


def lanes_of(rows):
    return lax.broadcasted_iota(jnp.int32, (rows, LANES), 1)


def rows_of(rows):
    return lax.broadcasted_iota(jnp.int32, (rows, LANES), 0)


def roll(value, shift, axis=1):
    return pltpu.roll(value, shift % value.shape[axis], axis)


def pair_sum(value, stride):
    odd = (lanes_of(value.shape[0]) // stride) % 2 == 1
    return value + jnp.where(odd, roll(value, stride), roll(value, -stride))


class Level:
    def __init__(self, level, gx, gz, brick, cells, first_plane, refs):
        self.stride, self.scale = (2**level, 0.25**level)
        self.gx, self.gz, self.brick, self.cells, self.first_plane = (gx, gz, brick, cells, first_plane)
        self.half, self.fx, self.fz, self.left, self.right, self.diag, self.inverse = refs

    def coefs(self, planes, row, count):
        half, stride = (self.half, self.stride)
        lane = lanes_of(count)
        here = rows_of(count) + (row - ROW + self.gz * self.brick[1])
        first, last = (planes[0], planes[-1])
        for p in planes:
            self.fx[p, row : row + count, :] = half[p - 1, row : row + count, :] + half[p, row : row + count, :]
        p = last + 1
        self.fx[p, row : row + count, :] = half[p - 1, row : row + count, :] + half[p, row : row + count, :]
        more = count + 8
        for p in planes:
            self.fz[p, row : row + more, :] = half[p, row - 1 : row - 1 + more, :] + half[p, row : row + more, :]
        for p in planes:
            center = half[p, row : row + count, :]
            face_left = center + jnp.where(lane >= stride, roll(center, stride), 0.0)
            face_right = center + jnp.where(lane < LANES - stride, roll(center, -stride), 0.0)
            diagonal = (
                self.fx[p, row : row + count, :]
                + self.fx[p + 1, row : row + count, :]
                + self.fz[p, row : row + count, :]
                + self.fz[p, row + 1 : row + 1 + count, :]
                + face_left
                + face_right
            )
            self.left[p, row : row + count, :] = jnp.where(lane >= stride, face_left, 0.0)
            self.right[p, row : row + count, :] = jnp.where(lane < LANES - stride, face_right, 0.0)
            self.diag[p, row : row + count, :] = diagonal
            plane = p - self.first_plane + self.gx * self.brick[0]
            outside = jnp.where(jnp.logical_and(plane >= 0, plane < self.cells[0]), 0, 1 << 20)
            index = here + outside
            inside = (index >= 0) & (index < self.cells[1]) & (diagonal > 0.0)
            self.inverse[p, row : row + count, :] = jnp.where(inside, 1.0 / (self.scale * diagonal), 0.0)

    def remainder(self, source, guess, p, row, count):
        center = guess[p, row : row + count, :]
        beside = (
            self.fx[p, row : row + count, :] * guess[p - 1, row : row + count, :]
            + self.fx[p + 1, row : row + count, :] * guess[p + 1, row : row + count, :]
        )
        beside = beside + (
            self.fz[p, row : row + count, :] * guess[p, row - 1 : row - 1 + count, :]
            + self.fz[p, row + 1 : row + 1 + count, :] * guess[p, row + 1 : row + 1 + count, :]
        )
        beside = beside + (
            self.left[p, row : row + count, :] * roll(center, self.stride)
            + self.right[p, row : row + count, :] * roll(center, -self.stride)
        )
        applied = self.diag[p, row : row + count, :] * center - beside
        return source[p, row : row + count, :] - self.scale * applied

    def second_down(self, source, first, out, planes, row, count):
        for p in planes:
            rest = self.remainder(source, first, p, row, count)
            start = first[p, row : row + count, :]
            update = CARRY * start + GAIN * (self.inverse[p, row : row + count, :] * rest)
            out[p, row : row + count, :] = start + update

    def restricted_remainder(self, source, guess, temp, planes, rows):
        parts = []
        for p in planes[::2]:
            both = self.remainder(source, guess, p, ROW, rows) + self.remainder(source, guess, p + 1, ROW, rows)
            temp[0:rows, :] = pair_sum(both, self.stride)
            parts.append(0.125 * (temp[pl.ds(0, rows // 2, stride=2), :] + temp[pl.ds(1, rows // 2, stride=2), :]))
        return parts

    def up(self, source, start, middle, update, out, planes, row, count, out_row, out_count):
        for p in range(planes[0] - 1, planes[-1] + 2):
            first = GAIN_FIRST * (
                self.inverse[p, row : row + count, :] * self.remainder(source, start, p, row, count)
            )
            update[p, row : row + count, :] = first
            middle[p, row : row + count, :] = start[p, row : row + count, :] + first
        for p in planes:
            second = CARRY * update[p, out_row : out_row + out_count, :] + GAIN * (
                self.inverse[p, out_row : out_row + out_count, :]
                * self.remainder(source, middle, p, out_row, out_count)
            )
            out(p, middle[p, out_row : out_row + out_count, :] + second)


def restricted(half, temp, stride, planes, row, rows):
    parts = []
    for p in planes[::2]:
        both = half[p, row : row + rows, :] + half[p + 1, row : row + rows, :]
        temp[0:rows, :] = pair_sum(both, stride)
        parts.append(0.125 * (temp[pl.ds(0, rows // 2, stride=2), :] + temp[pl.ds(1, rows // 2, stride=2), :]))
    return parts


def first_iterate(source, half, p, row, count, level, stride):
    center = half[p][1 : 1 + count]
    lane = lanes_of(count)
    diagonal = 6.0 * center + half[p - 1][1 : 1 + count] + half[p + 1][1 : 1 + count]
    diagonal = diagonal + half[p][0:count] + half[p][2 : 2 + count]
    diagonal = diagonal + jnp.where(lane >= stride, roll(center, stride), 0.0)
    diagonal = diagonal + jnp.where(lane < LANES - stride, roll(center, -stride), 0.0)
    return GAIN_FIRST * source * (1.0 / (0.25**level * diagonal))


def cut(half_ref, planes, row, count):
    return [half_ref[p, row : row + count, :] for p in planes]


def edge_rows_0(source, cond, low, high, to_high, to_low):
    bx, bz = source.shape[0:2]
    zero = jnp.zeros((4, LANES), jnp.float32)
    for rows, out in ((slice(bz - 4, bz), to_high), (slice(0, 4), to_low)):
        out[0, 0:4, :] = zero
        out[bx + 7, 0:4, :] = zero
        for p in range(3):
            out[p + 1, 0:4, :] = low[p, rows, :]
            out[p + bx + 4, 0:4, :] = high[p, rows, :]
        for p in range(4):
            out[p, 4:8, :] = low[p + 3, rows, :]
            out[p + bx + 4, 4:8, :] = high[p + 3, rows, :]
        for p in range(bx):
            out[p + 4, 0:4, :] = source[p, rows, :]
            out[p + 4, 4:8, :] = cond[p, rows, :]


def down_0(cells, pos, source, cond, low, high, z_low, z_high, win_s, win_h, guess, message, fx, fz, left, right, diag, inverse, first, temp, next_half):
    gx, gz = (pos[0], pos[1])
    bx, bz = source.shape[0:2]
    planes = bx + 8
    zero = jnp.zeros((8, LANES), jnp.float32)
    end = ROW + bz
    for p in range(planes):
        for edge in (8, end, end + 8):
            win_s[p, edge : edge + 8, :] = zero
            win_h[p, edge : edge + 8, :] = zero
            guess[p, edge : edge + 8, :] = zero
            first[p, edge : edge + 8, :] = zero
        win_s[p, ROW - 4 : ROW, :] = z_low[p, 0:4, :]
        win_s[p, end : end + 4, :] = z_high[p, 0:4, :]
        win_h[p, ROW - 4 : ROW, :] = 0.5 * z_low[p, 4:8, :]
        win_h[p, end : end + 4, :] = 0.5 * z_high[p, 4:8, :]
    for p in range(bx):
        win_s[p + 4, ROW:end, :] = source[p, :, :]
        win_h[p + 4, ROW:end, :] = 0.5 * cond[p, :, :]
    for p in range(3):
        win_s[p + 1, ROW:end, :] = low[p, :, :]
        win_s[p + bx + 4, ROW:end, :] = high[p, :, :]
    for p in range(4):
        win_h[p, ROW:end, :] = 0.5 * low[p + 3, :, :]
        win_h[p + bx + 4, ROW:end, :] = 0.5 * high[p + 3, :, :]

    level = Level(0, gx, gz, (bx, bz), cells, 4, (win_h, fx, fz, left, right, diag, inverse))
    row, count = (ROW - 4, bz + 8)
    level.coefs(range(1, planes - 1), row, count)
    for p in range(1, planes - 1):
        first[p, row : row + count, :] = GAIN_FIRST * (
            inverse[p, row : row + count, :] * win_s[p, row : row + count, :]
        )
    level.second_down(win_s, first, guess, range(2, planes - 2), row, count)
    sources = level.restricted_remainder(win_s, guess, temp, range(4, 4 + bx), bz)
    halves = restricted(win_h, temp, 1, range(2, planes - 2), ROW - 8, bz + 16)
    for p, value in enumerate(halves):
        next_half[p, :, :] = value
    own = bz // 2
    odd = lanes_of(own) % 2 == 1
    padded = cut(next_half, range(bx // 2 + 2), 3, own + 2)
    for p, value in enumerate(sources):
        message[p, :, :] = jnp.where(odd, padded[p + 1][1 : 1 + own], value)
        message[p + bx // 2, :, :] = first_iterate(value, padded, p + 1, 0, own, 1, 2)


def edge_rows(*refs):
    parts, (to_high, to_low) = (refs[:-2], refs[-2:])
    at = 0
    for part in parts:
        count, rows = part.shape[0:2]
        to_high[at : at + count, :, :] = part[:, rows - 8 : rows, :]
        to_low[at : at + count, :, :] = part[:, 0:8, :]
        at += count


def down_1(cells, pos, own_ref, low, high, z_low, z_high, win_s, win_h, guess, message, fx, fz, left, right, diag, inverse, first, temp, next_half):
    gx, gz = (pos[0], pos[1])
    bx, bz = (own_ref.shape[0] // 2, own_ref.shape[1])
    planes = 3 * bx
    end = ROW + bz
    zero = jnp.zeros((8, LANES), jnp.float32)

    def unpack(p, start, rows, mixed, iterate):
        odd = lanes_of(rows) % 2 == 1
        win_s[p, start : start + rows, :] = jnp.where(odd, roll(mixed, 1), mixed)
        win_h[p, start : start + rows, :] = jnp.where(odd, mixed, roll(mixed, -1))
        first[p, start : start + rows, :] = iterate

    for b, part in enumerate((low, own_ref, high)):
        for p in range(bx):
            q = b * bx + p
            unpack(q, ROW, bz, part[p, :, :], part[p + bx, :, :])
            unpack(q, ROW - 8, 8, z_low[2 * b * bx + p, :, :], z_low[(2 * b + 1) * bx + p, :, :])
            unpack(q, end, 8, z_high[2 * b * bx + p, :, :], z_high[(2 * b + 1) * bx + p, :, :])
    for p in range(planes):
        for ref in (win_s, win_h, first):
            ref[p, 0:8, :] = zero
            ref[p, end + 8 : end + 16, :] = zero
        guess[p, 8:16, :] = zero
        guess[p, end : end + 8, :] = zero

    level = Level(1, gx, gz, (bx, bz), cells, bx, (win_h, fx, fz, left, right, diag, inverse))
    row, count = (ROW - 4, bz + 8)
    level.coefs(range(1, planes - 1), row, count)
    level.second_down(win_s, first, guess, range(1, planes - 1), row, count)
    sources = level.restricted_remainder(win_s, guess, temp, range(bx, 2 * bx), bz)
    halves = restricted(win_h, temp, 2, range(bx - 2, 2 * bx + 2), ROW - 8, bz + 16)
    for p, value in enumerate(halves):
        next_half[p, :, :] = value
    own = bz // 2
    lane = lanes_of(own) % 4
    padded = cut(next_half, range(bx // 2 + 2), 3, own + 2)
    for p, value in enumerate(sources):
        iterate = first_iterate(value, padded, p + 1, 0, own, 2, 4)
        mixed = jnp.where(lane == 0, value, jnp.where(lane == 1, padded[p + 1][1 : 1 + own], iterate))
        message[p, :, :] = mixed


def spread(mixed, which):
    only = jnp.where(lanes_of(mixed.shape[0]) % 4 == which, mixed, 0.0)
    only = roll(only, -which) if which else only
    twice = only + roll(only, 1)
    return twice + roll(twice, 2)


def down_2(cells, pos, *refs):
    bricks, refs = (refs[:7], refs[7:])
    z_low, z_high, win_s, win_h, guess, message, fx, fz, left, right, diag, inverse, first, temp = refs
    gx, gz = (pos[0], pos[1])
    bx, bz = bricks[0].shape[0:2]
    planes = 7 * bx
    end = ROW + bz
    zero = jnp.zeros((8, LANES), jnp.float32)

    def unpack(p, start, rows, mixed):
        win_s[p, start : start + rows, :] = spread(mixed, 0)
        win_h[p, start : start + rows, :] = spread(mixed, 1)
        first[p, start : start + rows, :] = spread(mixed, 2)

    for b, part in enumerate(bricks):
        for p in range(bx):
            q = b * bx + p
            unpack(q, ROW, bz, part[p, :, :])
            unpack(q, ROW - 8, 8, z_low[q, :, :])
            unpack(q, end, 8, z_high[q, :, :])
    for p in range(planes):
        for ref in (win_s, win_h, first):
            ref[p, 0:8, :] = zero
            ref[p, end + 8 : end + 16, :] = zero
    level = Level(2, gx, gz, (bx, bz), cells, 3 * bx, (win_h, fx, fz, left, right, diag, inverse))
    row, count = (ROW - 8, bz + 16)
    own = 3 * bx
    level.coefs(range(own - 4, own + bx + 4), row, count)
    level.second_down(win_s, first, guess, range(own - 4, own + bx + 4), row, count)
    sources = level.restricted_remainder(win_s, guess, temp, range(own, own + bx), bz)
    halves = restricted(win_h, temp, 4, range(own, own + bx), ROW, bz)
    rows = bz // 2
    cell = lax.broadcasted_iota(jnp.int32, (LANES, LANES), 0)
    lane = lax.broadcasted_iota(jnp.int32, (LANES, LANES), 1)
    pick = jnp.where((cell // 8 == lane % 16) & (cell % 8 == 0), 1.0, 0.0)
    keep = lanes_of(rows) // 16 == rows_of(rows)
    for at, value in enumerate((sources[0], halves[0])):
        dense = jnp.dot(value, pick, precision=lax.Precision.HIGHEST, preferred_element_type=jnp.float32)
        message[at : at + 1, :] = jnp.sum(jnp.where(keep, dense, 0.0), axis=0, keepdims=True)


def before_z(value):
    moved = roll(value, 16)
    return jnp.where(lanes_of(8) < 16, roll(moved, 1, 0), moved)


def after_z(value):
    moved = roll(value, -16)
    return jnp.where(lanes_of(8) >= LANES - 16, roll(moved, -1, 0), moved)


def solve_coarsest(gathered, source, half, base, weights, state, update):
    planes = gathered.shape[0] // 16
    for g in range(8):
        first = 2 * planes * g
        source[pl.ds(g, planes, stride=8), :] = gathered[pl.ds(first, planes, stride=2), :]
        half[pl.ds(g, planes, stride=8), :] = gathered[pl.ds(first + 1, planes, stride=2), :]
    lane, sub = (lanes_of(8), rows_of(8))
    in_left, in_right = (lane % 16 > 0, lane % 16 < 15)
    in_before = (lane >= 16) | (sub > 0)
    in_after = (lane < LANES - 16) | (sub < 7)
    zero = jnp.zeros((8, LANES), jnp.float32)
    first_gain = cheb_weights(COARSE_ITERS, 0.02, 2.0)[1][0]
    for buffer in range(2):
        state[buffer, 0, :, :] = zero
        state[buffer, planes + 1, :, :] = zero

    def at(ref, p):
        return ref[8 * p : 8 * p + 8, :]

    for p in range(planes):
        center = at(half, p)
        low = at(half, p - 1) if p else zero
        high = at(half, p + 1) if p < planes - 1 else zero
        neighbours = (
            (low, None),
            (high, None),
            (before_z(center), in_before),
            (after_z(center), in_after),
            (roll(center, 1), in_left),
            (roll(center, -1), in_right),
        )
        faces = [center + (value if mask is None else jnp.where(mask, value, 0.0)) for value, mask in neighbours]
        diagonal = faces[0] + faces[1] + faces[2] + faces[3] + faces[4] + faces[5]
        inverse = 1.0 / diagonal
        for which, (face, (_, mask)) in enumerate(zip(faces, neighbours)):
            scaled = face * inverse
            base[which, p, :, :] = scaled if mask is None else jnp.where(mask, scaled, 0.0)
        scaled = 64.0 * (at(source, p) * inverse)
        base[6, p, :, :] = scaled
        start = first_gain * scaled
        update[p, :, :] = start
        state[0, p + 1, :, :] = start

    def step(index, old, new):
        carry, gain = (weights[index, 0], weights[index, 1])
        before, center = (zero, state[old, 1, :, :])
        for p in range(planes):
            after = state[old, p + 2, :, :]
            beside = base[0, p, :, :] * before + base[1, p, :, :] * after
            beside = beside + (base[2, p, :, :] * before_z(center) + base[3, p, :, :] * after_z(center))
            beside = beside + (base[4, p, :, :] * roll(center, 1) + base[5, p, :, :] * roll(center, -1))
            change = carry * update[p, :, :] + gain * (base[6, p, :, :] - center + beside)
            update[p, :, :] = change
            state[new, p + 1, :, :] = center + change
            before, center = (center, after)

    def two_steps(pair, unused):
        step(2 * pair + 1, 0, 1)
        step(2 * pair + 2, 1, 0)
        return unused

    lax.fori_loop(0, (COARSE_ITERS - 1) // 2, two_steps, 0)
    step(COARSE_ITERS - 1, 0, 1)
    return 1


def finish(cells, pos, weights, gathered, s2, h2, g2, s1, h1, g1, s0, h0, g0, out, *scratch):
    gx, gz = (pos[0], pos[1])
    source3, half3, base, state, update3, coarse2, temp = scratch[:7]
    f2, f1, f0 = (scratch[7:16], scratch[16:25], scratch[25:34])
    planes3 = gathered.shape[0] // 16
    last = solve_coarsest(gathered, source3, half3, base, weights, state, update3)

    bx2, bz2 = (2, s2.shape[1] - 32)
    rows = bz2 + 8
    cell = lax.broadcasted_iota(jnp.int32, (LANES, LANES), 0)
    lane = lax.broadcasted_iota(jnp.int32, (LANES, LANES), 1)
    pick = jnp.where(cell % 16 == lane // 8, 1.0, 0.0)
    z3 = rows_of(rows) // 2 - 2
    keep = lanes_of(rows) // 16 == (z3 + 8) % 8
    sub = rows_of(8)
    for q in range(5):
        plane = gx + q - 2
        inside = jnp.logical_and(plane >= 0, plane < planes3)
        value = state[last, pl.ds(jnp.clip(plane, -1, planes3) + 1, 1), :, :][0]
        picked = [jnp.sum(jnp.where(sub == gz + d, value, 0.0), axis=0, keepdims=True) for d in (-1, 0, 1)]
        wide = jnp.where(z3 < 0, picked[0], jnp.where(z3 < 8, picked[1], picked[2]))
        coarse2[q * rows : (q + 1) * rows, :] = jnp.where(keep, wide, 0.0)
    spread_out = jnp.dot(coarse2[...], pick, precision=lax.Precision.HIGHEST, preferred_element_type=jnp.float32)
    coarse2[...] = spread_out

    half_planes = s2.shape[0] // 2
    start, middle, update = f2[6:9]
    own = half_planes - 1
    row, count = (ROW - 4, rows)
    zero = jnp.zeros((8, LANES), jnp.float32)
    for q in range(5):
        for p in (own - 4 + 2 * q, own - 3 + 2 * q):
            start[p, 8:16, :] = zero
            start[p, ROW + bz2 : ROW + bz2 + 8, :] = zero
            start[p, row : row + count, :] = g2[p, row : row + count, :] + coarse2[q * rows : (q + 1) * rows, :]
    level = Level(2, gx, gz, (bx2, bz2), cells[2], own, (h2,) + tuple(f2[0:6]))
    level.coefs(range(own - 3, own + 5), row, count)

    bx1, bz1 = (4, s1.shape[1] - 32)
    start1, middle1, update1 = f1[6:9]

    def to_level_1(p, value):
        q = 2 * (p - own) + 4
        temp[pl.ds(0, value.shape[0], stride=2), :] = value
        temp[pl.ds(1, value.shape[0], stride=2), :] = value
        for r in (q, q + 1):
            if 1 <= r <= 10:
                start1[r, ROW - 4 : ROW + bz1 + 4, :] = (
                    g1[r, ROW - 4 : ROW + bz1 + 4, :] + temp[0 : bz1 + 8, :]
                )

    for r in range(1, 11):
        start1[r, 8:16, :] = zero
        start1[r, ROW + bz1 : ROW + bz1 + 8, :] = zero
    level.up(s2, start, middle, update, to_level_1, range(own - 2, own + 4), row, count, ROW - 2, bz2 + 4)
    level = Level(1, gx, gz, (bx1, bz1), cells[1], 4, (h1,) + tuple(f1[0:6]))
    row, count = (ROW - 4, bz1 + 8)
    level.coefs(range(2, 10), row, count)

    bx0, bz0 = (out.shape[0], out.shape[1])
    start0, middle0, update0 = f0[6:9]
    for r in range(2, 14):
        start0[r, 8:16, :] = zero
        start0[r, ROW + bz0 : ROW + bz0 + 8, :] = zero

    def to_level_0(p, value):
        q = 2 * (p - 4) + 4
        temp[pl.ds(0, value.shape[0], stride=2), :] = value
        temp[pl.ds(1, value.shape[0], stride=2), :] = value
        for r in (q, q + 1):
            start0[r, ROW - 4 : ROW + bz0 + 4, :] = g0[r, ROW - 4 : ROW + bz0 + 4, :] + temp[0 : bz0 + 8, :]

    level.up(s1, start1, middle1, update1, to_level_0, range(3, 9), row, count, ROW - 2, bz1 + 4)
    level = Level(0, gx, gz, (bx0, bz0), cells[0], 4, (h0,) + tuple(f0[0:6]))
    level.coefs(range(3, 13), ROW - 4, bz0 + 8)

    def to_out(p, value):
        out[p - 4, :, :] = value

    level.up(s0, start0, middle0, update0, to_out, range(4, 12), ROW - 4, bz0 + 8, ROW, bz0)


def f32(*shape):
    return jax.ShapeDtypeStruct(shape, jnp.float32)


def scratch(*shape):
    return pltpu.VMEM(shape, jnp.float32)


def call(kernel, name, outs, scratches, scalars, *args):
    smem = pl.BlockSpec(memory_space=pltpu.SMEM)
    vmem = pl.BlockSpec(memory_space=pltpu.VMEM)
    return pl.pallas_call(
        kernel,
        name=name,
        out_shape=outs,
        in_specs=[smem] * scalars + [vmem] * (len(args) - scalars),
        out_specs=[vmem] * len(outs),
        scratch_shapes=scratches,
        compiler_params=pltpu.CompilerParams(vmem_limit_bytes=VMEM_LIMIT),
    )(*args)


def shift(array, axis, by):
    devices = lax.axis_size(axis)
    return lax.ppermute(array, axis, [(i, i + by) for i in range(devices) if 0 <= i + by < devices])


def on_device(right_side, conductivity):
    nx, nz = (lax.axis_size("gx"), lax.axis_size("gz"))
    bx, bz = right_side.shape[0:2]
    cells = [(nx * bx >> level, nz * bz >> level) for level in range(4)]
    pos = jnp.stack([lax.axis_index("gx"), lax.axis_index("gz")]).astype(jnp.int32)
    weights = jnp.asarray(list(zip(*cheb_weights(COARSE_ITERS, 0.02, 2.0))), jnp.float32)

    low = shift(jnp.concatenate([right_side[bx - 3 :], conductivity[bx - 4 :]]), "gx", 1)
    high = shift(jnp.concatenate([right_side[:3], conductivity[:4]]), "gx", -1)
    planes = bx + 8
    to_high, to_low = call(
        edge_rows_0, "edge_rows_0", [f32(planes, 8, LANES)] * 2, [], 0, right_side, conductivity, low, high
    )
    z_low, z_high = (shift(to_high, "gz", 1), shift(to_low, "gz", -1))
    window = (planes, bz + 32, LANES)
    s0, h0, g0, brick1 = call(
        functools.partial(down_0, cells[0]),
        "down_0",
        [f32(*window)] * 3 + [f32(bx, bz // 2, LANES)],
        [scratch(*window)] * 7 + [scratch(bz + 16, LANES), scratch(bx // 2 + 2, bz // 2 + 8, LANES)],
        1,
        pos,
        right_side,
        conductivity,
        low,
        high,
        z_low,
        z_high,
    )

    low, high = (shift(brick1, "gx", 1), shift(brick1, "gx", -1))
    to_high, to_low = call(edge_rows, "edge_rows_1", [f32(3 * bx, 8, LANES)] * 2, [], 0, low, brick1, high)
    z_low, z_high = (shift(to_high, "gz", 1), shift(to_low, "gz", -1))
    bx, bz = (bx // 2, bz // 2)
    window1 = (3 * bx, bz + 32, LANES)
    s1, h1, g1, brick2 = call(
        functools.partial(down_1, cells[1]),
        "down_1",
        [f32(*window1)] * 3 + [f32(bx // 2, bz // 2, LANES)],
        [scratch(*window1)] * 7 + [scratch(bz + 16, LANES), scratch(bx // 2 + 2, bz // 2 + 8, LANES)],
        1,
        pos,
        brick1,
        low,
        high,
        z_low,
        z_high,
    )

    bx, bz = (bx // 2, bz // 2)
    bricks = [shift(brick2, "gx", by) if by else brick2 for by in (3, 2, 1, 0, -1, -2, -3)]
    to_high, to_low = call(edge_rows, "edge_rows_2", [f32(7 * bx, 8, LANES)] * 2, [], 0, *bricks)
    z_low, z_high = (shift(to_high, "gz", 1), shift(to_low, "gz", -1))
    window2 = (7 * bx, bz + 32, LANES)
    s2, h2, g2, brick3 = call(
        functools.partial(down_2, cells[2]),
        "down_2",
        [f32(*window2)] * 3 + [f32(2, LANES)],
        [scratch(*window2)] * 7 + [scratch(bz + 16, LANES)],
        1,
        pos,
        *bricks,
        z_low,
        z_high,
    )

    everywhere = lax.all_to_all(jnp.broadcast_to(brick3[None], (nx, 2, LANES)), "gx", 0, 0, tiled=True)
    gathered = lax.all_gather(everywhere, "gz", axis=0).reshape(nz * 2 * nx, LANES)
    work = (
        [scratch(8 * nx, LANES)] * 2
        + [scratch(7, nx, 8, LANES), scratch(2, nx + 2, 8, LANES), scratch(nx, 8, LANES)]
        + [scratch(5 * (bz + 8), LANES), scratch(96, LANES)]
        + [scratch(*window2)] * 9
        + [scratch(*window1)] * 9
        + [scratch(*window)] * 9
    )
    (result,) = call(
        functools.partial(finish, cells), "finish", [f32(*right_side.shape)], work, 2, pos, weights, gathered,
        s2, h2, g2, s1, h1, g1, s0, h0, g0,
    )
    return result


def solution(mesh):
    return jax.shard_map(
        on_device,
        mesh=mesh,
        in_specs=(P("gx", "gz", None), P("gx", "gz", None)),
        out_specs=P("gx", "gz", None),
        check_vma=False,
    )
```

time: 833 us -> 144 us (0.17)
  the two profiles are of different devices: /device:TPU:6 before, /device:TPU:1 now
where the time goes in v1:
time: 144 us
  starting transfers between devices  55.6 us (39%)
  blocking collectives  46.7 us (32%)
  Pallas kernels  19.7 us (14%)
  waiting for transfers between devices  19.5 us (14%)
  local copies, waits for them, and re-layouts  1.79 us (1%)
    ppermute x16, starting transfers between devices, shift(): lax.ppermute(array, axis, [(i, i + by) for i in range(devices) if 0 <= i...  55.6 us
    all_to_all x1, blocking collectives, on_device(): lax.all_to_all(jnp.broadcast_to(brick3[None], (nx, 2, LANES)), 'gx', 0, 0...  32.8 us
    pallas_call x7, Pallas kernels, call(): pl.pallas_call(kernel, name=name, out_shape=outs, in_specs=[smem] * scala...  19.7 us
    ppermute x16, waiting for transfers between devices, shift(): lax.ppermute(array, axis, [(i, i + by) for i in range(devices) if 0 <= i...  19.5 us
    all_gather x1, blocking collectives, on_device(): lax.all_gather(everywhere, 'gz', axis=0).reshape(nz * 2 * nx, LANES)  13.9 us
  transfers between devices with their start and end apart: 16, of which 8 were waited for; matrix products, arithmetic and copies ran while one was open for 0% of the time, Pallas kernels for 0%

profile of v1, /device:TPU:1, one launch (start us, length us, event | category | flops | bytes accessed | tf_op | source)
XLA Modules:
  0.0 143.8 jit_solution(10168166405863932200)
XLA Ops:
  0.0 1.0 fusion
  1.1 4.5 %collective-permute-start = (f32[7,64,128]{2,1,0:T(8,128)S(1)}, f32[7,64,128]{2,1,0:T(8,128)S(1)}, u32[]{:S(2)}, u32[]{:S(2)}) collective-permute-start(f32[7,64,128]{2,1,0:T(8,128)S(1)} %pad_maximum_fusion), channel_id=1, source_target_pairs={{0,8},{8,16},{16,24},{24,32},{32,40},{40,48},{48,56},{56,64},{64,7... | collective-permute-start | bytes 688136 | tf_op jit(solution)/shard_map/ppermute | solution.py:506
  5.7 1.3 collective-permute-start.1
  7.0 1.6 %collective-permute-done.low = f32[7,64,128]{2,1,0:T(8,128)S(1)} collective-permute-done((f32[7,64,128]{2,1,0:T(8,128)S(1)}, f32[7,64,128]{2,1,0:T(8,128)S(1)}, u32[]{:S(2)}, u32[]{:S(2)}) %collective-permute-start) | collective-permute-done | bytes 229408 | tf_op jit(solution)/shard_map/ppermute | solution.py:506
  8.6 4.0 %collective-permute-done.1.high = f32[7,64,128]{2,1,0:T(8,128)S(1)} collective-permute-done((f32[7,64,128]{2,1,0:T(8,128)S(1)}, f32[7,64,128]{2,1,0:T(8,128)S(1)}, u32[]{:S(2)}, u32[]{:S(2)}) %collective-permute-start.1) | collective-permute-done | bytes 229408 | tf_op jit(solution)/shard_map/ppermute | solution.py:506
  12.6 6.2 %collective-permute-start.2 = (f32[16,8,128]{2,1,0:T(8,128)S(1)}, f32[16,8,128]{2,1,0:T(8,128)S(1)}, u32[]{:S(2)}, u32[]{:S(2)}) collective-permute-start(f32[16,8,128]{2,1,0:T(8,128)S(1)} %get-tuple-element.23), channel_id=1, source_target_pairs={{0,1},{1,2},{2,3},{3,4},{4,5},{5,6},{6,7},{8,9},{9,10},{10,11},{11... | collective-permute-start | bytes 196616 | tf_op jit(solution)/shard_map/ppermute | solution.py:506
  18.9 1.9 %collective-permute-start.3 = (f32[16,8,128]{2,1,0:T(8,128)S(1)}, f32[16,8,128]{2,1,0:T(8,128)S(1)}, u32[]{:S(2)}, u32[]{:S(2)}) collective-permute-start(f32[16,8,128]{2,1,0:T(8,128)S(1)} %get-tuple-element.24), channel_id=1, source_target_pairs={{1,0},{2,1},{3,2},{4,3},{5,4},{6,5},{7,6},{9,8},{10,9},{11,10},{12... | collective-permute-start | bytes 196616 | tf_op jit(solution)/shard_map/ppermute | solution.py:506
  20.9 3.6 %collective-permute-done.3.z_high = f32[16,8,128]{2,1,0:T(8,128)S(1)} collective-permute-done((f32[16,8,128]{2,1,0:T(8,128)S(1)}, f32[16,8,128]{2,1,0:T(8,128)S(1)}, u32[]{:S(2)}, u32[]{:S(2)}) %collective-permute-start.3) | collective-permute-done | bytes 65568 | tf_op jit(solution)/shard_map/ppermute | solution.py:506
  24.5 2.2 %down_0.1 = (f32[16,96,128]{2,1,0:T(8,128)S(1)}, f32[16,96,128]{2,1,0:T(8,128)S(1)}, f32[16,96,128]{2,1,0:T(8,128)S(1)}, f32[8,32,128]{2,1,0:T(8,128)S(1)}) custom-call(s32[2]{0:T(128)S(1)} %pad_add_fusion.pos, f32[8,64,128]{2,1,0:T(8,128)S(1)} %copy-done.1, f32[8,64,128]{2,1,0:T(8,128)S(1)} %copy-done, f32[7,64,128]{2,1,0:T(8,128)S(1)} %collective-permute-done.low, ...), custom_call_target="tpu_custom_call" | custom-call | tf_op jit(solution)/shard_map/down_0/pallas_call | solution.py:493
  26.7 1.3 collective-permute-start.5
  28.0 4.2 %collective-permute-start.4 = (f32[8,32,128]{2,1,0:T(8,128)S(1)}, f32[8,32,128]{2,1,0:T(8,128)S(1)}, u32[]{:S(2)}, u32[]{:S(2)}) collective-permute-start(f32[8,32,128]{2,1,0:T(8,128)S(1)} %get-tuple-element.25.refs_1_.own_ref), channel_id=1, source_target_pairs={{0,8},{8,16},{16,24},{24,32},{32,40},{40,48},{48,56},{56,64},{64,7... | collective-permute-start | bytes 393224 | tf_op jit(solution)/shard_map/ppermute | solution.py:506
  32.2 0.4 collective-permute-done.5.refs_2_.high
  32.6 1.5 %collective-permute-done.4.refs_0_.low = f32[8,32,128]{2,1,0:T(8,128)S(1)} collective-permute-done((f32[8,32,128]{2,1,0:T(8,128)S(1)}, f32[8,32,128]{2,1,0:T(8,128)S(1)}, u32[]{:S(2)}, u32[]{:S(2)}) %collective-permute-start.4) | collective-permute-done | bytes 131104 | tf_op jit(solution)/shard_map/ppermute | solution.py:506
  34.1 3.6 %collective-permute-start.6 = (f32[24,8,128]{2,1,0:T(8,128)S(1)}, f32[24,8,128]{2,1,0:T(8,128)S(1)}, u32[]{:S(2)}, u32[]{:S(2)}) collective-permute-start(f32[24,8,128]{2,1,0:T(8,128)S(1)} %get-tuple-element.26), channel_id=1, source_target_pairs={{0,1},{1,2},{2,3},{3,4},{4,5},{5,6},{6,7},{8,9},{9,10},{10,11},{11... | collective-permute-start | bytes 294920 | tf_op jit(solution)/shard_map/ppermute | solution.py:506
  37.7 1.9 %collective-permute-start.7 = (f32[24,8,128]{2,1,0:T(8,128)S(1)}, f32[24,8,128]{2,1,0:T(8,128)S(1)}, u32[]{:S(2)}, u32[]{:S(2)}) collective-permute-start(f32[24,8,128]{2,1,0:T(8,128)S(1)} %get-tuple-element.27), channel_id=1, source_target_pairs={{1,0},{2,1},{3,2},{4,3},{5,4},{6,5},{7,6},{9,8},{10,9},{11,10},{12... | collective-permute-start | bytes 294920 | tf_op jit(solution)/shard_map/ppermute | solution.py:506
  39.6 4.0 %collective-permute-done.7.z_high = f32[24,8,128]{2,1,0:T(8,128)S(1)} collective-permute-done((f32[24,8,128]{2,1,0:T(8,128)S(1)}, f32[24,8,128]{2,1,0:T(8,128)S(1)}, u32[]{:S(2)}, u32[]{:S(2)}) %collective-permute-start.7) | collective-permute-done | bytes 98336 | tf_op jit(solution)/shard_map/ppermute | solution.py:506
  43.6 1.4 down_1.1
  45.0 1.3 collective-permute-start.13
  46.3 1.3 collective-permute-start.12
  47.6 1.3 collective-permute-start.11
  48.9 5.2 %collective-permute-start.10 = (f32[2,16,128]{2,1,0:T(8,128)S(1)}, f32[2,16,128]{2,1,0:T(8,128)S(1)}, u32[]{:S(2)}, u32[]{:S(2)}) collective-permute-start(f32[2,16,128]{2,1,0:T(8,128)S(1)} %get-tuple-element.28.refs_3_), channel_id=1, source_target_pairs={{0,8},{8,16},{16,24},{24,32},{32,40},{40,48},{48,56},{56,64},{64,7... | collective-permute-start | bytes 49160 | tf_op jit(solution)/shard_map/ppermute | solution.py:506
  54.1 8.8 %collective-permute-start.9 = (f32[2,16,128]{2,1,0:T(8,128)S(1)}, f32[2,16,128]{2,1,0:T(8,128)S(1)}, u32[]{:S(2)}, u32[]{:S(2)}) collective-permute-start(f32[2,16,128]{2,1,0:T(8,128)S(1)} %get-tuple-element.28.refs_3_), channel_id=1, source_target_pairs={{0,16},{8,24},{16,32},{24,40},{32,48},{40,56},{48,64},{56,72},{64,... | collective-permute-start | bytes 49160 | tf_op jit(solution)/shard_map/ppermute | solution.py:506
  63.0 7.4 %collective-permute-start.8 = (f32[2,16,128]{2,1,0:T(8,128)S(1)}, f32[2,16,128]{2,1,0:T(8,128)S(1)}, u32[]{:S(2)}, u32[]{:S(2)}) collective-permute-start(f32[2,16,128]{2,1,0:T(8,128)S(1)} %get-tuple-element.28.refs_3_), channel_id=1, source_target_pairs={{0,24},{8,32},{16,40},{24,48},{32,56},{40,64},{48,72},{56,80},{64,... | collective-permute-start | bytes 49160 | tf_op jit(solution)/shard_map/ppermute | solution.py:506
  70.4 0.8 collective-permute-done.8.refs_0_
  71.2 3.5 %collective-permute-start.14 = (f32[14,8,128]{2,1,0:T(8,128)S(1)}, f32[14,8,128]{2,1,0:T(8,128)S(1)}, u32[]{:S(2)}, u32[]{:S(2)}) collective-permute-start(f32[14,8,128]{2,1,0:T(8,128)S(1)} %get-tuple-element.29), channel_id=1, source_target_pairs={{0,1},{1,2},{2,3},{3,4},{4,5},{5,6},{6,7},{8,9},{9,10},{10,11},{11... | collective-permute-start | bytes 172040 | tf_op jit(solution)/shard_map/ppermute | solution.py:506
  74.8 1.9 %collective-permute-start.15 = (f32[14,8,128]{2,1,0:T(8,128)S(1)}, f32[14,8,128]{2,1,0:T(8,128)S(1)}, u32[]{:S(2)}, u32[]{:S(2)}) collective-permute-start(f32[14,8,128]{2,1,0:T(8,128)S(1)} %get-tuple-element.30), channel_id=1, source_target_pairs={{1,0},{2,1},{3,2},{4,3},{5,4},{6,5},{7,6},{9,8},{10,9},{11,10},{12... | collective-permute-start | bytes 172040 | tf_op jit(solution)/shard_map/ppermute | solution.py:506
  76.7 3.6 %collective-permute-done.15.refs_8_ = f32[14,8,128]{2,1,0:T(8,128)S(1)} collective-permute-done((f32[14,8,128]{2,1,0:T(8,128)S(1)}, f32[14,8,128]{2,1,0:T(8,128)S(1)}, u32[]{:S(2)}, u32[]{:S(2)}) %collective-permute-start.15) | collective-permute-done | bytes 57376 | tf_op jit(solution)/shard_map/ppermute | solution.py:506
  80.2 6.6 %down_2.1 = (f32[14,48,128]{2,1,0:T(8,128)S(1)}, f32[14,48,128]{2,1,0:T(8,128)S(1)}, f32[14,48,128]{2,1,0:T(8,128)S(1)}, f32[2,128]{1,0:T(2,128)S(1)}) custom-call(s32[2]{0:T(128)S(1)} %pad_add_fusion.pos, f32[2,16,128]{2,1,0:T(8,128)S(1)} %collective-permute-done.8.refs_0_, f32[2,16,128]{2,1,0:T(8,128)S(1)} %collective-permute-done.9.refs_1_, ...), custom_call_target="tpu_custom_call" | custom-call | tf_op jit(solution)/shard_map/down_2/pallas_call | solution.py:493
  86.9 32.8 %all_to_all.5 = f32[64,2,128]{2,1,0:T(2,128)S(1)} all-to-all(f32[64,2,128]{2,1,0:T(2,128)S(1)} %broadcast_in_dim.2), channel_id=1, replica_groups=mesh['gx'=64,'gz'=8] {'gx'}, dimensions={0} | all-to-all | bytes 131072 | tf_op jit(solution)/shard_map/all_to_all | solution.py:575
  119.7 13.9 %all-gather = f32[512,2,128]{2,1,0:T(2,128)S(1)} all-gather(f32[64,2,128]{2,1,0:T(2,128)S(1)} %all_to_all.5), channel_id=2, replica_groups=mesh['gx'=64,'gz'=8] {'gz'}, dimensions={0}, use_global_device_ids=true | all-gather | bytes 589824 | tf_op jit(solution)/shard_map/all_gather | solution.py:576
  133.6 0.7 copy-done.2
  134.3 9.5 %finish.1 = f32[8,64,128]{2,1,0:T(8,128)} custom-call(s32[2]{0:T(128)S(1)} %pad_add_fusion.pos, f32[20,2]{1,0:T(8,128)S(1)} %copy-done.2, f32[1024,128]{1,0:T(8,128)S(1)} %bitcast.3, f32[14,48,128]{2,1,0:T(8,128)S(1)} %get-tuple-element.32.s2, f32[14,48,128]{2,1,0:T(8,128)S(1)} %get-tuple-element.33.h2, f32[14,48,128]{2,1,0:T(8,128)S(1)} %get-tuple-element.34.g2, ...), custom_call_target="tpu_custom_call" | custom-call | tf_op jit(solution)/shard_map/finish/pallas_call | solution.py:493
  (21 shorter events, 0.3 us)
Async XLA Ops:
  0.0 1.0 copy-start
  1.1 11.5 %copy-start.1 = (f32[8,64,128]{2,1,0:T(8,128)S(1)}, f32[8,64,128]{2,1,0:T(8,128)}, u32[]{:S(2)}) copy-start(f32[8,64,128]{2,1,0:T(8,128)} %source.3) | copy-start | bytes 786436
  1.1 7.5 %collective-permute-start = (f32[7,64,128]{2,1,0:T(8,128)S(1)}, f32[7,64,128]{2,1,0:T(8,128)S(1)}, u32[]{:S(2)}, u32[]{:S(2)}) collective-permute-start(f32[7,64,128]{2,1,0:T(8,128)S(1)} %pad_maximum_fusion), channel_id=1, source_target_pairs={{0,8},{8,16},{16,24},{24,32},{32,40},{40,48},{48,56},{56,64},{64,7... | collective-permute-start | bytes 688136 | tf_op jit(solution)/shard_map/ppermute | solution.py:506
  5.7 6.9 %collective-permute-start.1 = (f32[7,64,128]{2,1,0:T(8,128)S(1)}, f32[7,64,128]{2,1,0:T(8,128)S(1)}, u32[]{:S(2)}, u32[]{:S(2)}) collective-permute-start(f32[7,64,128]{2,1,0:T(8,128)S(1)} %pad_maximum_fusion.1), channel_id=1, source_target_pairs={{8,0},{16,8},{24,16},{32,24},{40,32},{48,40},{56,48},{64,56},{72,6... | collective-permute-start | bytes 688136 | tf_op jit(solution)/shard_map/ppermute | solution.py:506
  12.6 8.3 %collective-permute-start.2 = (f32[16,8,128]{2,1,0:T(8,128)S(1)}, f32[16,8,128]{2,1,0:T(8,128)S(1)}, u32[]{:S(2)}, u32[]{:S(2)}) collective-permute-start(f32[16,8,128]{2,1,0:T(8,128)S(1)} %get-tuple-element.23), channel_id=1, source_target_pairs={{0,1},{1,2},{2,3},{3,4},{4,5},{5,6},{6,7},{8,9},{9,10},{10,11},{11... | collective-permute-start | bytes 196616 | tf_op jit(solution)/shard_map/ppermute | solution.py:506
  18.9 5.6 %collective-permute-start.3 = (f32[16,8,128]{2,1,0:T(8,128)S(1)}, f32[16,8,128]{2,1,0:T(8,128)S(1)}, u32[]{:S(2)}, u32[]{:S(2)}) collective-permute-start(f32[16,8,128]{2,1,0:T(8,128)S(1)} %get-tuple-element.24), channel_id=1, source_target_pairs={{1,0},{2,1},{3,2},{4,3},{5,4},{6,5},{7,6},{9,8},{10,9},{11,10},{12... | collective-permute-start | bytes 196616 | tf_op jit(solution)/shard_map/ppermute | solution.py:506
  26.7 5.9 %collective-permute-start.5 = (f32[8,32,128]{2,1,0:T(8,128)S(1)}, f32[8,32,128]{2,1,0:T(8,128)S(1)}, u32[]{:S(2)}, u32[]{:S(2)}) collective-permute-start(f32[8,32,128]{2,1,0:T(8,128)S(1)} %get-tuple-element.25.refs_1_.own_ref), channel_id=1, source_target_pairs={{8,0},{16,8},{24,16},{32,24},{40,32},{48,40},{56,48},{64,56},{72,6... | collective-permute-start | bytes 393224 | tf_op jit(solution)/shard_map/ppermute | solution.py:506
  28.0 6.1 %collective-permute-start.4 = (f32[8,32,128]{2,1,0:T(8,128)S(1)}, f32[8,32,128]{2,1,0:T(8,128)S(1)}, u32[]{:S(2)}, u32[]{:S(2)}) collective-permute-start(f32[8,32,128]{2,1,0:T(8,128)S(1)} %get-tuple-element.25.refs_1_.own_ref), channel_id=1, source_target_pairs={{0,8},{8,16},{16,24},{24,32},{32,40},{40,48},{48,56},{56,64},{64,7... | collective-permute-start | bytes 393224 | tf_op jit(solution)/shard_map/ppermute | solution.py:506
  34.1 5.5 %collective-permute-start.6 = (f32[24,8,128]{2,1,0:T(8,128)S(1)}, f32[24,8,128]{2,1,0:T(8,128)S(1)}, u32[]{:S(2)}, u32[]{:S(2)}) collective-permute-start(f32[24,8,128]{2,1,0:T(8,128)S(1)} %get-tuple-element.26), channel_id=1, source_target_pairs={{0,1},{1,2},{2,3},{3,4},{4,5},{5,6},{6,7},{8,9},{9,10},{10,11},{11... | collective-permute-start | bytes 294920 | tf_op jit(solution)/shard_map/ppermute | solution.py:506
  37.7 5.9 %collective-permute-start.7 = (f32[24,8,128]{2,1,0:T(8,128)S(1)}, f32[24,8,128]{2,1,0:T(8,128)S(1)}, u32[]{:S(2)}, u32[]{:S(2)}) collective-permute-start(f32[24,8,128]{2,1,0:T(8,128)S(1)} %get-tuple-element.27), channel_id=1, source_target_pairs={{1,0},{2,1},{3,2},{4,3},{5,4},{6,5},{7,6},{9,8},{10,9},{11,10},{12... | collective-permute-start | bytes 294920 | tf_op jit(solution)/shard_map/ppermute | solution.py:506
  45.0 17.9 %collective-permute-start.13 = (f32[2,16,128]{2,1,0:T(8,128)S(1)}, f32[2,16,128]{2,1,0:T(8,128)S(1)}, u32[]{:S(2)}, u32[]{:S(2)}) collective-permute-start(f32[2,16,128]{2,1,0:T(8,128)S(1)} %get-tuple-element.28.refs_3_), channel_id=1, source_target_pairs={{24,0},{32,8},{40,16},{48,24},{56,32},{64,40},{72,48},{80,56},{88,... | collective-permute-start | bytes 49160 | tf_op jit(solution)/shard_map/ppermute | solution.py:506
  46.3 24.0 %collective-permute-start.12 = (f32[2,16,128]{2,1,0:T(8,128)S(1)}, f32[2,16,128]{2,1,0:T(8,128)S(1)}, u32[]{:S(2)}, u32[]{:S(2)}) collective-permute-start(f32[2,16,128]{2,1,0:T(8,128)S(1)} %get-tuple-element.28.refs_3_), channel_id=1, source_target_pairs={{16,0},{24,8},{32,16},{40,24},{48,32},{56,40},{64,48},{72,56},{80,... | collective-permute-start | bytes 49160 | tf_op jit(solution)/shard_map/ppermute | solution.py:506
  47.6 22.7 %collective-permute-start.11 = (f32[2,16,128]{2,1,0:T(8,128)S(1)}, f32[2,16,128]{2,1,0:T(8,128)S(1)}, u32[]{:S(2)}, u32[]{:S(2)}) collective-permute-start(f32[2,16,128]{2,1,0:T(8,128)S(1)} %get-tuple-element.28.refs_3_), channel_id=1, source_target_pairs={{8,0},{16,8},{24,16},{32,24},{40,32},{48,40},{56,48},{64,56},{72,6... | collective-permute-start | bytes 49160 | tf_op jit(solution)/shard_map/ppermute | solution.py:506
  48.9 21.4 %collective-permute-start.10 = (f32[2,16,128]{2,1,0:T(8,128)S(1)}, f32[2,16,128]{2,1,0:T(8,128)S(1)}, u32[]{:S(2)}, u32[]{:S(2)}) collective-permute-start(f32[2,16,128]{2,1,0:T(8,128)S(1)} %get-tuple-element.28.refs_3_), channel_id=1, source_target_pairs={{0,8},{8,16},{16,24},{24,32},{32,40},{40,48},{48,56},{56,64},{64,7... | collective-permute-start | bytes 49160 | tf_op jit(solution)/shard_map/ppermute | solution.py:506
  54.1 16.3 %collective-permute-start.9 = (f32[2,16,128]{2,1,0:T(8,128)S(1)}, f32[2,16,128]{2,1,0:T(8,128)S(1)}, u32[]{:S(2)}, u32[]{:S(2)}) collective-permute-start(f32[2,16,128]{2,1,0:T(8,128)S(1)} %get-tuple-element.28.refs_3_), channel_id=1, source_target_pairs={{0,16},{8,24},{16,32},{24,40},{32,48},{40,56},{48,64},{56,72},{64,... | collective-permute-start | bytes 49160 | tf_op jit(solution)/shard_map/ppermute | solution.py:506
  63.0 8.2 %collective-permute-start.8 = (f32[2,16,128]{2,1,0:T(8,128)S(1)}, f32[2,16,128]{2,1,0:T(8,128)S(1)}, u32[]{:S(2)}, u32[]{:S(2)}) collective-permute-start(f32[2,16,128]{2,1,0:T(8,128)S(1)} %get-tuple-element.28.refs_3_), channel_id=1, source_target_pairs={{0,24},{8,32},{16,40},{24,48},{32,56},{40,64},{48,72},{56,80},{64,... | collective-permute-start | bytes 49160 | tf_op jit(solution)/shard_map/ppermute | solution.py:506
  71.2 5.5 %collective-permute-start.14 = (f32[14,8,128]{2,1,0:T(8,128)S(1)}, f32[14,8,128]{2,1,0:T(8,128)S(1)}, u32[]{:S(2)}, u32[]{:S(2)}) collective-permute-start(f32[14,8,128]{2,1,0:T(8,128)S(1)} %get-tuple-element.29), channel_id=1, source_target_pairs={{0,1},{1,2},{2,3},{3,4},{4,5},{5,6},{6,7},{8,9},{9,10},{10,11},{11... | collective-permute-start | bytes 172040 | tf_op jit(solution)/shard_map/ppermute | solution.py:506
  74.8 5.5 %collective-permute-start.15 = (f32[14,8,128]{2,1,0:T(8,128)S(1)}, f32[14,8,128]{2,1,0:T(8,128)S(1)}, u32[]{:S(2)}, u32[]{:S(2)}) collective-permute-start(f32[14,8,128]{2,1,0:T(8,128)S(1)} %get-tuple-element.30), channel_id=1, source_target_pairs={{1,0},{2,1},{3,2},{4,3},{5,4},{6,5},{7,6},{9,8},{10,9},{11,10},{12... | collective-permute-start | bytes 172040 | tf_op jit(solution)/shard_map/ppermute | solution.py:506
  133.6 0.7 copy-start.2

commit v2 on v1

--- a/solution.py
+++ b/solution.py
@@ -44,7 +44,7 @@
 
 
 def pair_sum(value, stride):
-    odd = (lanes_of(value.shape[0]) // stride) % 2 == 1
+    odd = (lanes_of(value.shape[0]) & stride) != 0
     return value + jnp.where(odd, roll(value, stride), roll(value, -stride))
 
 
@@ -150,7 +150,8 @@
     diagonal = diagonal + half[p][0:count] + half[p][2 : 2 + count]
     diagonal = diagonal + jnp.where(lane >= stride, roll(center, stride), 0.0)
     diagonal = diagonal + jnp.where(lane < LANES - stride, roll(center, -stride), 0.0)
-    return GAIN_FIRST * source * (1.0 / (0.25**level * diagonal))
+    inverse = jnp.where(diagonal > 0.0, 1.0 / (0.25**level * diagonal), 0.0)
+    return GAIN_FIRST * source * inverse
 
 
 def cut(half_ref, planes, row, count):
@@ -180,6 +181,7 @@
     planes = bx + 8
     zero = jnp.zeros((8, LANES), jnp.float32)
     end = ROW + bz
+    has_low, has_high = inside_z(gz, cells[1] // bz)
     for p in range(planes):
         for edge in (8, end, end + 8):
             win_s[p, edge : edge + 8, :] = zero
@@ -188,8 +190,8 @@
             first[p, edge : edge + 8, :] = zero
         win_s[p, ROW - 4 : ROW, :] = z_low[p, 0:4, :]
         win_s[p, end : end + 4, :] = z_high[p, 0:4, :]
-        win_h[p, ROW - 4 : ROW, :] = 0.5 * z_low[p, 4:8, :]
-        win_h[p, end : end + 4, :] = 0.5 * z_high[p, 4:8, :]
+        win_h[p, ROW - 4 : ROW, :] = (0.5 * has_low) * z_low[p, 4:8, :]
+        win_h[p, end : end + 4, :] = (0.5 * has_high) * z_high[p, 4:8, :]
     for p in range(bx):
         win_s[p + 4, ROW:end, :] = source[p, :, :]
         win_h[p + 4, ROW:end, :] = 0.5 * cond[p, :, :]
@@ -213,11 +215,15 @@
     for p, value in enumerate(halves):
         next_half[p, :, :] = value
     own = bz // 2
-    odd = lanes_of(own) % 2 == 1
+    odd = (lanes_of(own) & 1) == 1
     padded = cut(next_half, range(bx // 2 + 2), 3, own + 2)
     for p, value in enumerate(sources):
         message[p, :, :] = jnp.where(odd, padded[p + 1][1 : 1 + own], value)
         message[p + bx // 2, :, :] = first_iterate(value, padded, p + 1, 0, own, 1, 2)
+
+
+def inside_z(gz, count):
+    return (jnp.where(gz > 0, 1.0, 0.0), jnp.where(gz < count - 1, 1.0, 0.0))
 
 
 def edge_rows(*refs):
@@ -230,15 +236,16 @@
         at += count
 
 
-def down_1(cells, pos, own_ref, low, high, z_low, z_high, win_s, win_h, guess, message, fx, fz, left, right, diag, inverse, first, temp, next_half):
+def down_1(cells, pos, own_ref, low, high, z_low, z_high, win_s, win_h, guess, to_next, to_prev, fx, fz, left, right, diag, inverse, first, temp, next_half):
     gx, gz = (pos[0], pos[1])
     bx, bz = (own_ref.shape[0] // 2, own_ref.shape[1])
     planes = 3 * bx
     end = ROW + bz
     zero = jnp.zeros((8, LANES), jnp.float32)
+    has_low, has_high = inside_z(gz, cells[1] // bz)
 
     def unpack(p, start, rows, mixed, iterate):
-        odd = lanes_of(rows) % 2 == 1
+        odd = (lanes_of(rows) & 1) == 1
         win_s[p, start : start + rows, :] = jnp.where(odd, roll(mixed, 1), mixed)
         win_h[p, start : start + rows, :] = jnp.where(odd, mixed, roll(mixed, -1))
         first[p, start : start + rows, :] = iterate
@@ -247,8 +254,8 @@
         for p in range(bx):
             q = b * bx + p
             unpack(q, ROW, bz, part[p, :, :], part[p + bx, :, :])
-            unpack(q, ROW - 8, 8, z_low[2 * b * bx + p, :, :], z_low[(2 * b + 1) * bx + p, :, :])
-            unpack(q, end, 8, z_high[2 * b * bx + p, :, :], z_high[(2 * b + 1) * bx + p, :, :])
+            unpack(q, ROW - 8, 8, has_low * z_low[2 * b * bx + p, :, :], has_low * z_low[(2 * b + 1) * bx + p, :, :])
+            unpack(q, end, 8, has_high * z_high[2 * b * bx + p, :, :], has_high * z_high[(2 * b + 1) * bx + p, :, :])
     for p in range(planes):
         for ref in (win_s, win_h, first):
             ref[p, 0:8, :] = zero
@@ -260,62 +267,83 @@
     row, count = (ROW - 4, bz + 8)
     level.coefs(range(1, planes - 1), row, count)
     level.second_down(win_s, first, guess, range(1, planes - 1), row, count)
-    sources = level.restricted_remainder(win_s, guess, temp, range(bx, 2 * bx), bz)
-    halves = restricted(win_h, temp, 2, range(bx - 2, 2 * bx + 2), ROW - 8, bz + 16)
+    sources = level.restricted_remainder(win_s, guess, temp, range(bx - 2, 2 * bx + 2), bz)
+    halves = restricted(win_h, temp, 2, range(planes), ROW - 8, bz + 16)
     for p, value in enumerate(halves):
         next_half[p, :, :] = value
     own = bz // 2
-    lane = lanes_of(own) % 4
-    padded = cut(next_half, range(bx // 2 + 2), 3, own + 2)
-    for p, value in enumerate(sources):
-        iterate = first_iterate(value, padded, p + 1, 0, own, 2, 4)
-        mixed = jnp.where(lane == 0, value, jnp.where(lane == 1, padded[p + 1][1 : 1 + own], iterate))
-        message[p, :, :] = mixed
+    lane = lanes_of(own) & 3
+    padded = cut(next_half, range(bx // 2 + 4), 3, own + 2)
+    for p, half in enumerate(padded):
+        mixed = half[1 : 1 + own]
+        if 0 < p < len(padded) - 1:
+            value = sources[p - 1]
+            iterate = first_iterate(value, padded, p, 0, own, 2, 4)
+            mixed = jnp.where(lane == 0, value, jnp.where(lane == 1, mixed, iterate))
+        else:
+            mixed = jnp.where(lane == 1, mixed, 0.0)
+        if p < bx // 2 + 2:
+            to_next[p, :, :] = mixed
+        if p >= 2:
+            to_prev[p - 2, :, :] = mixed
+
+
+def edge_rows_2(prev, here, next_, to_high, to_low):
+    at = 0
+    for part, first in ((prev, 0), (here, 2), (next_, 0)):
+        count, rows = (part.shape[0] - first, part.shape[1])
+        to_high[at : at + count, :, :] = part[first:, rows - 8 : rows, :]
+        to_low[at : at + count, :, :] = part[first:, 0:8, :]
+        at += count
 
 
 def spread(mixed, which):
-    only = jnp.where(lanes_of(mixed.shape[0]) % 4 == which, mixed, 0.0)
+    only = jnp.where((lanes_of(mixed.shape[0]) & 3) == which, mixed, 0.0)
     only = roll(only, -which) if which else only
     twice = only + roll(only, 1)
     return twice + roll(twice, 2)
 
 
-def down_2(cells, pos, *refs):
-    bricks, refs = (refs[:7], refs[7:])
-    z_low, z_high, win_s, win_h, guess, message, fx, fz, left, right, diag, inverse, first, temp = refs
+def down_2(cells, pos, prev, here, next_, z_low, z_high, win_s, win_h, guess, message, to_next, to_prev, fx, fz, left, right, diag, inverse, first, temp):
     gx, gz = (pos[0], pos[1])
-    bx, bz = bricks[0].shape[0:2]
-    planes = 7 * bx
+    bx, bz = (prev.shape[0] - 2, prev.shape[1])
+    own, planes = (bx + 2, 3 * bx + 4)
     end = ROW + bz
     zero = jnp.zeros((8, LANES), jnp.float32)
-
-    def unpack(p, start, rows, mixed):
+    has_low, has_high = inside_z(gz, cells[1] // bz)
+
+    def unpack(p, start, rows, mixed, inside):
         win_s[p, start : start + rows, :] = spread(mixed, 0)
         win_h[p, start : start + rows, :] = spread(mixed, 1)
-        first[p, start : start + rows, :] = spread(mixed, 2)
-
-    for b, part in enumerate(bricks):
-        for p in range(bx):
-            q = b * bx + p
-            unpack(q, ROW, bz, part[p, :, :])
-            unpack(q, ROW - 8, 8, z_low[q, :, :])
-            unpack(q, end, 8, z_high[q, :, :])
-    for p in range(planes):
+        first[p, start : start + rows, :] = inside * spread(mixed, 2)
+
+    bricks = [(prev, p) for p in range(bx + 2)] + [(here, p + 2) for p in range(bx)] + [(next_, p) for p in range(bx + 2)]
+    for p, (part, at) in enumerate(bricks):
+        plane = p - own + gx * bx
+        inside = jnp.where(jnp.logical_and(plane >= 0, plane < cells[0]), 1.0, 0.0)
+        unpack(p, ROW, bz, part[at, :, :], inside)
+        unpack(p, ROW - 8, 8, has_low * z_low[p, :, :], inside)
+        unpack(p, end, 8, has_high * z_high[p, :, :], inside)
         for ref in (win_s, win_h, first):
             ref[p, 0:8, :] = zero
             ref[p, end + 8 : end + 16, :] = zero
-    level = Level(2, gx, gz, (bx, bz), cells, 3 * bx, (win_h, fx, fz, left, right, diag, inverse))
+    level = Level(2, gx, gz, (bx, bz), cells, own, (win_h, fx, fz, left, right, diag, inverse))
     row, count = (ROW - 8, bz + 16)
-    own = 3 * bx
-    level.coefs(range(own - 4, own + bx + 4), row, count)
-    level.second_down(win_s, first, guess, range(own - 4, own + bx + 4), row, count)
+    level.coefs(range(own - 2, own + bx + 2), row, count)
+    level.second_down(win_s, first, guess, range(own - 2, own + bx + 2), row, count)
+    lane = lanes_of(count) & 3
+    for out, begin in ((to_next, own - 2), (to_prev, own)):
+        mixed = guess[begin, row : row + count, :]
+        for p in range(1, 4):
+            mixed = jnp.where(lane == p, guess[begin + p, row : row + count, :], mixed)
+        out[...] = mixed
     sources = level.restricted_remainder(win_s, guess, temp, range(own, own + bx), bz)
     halves = restricted(win_h, temp, 4, range(own, own + bx), ROW, bz)
     rows = bz // 2
     cell = lax.broadcasted_iota(jnp.int32, (LANES, LANES), 0)
     lane = lax.broadcasted_iota(jnp.int32, (LANES, LANES), 1)
-    pick = jnp.where((cell // 8 == lane % 16) & (cell % 8 == 0), 1.0, 0.0)
-    keep = lanes_of(rows) // 16 == rows_of(rows)
+    pick = jnp.where(((cell >> 3) == (lane & 15)) & ((cell & 7) == 0), 1.0, 0.0)
+    keep = (lanes_of(rows) >> 4) == rows_of(rows)
     for at, value in enumerate((sources[0], halves[0])):
         dense = jnp.dot(value, pick, precision=lax.Precision.HIGHEST, preferred_element_type=jnp.float32)
         message[at : at + 1, :] = jnp.sum(jnp.where(keep, dense, 0.0), axis=0, keepdims=True)
@@ -338,7 +366,7 @@
         source[pl.ds(g, planes, stride=8), :] = gathered[pl.ds(first, planes, stride=2), :]
         half[pl.ds(g, planes, stride=8), :] = gathered[pl.ds(first + 1, planes, stride=2), :]
     lane, sub = (lanes_of(8), rows_of(8))
-    in_left, in_right = (lane % 16 > 0, lane % 16 < 15)
+    in_left, in_right = ((lane & 15) > 0, (lane & 15) < 15)
     in_before = (lane >= 16) | (sub > 0)
     in_after = (lane < LANES - 16) | (sub < 7)
     zero = jnp.zeros((8, LANES), jnp.float32)
@@ -397,7 +425,7 @@
     return 1
 
 
-def finish(cells, pos, weights, gathered, s2, h2, g2, s1, h1, g1, s0, h0, g0, out, *scratch):
+def finish(cells, pos, weights, gathered, prev2, next2, s2, h2, g2, s1, h1, g1, s0, h0, g0, out, *scratch):
     gx, gz = (pos[0], pos[1])
     source3, half3, base, state, update3, coarse2, temp = scratch[:7]
     f2, f1, f0 = (scratch[7:16], scratch[16:25], scratch[25:34])
@@ -408,9 +436,9 @@
     rows = bz2 + 8
     cell = lax.broadcasted_iota(jnp.int32, (LANES, LANES), 0)
     lane = lax.broadcasted_iota(jnp.int32, (LANES, LANES), 1)
-    pick = jnp.where(cell % 16 == lane // 8, 1.0, 0.0)
-    z3 = rows_of(rows) // 2 - 2
-    keep = lanes_of(rows) // 16 == (z3 + 8) % 8
+    pick = jnp.where((cell & 15) == (lane >> 3), 1.0, 0.0)
+    z3 = (rows_of(rows) >> 1) - 2
+    keep = (lanes_of(rows) >> 4) == (z3 & 7)
     sub = rows_of(8)
     for q in range(5):
         plane = gx + q - 2
@@ -422,16 +450,19 @@
     spread_out = jnp.dot(coarse2[...], pick, precision=lax.Precision.HIGHEST, preferred_element_type=jnp.float32)
     coarse2[...] = spread_out
 
-    half_planes = s2.shape[0] // 2
     start, middle, update = f2[6:9]
-    own = half_planes - 1
+    own = 4
     row, count = (ROW - 4, rows)
     zero = jnp.zeros((8, LANES), jnp.float32)
     for q in range(5):
         for p in (own - 4 + 2 * q, own - 3 + 2 * q):
             start[p, 8:16, :] = zero
             start[p, ROW + bz2 : ROW + bz2 + 8, :] = zero
-            start[p, row : row + count, :] = g2[p, row : row + count, :] + coarse2[q * rows : (q + 1) * rows, :]
+            if q == 2:
+                guess = g2[p, row : row + count, :]
+            else:
+                guess = spread((prev2 if q < 2 else next2)[4 : 4 + count, :], p if q < 2 else p - own - bx2)
+            start[p, row : row + count, :] = guess + coarse2[q * rows : (q + 1) * rows, :]
     level = Level(2, gx, gz, (bx2, bz2), cells[2], own, (h2,) + tuple(f2[0:6]))
     level.coefs(range(own - 3, own + 5), row, count)
 
@@ -506,6 +537,11 @@
     return lax.ppermute(array, axis, [(i, i + by) for i in range(devices) if 0 <= i + by < devices])
 
 
+def turn(array, axis, by):
+    devices = lax.axis_size(axis)
+    return lax.ppermute(array, axis, [(i, (i + by) % devices) for i in range(devices)])
+
+
 def on_device(right_side, conductivity):
     nx, nz = (lax.axis_size("gx"), lax.axis_size("gz"))
     bx, bz = right_side.shape[0:2]
@@ -519,7 +555,7 @@
     to_high, to_low = call(
         edge_rows_0, "edge_rows_0", [f32(planes, 8, LANES)] * 2, [], 0, right_side, conductivity, low, high
     )
-    z_low, z_high = (shift(to_high, "gz", 1), shift(to_low, "gz", -1))
+    z_low, z_high = (turn(to_high, "gz", 1), turn(to_low, "gz", -1))
     window = (planes, bz + 32, LANES)
     s0, h0, g0, brick1 = call(
         functools.partial(down_0, cells[0]),
@@ -538,14 +574,14 @@
 
     low, high = (shift(brick1, "gx", 1), shift(brick1, "gx", -1))
     to_high, to_low = call(edge_rows, "edge_rows_1", [f32(3 * bx, 8, LANES)] * 2, [], 0, low, brick1, high)
-    z_low, z_high = (shift(to_high, "gz", 1), shift(to_low, "gz", -1))
+    z_low, z_high = (turn(to_high, "gz", 1), turn(to_low, "gz", -1))
     bx, bz = (bx // 2, bz // 2)
     window1 = (3 * bx, bz + 32, LANES)
-    s1, h1, g1, brick2 = call(
+    s1, h1, g1, for_next, for_prev = call(
         functools.partial(down_1, cells[1]),
         "down_1",
-        [f32(*window1)] * 3 + [f32(bx // 2, bz // 2, LANES)],
-        [scratch(*window1)] * 7 + [scratch(bz + 16, LANES), scratch(bx // 2 + 2, bz // 2 + 8, LANES)],
+        [f32(*window1)] * 3 + [f32(bx // 2 + 2, bz // 2, LANES)] * 2,
+        [scratch(*window1)] * 7 + [scratch(bz + 16, LANES), scratch(bx // 2 + 4, bz // 2 + 8, LANES)],
         1,
         pos,
         brick1,
@@ -556,14 +592,14 @@
     )
 
     bx, bz = (bx // 2, bz // 2)
-    bricks = [shift(brick2, "gx", by) if by else brick2 for by in (3, 2, 1, 0, -1, -2, -3)]
-    to_high, to_low = call(edge_rows, "edge_rows_2", [f32(7 * bx, 8, LANES)] * 2, [], 0, *bricks)
-    z_low, z_high = (shift(to_high, "gz", 1), shift(to_low, "gz", -1))
-    window2 = (7 * bx, bz + 32, LANES)
-    s2, h2, g2, brick3 = call(
+    bricks = [shift(for_next, "gx", 1), for_next, shift(for_prev, "gx", -1)]
+    to_high, to_low = call(edge_rows_2, "edge_rows_2", [f32(3 * bx + 4, 8, LANES)] * 2, [], 0, *bricks)
+    z_low, z_high = (turn(to_high, "gz", 1), turn(to_low, "gz", -1))
+    window2 = (3 * bx + 4, bz + 32, LANES)
+    s2, h2, g2, brick3, for_next, for_prev = call(
         functools.partial(down_2, cells[2]),
         "down_2",
-        [f32(*window2)] * 3 + [f32(2, LANES)],
+        [f32(*window2)] * 3 + [f32(2, LANES)] + [f32(bz + 16, LANES)] * 2,
         [scratch(*window2)] * 7 + [scratch(bz + 16, LANES)],
         1,
         pos,
@@ -571,6 +607,8 @@
         z_low,
         z_high,
     )
+
+    prev2, next2 = (shift(for_next, "gx", 1), shift(for_prev, "gx", -1))
 
     everywhere = lax.all_to_all(jnp.broadcast_to(brick3[None], (nx, 2, LANES)), "gx", 0, 0, tiled=True)
     gathered = lax.all_gather(everywhere, "gz", axis=0).reshape(nz * 2 * nx, LANES)
@@ -584,7 +622,7 @@
     )
     (result,) = call(
         functools.partial(finish, cells), "finish", [f32(*right_side.shape)], work, 2, pos, weights, gathered,
-        s2, h2, g2, s1, h1, g1, s0, h0, g0,
+        prev2, next2, s2, h2, g2, s1, h1, g1, s0, h0, g0,
     )
     return result
 

time: 144 us -> 124 us (0.86)
  blocking collectives: 46.7 us -> 16.4 us
  local copies, waits for them, and re-layouts: 1.79 us -> 9.05 us
  waiting for transfers between devices: 19.5 us -> 26 us
  Pallas kernels: 19.7 us -> 16.7 us
    ppermute x16 -> x8, starting transfers between devices: 55.6 us -> 22.2 us  [shift(): lax.ppermute(array, axis, [(i, i + by) for i in range(devices) if 0 <= i...]
    all_to_all x1 -> x0, blocking collectives: 32.8 us -> none  [on_device(): lax.all_to_all(jnp.broadcast_to(brick3[None], (nx, 2, LANES)), 'gx', 0, 0...]
    all_to_all x0 -> x1, starting transfers between devices: none -> 23.1 us  [on_device(): lax.all_to_all(jnp.broadcast_to(brick3[None], (nx, 2, LANES)), 'gx', 0, 0...]
    ppermute x16 -> x8, waiting for transfers between devices: 19.5 us -> 8.56 us  [shift(): lax.ppermute(array, axis, [(i, i + by) for i in range(devices) if 0 <= i...]
    ppermute x0 -> x6, starting transfers between devices: none -> 9.62 us  [turn(): lax.ppermute(array, axis, [(i, (i + by) % devices) for i in range(devices)])]
    all_to_all x0 -> x1, waiting for transfers between devices: none -> 9.3 us  [on_device(): lax.all_to_all(jnp.broadcast_to(brick3[None], (nx, 2, LANES)), 'gx', 0, 0...]
    ppermute x0 -> x6, waiting for transfers between devices: none -> 8.13 us  [turn(): lax.ppermute(array, axis, [(i, (i + by) % devices) for i in range(devices)])]
    unnamed x6 -> x22, local copies, waits for them, and re-layouts: 0.76 us -> 7.39 us
  transfers between devices with their start and end apart: 16 -> 15, of which waited for: 8 -> 12; matrix products, arithmetic and copies ran while one was open for 0% -> 0% of each run, Pallas kernels for 0% -> 0%
where the time goes in v2:
time: 124 us; the launch traced here: 123 us
  starting transfers between devices  55 us (44%)
  waiting for transfers between devices  26 us (21%)
  Pallas kernels  16.7 us (13%)
  blocking collectives  16.4 us (13%)
  local copies, waits for them, and re-layouts  9.05 us (7%)
    all_to_all x1, starting transfers between devices, on_device(): lax.all_to_all(jnp.broadcast_to(brick3[None], (nx, 2, LANES)), 'gx', 0, 0...  23.1 us
    ppermute x8, starting transfers between devices, shift(): lax.ppermute(array, axis, [(i, i + by) for i in range(devices) if 0 <= i...  22.2 us
    pallas_call x7, Pallas kernels, call(): pl.pallas_call(kernel, name=name, out_shape=outs, in_specs=[smem] * scala...  16.7 us
    all_gather x1, blocking collectives, on_device(): lax.all_gather(everywhere, 'gz', axis=0).reshape(nz * 2 * nx, LANES)  16.4 us
    ppermute x6, starting transfers between devices, turn(): lax.ppermute(array, axis, [(i, (i + by) % devices) for i in range(devices)])  9.62 us
    all_to_all x1, waiting for transfers between devices, on_device(): lax.all_to_all(jnp.broadcast_to(brick3[None], (nx, 2, LANES)), 'gx', 0, 0...  9.3 us
    ppermute x8, waiting for transfers between devices, shift(): lax.ppermute(array, axis, [(i, i + by) for i in range(devices) if 0 <= i...  8.56 us
    ppermute x6, waiting for transfers between devices, turn(): lax.ppermute(array, axis, [(i, (i + by) % devices) for i in range(devices)])  8.13 us
  transfers between devices with their start and end apart: 15, of which 12 were waited for; matrix products, arithmetic and copies ran while one was open for 0% of the time, Pallas kernels for 0%

profile of v2, /device:TPU:1, one launch (start us, length us, event | category | flops | bytes accessed | tf_op | source)
XLA Modules:
  0.0 123.4 jit_solution(13435099380164625278)
XLA Ops:
  0.0 1.0 fusion
  1.1 4.5 %collective-permute-start = (f32[7,64,128]{2,1,0:T(8,128)S(1)}, f32[7,64,128]{2,1,0:T(8,128)S(1)}, u32[]{:S(2)}, u32[]{:S(2)}) collective-permute-start(f32[7,64,128]{2,1,0:T(8,128)S(1)} %pad_maximum_fusion), channel_id=1, source_target_pairs={{0,8},{8,16},{16,24},{24,32},{32,40},{40,48},{48,56},{56,64},{64,7... | collective-permute-start | bytes 688136 | tf_op jit(solution)/shard_map/ppermute | solution.py:537
  5.7 1.3 %collective-permute-start.1 = (f32[7,64,128]{2,1,0:T(8,128)S(1)}, f32[7,64,128]{2,1,0:T(8,128)S(1)}, u32[]{:S(2)}, u32[]{:S(2)}) collective-permute-start(f32[7,64,128]{2,1,0:T(8,128)S(1)} %pad_maximum_fusion.1), channel_id=1, source_target_pairs={{8,0},{16,8},{24,16},{32,24},{40,32},{48,40},{56,48},{64,56},{72,6... | collective-permute-start | bytes 688136 | tf_op jit(solution)/shard_map/ppermute | solution.py:537
  7.0 1.6 %collective-permute-done.low = f32[7,64,128]{2,1,0:T(8,128)S(1)} collective-permute-done((f32[7,64,128]{2,1,0:T(8,128)S(1)}, f32[7,64,128]{2,1,0:T(8,128)S(1)}, u32[]{:S(2)}, u32[]{:S(2)}) %collective-permute-start) | collective-permute-done | bytes 229408 | tf_op jit(solution)/shard_map/ppermute | solution.py:537
  8.6 4.0 %collective-permute-done.1.high = f32[7,64,128]{2,1,0:T(8,128)S(1)} collective-permute-done((f32[7,64,128]{2,1,0:T(8,128)S(1)}, f32[7,64,128]{2,1,0:T(8,128)S(1)}, u32[]{:S(2)}, u32[]{:S(2)}) %collective-permute-start.1) | collective-permute-done | bytes 229408 | tf_op jit(solution)/shard_map/ppermute | solution.py:537
  12.6 4.3 %collective-permute-start.2 = (f32[16,8,128]{2,1,0:T(8,128)S(1)}, f32[16,8,128]{2,1,0:T(8,128)S(1)}, u32[]{:S(2)}, u32[]{:S(2)}) collective-permute-start(f32[16,8,128]{2,1,0:T(8,128)S(1)} %get-tuple-element.26), channel_id=1, source_target_pairs={{0,1},{1,2},{2,3},{3,4},{4,5},{5,6},{6,7},{7,0},{8,9},{9,10},{10,1... | collective-permute-start | bytes 196616 | tf_op jit(solution)/shard_map/ppermute | solution.py:542
  17.5 0.8 collective-permute-done.2.z_low
  18.3 2.4 %collective-permute-done.3.z_high = f32[16,8,128]{2,1,0:T(8,128)S(1)} collective-permute-done((f32[16,8,128]{2,1,0:T(8,128)S(1)}, f32[16,8,128]{2,1,0:T(8,128)S(1)}, u32[]{:S(2)}, u32[]{:S(2)}) %collective-permute-start.3) | collective-permute-done | bytes 65568 | tf_op jit(solution)/shard_map/ppermute | solution.py:542
  20.7 2.2 %down_0.1 = (f32[16,96,128]{2,1,0:T(8,128)S(1)}, f32[16,96,128]{2,1,0:T(8,128)S(1)}, f32[16,96,128]{2,1,0:T(8,128)S(1)}, f32[8,32,128]{2,1,0:T(8,128)S(1)}) custom-call(s32[2]{0:T(128)S(1)} %pad_add_fusion.pos, f32[8,64,128]{2,1,0:T(8,128)S(1)} %copy-done.1, f32[8,64,128]{2,1,0:T(8,128)S(1)} %copy-done, f32[7,64,128]{2,1,0:T(8,128)S(1)} %collective-permute-done.low, ...), custom_call_target="tpu_custom_call" | custom-call | tf_op jit(solution)/shard_map/down_0/pallas_call | solution.py:524
  22.9 1.3 %collective-permute-start.5 = (f32[8,32,128]{2,1,0:T(8,128)S(1)}, f32[8,32,128]{2,1,0:T(8,128)S(1)}, u32[]{:S(2)}, u32[]{:S(2)}) collective-permute-start(f32[8,32,128]{2,1,0:T(8,128)S(1)} %get-tuple-element.28.refs_1_.own_ref), channel_id=1, source_target_pairs={{8,0},{16,8},{24,16},{32,24},{40,32},{48,40},{56,48},{64,56},{72,6... | collective-permute-start | bytes 393224 | tf_op jit(solution)/shard_map/ppermute | solution.py:537
  24.2 4.2 %collective-permute-start.4 = (f32[8,32,128]{2,1,0:T(8,128)S(1)}, f32[8,32,128]{2,1,0:T(8,128)S(1)}, u32[]{:S(2)}, u32[]{:S(2)}) collective-permute-start(f32[8,32,128]{2,1,0:T(8,128)S(1)} %get-tuple-element.28.refs_1_.own_ref), channel_id=1, source_target_pairs={{0,8},{8,16},{16,24},{24,32},{32,40},{40,48},{48,56},{56,64},{64,7... | collective-permute-start | bytes 393224 | tf_op jit(solution)/shard_map/ppermute | solution.py:537
  28.8 1.5 %collective-permute-done.4.refs_0_.low = f32[8,32,128]{2,1,0:T(8,128)S(1)} collective-permute-done((f32[8,32,128]{2,1,0:T(8,128)S(1)}, f32[8,32,128]{2,1,0:T(8,128)S(1)}, u32[]{:S(2)}, u32[]{:S(2)}) %collective-permute-start.4) | collective-permute-done | bytes 131104 | tf_op jit(solution)/shard_map/ppermute | solution.py:537
  30.3 1.8 %collective-permute-start.6 = (f32[24,8,128]{2,1,0:T(8,128)S(1)}, f32[24,8,128]{2,1,0:T(8,128)S(1)}, u32[]{:S(2)}, u32[]{:S(2)}) collective-permute-start(f32[24,8,128]{2,1,0:T(8,128)S(1)} %get-tuple-element.29), channel_id=1, source_target_pairs={{0,1},{1,2},{2,3},{3,4},{4,5},{5,6},{6,7},{7,0},{8,9},{9,10},{10,1... | collective-permute-start | bytes 294920 | tf_op jit(solution)/shard_map/ppermute | solution.py:542
  32.1 0.9 collective-permute-start.7
  33.7 2.4 %collective-permute-done.7.z_high = f32[24,8,128]{2,1,0:T(8,128)S(1)} collective-permute-done((f32[24,8,128]{2,1,0:T(8,128)S(1)}, f32[24,8,128]{2,1,0:T(8,128)S(1)}, u32[]{:S(2)}, u32[]{:S(2)}) %collective-permute-start.7) | collective-permute-done | bytes 98336 | tf_op jit(solution)/shard_map/ppermute | solution.py:542
  36.1 1.6 %down_1.1 = (f32[12,64,128]{2,1,0:T(8,128)S(1)}, f32[12,64,128]{2,1,0:T(8,128)S(1)}, f32[12,64,128]{2,1,0:T(8,128)S(1)}, f32[4,16,128]{2,1,0:T(8,128)S(1)}, f32[4,16,128]{2,1,0:T(8,128)S(1)}) custom-call(s32[2]{0:T(128)S(1)} %pad_add_fusion.pos, f32[8,32,128]{2,1,0:T(8,128)S(1)} %get-tuple-element.28.refs_1_.own_ref, ...), custom_call_target="tpu_custom_call" | custom-call | tf_op jit(solution)/shard_map/down_1/pallas_call | solution.py:524
  38.4 1.3 %collective-permute-start.9 = (f32[4,16,128]{2,1,0:T(8,128)S(1)}, f32[4,16,128]{2,1,0:T(8,128)S(1)}, u32[]{:S(2)}, u32[]{:S(2)}) collective-permute-start(f32[4,16,128]{2,1,0:T(8,128)S(1)} %get-tuple-element.32), channel_id=1, source_target_pairs={{8,0},{16,8},{24,16},{32,24},{40,32},{48,40},{56,48},{64,56},{72,6... | collective-permute-start | bytes 98312 | tf_op jit(solution)/shard_map/ppermute | solution.py:537
  39.7 5.5 %collective-permute-start.8 = (f32[4,16,128]{2,1,0:T(8,128)S(1)}, f32[4,16,128]{2,1,0:T(8,128)S(1)}, u32[]{:S(2)}, u32[]{:S(2)}) collective-permute-start(f32[4,16,128]{2,1,0:T(8,128)S(1)} %get-tuple-element.31.here), channel_id=1, source_target_pairs={{0,8},{8,16},{16,24},{24,32},{32,40},{40,48},{48,56},{56,64},{64,7... | collective-permute-start | bytes 98312 | tf_op jit(solution)/shard_map/ppermute | solution.py:537
  45.2 1.0 collective-permute-done.8.prev
  46.8 1.6 %collective-permute-start.11 = (f32[10,8,128]{2,1,0:T(8,128)S(1)}, f32[10,8,128]{2,1,0:T(8,128)S(1)}, u32[]{:S(2)}, u32[]{:S(2)}) collective-permute-start(f32[10,8,128]{2,1,0:T(8,128)S(1)} %get-tuple-element.34), channel_id=1, source_target_pairs={{0,7},{1,0},{2,1},{3,2},{4,3},{5,4},{6,5},{7,6},{8,15},{9,8},{10,9... | collective-permute-start | bytes 122888 | tf_op jit(solution)/shard_map/ppermute | solution.py:542
  49.1 1.1 collective-permute-done.11.z_high
  50.2 2.6 %down_2.1 = (f32[10,48,128]{2,1,0:T(8,128)S(1)}, f32[10,48,128]{2,1,0:T(8,128)S(1)}, f32[10,48,128]{2,1,0:T(8,128)S(1)}, f32[2,128]{1,0:T(2,128)S(1)}, f32[32,128]{1,0:T(8,128)S(1)}, /*index=5*/f32[32,128]{1,0:T(8,128)S(1)}) custom-call(s32[2]{0:T(128)S(1)} %pad_add_fusion.pos, f32[4,16,128]{2,1,0:T(8,128)S(1)} %collective-permute-done.8.prev, ...), custom_call_target="tpu_custom_call" | custom-call | tf_op jit(solution)/shard_map/down_2/pallas_call | solution.py:524
  55.6 23.1 %all-to-all-start = ((f32[64,2,128]{2,1,0:T(2,128)}), f32[64,2,128]{2,1,0:T(2,128)S(1)}, u32[]{:S(2)}, u32[]{:S(2)}) async-start(f32[64,2,128]{2,1,0:T(2,128)} %broadcast_in_dim.2), calls=%async_computation | async-start | bytes 131072 | tf_op jit(solution)/shard_map/all_to_all | solution.py:613
  78.7 2.9 %collective-permute-start.12 = (f32[32,128]{1,0:T(8,128)S(1)}, f32[32,128]{1,0:T(8,128)S(1)}, u32[]{:S(2)}, u32[]{:S(2)}) collective-permute-start(f32[32,128]{1,0:T(8,128)S(1)} %get-tuple-element.36), channel_id=1, source_target_pairs={{0,8},{8,16},{16,24},{24,32},{32,40},{40,48},{48,56},{56,64},{64,7... | collective-permute-start | bytes 49160 | tf_op jit(solution)/shard_map/ppermute | solution.py:537
  81.6 1.3 %collective-permute-start.13 = (f32[32,128]{1,0:T(8,128)S(1)}, f32[32,128]{1,0:T(8,128)S(1)}, u32[]{:S(2)}, u32[]{:S(2)}) collective-permute-start(f32[32,128]{1,0:T(8,128)S(1)} %get-tuple-element.37), channel_id=1, source_target_pairs={{8,0},{16,8},{24,16},{32,24},{40,32},{48,40},{56,48},{64,56},{72,6... | collective-permute-start | bytes 49160 | tf_op jit(solution)/shard_map/ppermute | solution.py:537
  82.9 9.3 %all-to-all-done = f32[64,2,128]{2,1,0:T(2,128)S(1)} async-done(((f32[64,2,128]{2,1,0:T(2,128)}), f32[64,2,128]{2,1,0:T(2,128)S(1)}, u32[]{:S(2)}, u32[]{:S(2)}) %all-to-all-start) | async-done | bytes 65568 | tf_op jit(solution)/shard_map/all_to_all | solution.py:613
  92.2 16.4 %all-gather = f32[512,2,128]{2,1,0:T(2,128)S(1)} all-gather(f32[64,2,128]{2,1,0:T(2,128)S(1)} %all-to-all-done), channel_id=2, replica_groups=mesh['gx'=64,'gz'=8] {'gz'}, dimensions={0}, use_global_device_ids=true | all-gather | bytes 589824 | tf_op jit(solution)/shard_map/all_gather | solution.py:614
  109.4 1.0 copy-done.3
  110.4 0.9 copy-done.5
  111.3 0.9 copy-done.7
  112.3 0.9 copy-done.9
  113.2 10.2 %finish.1 = f32[8,64,128]{2,1,0:T(8,128)} custom-call(s32[2]{0:T(128)S(1)} %pad_add_fusion.pos, f32[20,2]{1,0:T(8,128)S(1)} %copy-done.10, f32[1024,128]{1,0:T(8,128)S(1)} %bitcast.3, f32[32,128]{1,0:T(8,128)S(1)} %collective-permute-done.12.prev2, f32[32,128]{1,0:T(8,128)S(1)} %collective-permute-done.13.next2, f32[10,48,128]{2,1,0:T(8,128)S(1)} %copy-done.5, ...), custom_call_target="tpu_custom_call" | custom-call | tf_op jit(solution)/shard_map/finish/pallas_call | solution.py:524
  (34 shorter events, 7.3 us)
Async XLA Ops:
  0.0 1.0 copy-start
  1.1 11.5 %copy-start.1 = (f32[8,64,128]{2,1,0:T(8,128)S(1)}, f32[8,64,128]{2,1,0:T(8,128)}, u32[]{:S(2)}) copy-start(f32[8,64,128]{2,1,0:T(8,128)} %source.3) | copy-start | bytes 786436
  1.1 7.5 %collective-permute-start = (f32[7,64,128]{2,1,0:T(8,128)S(1)}, f32[7,64,128]{2,1,0:T(8,128)S(1)}, u32[]{:S(2)}, u32[]{:S(2)}) collective-permute-start(f32[7,64,128]{2,1,0:T(8,128)S(1)} %pad_maximum_fusion), channel_id=1, source_target_pairs={{0,8},{8,16},{16,24},{24,32},{32,40},{40,48},{48,56},{56,64},{64,7... | collective-permute-start | bytes 688136 | tf_op jit(solution)/shard_map/ppermute | solution.py:537
  5.7 6.9 %collective-permute-start.1 = (f32[7,64,128]{2,1,0:T(8,128)S(1)}, f32[7,64,128]{2,1,0:T(8,128)S(1)}, u32[]{:S(2)}, u32[]{:S(2)}) collective-permute-start(f32[7,64,128]{2,1,0:T(8,128)S(1)} %pad_maximum_fusion.1), channel_id=1, source_target_pairs={{8,0},{16,8},{24,16},{32,24},{40,32},{48,40},{56,48},{64,56},{72,6... | collective-permute-start | bytes 688136 | tf_op jit(solution)/shard_map/ppermute | solution.py:537
  12.6 5.7 %collective-permute-start.2 = (f32[16,8,128]{2,1,0:T(8,128)S(1)}, f32[16,8,128]{2,1,0:T(8,128)S(1)}, u32[]{:S(2)}, u32[]{:S(2)}) collective-permute-start(f32[16,8,128]{2,1,0:T(8,128)S(1)} %get-tuple-element.26), channel_id=1, source_target_pairs={{0,1},{1,2},{2,3},{3,4},{4,5},{5,6},{6,7},{7,0},{8,9},{9,10},{10,1... | collective-permute-start | bytes 196616 | tf_op jit(solution)/shard_map/ppermute | solution.py:542
  17.0 3.7 %collective-permute-start.3 = (f32[16,8,128]{2,1,0:T(8,128)S(1)}, f32[16,8,128]{2,1,0:T(8,128)S(1)}, u32[]{:S(2)}, u32[]{:S(2)}) collective-permute-start(f32[16,8,128]{2,1,0:T(8,128)S(1)} %get-tuple-element.27), channel_id=1, source_target_pairs={{0,7},{1,0},{2,1},{3,2},{4,3},{5,4},{6,5},{7,6},{8,15},{9,8},{10,9... | collective-permute-start | bytes 196616 | tf_op jit(solution)/shard_map/ppermute | solution.py:542
  22.9 5.9 %collective-permute-start.5 = (f32[8,32,128]{2,1,0:T(8,128)S(1)}, f32[8,32,128]{2,1,0:T(8,128)S(1)}, u32[]{:S(2)}, u32[]{:S(2)}) collective-permute-start(f32[8,32,128]{2,1,0:T(8,128)S(1)} %get-tuple-element.28.refs_1_.own_ref), channel_id=1, source_target_pairs={{8,0},{16,8},{24,16},{32,24},{40,32},{48,40},{56,48},{64,56},{72,6... | collective-permute-start | bytes 393224 | tf_op jit(solution)/shard_map/ppermute | solution.py:537
  24.2 6.1 %collective-permute-start.4 = (f32[8,32,128]{2,1,0:T(8,128)S(1)}, f32[8,32,128]{2,1,0:T(8,128)S(1)}, u32[]{:S(2)}, u32[]{:S(2)}) collective-permute-start(f32[8,32,128]{2,1,0:T(8,128)S(1)} %get-tuple-element.28.refs_1_.own_ref), channel_id=1, source_target_pairs={{0,8},{8,16},{16,24},{24,32},{32,40},{40,48},{48,56},{56,64},{64,7... | collective-permute-start | bytes 393224 | tf_op jit(solution)/shard_map/ppermute | solution.py:537
  30.3 3.4 %collective-permute-start.6 = (f32[24,8,128]{2,1,0:T(8,128)S(1)}, f32[24,8,128]{2,1,0:T(8,128)S(1)}, u32[]{:S(2)}, u32[]{:S(2)}) collective-permute-start(f32[24,8,128]{2,1,0:T(8,128)S(1)} %get-tuple-element.29), channel_id=1, source_target_pairs={{0,1},{1,2},{2,3},{3,4},{4,5},{5,6},{6,7},{7,0},{8,9},{9,10},{10,1... | collective-permute-start | bytes 294920 | tf_op jit(solution)/shard_map/ppermute | solution.py:542
  32.1 4.0 %collective-permute-start.7 = (f32[24,8,128]{2,1,0:T(8,128)S(1)}, f32[24,8,128]{2,1,0:T(8,128)S(1)}, u32[]{:S(2)}, u32[]{:S(2)}) collective-permute-start(f32[24,8,128]{2,1,0:T(8,128)S(1)} %get-tuple-element.30), channel_id=1, source_target_pairs={{0,7},{1,0},{2,1},{3,2},{4,3},{5,4},{6,5},{7,6},{8,15},{9,8},{10,9... | collective-permute-start | bytes 294920 | tf_op jit(solution)/shard_map/ppermute | solution.py:542
  37.7 0.7 copy-start.2
  38.4 6.8 %collective-permute-start.9 = (f32[4,16,128]{2,1,0:T(8,128)S(1)}, f32[4,16,128]{2,1,0:T(8,128)S(1)}, u32[]{:S(2)}, u32[]{:S(2)}) collective-permute-start(f32[4,16,128]{2,1,0:T(8,128)S(1)} %get-tuple-element.32), channel_id=1, source_target_pairs={{8,0},{16,8},{24,16},{32,24},{40,32},{48,40},{56,48},{64,56},{72,6... | collective-permute-start | bytes 98312 | tf_op jit(solution)/shard_map/ppermute | solution.py:537
  39.7 6.5 %collective-permute-start.8 = (f32[4,16,128]{2,1,0:T(8,128)S(1)}, f32[4,16,128]{2,1,0:T(8,128)S(1)}, u32[]{:S(2)}, u32[]{:S(2)}) collective-permute-start(f32[4,16,128]{2,1,0:T(8,128)S(1)} %get-tuple-element.31.here), channel_id=1, source_target_pairs={{0,8},{8,16},{16,24},{24,32},{32,40},{40,48},{48,56},{56,64},{64,7... | collective-permute-start | bytes 98312 | tf_op jit(solution)/shard_map/ppermute | solution.py:537
  46.2 2.9 %collective-permute-start.10 = (f32[10,8,128]{2,1,0:T(8,128)S(1)}, f32[10,8,128]{2,1,0:T(8,128)S(1)}, u32[]{:S(2)}, u32[]{:S(2)}) collective-permute-start(f32[10,8,128]{2,1,0:T(8,128)S(1)} %get-tuple-element.33), channel_id=1, source_target_pairs={{0,1},{1,2},{2,3},{3,4},{4,5},{5,6},{6,7},{7,0},{8,9},{9,10},{10,1... | collective-permute-start | bytes 122888 | tf_op jit(solution)/shard_map/ppermute | solution.py:542
  46.8 3.4 %collective-permute-start.11 = (f32[10,8,128]{2,1,0:T(8,128)S(1)}, f32[10,8,128]{2,1,0:T(8,128)S(1)}, u32[]{:S(2)}, u32[]{:S(2)}) collective-permute-start(f32[10,8,128]{2,1,0:T(8,128)S(1)} %get-tuple-element.34), channel_id=1, source_target_pairs={{0,7},{1,0},{2,1},{3,2},{4,3},{5,4},{6,5},{7,6},{8,15},{9,8},{10,9... | collective-permute-start | bytes 122888 | tf_op jit(solution)/shard_map/ppermute | solution.py:542
  52.9 0.7 copy-start.4
  53.6 0.7 copy-start.6
  54.3 0.7 copy-start.8
  55.6 36.6 %all-to-all-start = ((f32[64,2,128]{2,1,0:T(2,128)}), f32[64,2,128]{2,1,0:T(2,128)S(1)}, u32[]{:S(2)}, u32[]{:S(2)}) async-start(f32[64,2,128]{2,1,0:T(2,128)} %broadcast_in_dim.2), calls=%async_computation | async-start | bytes 131072 | tf_op jit(solution)/shard_map/all_to_all | solution.py:613
  78.7 30.0 %collective-permute-start.12 = (f32[32,128]{1,0:T(8,128)S(1)}, f32[32,128]{1,0:T(8,128)S(1)}, u32[]{:S(2)}, u32[]{:S(2)}) collective-permute-start(f32[32,128]{1,0:T(8,128)S(1)} %get-tuple-element.36), channel_id=1, source_target_pairs={{0,8},{8,16},{16,24},{24,32},{32,40},{40,48},{48,56},{56,64},{64,7... | collective-permute-start | bytes 49160 | tf_op jit(solution)/shard_map/ppermute | solution.py:537
  81.6 27.1 %collective-permute-start.13 = (f32[32,128]{1,0:T(8,128)S(1)}, f32[32,128]{1,0:T(8,128)S(1)}, u32[]{:S(2)}, u32[]{:S(2)}) collective-permute-start(f32[32,128]{1,0:T(8,128)S(1)} %get-tuple-element.37), channel_id=1, source_target_pairs={{8,0},{16,8},{24,16},{32,24},{40,32},{48,40},{56,48},{64,56},{72,6... | collective-permute-start | bytes 49160 | tf_op jit(solution)/shard_map/ppermute | solution.py:537
  108.7 0.7 copy-start.10
  109.4 1.0 copy-start.3
  110.4 0.9 copy-start.5
  111.3 0.9 copy-start.7
  112.3 0.9 copy-start.9

commit v3 on v2

v3 whole, which is shorter than its diff:
```python
import functools
import math

import jax
import jax.numpy as jnp
from jax import lax
from jax.experimental import pallas as pl
from jax.experimental.pallas import tpu as pltpu
from jax.sharding import PartitionSpec as P

COARSE_ITERS = 20
LANES = 128
ROW = 16
SOLVE = (8, 16)


def cheb_weights(count, lower, upper):
    theta = 0.5 * (upper + lower)
    delta = 0.5 * (upper - lower)
    sigma = theta / delta
    rho_prev = 1.0 / sigma
    carry_terms = [0.0]
    gain_terms = [1.0 / theta]
    for step in range(1, count):
        rho_next = 1.0 / (2.0 * sigma - rho_prev)
        carry_terms.append(rho_next * rho_prev)
        gain_terms.append(2.0 * rho_next / delta)
        rho_prev = rho_next
    return (carry_terms, gain_terms)


(_, CARRY), (GAIN_FIRST, GAIN) = cheb_weights(2, 0.25, 2.0)


def lanes_of(rows):
    return lax.broadcasted_iota(jnp.int32, (rows, LANES), 1)


def rows_of(rows):
    return lax.broadcasted_iota(jnp.int32, (rows, LANES), 0)


def roll(value, shift, axis=1):
    return pltpu.roll(value, shift % value.shape[axis], axis)


def pair_sum(value, stride):
    odd = (lanes_of(value.shape[0]) & stride) != 0
    return value + jnp.where(odd, roll(value, stride), roll(value, -stride))


class View:
    def __init__(self, ref, plane, row):
        self.ref, self.plane, self.row = (ref, plane, row)

    def __getitem__(self, index):
        plane, rows, lanes = index
        return self.ref[plane - self.plane, rows.start - self.row : rows.stop - self.row, lanes]


class Level:
    def __init__(self, level, gx, gz, brick, cells, first_plane, refs, first_row=ROW):
        self.stride, self.scale, self.first_row = (2**level, 0.25**level, first_row)
        self.gx, self.gz, self.brick, self.cells, self.first_plane = (gx, gz, brick, cells, first_plane)
        self.half, self.fx, self.fz, self.left, self.right, self.diag, self.inverse = refs

    def coefs(self, planes, row, count):
        half, stride = (self.half, self.stride)
        lane = lanes_of(count)
        here = rows_of(count) + (row - self.first_row + self.gz * self.brick[1])
        first, last = (planes[0], planes[-1])
        for p in planes:
            self.fx[p, row : row + count, :] = half[p - 1, row : row + count, :] + half[p, row : row + count, :]
        p = last + 1
        self.fx[p, row : row + count, :] = half[p - 1, row : row + count, :] + half[p, row : row + count, :]
        more = count + 1
        for p in planes:
            self.fz[p, row : row + more, :] = half[p, row - 1 : row - 1 + more, :] + half[p, row : row + more, :]
        for p in planes:
            center = half[p, row : row + count, :]
            face_left = center + jnp.where(lane >= stride, roll(center, stride), 0.0)
            face_right = center + jnp.where(lane < LANES - stride, roll(center, -stride), 0.0)
            diagonal = (
                self.fx[p, row : row + count, :]
                + self.fx[p + 1, row : row + count, :]
                + self.fz[p, row : row + count, :]
                + self.fz[p, row + 1 : row + 1 + count, :]
                + face_left
                + face_right
            )
            self.left[p, row : row + count, :] = jnp.where(lane >= stride, face_left, 0.0)
            self.right[p, row : row + count, :] = jnp.where(lane < LANES - stride, face_right, 0.0)
            self.diag[p, row : row + count, :] = diagonal
            plane = p - self.first_plane + self.gx * self.brick[0]
            outside = jnp.where(jnp.logical_and(plane >= 0, plane < self.cells[0]), 0, 1 << 20)
            index = here + outside
            inside = (index >= 0) & (index < self.cells[1]) & (diagonal > 0.0)
            self.inverse[p, row : row + count, :] = jnp.where(inside, 1.0 / (self.scale * diagonal), 0.0)

    def remainder(self, source, guess, p, row, count):
        center = guess[p, row : row + count, :]
        beside = (
            self.fx[p, row : row + count, :] * guess[p - 1, row : row + count, :]
            + self.fx[p + 1, row : row + count, :] * guess[p + 1, row : row + count, :]
        )
        beside = beside + (
            self.fz[p, row : row + count, :] * guess[p, row - 1 : row - 1 + count, :]
            + self.fz[p, row + 1 : row + 1 + count, :] * guess[p, row + 1 : row + 1 + count, :]
        )
        beside = beside + (
            self.left[p, row : row + count, :] * roll(center, self.stride)
            + self.right[p, row : row + count, :] * roll(center, -self.stride)
        )
        applied = self.diag[p, row : row + count, :] * center - beside
        return source[p, row : row + count, :] - self.scale * applied

    def second_down(self, source, first, out, planes, row, count):
        for p in planes:
            rest = self.remainder(source, first, p, row, count)
            start = first[p, row : row + count, :]
            update = CARRY * start + GAIN * (self.inverse[p, row : row + count, :] * rest)
            out[p, row : row + count, :] = start + update

    def first_down(self, source, first, planes, row, count):
        for p in planes:
            first[p, row : row + count, :] = GAIN_FIRST * (
                self.inverse[p, row : row + count, :] * source[p, row : row + count, :]
            )

    def restricted_remainder(self, source, guess, temp, planes, row, rows):
        parts = []
        for p in planes[::2]:
            both = self.remainder(source, guess, p, row, rows) + self.remainder(source, guess, p + 1, row, rows)
            temp[0:rows, :] = pair_sum(both, self.stride)
            parts.append(0.125 * (temp[pl.ds(0, rows // 2, stride=2), :] + temp[pl.ds(1, rows // 2, stride=2), :]))
        return parts

    def up(self, source, start, middle, update, out, planes, row, count, out_row, out_count):
        for p in range(planes[0] - 1, planes[-1] + 2):
            first = GAIN_FIRST * (
                self.inverse[p, row : row + count, :] * self.remainder(source, start, p, row, count)
            )
            update[p, row : row + count, :] = first
            middle[p, row : row + count, :] = start[p, row : row + count, :] + first
        for p in planes:
            second = CARRY * update[p, out_row : out_row + out_count, :] + GAIN * (
                self.inverse[p, out_row : out_row + out_count, :]
                * self.remainder(source, middle, p, out_row, out_count)
            )
            out(p, middle[p, out_row : out_row + out_count, :] + second)


def restricted(half, temp, stride, planes, row, rows):
    parts = []
    for p in planes[::2]:
        both = half[p, row : row + rows, :] + half[p + 1, row : row + rows, :]
        temp[0:rows, :] = pair_sum(both, stride)
        parts.append(0.125 * (temp[pl.ds(0, rows // 2, stride=2), :] + temp[pl.ds(1, rows // 2, stride=2), :]))
    return parts


def first_iterate(source, half, p, count, level, stride):
    center = half[p][1 : 1 + count]
    lane = lanes_of(count)
    diagonal = 6.0 * center + half[p - 1][1 : 1 + count] + half[p + 1][1 : 1 + count]
    diagonal = diagonal + half[p][0:count] + half[p][2 : 2 + count]
    diagonal = diagonal + jnp.where(lane >= stride, roll(center, stride), 0.0)
    diagonal = diagonal + jnp.where(lane < LANES - stride, roll(center, -stride), 0.0)
    inverse = jnp.where(diagonal > 0.0, 1.0 / (0.25**level * diagonal), 0.0)
    return GAIN_FIRST * source * inverse


def keep_window(out, window, first_plane, first_row):
    planes, rows = out.shape[0:2]
    out[...] = window[first_plane : first_plane + planes, first_row : first_row + rows, :]


def cut(half_ref, planes, row, count):
    return [half_ref[p, row : row + count, :] for p in planes]


def edge_rows_0(source, cond, low, high, to_high, to_low):
    bx, bz = source.shape[0:2]
    zero = jnp.zeros((4, LANES), jnp.float32)
    for rows, out in ((slice(bz - 4, bz), to_high), (slice(0, 4), to_low)):
        out[0, 0:4, :] = zero
        out[bx + 7, 0:4, :] = zero
        for p in range(3):
            out[p + 1, 0:4, :] = low[p, rows, :]
            out[p + bx + 4, 0:4, :] = high[p, rows, :]
        for p in range(4):
            out[p, 4:8, :] = low[p + 3, rows, :]
            out[p + bx + 4, 4:8, :] = high[p + 3, rows, :]
        for p in range(bx):
            out[p + 4, 0:4, :] = source[p, rows, :]
            out[p + 4, 4:8, :] = cond[p, rows, :]


def down_0(cells, pos, source, cond, low, high, z_low, z_high, kept_s, kept_h, kept_g, to_next, to_prev, win_s, win_h, guess, fx, fz, left, right, diag, inverse, first, temp, next_half):
    gx, gz = (pos[0], pos[1])
    bx, bz = source.shape[0:2]
    planes = bx + 8
    zero = jnp.zeros((8, LANES), jnp.float32)
    end = ROW + bz
    has_low, has_high = inside_z(gz, cells[1] // bz)
    for p in range(planes):
        for edge in (8, end, end + 8):
            win_s[p, edge : edge + 8, :] = zero
            win_h[p, edge : edge + 8, :] = zero
            guess[p, edge : edge + 8, :] = zero
            first[p, edge : edge + 8, :] = zero
        win_s[p, ROW - 4 : ROW, :] = z_low[p, 0:4, :]
        win_s[p, end : end + 4, :] = z_high[p, 0:4, :]
        win_h[p, ROW - 4 : ROW, :] = (0.5 * has_low) * z_low[p, 4:8, :]
        win_h[p, end : end + 4, :] = (0.5 * has_high) * z_high[p, 4:8, :]
    for p in range(bx):
        win_s[p + 4, ROW:end, :] = source[p, :, :]
        win_h[p + 4, ROW:end, :] = 0.5 * cond[p, :, :]
    for p in range(3):
        win_s[p + 1, ROW:end, :] = low[p, :, :]
        win_s[p + bx + 4, ROW:end, :] = high[p, :, :]
    for p in range(4):
        win_h[p, ROW:end, :] = 0.5 * low[p + 3, :, :]
        win_h[p + bx + 4, ROW:end, :] = 0.5 * high[p + 3, :, :]

    level = Level(0, gx, gz, (bx, bz), cells, 4, (win_h, fx, fz, left, right, diag, inverse))
    row, count = (ROW - 4, bz + 8)
    level.coefs(range(1, planes - 1), row, count)
    level.first_down(win_s, first, range(1, planes - 1), row, count)
    level.second_down(win_s, first, guess, range(2, planes - 2), row, count)
    sources = level.restricted_remainder(win_s, guess, temp, range(4, 4 + bx), ROW, bz)
    halves = restricted(win_h, temp, 1, range(2, planes - 2), ROW - 8, bz + 16)
    for p, value in enumerate(halves):
        next_half[p, :, :] = value
    own = bz // 2
    odd = (lanes_of(own) & 1) == 1
    padded = cut(next_half, range(bx // 2 + 2), 3, own + 2)
    for p, value in enumerate(sources):
        mixed = jnp.where(odd, padded[p + 1][1 : 1 + own], value)
        to_next[p, :, :] = mixed
        to_prev[p, :, :] = mixed
    end = bx // 2 - 1
    to_next[end + 1, :, :] = first_iterate(sources[0], padded, 1, own, 1, 2)
    to_prev[end + 1, :, :] = first_iterate(sources[end], padded, end + 1, own, 1, 2)
    keep_window(kept_s, win_s, 3, 8)
    keep_window(kept_h, win_h, 2, 8)
    keep_window(kept_g, guess, 2, 8)


def inside_z(gz, count):
    return (jnp.where(gz > 0, 1.0, 0.0), jnp.where(gz < count - 1, 1.0, 0.0))


def edge_rows_1(low, here, high, to_high, to_low):
    at = 0
    for part, count in ((low, low.shape[0]), (here, here.shape[0] - 1), (high, high.shape[0])):
        rows = part.shape[1]
        to_high[at : at + count, :, :] = part[0:count, rows - 16 : rows, :]
        to_low[at : at + count, :, :] = part[0:count, 0:16, :]
        at += count


def down_1(cells, pos, here, low, high, z_low, z_high, kept_s, kept_h, kept_g, to_next, to_prev, win_s, win_h, guess, fx, fz, left, right, diag, inverse, first, temp, next_source, next_half):
    gx, gz = (pos[0], pos[1])
    bx, bz = (here.shape[0] - 1, here.shape[1])
    planes, base = (3 * bx, 24)
    end = base + bz
    zero = jnp.zeros((8, LANES), jnp.float32)
    has_low, has_high = inside_z(gz, cells[1] // bz)

    def unpack(p, start, rows, mixed):
        odd = (lanes_of(rows) & 1) == 1
        win_s[p, start : start + rows, :] = jnp.where(odd, roll(mixed, 1), mixed)
        win_h[p, start : start + rows, :] = jnp.where(odd, mixed, roll(mixed, -1))

    edges = 0
    for b, part in enumerate((low, here, high)):
        for p in range(bx):
            unpack(b * bx + p, base, bz, part[p, :, :])
            unpack(b * bx + p, base - 16, 16, has_low * z_low[edges + p, :, :])
            unpack(b * bx + p, end, 16, has_high * z_high[edges + p, :, :])
        edges += bx
        if b != 1:
            q = 0 if b == 0 else planes - 1
            first[q, base:end, :] = part[bx, :, :]
            first[q, base - 16 : base, :] = has_low * z_low[edges, :, :]
            first[q, end : end + 16, :] = has_high * z_high[edges, :, :]
            edges += 1
    for p in range(planes):
        for ref in (win_s, win_h):
            ref[p, 0:8, :] = zero
            ref[p, end + 16 : end + 24, :] = zero
        for ref in (first, guess):
            ref[p, 8:16, :] = zero if 0 < p < planes - 1 or ref is guess else ref[p, 8:16, :]
            ref[p, end + 8 : end + 16, :] = zero if 0 < p < planes - 1 or ref is guess else ref[p, end + 8 : end + 16, :]

    level = Level(1, gx, gz, (bx, bz), cells, bx, (win_h, fx, fz, left, right, diag, inverse), base)
    row, count = (base - 12, bz + 24)
    level.coefs(range(1, planes - 1), row, count)
    level.first_down(win_s, first, range(1, planes - 1), row, count)
    level.second_down(win_s, first, guess, range(1, planes - 1), row, count)
    own = bz // 2
    sources = level.restricted_remainder(win_s, guess, temp, range(bx - 2, 2 * bx + 2), row, count)
    halves = restricted(win_h, temp, 2, range(planes), base - 16, bz + 32)
    next_source[...] = jnp.zeros(next_source.shape, jnp.float32)
    for p, value in enumerate(sources):
        next_source[p + 1, 2 : 2 + count // 2, :] = value
    for p, value in enumerate(halves):
        next_half[p, :, :] = value
    lane = lanes_of(own + 16) & 3

    def pair(p):
        mixed = jnp.where(lane == 0, next_source[p, :, :], next_half[p, :, :])
        mixed = jnp.where(lane == 2, next_source[p + 1, :, :], mixed)
        return jnp.where(lane == 3, next_half[p + 1, :, :], mixed)

    middle = pair(2)
    to_next[0, :, :] = pair(0)
    to_next[1, :, :] = middle
    to_prev[0, :, :] = middle
    to_prev[1, :, :] = pair(4)
    keep_window(kept_s, win_s, 2, base - 8)
    keep_window(kept_h, win_h, 1, base - 8)
    keep_window(kept_g, guess, 1, base - 8)


def spread(mixed, which):
    only = jnp.where((lanes_of(mixed.shape[0]) & 3) == which, mixed, 0.0)
    only = roll(only, -which) if which else only
    twice = only + roll(only, 1)
    return twice + roll(twice, 2)


def down_2(cells, pos, prev, here, next_, kept_s, kept_h, kept_g, message, to_next, to_prev, win_s, win_h, guess, fx, fz, left, right, diag, inverse, first, temp):
    gx, gz = (pos[0], pos[1])
    bx, bz = (2, prev.shape[1] - 16)
    own, planes = (4, 10)
    end = ROW + bz
    zero = jnp.zeros((8, LANES), jnp.float32)
    pairs = (prev, 0), (prev, 1), (here, 1), (next_, 0), (next_, 1)
    for q, (part, at) in enumerate(pairs):
        mixed = part[at, :, :]
        for p in range(2):
            win_s[2 * q + p, 8 : end + 8, :] = spread(mixed, 2 * p)
            win_h[2 * q + p, 8 : end + 8, :] = spread(mixed, 2 * p + 1)
    for p in range(planes):
        for ref in (win_s, win_h, first):
            ref[p, 0:8, :] = zero
            ref[p, end + 8 : end + 16, :] = zero
    level = Level(2, gx, gz, (bx, bz), cells, own, (win_h, fx, fz, left, right, diag, inverse))
    row, count = (ROW - 8, bz + 16)
    level.coefs(range(own - 3, own + 5), row, count)
    level.first_down(win_s, first, range(own - 3, own + 5), row, count)
    level.second_down(win_s, first, guess, range(own - 2, own + 4), row, count)
    keep_window(kept_s, win_s, 1, 8)
    keep_window(kept_h, win_h, 0, 8)
    keep_window(kept_g, guess, own, 8)
    lane = lanes_of(count) & 3
    for out, begin in ((to_next, own - 2), (to_prev, own)):
        mixed = guess[begin, row : row + count, :]
        for p in range(1, 4):
            mixed = jnp.where(lane == p, guess[begin + p, row : row + count, :], mixed)
        out[...] = mixed
    sources = level.restricted_remainder(win_s, guess, temp, range(own, own + bx), ROW, bz)
    halves = restricted(win_h, temp, 4, range(own, own + bx), ROW, bz)
    rows = bz // 2
    cell = lax.broadcasted_iota(jnp.int32, (LANES, LANES), 0)
    lane = lax.broadcasted_iota(jnp.int32, (LANES, LANES), 1)
    pick = jnp.where(((cell >> 3) == (lane & 15)) & ((cell & 7) == 0), 1.0, 0.0)
    keep = (lanes_of(rows) >> 4) == rows_of(rows)
    for at, value in enumerate((sources[0], halves[0])):
        dense = jnp.dot(value, pick, precision=lax.Precision.HIGHEST, preferred_element_type=jnp.float32)
        dense = jnp.sum(jnp.where(keep, dense, 0.0), axis=0, keepdims=True)
        for device in range(message.shape[0]):
            message[device, at : at + 1, :] = dense


class Coarsest:
    def __init__(self, base, state, update):
        self.base, self.state, self.update, self.now = (base, state, update, 0)
        self.planes = update.shape[1]
        self.weights = list(zip(*cheb_weights(COARSE_ITERS, 0.02, 2.0)))
        zero = jnp.zeros((8, LANES), jnp.float32)
        for buffer in range(2):
            for b in range(3):
                state[buffer, b, 0:8, :] = zero
                state[buffer, b, self.planes + 8 : self.planes + 16, :] = zero

    def beside_z(self, values):
        lane = lanes_of(values[0].shape[0])
        ahead, back = ([roll(v, 16) for v in values], [roll(v, -16) for v in values])
        before = [jnp.where(lane < 16, ahead[max(b - 1, 0)], ahead[b]) for b in range(3)]
        after = [jnp.where(lane >= LANES - 16, back[min(b + 1, 2)], back[b]) for b in range(3)]
        return before, after

    def start(self, parts, half, flags):
        planes, zero = (self.planes, jnp.zeros((8, LANES), jnp.float32))
        gain = self.weights[0][1]
        for b in range(3):
            half[b, 0:8, :] = zero
            half[b, planes + 8 : planes + 16, :] = zero
            half[b, 8 : planes + 8, :] = flags[b] * parts[b][pl.ds(1, planes, stride=2), :]
        lane = lanes_of(8)
        in_left, in_right = ((lane & 15) > 0, (lane & 15) < 15)
        for x in range(0, planes, 8):
            centers = [half[b, x + 8 : x + 16, :] for b in range(3)]
            before, after = self.beside_z(centers)
            for b, center in enumerate(centers):
                faces = [
                    center + half[b, x + 7 : x + 15, :],
                    center + half[b, x + 9 : x + 17, :],
                    center + before[b],
                    center + after[b],
                    center + jnp.where(in_left, roll(center, 1), 0.0),
                    center + jnp.where(in_right, roll(center, -1), 0.0),
                ]
                diagonal = faces[0] + faces[1] + faces[2] + faces[3] + faces[4] + faces[5]
                inverse = flags[b] * jnp.where(diagonal > 0.0, 1.0 / diagonal, 0.0)
                faces = [face * inverse for face in faces]
                faces[4] = jnp.where(in_left, faces[4], 0.0)
                faces[5] = jnp.where(in_right, faces[5], 0.0)
                for which, face in enumerate(faces):
                    self.base[7 * b + which, x : x + 8, :] = face
                scaled = 64.0 * (parts[b][pl.ds(2 * x, 8, stride=2), :] * inverse)
                self.base[7 * b + 6, x : x + 8, :] = scaled
                self.update[b, x : x + 8, :] = gain * scaled
                self.state[self.now, b, x + 8 : x + 16, :] = gain * scaled

    def resume(self, parts, flags):
        for b in range(3):
            self.state[self.now, b, 8 : self.planes + 8, :] = flags[b] * parts[b][0, :, :]
            self.update[b, :, :] = flags[b] * parts[b][1, :, :]

    def steps(self, which):
        for index in which:
            carry, gain = self.weights[index]
            old, new = (self.now, 1 - self.now)
            for x in range(0, self.planes, 8):
                centers = [self.state[old, b, x + 8 : x + 16, :] for b in range(3)]
                before, after = self.beside_z(centers)
                for b, center in enumerate(centers):
                    face = [self.base[7 * b + k, x : x + 8, :] for k in range(7)]
                    beside = face[0] * self.state[old, b, x + 7 : x + 15, :] + face[1] * self.state[old, b, x + 9 : x + 17, :]
                    beside = beside + (face[2] * before[b] + face[3] * after[b])
                    beside = beside + (face[4] * roll(center, 1) + face[5] * roll(center, -1))
                    change = carry * self.update[b, x : x + 8, :] + gain * (face[6] - center + beside)
                    self.update[b, x : x + 8, :] = change
                    self.state[new, b, x + 8 : x + 16, :] = center + change
            self.now = new

    def leave(self, out):
        out[0, :, :] = self.state[self.now, 1, 8 : self.planes + 8, :]
        out[1, :, :] = self.update[1, :, :]


def solve_first(count, pos, low, here, high, base, out, half, state, update):
    has_low, has_high = inside_z(pos[1], count)
    level = Coarsest(base, state, update)
    level.start((low, here, high), half, (has_low, 1.0, has_high))
    level.steps(range(1, SOLVE[0]))
    level.leave(out)


def solve_next(count, pos, base, low, here, high, out, state, update):
    has_low, has_high = inside_z(pos[1], count)
    level = Coarsest(base, state, update)
    level.resume((low, here, high), (has_low, 1.0, has_high))
    level.steps(range(SOLVE[0], SOLVE[1]))
    level.leave(out)


def finish(cells, pos, base, low, here, high, prev2, next2, s2, h2, g2, s1, h1, g1, s0, h0, g0, out, *scratch):
    gx, gz = (pos[0], pos[1])
    state, update3, coarse2, temp, start2, start1, start0 = scratch[:7]
    shared, middle, update = (scratch[7:13], scratch[13], scratch[14])
    s2, h2, g2 = (View(s2, 1, 8), View(h2, 0, 8), View(g2, 4, 8))
    s1, h1, g1 = (View(s1, 2, 8), View(h1, 1, 8), View(g1, 1, 8))
    s0, h0, g0 = (View(s0, 3, 8), View(h0, 2, 8), View(g0, 2, 8))
    bz0 = out.shape[1]
    bz1, bz2 = (bz0 // 2, bz0 // 4)
    has_low, has_high = inside_z(gz, cells[0][1] // bz0)
    level = Coarsest(base, state, update3)
    level.resume((low, here, high), (has_low, 1.0, has_high))
    level.steps(range(SOLVE[1], COARSE_ITERS))
    last = level.now

    bx2 = 2
    rows = bz2 + 8
    cell = lax.broadcasted_iota(jnp.int32, (LANES, LANES), 0)
    lane = lax.broadcasted_iota(jnp.int32, (LANES, LANES), 1)
    pick = jnp.where((cell & 15) == (lane >> 3), 1.0, 0.0)
    z3 = (rows_of(rows) >> 1) - 2
    keep = (lanes_of(rows) >> 4) == (z3 & 7)
    columns = [state[last, b, pl.ds(gx + 6, 8), :] for b in range(3)]
    for q in range(5):
        picked = [column[q : q + 1, :] for column in columns]
        wide = jnp.where(z3 < 0, picked[0], jnp.where(z3 < 8, picked[1], picked[2]))
        coarse2[q * rows : (q + 1) * rows, :] = jnp.where(keep, wide, 0.0)
    spread_out = jnp.dot(coarse2[...], pick, precision=lax.Precision.HIGHEST, preferred_element_type=jnp.float32)
    coarse2[...] = spread_out

    start, own = (start2, 4)
    row, count = (ROW - 4, rows)
    zero = jnp.zeros((8, LANES), jnp.float32)
    for q in range(5):
        for p in (own - 4 + 2 * q, own - 3 + 2 * q):
            start[p, 8:16, :] = zero
            start[p, ROW + bz2 : ROW + bz2 + 8, :] = zero
            if q == 2:
                guess = g2[p, row : row + count, :]
            else:
                guess = spread((prev2 if q < 2 else next2)[4 : 4 + count, :], p if q < 2 else p - own - bx2)
            start[p, row : row + count, :] = guess + coarse2[q * rows : (q + 1) * rows, :]
    level = Level(2, gx, gz, (bx2, bz2), cells[2], own, (h2,) + tuple(shared))
    level.coefs(range(own - 3, own + 5), row, count)

    bx1 = 4

    def to_level_1(p, value):
        q = 2 * (p - own) + 4
        temp[pl.ds(0, value.shape[0], stride=2), :] = value
        temp[pl.ds(1, value.shape[0], stride=2), :] = value
        for r in (q, q + 1):
            if 1 <= r <= 10:
                start1[r, ROW - 4 : ROW + bz1 + 4, :] = (
                    g1[r, ROW - 4 : ROW + bz1 + 4, :] + temp[0 : bz1 + 8, :]
                )

    for r in range(1, 11):
        start1[r, 8:16, :] = zero
        start1[r, ROW + bz1 : ROW + bz1 + 8, :] = zero
    level.up(s2, start, middle, update, to_level_1, range(own - 2, own + 4), row, count, ROW - 2, bz2 + 4)
    level = Level(1, gx, gz, (bx1, bz1), cells[1], 4, (h1,) + tuple(shared))
    row, count = (ROW - 4, bz1 + 8)
    level.coefs(range(2, 10), row, count)

    bx0 = out.shape[0]
    for r in range(2, 14):
        start0[r, 8:16, :] = zero
        start0[r, ROW + bz0 : ROW + bz0 + 8, :] = zero

    def to_level_0(p, value):
        q = 2 * (p - 4) + 4
        temp[pl.ds(0, value.shape[0], stride=2), :] = value
        temp[pl.ds(1, value.shape[0], stride=2), :] = value
        for r in (q, q + 1):
            start0[r, ROW - 4 : ROW + bz0 + 4, :] = g0[r, ROW - 4 : ROW + bz0 + 4, :] + temp[0 : bz0 + 8, :]

    level.up(s1, start1, middle, update, to_level_0, range(3, 9), row, count, ROW - 2, bz1 + 4)
    level = Level(0, gx, gz, (bx0, bz0), cells[0], 4, (h0,) + tuple(shared))
    level.coefs(range(3, 13), ROW - 4, bz0 + 8)

    def to_out(p, value):
        out[p - 4, :, :] = value

    level.up(s0, start0, middle, update, to_out, range(4, 12), ROW - 4, bz0 + 8, ROW, bz0)


def f32(*shape):
    return jax.ShapeDtypeStruct(shape, jnp.float32)


def scratch(*shape):
    return pltpu.VMEM(shape, jnp.float32)


def call(kernel, name, outs, scratches, *args):
    smem = pl.BlockSpec(memory_space=pltpu.SMEM)
    limit = 4 * 2**20 + sum(4 * math.prod(ref.shape) for ref in scratches)
    vmem = pl.BlockSpec(memory_space=pltpu.VMEM)
    return pl.pallas_call(
        kernel,
        name=name,
        out_shape=outs,
        in_specs=[smem if arg.dtype == jnp.int32 else vmem for arg in args],
        out_specs=[vmem] * len(outs),
        scratch_shapes=scratches,
        compiler_params=pltpu.CompilerParams(vmem_limit_bytes=limit),
    )(*args)


def shift(array, axis, by):
    devices = lax.axis_size(axis)
    return lax.ppermute(array, axis, [(i, i + by) for i in range(devices) if 0 <= i + by < devices])


def turn(array, axis, by):
    devices = lax.axis_size(axis)
    return lax.ppermute(array, axis, [(i, (i + by) % devices) for i in range(devices)])


def on_device(right_side, conductivity):
    nx, nz = (lax.axis_size("gx"), lax.axis_size("gz"))
    bx, bz = right_side.shape[0:2]
    cells = [(nx * bx >> level, nz * bz >> level) for level in range(4)]
    pos = jnp.stack([lax.axis_index("gx"), lax.axis_index("gz")]).astype(jnp.int32)
    low = shift(jnp.concatenate([right_side[bx - 3 :], conductivity[bx - 4 :]]), "gx", 1)
    high = shift(jnp.concatenate([right_side[:3], conductivity[:4]]), "gx", -1)
    planes = bx + 8
    to_high, to_low = call(
        edge_rows_0, "edge_rows_0", [f32(planes, 8, LANES)] * 2, [], right_side, conductivity, low, high
    )
    z_low, z_high = (turn(to_high, "gz", 1), turn(to_low, "gz", -1))
    window = (planes, bz + 32, LANES)
    s0, h0, g0, for_next, for_prev = call(
        functools.partial(down_0, cells[0]),
        "down_0",
        [f32(bx + 2, bz + 16, LANES)] + [f32(bx + 4, bz + 16, LANES)] * 2 + [f32(bx // 2 + 1, bz // 2, LANES)] * 2,
        [scratch(*window)] * 10 + [scratch(bz + 16, LANES), scratch(bx // 2 + 2, bz // 2 + 8, LANES)],
        pos,
        right_side,
        conductivity,
        low,
        high,
        z_low,
        z_high,
    )

    bx, bz = (bx // 2, bz // 2)
    low, high = (shift(for_next, "gx", 1), shift(for_prev, "gx", -1))
    to_high, to_low = call(
        edge_rows_1, "edge_rows_1", [f32(3 * bx + 2, 16, LANES)] * 2, [], low, for_next, high
    )
    z_low, z_high = (turn(to_high, "gz", 1), turn(to_low, "gz", -1))
    window = (3 * bx, bz + 48, LANES)
    s1, h1, g1, for_next, for_prev = call(
        functools.partial(down_1, cells[1]),
        "down_1",
        [f32(bx + 4, bz + 16, LANES)] + [f32(bx + 6, bz + 16, LANES)] * 2 + [f32(2, bz // 2 + 16, LANES)] * 2,
        [scratch(*window)] * 10 + [scratch(bz + 32, LANES)] + [scratch(bx // 2 + 4, bz // 2 + 16, LANES)] * 2,
        pos,
        for_next,
        low,
        high,
        z_low,
        z_high,
    )

    bx, bz = (bx // 2, bz // 2)
    prev, next_ = (shift(for_next, "gx", 1), shift(for_prev, "gx", -1))
    window = (bx + 8, bz + 32, LANES)
    s2, h2, g2, row3, for_next, for_prev = call(
        functools.partial(down_2, cells[2]),
        "down_2",
        [f32(bx + 6, bz + 16, LANES), f32(bx + 8, bz + 16, LANES), f32(bx, bz + 16, LANES)]
        + [f32(nx, 2, LANES)]
        + [f32(bz + 16, LANES)] * 2,
        [scratch(*window)] * 10 + [scratch(bz + 16, LANES)],
        pos,
        prev,
        for_next,
        next_,
    )

    here = lax.all_to_all(row3, "gx", 0, 0, tiled=True)
    low, high = (turn(here, "gz", 1), turn(here, "gz", -1))
    blocks = [part.reshape(2 * nx, LANES) for part in (low, here, high)]
    solving = [scratch(2, 3, nx + 16, LANES), scratch(3, nx, LANES)]
    for_next, _ = lax.optimization_barrier((for_next, here))
    prev2 = shift(for_next, "gx", 1)
    base, here = call(
        functools.partial(solve_first, nz),
        "solve_first",
        [f32(21, nx, LANES), f32(2, nx, LANES)],
        [scratch(3, nx + 16, LANES)] + solving,
        pos,
        *blocks,
    )
    low, high = (turn(here, "gz", 1), turn(here, "gz", -1))
    for_prev, _ = lax.optimization_barrier((for_prev, here))
    next2 = shift(for_prev, "gx", -1)
    (here,) = call(
        functools.partial(solve_next, nz), "solve_next", [f32(2, nx, LANES)], solving, pos, base, low, here, high
    )
    low, high = (turn(here, "gz", 1), turn(here, "gz", -1))

    bx, bz = right_side.shape[0:2]
    window = (bx + 8, bz + 32, LANES)
    work = solving + [scratch(5 * (bz // 4 + 8), LANES), scratch(bz + 32, LANES)]
    work += [scratch(bx // 4 + 8, bz // 4 + 32, LANES), scratch(bx // 2 + 8, bz // 2 + 32, LANES)]
    work += [scratch(*window)] * 9
    (result,) = call(
        functools.partial(finish, cells), "finish", [f32(*right_side.shape)], work, pos, base, low, here, high,
        prev2, next2, s2, h2, g2, s1, h1, g1, s0, h0, g0,
    )
    return result


def solution(mesh):
    return jax.shard_map(
        on_device,
        mesh=mesh,
        in_specs=(P("gx", "gz", None), P("gx", "gz", None)),
        out_specs=P("gx", "gz", None),
        check_vma=False,
    )
```

time: 124 us -> 112 us (0.903)
  the two profiles are of different devices: /device:TPU:1 before, /device:TPU:6 now
where the time goes in v3:
time: 112 us; the launch traced here: 111 us
  starting transfers between devices  44.5 us (40%)
  waiting for transfers between devices  30.5 us (27%)
  blocking collectives  22 us (20%)
  Pallas kernels  12.8 us (11%)
    ppermute x8, starting transfers between devices, shift(): lax.ppermute(array, axis, [(i, i + by) for i in range(devices) if 0 <= i...  35.9 us
    all_to_all x1, blocking collectives, on_device(): here = lax.all_to_all(row3, 'gx', 0, 0, tiled=True)  22 us
    ppermute x8, waiting for transfers between devices, shift(): lax.ppermute(array, axis, [(i, i + by) for i in range(devices) if 0 <= i...  16.8 us
    ppermute x10, waiting for transfers between devices, turn(): lax.ppermute(array, axis, [(i, (i + by) % devices) for i in range(devices)])  13.7 us
    pallas_call x8, Pallas kernels, call(): pl.pallas_call(kernel, name=name, out_shape=outs, in_specs=[smem if arg.d...  12.8 us
    ppermute x10, starting transfers between devices, turn(): lax.ppermute(array, axis, [(i, (i + by) % devices) for i in range(devices)])  8.6 us
  transfers between devices with their start and end apart: 18, of which 12 were waited for; matrix products, arithmetic and copies ran while one was open for 0% of the time, Pallas kernels for 0%

profile of v3, /device:TPU:6, one launch (start us, length us, event | category | flops | bytes accessed | tf_op | source)
XLA Modules:
  0.0 111.2 jit_solution(809156202402648517)
XLA Ops:
  0.0 1.0 fusion
  1.1 4.0 %collective-permute-start = (f32[7,64,128]{2,1,0:T(8,128)S(1)}, f32[7,64,128]{2,1,0:T(8,128)S(1)}, u32[]{:S(2)}, u32[]{:S(2)}) collective-permute-start(f32[7,64,128]{2,1,0:T(8,128)S(1)} %pad_maximum_fusion), channel_id=1, source_target_pairs={{0,8},{8,16},{16,24},{24,32},{32,40},{40,48},{48,56},{56,64},{64,7... | collective-permute-start | bytes 688136 | tf_op jit(solution)/shard_map/ppermute | solution.py:584
  5.1 9.8 %collective-permute-start.1 = (f32[7,64,128]{2,1,0:T(8,128)S(1)}, f32[7,64,128]{2,1,0:T(8,128)S(1)}, u32[]{:S(2)}, u32[]{:S(2)}) collective-permute-start(f32[7,64,128]{2,1,0:T(8,128)S(1)} %pad_maximum_fusion.1), channel_id=1, source_target_pairs={{8,0},{16,8},{24,16},{32,24},{40,32},{48,40},{56,48},{64,56},{72,6... | collective-permute-start | bytes 688136 | tf_op jit(solution)/shard_map/ppermute | solution.py:584
  14.9 3.6 %collective-permute-done.low = f32[7,64,128]{2,1,0:T(8,128)S(1)} collective-permute-done((f32[7,64,128]{2,1,0:T(8,128)S(1)}, f32[7,64,128]{2,1,0:T(8,128)S(1)}, u32[]{:S(2)}, u32[]{:S(2)}) %collective-permute-start) | collective-permute-done | bytes 229408 | tf_op jit(solution)/shard_map/ppermute | solution.py:584
  18.5 1.2 %collective-permute-done.1.high = f32[7,64,128]{2,1,0:T(8,128)S(1)} collective-permute-done((f32[7,64,128]{2,1,0:T(8,128)S(1)}, f32[7,64,128]{2,1,0:T(8,128)S(1)}, u32[]{:S(2)}, u32[]{:S(2)}) %collective-permute-start.1) | collective-permute-done | bytes 229408 | tf_op jit(solution)/shard_map/ppermute | solution.py:584
  19.8 2.9 %collective-permute-start.3 = (f32[16,8,128]{2,1,0:T(8,128)S(1)}, f32[16,8,128]{2,1,0:T(8,128)S(1)}, u32[]{:S(2)}, u32[]{:S(2)}) collective-permute-start(f32[16,8,128]{2,1,0:T(8,128)S(1)} %get-tuple-element.30), channel_id=1, source_target_pairs={{0,7},{1,0},{2,1},{3,2},{4,3},{5,4},{6,5},{7,6},{8,15},{9,8},{10,9... | collective-permute-start | bytes 196616 | tf_op jit(solution)/shard_map/ppermute | solution.py:589
  22.8 1.9 %collective-permute-done.2.z_low = f32[16,8,128]{2,1,0:T(8,128)S(1)} collective-permute-done((f32[16,8,128]{2,1,0:T(8,128)S(1)}, f32[16,8,128]{2,1,0:T(8,128)S(1)}, u32[]{:S(2)}, u32[]{:S(2)}) %collective-permute-start.2) | collective-permute-done | bytes 65568 | tf_op jit(solution)/shard_map/ppermute | solution.py:589
  24.7 2.3 %down_0.1 = (f32[10,80,128]{2,1,0:T(8,128)S(1)}, f32[12,80,128]{2,1,0:T(8,128)S(1)}, f32[12,80,128]{2,1,0:T(8,128)S(1)}, f32[5,32,128]{2,1,0:T(8,128)S(1)}, f32[5,32,128]{2,1,0:T(8,128)S(1)}) custom-call(s32[2]{0:T(128)S(1)} %pad_add_fusion.pos, f32[8,64,128]{2,1,0:T(8,128)S(1)} %copy-done.1, f32[8,64,128]{2,1,0:T(8,128)S(1)} %copy-done, ...), custom_call_target="tpu_custom_call" | custom-call | tf_op jit(solution)/shard_map/down_0/pallas_call | solution.py:571
  27.0 6.5 %collective-permute-start.5 = (f32[5,32,128]{2,1,0:T(8,128)S(1)}, f32[5,32,128]{2,1,0:T(8,128)S(1)}, u32[]{:S(2)}, u32[]{:S(2)}) collective-permute-start(f32[5,32,128]{2,1,0:T(8,128)S(1)} %get-tuple-element.32), channel_id=1, source_target_pairs={{8,0},{16,8},{24,16},{32,24},{40,32},{48,40},{56,48},{64,56},{72,6... | collective-permute-start | bytes 245768 | tf_op jit(solution)/shard_map/ppermute | solution.py:584
  33.5 1.9 %collective-permute-start.4 = (f32[5,32,128]{2,1,0:T(8,128)S(1)}, f32[5,32,128]{2,1,0:T(8,128)S(1)}, u32[]{:S(2)}, u32[]{:S(2)}) collective-permute-start(f32[5,32,128]{2,1,0:T(8,128)S(1)} %get-tuple-element.31.here), channel_id=1, source_target_pairs={{0,8},{8,16},{16,24},{24,32},{32,40},{40,48},{48,56},{56,64},{64,7... | collective-permute-start | bytes 245768 | tf_op jit(solution)/shard_map/ppermute | solution.py:584
  35.8 6.2 %collective-permute-done.4.low = f32[5,32,128]{2,1,0:T(8,128)S(1)} collective-permute-done((f32[5,32,128]{2,1,0:T(8,128)S(1)}, f32[5,32,128]{2,1,0:T(8,128)S(1)}, u32[]{:S(2)}, u32[]{:S(2)}) %collective-permute-start.4) | collective-permute-done | bytes 81952 | tf_op jit(solution)/shard_map/ppermute | solution.py:584
  42.1 2.9 %collective-permute-start.7 = (f32[14,16,128]{2,1,0:T(8,128)S(1)}, f32[14,16,128]{2,1,0:T(8,128)S(1)}, u32[]{:S(2)}, u32[]{:S(2)}) collective-permute-start(f32[14,16,128]{2,1,0:T(8,128)S(1)} %get-tuple-element.34), channel_id=1, source_target_pairs={{0,7},{1,0},{2,1},{3,2},{4,3},{5,4},{6,5},{7,6},{8,15},{9,8},{10,9... | collective-permute-start | bytes 344072 | tf_op jit(solution)/shard_map/ppermute | solution.py:589
  45.0 2.5 %collective-permute-done.6.z_low = f32[14,16,128]{2,1,0:T(8,128)S(1)} collective-permute-done((f32[14,16,128]{2,1,0:T(8,128)S(1)}, f32[14,16,128]{2,1,0:T(8,128)S(1)}, u32[]{:S(2)}, u32[]{:S(2)}) %collective-permute-start.6) | collective-permute-done | bytes 114720 | tf_op jit(solution)/shard_map/ppermute | solution.py:589
  47.5 1.9 %down_1.1 = (f32[8,48,128]{2,1,0:T(8,128)S(1)}, f32[10,48,128]{2,1,0:T(8,128)S(1)}, f32[10,48,128]{2,1,0:T(8,128)S(1)}, f32[2,32,128]{2,1,0:T(8,128)S(1)}, f32[2,32,128]{2,1,0:T(8,128)S(1)}) custom-call(s32[2]{0:T(128)S(1)} %pad_add_fusion.pos, f32[5,32,128]{2,1,0:T(8,128)S(1)} %get-tuple-element.31.here, f32[5,32,128]{2,1,0:T(8,128)S(1)} %collective-permute-done.4.low, ...), custom_call_target="tpu_custom_call" | custom-call | tf_op jit(solution)/shard_map/down_1/pallas_call | solution.py:571
  49.4 1.9 %collective-permute-start.9 = (f32[2,32,128]{2,1,0:T(8,128)S(1)}, f32[2,32,128]{2,1,0:T(8,128)S(1)}, u32[]{:S(2)}, u32[]{:S(2)}) collective-permute-start(f32[2,32,128]{2,1,0:T(8,128)S(1)} %get-tuple-element.36), channel_id=1, source_target_pairs={{8,0},{16,8},{24,16},{32,24},{40,32},{48,40},{56,48},{64,56},{72,6... | collective-permute-start | bytes 98312 | tf_op jit(solution)/shard_map/ppermute | solution.py:584
  51.4 3.9 %collective-permute-start.8 = (f32[2,32,128]{2,1,0:T(8,128)S(1)}, f32[2,32,128]{2,1,0:T(8,128)S(1)}, u32[]{:S(2)}, u32[]{:S(2)}) collective-permute-start(f32[2,32,128]{2,1,0:T(8,128)S(1)} %get-tuple-element.35.here), channel_id=1, source_target_pairs={{0,8},{8,16},{16,24},{24,32},{32,40},{40,48},{48,56},{56,64},{64,7... | collective-permute-start | bytes 98312 | tf_op jit(solution)/shard_map/ppermute | solution.py:584
  55.3 4.0 %collective-permute-done.8.prev = f32[2,32,128]{2,1,0:T(8,128)S(1)} collective-permute-done((f32[2,32,128]{2,1,0:T(8,128)S(1)}, f32[2,32,128]{2,1,0:T(8,128)S(1)}, u32[]{:S(2)}, u32[]{:S(2)}) %collective-permute-start.8) | collective-permute-done | bytes 32800 | tf_op jit(solution)/shard_map/ppermute | solution.py:584
  59.3 1.4 %down_2.1 = (f32[8,32,128]{2,1,0:T(8,128)S(1)}, f32[10,32,128]{2,1,0:T(8,128)S(1)}, f32[2,32,128]{2,1,0:T(8,128)S(1)}, f32[64,2,128]{2,1,0:T(2,128)S(1)}, f32[32,128]{1,0:T(8,128)S(1)}, /*index=5*/f32[32,128]{1,0:T(8,128)S(1)}) custom-call(s32[2]{0:T(128)S(1)} %pad_add_fusion.pos, f32[2,32,128]{2,1,0:T(8,128)S(1)} %collective-permute-done.8.prev, ...), custom_call_target="tpu_custom_call" | custom-call | tf_op jit(solution)/shard_map/down_2/pallas_call | solution.py:571
  60.7 22.0 %all_to_all.5 = f32[64,2,128]{2,1,0:T(2,128)S(1)} all-to-all(f32[64,2,128]{2,1,0:T(2,128)S(1)} %get-tuple-element.37), channel_id=1, replica_groups=mesh['gx'=64,'gz'=8] {'gx'}, dimensions={0} | all-to-all | bytes 131072 | tf_op jit(solution)/shard_map/all_to_all | solution.py:655
  82.6 1.6 %collective-permute-start.11 = (f32[64,2,128]{2,1,0:T(2,128)S(1)}, f32[64,2,128]{2,1,0:T(2,128)S(1)}, u32[]{:S(2)}, u32[]{:S(2)}) collective-permute-start(f32[64,2,128]{2,1,0:T(2,128)S(1)} %all_to_all.5), channel_id=1, source_target_pairs={{0,7},{1,0},{2,1},{3,2},{4,3},{5,4},{6,5},{7,6},{8,15},{9,8},{10,9... | collective-permute-start | bytes 196616 | tf_op jit(solution)/shard_map/ppermute | solution.py:589
  84.3 1.9 %collective-permute-done.11 = f32[64,2,128]{2,1,0:T(2,128)S(1)} collective-permute-done((f32[64,2,128]{2,1,0:T(2,128)S(1)}, f32[64,2,128]{2,1,0:T(2,128)S(1)}, u32[]{:S(2)}, u32[]{:S(2)}) %collective-permute-start.11) | collective-permute-done | bytes 65568 | tf_op jit(solution)/shard_map/ppermute | solution.py:589
  86.2 3.0 %collective-permute-done.10 = f32[64,2,128]{2,1,0:T(2,128)S(1)} collective-permute-done((f32[64,2,128]{2,1,0:T(2,128)S(1)}, f32[64,2,128]{2,1,0:T(2,128)S(1)}, u32[]{:S(2)}, u32[]{:S(2)}) %collective-permute-start.10) | collective-permute-done | bytes 65568 | tf_op jit(solution)/shard_map/ppermute | solution.py:589
  89.2 1.5 %solve_first.1 = (f32[21,64,128]{2,1,0:T(8,128)S(1)}, f32[2,64,128]{2,1,0:T(8,128)S(1)}) custom-call(s32[2]{0:T(128)S(1)} %pad_add_fusion.pos, f32[128,128]{1,0:T(8,128)S(1)} %bitcast.7, f32[128,128]{1,0:T(8,128)S(1)} %bitcast.5, f32[128,128]{1,0:T(8,128)S(1)} %bitcast.6), custom_call_target="tpu_custom_call" | custom-call | tf_op jit(solution)/shard_map/solve_first/pallas_call | solution.py:571
  90.7 0.5 collective-permute-start.12
  91.2 1.4 %collective-permute-done.13.high = f32[2,64,128]{2,1,0:T(8,128)S(1)} collective-permute-done((f32[2,64,128]{2,1,0:T(8,128)S(1)}, f32[2,64,128]{2,1,0:T(8,128)S(1)}, u32[]{:S(2)}, u32[]{:S(2)}) %collective-permute-start.13) | collective-permute-done | bytes 65568 | tf_op jit(solution)/shard_map/ppermute | solution.py:589
  92.6 3.0 %collective-permute-done.12.low = f32[2,64,128]{2,1,0:T(8,128)S(1)} collective-permute-done((f32[2,64,128]{2,1,0:T(8,128)S(1)}, f32[2,64,128]{2,1,0:T(8,128)S(1)}, u32[]{:S(2)}, u32[]{:S(2)}) %collective-permute-start.12) | collective-permute-done | bytes 65568 | tf_op jit(solution)/shard_map/ppermute | solution.py:589
  95.6 1.4 %solve_next.1.here = f32[2,64,128]{2,1,0:T(8,128)S(1)} custom-call(s32[2]{0:T(128)S(1)} %pad_add_fusion.pos, f32[21,64,128]{2,1,0:T(8,128)S(1)} %get-tuple-element.38.base, f32[2,64,128]{2,1,0:T(8,128)S(1)} %collective-permute-done.12.low, f32[2,64,128]{2,1,0:T(8,128)S(1)} %get-tuple-element.39.here, f32[2,64,128]{2,1,0:T(8,128)S(1)} %collective-permute-done.13.high), custom_call_target="tpu_custom_call" | custom-call | tf_op jit(solution)/shard_map/solve_next/pallas_call | solution.py:571
  97.1 0.5 collective-permute-start.14
  97.6 2.3 %collective-permute-start.16 = (f32[32,128]{1,0:T(8,128)S(1)}, f32[32,128]{1,0:T(8,128)S(1)}, u32[]{:S(2)}, u32[]{:S(2)}) collective-permute-start(f32[32,128]{1,0:T(8,128)S(1)} %get-tuple-element.41), channel_id=1, source_target_pairs={{0,8},{8,16},{16,24},{24,32},{32,40},{40,48},{48,56},{56,64},{64,7... | collective-permute-start | bytes 49160 | tf_op jit(solution)/shard_map/ppermute | solution.py:584
  99.9 5.6 %collective-permute-start.17 = (f32[32,128]{1,0:T(8,128)S(1)}, f32[32,128]{1,0:T(8,128)S(1)}, u32[]{:S(2)}, u32[]{:S(2)}) collective-permute-start(f32[32,128]{1,0:T(8,128)S(1)} %get-tuple-element.43), channel_id=1, source_target_pairs={{8,0},{16,8},{24,16},{32,24},{40,32},{48,40},{56,48},{64,56},{72,6... | collective-permute-start | bytes 49160 | tf_op jit(solution)/shard_map/ppermute | solution.py:584
  105.5 1.4 %collective-permute-done.17.next2 = f32[32,128]{1,0:T(8,128)S(1)} collective-permute-done((f32[32,128]{1,0:T(8,128)S(1)}, f32[32,128]{1,0:T(8,128)S(1)}, u32[]{:S(2)}, u32[]{:S(2)}) %collective-permute-start.17) | collective-permute-done | bytes 16416 | tf_op jit(solution)/shard_map/ppermute | solution.py:584
  107.0 4.3 %finish.1 = f32[8,64,128]{2,1,0:T(8,128)} custom-call(s32[2]{0:T(128)S(1)} %pad_add_fusion.pos, f32[21,64,128]{2,1,0:T(8,128)S(1)} %get-tuple-element.38.base, f32[2,64,128]{2,1,0:T(8,128)S(1)} %collective-permute-done.14.low, f32[2,64,128]{2,1,0:T(8,128)S(1)} %solve_next.1.here, f32[2,64,128]{2,1,0:T(8,128)S(1)} %collective-permute-done.15.high, ...), custom_call_target="tpu_custom_call" | custom-call | tf_op jit(solution)/shard_map/finish/pallas_call | solution.py:571
  (22 shorter events, 0.7 us)
Async XLA Ops:
  0.0 1.0 copy-start
  1.1 18.6 %copy-start.1 = (f32[8,64,128]{2,1,0:T(8,128)S(1)}, f32[8,64,128]{2,1,0:T(8,128)}, u32[]{:S(2)}) copy-start(f32[8,64,128]{2,1,0:T(8,128)} %source.3) | copy-start | bytes 786436
  1.1 17.4 %collective-permute-start = (f32[7,64,128]{2,1,0:T(8,128)S(1)}, f32[7,64,128]{2,1,0:T(8,128)S(1)}, u32[]{:S(2)}, u32[]{:S(2)}) collective-permute-start(f32[7,64,128]{2,1,0:T(8,128)S(1)} %pad_maximum_fusion), channel_id=1, source_target_pairs={{0,8},{8,16},{16,24},{24,32},{32,40},{40,48},{48,56},{56,64},{64,7... | collective-permute-start | bytes 688136 | tf_op jit(solution)/shard_map/ppermute | solution.py:584
  5.1 14.6 %collective-permute-start.1 = (f32[7,64,128]{2,1,0:T(8,128)S(1)}, f32[7,64,128]{2,1,0:T(8,128)S(1)}, u32[]{:S(2)}, u32[]{:S(2)}) collective-permute-start(f32[7,64,128]{2,1,0:T(8,128)S(1)} %pad_maximum_fusion.1), channel_id=1, source_target_pairs={{8,0},{16,8},{24,16},{32,24},{40,32},{48,40},{56,48},{64,56},{72,6... | collective-permute-start | bytes 688136 | tf_op jit(solution)/shard_map/ppermute | solution.py:584
  19.7 4.9 %collective-permute-start.2 = (f32[16,8,128]{2,1,0:T(8,128)S(1)}, f32[16,8,128]{2,1,0:T(8,128)S(1)}, u32[]{:S(2)}, u32[]{:S(2)}) collective-permute-start(f32[16,8,128]{2,1,0:T(8,128)S(1)} %get-tuple-element.29), channel_id=1, source_target_pairs={{0,1},{1,2},{2,3},{3,4},{4,5},{5,6},{6,7},{7,0},{8,9},{9,10},{10,1... | collective-permute-start | bytes 196616 | tf_op jit(solution)/shard_map/ppermute | solution.py:589
  19.8 4.9 %collective-permute-start.3 = (f32[16,8,128]{2,1,0:T(8,128)S(1)}, f32[16,8,128]{2,1,0:T(8,128)S(1)}, u32[]{:S(2)}, u32[]{:S(2)}) collective-permute-start(f32[16,8,128]{2,1,0:T(8,128)S(1)} %get-tuple-element.30), channel_id=1, source_target_pairs={{0,7},{1,0},{2,1},{3,2},{4,3},{5,4},{6,5},{7,6},{8,15},{9,8},{10,9... | collective-permute-start | bytes 196616 | tf_op jit(solution)/shard_map/ppermute | solution.py:589
  27.0 8.8 %collective-permute-start.5 = (f32[5,32,128]{2,1,0:T(8,128)S(1)}, f32[5,32,128]{2,1,0:T(8,128)S(1)}, u32[]{:S(2)}, u32[]{:S(2)}) collective-permute-start(f32[5,32,128]{2,1,0:T(8,128)S(1)} %get-tuple-element.32), channel_id=1, source_target_pairs={{8,0},{16,8},{24,16},{32,24},{40,32},{48,40},{56,48},{64,56},{72,6... | collective-permute-start | bytes 245768 | tf_op jit(solution)/shard_map/ppermute | solution.py:584
  33.5 8.5 %collective-permute-start.4 = (f32[5,32,128]{2,1,0:T(8,128)S(1)}, f32[5,32,128]{2,1,0:T(8,128)S(1)}, u32[]{:S(2)}, u32[]{:S(2)}) collective-permute-start(f32[5,32,128]{2,1,0:T(8,128)S(1)} %get-tuple-element.31.here), channel_id=1, source_target_pairs={{0,8},{8,16},{16,24},{24,32},{32,40},{40,48},{48,56},{56,64},{64,7... | collective-permute-start | bytes 245768 | tf_op jit(solution)/shard_map/ppermute | solution.py:584
  42.1 5.4 %collective-permute-start.6 = (f32[14,16,128]{2,1,0:T(8,128)S(1)}, f32[14,16,128]{2,1,0:T(8,128)S(1)}, u32[]{:S(2)}, u32[]{:S(2)}) collective-permute-start(f32[14,16,128]{2,1,0:T(8,128)S(1)} %get-tuple-element.33), channel_id=1, source_target_pairs={{0,1},{1,2},{2,3},{3,4},{4,5},{5,6},{6,7},{7,0},{8,9},{9,10},{10,1... | collective-permute-start | bytes 344072 | tf_op jit(solution)/shard_map/ppermute | solution.py:589
  42.1 5.4 %collective-permute-start.7 = (f32[14,16,128]{2,1,0:T(8,128)S(1)}, f32[14,16,128]{2,1,0:T(8,128)S(1)}, u32[]{:S(2)}, u32[]{:S(2)}) collective-permute-start(f32[14,16,128]{2,1,0:T(8,128)S(1)} %get-tuple-element.34), channel_id=1, source_target_pairs={{0,7},{1,0},{2,1},{3,2},{4,3},{5,4},{6,5},{7,6},{8,15},{9,8},{10,9... | collective-permute-start | bytes 344072 | tf_op jit(solution)/shard_map/ppermute | solution.py:589
  49.4 5.9 %collective-permute-start.9 = (f32[2,32,128]{2,1,0:T(8,128)S(1)}, f32[2,32,128]{2,1,0:T(8,128)S(1)}, u32[]{:S(2)}, u32[]{:S(2)}) collective-permute-start(f32[2,32,128]{2,1,0:T(8,128)S(1)} %get-tuple-element.36), channel_id=1, source_target_pairs={{8,0},{16,8},{24,16},{32,24},{40,32},{48,40},{56,48},{64,56},{72,6... | collective-permute-start | bytes 98312 | tf_op jit(solution)/shard_map/ppermute | solution.py:584
  51.4 7.9 %collective-permute-start.8 = (f32[2,32,128]{2,1,0:T(8,128)S(1)}, f32[2,32,128]{2,1,0:T(8,128)S(1)}, u32[]{:S(2)}, u32[]{:S(2)}) collective-permute-start(f32[2,32,128]{2,1,0:T(8,128)S(1)} %get-tuple-element.35.here), channel_id=1, source_target_pairs={{0,8},{8,16},{16,24},{24,32},{32,40},{40,48},{48,56},{56,64},{64,7... | collective-permute-start | bytes 98312 | tf_op jit(solution)/shard_map/ppermute | solution.py:584
  82.6 3.6 %collective-permute-start.11 = (f32[64,2,128]{2,1,0:T(2,128)S(1)}, f32[64,2,128]{2,1,0:T(2,128)S(1)}, u32[]{:S(2)}, u32[]{:S(2)}) collective-permute-start(f32[64,2,128]{2,1,0:T(2,128)S(1)} %all_to_all.5), channel_id=1, source_target_pairs={{0,7},{1,0},{2,1},{3,2},{4,3},{5,4},{6,5},{7,6},{8,15},{9,8},{10,9... | collective-permute-start | bytes 196616 | tf_op jit(solution)/shard_map/ppermute | solution.py:589
  84.3 4.9 %collective-permute-start.10 = (f32[64,2,128]{2,1,0:T(2,128)S(1)}, f32[64,2,128]{2,1,0:T(2,128)S(1)}, u32[]{:S(2)}, u32[]{:S(2)}) collective-permute-start(f32[64,2,128]{2,1,0:T(2,128)S(1)} %all_to_all.5), channel_id=1, source_target_pairs={{0,1},{1,2},{2,3},{3,4},{4,5},{5,6},{6,7},{7,0},{8,9},{9,10},{10,1... | collective-permute-start | bytes 196616 | tf_op jit(solution)/shard_map/ppermute | solution.py:589
  90.7 1.9 %collective-permute-start.13 = (f32[2,64,128]{2,1,0:T(8,128)S(1)}, f32[2,64,128]{2,1,0:T(8,128)S(1)}, u32[]{:S(2)}, u32[]{:S(2)}) collective-permute-start(f32[2,64,128]{2,1,0:T(8,128)S(1)} %get-tuple-element.39.here), channel_id=1, source_target_pairs={{0,7},{1,0},{2,1},{3,2},{4,3},{5,4},{6,5},{7,6},{8,15},{9,8},{10,9... | collective-permute-start | bytes 196616 | tf_op jit(solution)/shard_map/ppermute | solution.py:589
  90.7 4.9 %collective-permute-start.12 = (f32[2,64,128]{2,1,0:T(8,128)S(1)}, f32[2,64,128]{2,1,0:T(8,128)S(1)}, u32[]{:S(2)}, u32[]{:S(2)}) collective-permute-start(f32[2,64,128]{2,1,0:T(8,128)S(1)} %get-tuple-element.39.here), channel_id=1, source_target_pairs={{0,1},{1,2},{2,3},{3,4},{4,5},{5,6},{6,7},{7,0},{8,9},{9,10},{10,1... | collective-permute-start | bytes 196616 | tf_op jit(solution)/shard_map/ppermute | solution.py:589
  97.0 9.9 %collective-permute-start.15 = (f32[2,64,128]{2,1,0:T(8,128)S(1)}, f32[2,64,128]{2,1,0:T(8,128)S(1)}, u32[]{:S(2)}, u32[]{:S(2)}) collective-permute-start(f32[2,64,128]{2,1,0:T(8,128)S(1)} %solve_next.1.here), channel_id=1, source_target_pairs={{0,7},{1,0},{2,1},{3,2},{4,3},{5,4},{6,5},{7,6},{8,15},{9,8},{10,9... | collective-permute-start | bytes 196616 | tf_op jit(solution)/shard_map/ppermute | solution.py:589
  97.1 9.9 %collective-permute-start.14 = (f32[2,64,128]{2,1,0:T(8,128)S(1)}, f32[2,64,128]{2,1,0:T(8,128)S(1)}, u32[]{:S(2)}, u32[]{:S(2)}) collective-permute-start(f32[2,64,128]{2,1,0:T(8,128)S(1)} %solve_next.1.here), channel_id=1, source_target_pairs={{0,1},{1,2},{2,3},{3,4},{4,5},{5,6},{6,7},{7,0},{8,9},{9,10},{10,1... | collective-permute-start | bytes 196616 | tf_op jit(solution)/shard_map/ppermute | solution.py:589
  97.6 8.0 %collective-permute-start.16 = (f32[32,128]{1,0:T(8,128)S(1)}, f32[32,128]{1,0:T(8,128)S(1)}, u32[]{:S(2)}, u32[]{:S(2)}) collective-permute-start(f32[32,128]{1,0:T(8,128)S(1)} %get-tuple-element.41), channel_id=1, source_target_pairs={{0,8},{8,16},{16,24},{24,32},{32,40},{40,48},{48,56},{56,64},{64,7... | collective-permute-start | bytes 49160 | tf_op jit(solution)/shard_map/ppermute | solution.py:584
  99.9 7.1 %collective-permute-start.17 = (f32[32,128]{1,0:T(8,128)S(1)}, f32[32,128]{1,0:T(8,128)S(1)}, u32[]{:S(2)}, u32[]{:S(2)}) collective-permute-start(f32[32,128]{1,0:T(8,128)S(1)} %get-tuple-element.43), channel_id=1, source_target_pairs={{8,0},{16,8},{24,16},{32,24},{40,32},{48,40},{56,48},{64,56},{72,6... | collective-permute-start | bytes 49160 | tf_op jit(solution)/shard_map/ppermute | solution.py:584

commit v4 on v3

--- a/solution.py
+++ b/solution.py
@@ -453,7 +453,7 @@
         out[1, :, :] = self.update[1, :, :]
 
 
-def solve_first(count, pos, low, here, high, base, out, half, state, update):
+def solve_first(count, pos, low, here, high, arrived, base, out, half, state, update):
     has_low, has_high = inside_z(pos[1], count)
     level = Coarsest(base, state, update)
     level.start((low, here, high), half, (has_low, 1.0, has_high))
@@ -461,7 +461,7 @@
     level.leave(out)
 
 
-def solve_next(count, pos, base, low, here, high, out, state, update):
+def solve_next(count, pos, base, low, here, high, arrived, out, state, update):
     has_low, has_high = inside_z(pos[1], count)
     level = Coarsest(base, state, update)
     level.resume((low, here, high), (has_low, 1.0, has_high))
@@ -665,12 +665,13 @@
         [scratch(3, nx + 16, LANES)] + solving,
         pos,
         *blocks,
+        prev2,
     )
     low, high = (turn(here, "gz", 1), turn(here, "gz", -1))
     for_prev, _ = lax.optimization_barrier((for_prev, here))
     next2 = shift(for_prev, "gx", -1)
     (here,) = call(
-        functools.partial(solve_next, nz), "solve_next", [f32(2, nx, LANES)], solving, pos, base, low, here, high
+        functools.partial(solve_next, nz), "solve_next", [f32(2, nx, LANES)], solving, pos, base, low, here, high, next2
     )
     low, high = (turn(here, "gz", 1), turn(here, "gz", -1))
 

time: 112 us -> 114 us (1.018)
  waiting for transfers between devices: 30.5 us -> 33.8 us
    ppermute x8, waiting for transfers between devices: 16.8 us -> 24.5 us  [shift(): lax.ppermute(array, axis, [(i, i + by) for i in range(devices) if 0 <= i...]
    ppermute x10, waiting for transfers between devices: 13.7 us -> 9.25 us  [turn(): lax.ppermute(array, axis, [(i, (i + by) % devices) for i in range(devices)])]
    ppermute x8, starting transfers between devices: 35.9 us -> 32.2 us  [shift(): lax.ppermute(array, axis, [(i, i + by) for i in range(devices) if 0 <= i...]
    ppermute x10, starting transfers between devices: 8.6 us -> 11.2 us  [turn(): lax.ppermute(array, axis, [(i, (i + by) % devices) for i in range(devices)])]
  transfers between devices with their start and end apart: 18 -> 18, of which waited for: 12 -> 11; matrix products, arithmetic and copies ran while one was open for 0% -> 0% of each run, Pallas kernels for 0% -> 0%
where the time goes in v4:
time: 114 us; the launch traced here: 113 us
  starting transfers between devices  43.4 us (38%)
  waiting for transfers between devices  33.8 us (30%)
  blocking collectives  22 us (19%)
  Pallas kernels  12.8 us (11%)
    ppermute x8, starting transfers between devices, shift(): lax.ppermute(array, axis, [(i, i + by) for i in range(devices) if 0 <= i...  32.2 us
    ppermute x8, waiting for transfers between devices, shift(): lax.ppermute(array, axis, [(i, i + by) for i in range(devices) if 0 <= i...  24.5 us
    all_to_all x1, blocking collectives, on_device(): here = lax.all_to_all(row3, 'gx', 0, 0, tiled=True)  22 us
    pallas_call x8, Pallas kernels, call(): pl.pallas_call(kernel, name=name, out_shape=outs, in_specs=[smem if arg.d...  12.8 us
    ppermute x10, starting transfers between devices, turn(): lax.ppermute(array, axis, [(i, (i + by) % devices) for i in range(devices)])  11.2 us
    ppermute x10, waiting for transfers between devices, turn(): lax.ppermute(array, axis, [(i, (i + by) % devices) for i in range(devices)])  9.25 us
  transfers between devices with their start and end apart: 18, of which 11 were waited for; matrix products, arithmetic and copies ran while one was open for 0% of the time, Pallas kernels for 0%

profile of v4, /device:TPU:6, one launch (start us, length us, event | category | flops | bytes accessed | tf_op | source)
XLA Modules:
  0.0 113.4 jit_solution(14297935776250923808)
XLA Ops:
  0.0 1.0 fusion
  1.1 4.0 %collective-permute-start = (f32[7,64,128]{2,1,0:T(8,128)S(1)}, f32[7,64,128]{2,1,0:T(8,128)S(1)}, u32[]{:S(2)}, u32[]{:S(2)}) collective-permute-start(f32[7,64,128]{2,1,0:T(8,128)S(1)} %pad_maximum_fusion), channel_id=1, source_target_pairs={{0,8},{8,16},{16,24},{24,32},{32,40},{40,48},{48,56},{56,64},{64,7... | collective-permute-start | bytes 688136 | tf_op jit(solution)/shard_map/ppermute | solution.py:584
  5.1 9.8 %collective-permute-start.1 = (f32[7,64,128]{2,1,0:T(8,128)S(1)}, f32[7,64,128]{2,1,0:T(8,128)S(1)}, u32[]{:S(2)}, u32[]{:S(2)}) collective-permute-start(f32[7,64,128]{2,1,0:T(8,128)S(1)} %pad_maximum_fusion.1), channel_id=1, source_target_pairs={{8,0},{16,8},{24,16},{32,24},{40,32},{48,40},{56,48},{64,56},{72,6... | collective-permute-start | bytes 688136 | tf_op jit(solution)/shard_map/ppermute | solution.py:584
  14.9 3.6 %collective-permute-done.low = f32[7,64,128]{2,1,0:T(8,128)S(1)} collective-permute-done((f32[7,64,128]{2,1,0:T(8,128)S(1)}, f32[7,64,128]{2,1,0:T(8,128)S(1)}, u32[]{:S(2)}, u32[]{:S(2)}) %collective-permute-start) | collective-permute-done | bytes 229408 | tf_op jit(solution)/shard_map/ppermute | solution.py:584
  18.5 1.2 %collective-permute-done.1.high = f32[7,64,128]{2,1,0:T(8,128)S(1)} collective-permute-done((f32[7,64,128]{2,1,0:T(8,128)S(1)}, f32[7,64,128]{2,1,0:T(8,128)S(1)}, u32[]{:S(2)}, u32[]{:S(2)}) %collective-permute-start.1) | collective-permute-done | bytes 229408 | tf_op jit(solution)/shard_map/ppermute | solution.py:584
  19.8 2.9 %collective-permute-start.3 = (f32[16,8,128]{2,1,0:T(8,128)S(1)}, f32[16,8,128]{2,1,0:T(8,128)S(1)}, u32[]{:S(2)}, u32[]{:S(2)}) collective-permute-start(f32[16,8,128]{2,1,0:T(8,128)S(1)} %get-tuple-element.30), channel_id=1, source_target_pairs={{0,7},{1,0},{2,1},{3,2},{4,3},{5,4},{6,5},{7,6},{8,15},{9,8},{10,9... | collective-permute-start | bytes 196616 | tf_op jit(solution)/shard_map/ppermute | solution.py:589
  22.8 1.9 %collective-permute-done.2.z_low = f32[16,8,128]{2,1,0:T(8,128)S(1)} collective-permute-done((f32[16,8,128]{2,1,0:T(8,128)S(1)}, f32[16,8,128]{2,1,0:T(8,128)S(1)}, u32[]{:S(2)}, u32[]{:S(2)}) %collective-permute-start.2) | collective-permute-done | bytes 65568 | tf_op jit(solution)/shard_map/ppermute | solution.py:589
  24.7 2.3 %down_0.1 = (f32[10,80,128]{2,1,0:T(8,128)S(1)}, f32[12,80,128]{2,1,0:T(8,128)S(1)}, f32[12,80,128]{2,1,0:T(8,128)S(1)}, f32[5,32,128]{2,1,0:T(8,128)S(1)}, f32[5,32,128]{2,1,0:T(8,128)S(1)}) custom-call(s32[2]{0:T(128)S(1)} %pad_add_fusion.pos, f32[8,64,128]{2,1,0:T(8,128)S(1)} %copy-done.1, f32[8,64,128]{2,1,0:T(8,128)S(1)} %copy-done, ...), custom_call_target="tpu_custom_call" | custom-call | tf_op jit(solution)/shard_map/down_0/pallas_call | solution.py:571
  27.0 6.5 %collective-permute-start.5 = (f32[5,32,128]{2,1,0:T(8,128)S(1)}, f32[5,32,128]{2,1,0:T(8,128)S(1)}, u32[]{:S(2)}, u32[]{:S(2)}) collective-permute-start(f32[5,32,128]{2,1,0:T(8,128)S(1)} %get-tuple-element.32), channel_id=1, source_target_pairs={{8,0},{16,8},{24,16},{32,24},{40,32},{48,40},{56,48},{64,56},{72,6... | collective-permute-start | bytes 245768 | tf_op jit(solution)/shard_map/ppermute | solution.py:584
  33.5 1.9 %collective-permute-start.4 = (f32[5,32,128]{2,1,0:T(8,128)S(1)}, f32[5,32,128]{2,1,0:T(8,128)S(1)}, u32[]{:S(2)}, u32[]{:S(2)}) collective-permute-start(f32[5,32,128]{2,1,0:T(8,128)S(1)} %get-tuple-element.31.here), channel_id=1, source_target_pairs={{0,8},{8,16},{16,24},{24,32},{32,40},{40,48},{48,56},{56,64},{64,7... | collective-permute-start | bytes 245768 | tf_op jit(solution)/shard_map/ppermute | solution.py:584
  35.4 0.4 collective-permute-done.5.high
  35.8 6.2 %collective-permute-done.4.low = f32[5,32,128]{2,1,0:T(8,128)S(1)} collective-permute-done((f32[5,32,128]{2,1,0:T(8,128)S(1)}, f32[5,32,128]{2,1,0:T(8,128)S(1)}, u32[]{:S(2)}, u32[]{:S(2)}) %collective-permute-start.4) | collective-permute-done | bytes 81952 | tf_op jit(solution)/shard_map/ppermute | solution.py:584
  42.1 2.9 %collective-permute-start.7 = (f32[14,16,128]{2,1,0:T(8,128)S(1)}, f32[14,16,128]{2,1,0:T(8,128)S(1)}, u32[]{:S(2)}, u32[]{:S(2)}) collective-permute-start(f32[14,16,128]{2,1,0:T(8,128)S(1)} %get-tuple-element.34), channel_id=1, source_target_pairs={{0,7},{1,0},{2,1},{3,2},{4,3},{5,4},{6,5},{7,6},{8,15},{9,8},{10,9... | collective-permute-start | bytes 344072 | tf_op jit(solution)/shard_map/ppermute | solution.py:589
  45.0 2.5 %collective-permute-done.6.z_low = f32[14,16,128]{2,1,0:T(8,128)S(1)} collective-permute-done((f32[14,16,128]{2,1,0:T(8,128)S(1)}, f32[14,16,128]{2,1,0:T(8,128)S(1)}, u32[]{:S(2)}, u32[]{:S(2)}) %collective-permute-start.6) | collective-permute-done | bytes 114720 | tf_op jit(solution)/shard_map/ppermute | solution.py:589
  47.5 1.9 %down_1.1 = (f32[8,48,128]{2,1,0:T(8,128)S(1)}, f32[10,48,128]{2,1,0:T(8,128)S(1)}, f32[10,48,128]{2,1,0:T(8,128)S(1)}, f32[2,32,128]{2,1,0:T(8,128)S(1)}, f32[2,32,128]{2,1,0:T(8,128)S(1)}) custom-call(s32[2]{0:T(128)S(1)} %pad_add_fusion.pos, f32[5,32,128]{2,1,0:T(8,128)S(1)} %get-tuple-element.31.here, f32[5,32,128]{2,1,0:T(8,128)S(1)} %collective-permute-done.4.low, ...), custom_call_target="tpu_custom_call" | custom-call | tf_op jit(solution)/shard_map/down_1/pallas_call | solution.py:571
  49.4 1.9 %collective-permute-start.9 = (f32[2,32,128]{2,1,0:T(8,128)S(1)}, f32[2,32,128]{2,1,0:T(8,128)S(1)}, u32[]{:S(2)}, u32[]{:S(2)}) collective-permute-start(f32[2,32,128]{2,1,0:T(8,128)S(1)} %get-tuple-element.36), channel_id=1, source_target_pairs={{8,0},{16,8},{24,16},{32,24},{40,32},{48,40},{56,48},{64,56},{72,6... | collective-permute-start | bytes 98312 | tf_op jit(solution)/shard_map/ppermute | solution.py:584
  51.4 3.9 %collective-permute-start.8 = (f32[2,32,128]{2,1,0:T(8,128)S(1)}, f32[2,32,128]{2,1,0:T(8,128)S(1)}, u32[]{:S(2)}, u32[]{:S(2)}) collective-permute-start(f32[2,32,128]{2,1,0:T(8,128)S(1)} %get-tuple-element.35.here), channel_id=1, source_target_pairs={{0,8},{8,16},{16,24},{24,32},{32,40},{40,48},{48,56},{56,64},{64,7... | collective-permute-start | bytes 98312 | tf_op jit(solution)/shard_map/ppermute | solution.py:584
  55.3 4.0 %collective-permute-done.8.prev = f32[2,32,128]{2,1,0:T(8,128)S(1)} collective-permute-done((f32[2,32,128]{2,1,0:T(8,128)S(1)}, f32[2,32,128]{2,1,0:T(8,128)S(1)}, u32[]{:S(2)}, u32[]{:S(2)}) %collective-permute-start.8) | collective-permute-done | bytes 32800 | tf_op jit(solution)/shard_map/ppermute | solution.py:584
  59.3 1.4 %down_2.1 = (f32[8,32,128]{2,1,0:T(8,128)S(1)}, f32[10,32,128]{2,1,0:T(8,128)S(1)}, f32[2,32,128]{2,1,0:T(8,128)S(1)}, f32[64,2,128]{2,1,0:T(2,128)S(1)}, f32[32,128]{1,0:T(8,128)S(1)}, /*index=5*/f32[32,128]{1,0:T(8,128)S(1)}) custom-call(s32[2]{0:T(128)S(1)} %pad_add_fusion.pos, f32[2,32,128]{2,1,0:T(8,128)S(1)} %collective-permute-done.8.prev, ...), custom_call_target="tpu_custom_call" | custom-call | tf_op jit(solution)/shard_map/down_2/pallas_call | solution.py:571
  60.7 22.0 %all_to_all.5 = f32[64,2,128]{2,1,0:T(2,128)S(1)} all-to-all(f32[64,2,128]{2,1,0:T(2,128)S(1)} %get-tuple-element.37), channel_id=1, replica_groups=mesh['gx'=64,'gz'=8] {'gx'}, dimensions={0} | all-to-all | bytes 131072 | tf_op jit(solution)/shard_map/all_to_all | solution.py:655
  82.6 1.6 %collective-permute-start.11 = (f32[64,2,128]{2,1,0:T(2,128)S(1)}, f32[64,2,128]{2,1,0:T(2,128)S(1)}, u32[]{:S(2)}, u32[]{:S(2)}) collective-permute-start(f32[64,2,128]{2,1,0:T(2,128)S(1)} %all_to_all.5), channel_id=1, source_target_pairs={{0,7},{1,0},{2,1},{3,2},{4,3},{5,4},{6,5},{7,6},{8,15},{9,8},{10,9... | collective-permute-start | bytes 196616 | tf_op jit(solution)/shard_map/ppermute | solution.py:589
  84.3 2.3 %collective-permute-start.12 = (f32[32,128]{1,0:T(8,128)S(1)}, f32[32,128]{1,0:T(8,128)S(1)}, u32[]{:S(2)}, u32[]{:S(2)}) collective-permute-start(f32[32,128]{1,0:T(8,128)S(1)} %get-tuple-element.39), channel_id=1, source_target_pairs={{0,8},{8,16},{16,24},{24,32},{32,40},{40,48},{48,56},{56,64},{64,7... | collective-permute-start | bytes 49160 | tf_op jit(solution)/shard_map/ppermute | solution.py:584
  86.6 5.4 %collective-permute-done.12.arrived.prev2 = f32[32,128]{1,0:T(8,128)S(1)} collective-permute-done((f32[32,128]{1,0:T(8,128)S(1)}, f32[32,128]{1,0:T(8,128)S(1)}, u32[]{:S(2)}, u32[]{:S(2)}) %collective-permute-start.12) | collective-permute-done | bytes 16416 | tf_op jit(solution)/shard_map/ppermute | solution.py:584
  92.0 1.5 %solve_first.1 = (f32[21,64,128]{2,1,0:T(8,128)S(1)}, f32[2,64,128]{2,1,0:T(8,128)S(1)}) custom-call(s32[2]{0:T(128)S(1)} %pad_add_fusion.pos, f32[128,128]{1,0:T(8,128)S(1)} %bitcast.7, f32[128,128]{1,0:T(8,128)S(1)} %bitcast.5, f32[128,128]{1,0:T(8,128)S(1)} %bitcast.6, f32[32,128]{1,0:T(8,128)S(1)} %collective-permute-done.12.arrived.prev2), custom_call_target="tpu_custom_call" | custom-call | tf_op jit(solution)/shard_map/solve_first/pallas_call | solution.py:571
  93.5 1.8 %collective-permute-start.14 = (f32[2,64,128]{2,1,0:T(8,128)S(1)}, f32[2,64,128]{2,1,0:T(8,128)S(1)}, u32[]{:S(2)}, u32[]{:S(2)}) collective-permute-start(f32[2,64,128]{2,1,0:T(8,128)S(1)} %get-tuple-element.41.here), channel_id=1, source_target_pairs={{0,7},{1,0},{2,1},{3,2},{4,3},{5,4},{6,5},{7,6},{8,15},{9,8},{10,9... | collective-permute-start | bytes 196616 | tf_op jit(solution)/shard_map/ppermute | solution.py:589
  95.3 1.9 %collective-permute-start.15 = (f32[32,128]{1,0:T(8,128)S(1)}, f32[32,128]{1,0:T(8,128)S(1)}, u32[]{:S(2)}, u32[]{:S(2)}) collective-permute-start(f32[32,128]{1,0:T(8,128)S(1)} %get-tuple-element.43), channel_id=1, source_target_pairs={{8,0},{16,8},{24,16},{32,24},{40,32},{48,40},{56,48},{64,56},{72,6... | collective-permute-start | bytes 49160 | tf_op jit(solution)/shard_map/ppermute | solution.py:584
  97.3 3.7 %collective-permute-done.15.arrived.next2 = f32[32,128]{1,0:T(8,128)S(1)} collective-permute-done((f32[32,128]{1,0:T(8,128)S(1)}, f32[32,128]{1,0:T(8,128)S(1)}, u32[]{:S(2)}, u32[]{:S(2)}) %collective-permute-start.15) | collective-permute-done | bytes 16416 | tf_op jit(solution)/shard_map/ppermute | solution.py:584
  101.0 1.4 %solve_next.1.here = f32[2,64,128]{2,1,0:T(8,128)S(1)} custom-call(s32[2]{0:T(128)S(1)} %pad_add_fusion.pos, f32[21,64,128]{2,1,0:T(8,128)S(1)} %get-tuple-element.40.base, f32[2,64,128]{2,1,0:T(8,128)S(1)} %collective-permute-done.13.low, f32[2,64,128]{2,1,0:T(8,128)S(1)} %get-tuple-element.41.here, f32[2,64,128]{2,1,0:T(8,128)S(1)} %collective-permute-done.14.high, ...), custom_call_target="tpu_custom_call" | custom-call | tf_op jit(solution)/shard_map/solve_next/pallas_call | solution.py:571
  102.4 1.8 %collective-permute-start.17 = (f32[2,64,128]{2,1,0:T(8,128)S(1)}, f32[2,64,128]{2,1,0:T(8,128)S(1)}, u32[]{:S(2)}, u32[]{:S(2)}) collective-permute-start(f32[2,64,128]{2,1,0:T(8,128)S(1)} %solve_next.1.here), channel_id=1, source_target_pairs={{0,7},{1,0},{2,1},{3,2},{4,3},{5,4},{6,5},{7,6},{8,15},{9,8},{10,9... | collective-permute-start | bytes 196616 | tf_op jit(solution)/shard_map/ppermute | solution.py:589
  104.2 1.9 %collective-permute-done.17.high = f32[2,64,128]{2,1,0:T(8,128)S(1)} collective-permute-done((f32[2,64,128]{2,1,0:T(8,128)S(1)}, f32[2,64,128]{2,1,0:T(8,128)S(1)}, u32[]{:S(2)}, u32[]{:S(2)}) %collective-permute-start.17) | collective-permute-done | bytes 65568 | tf_op jit(solution)/shard_map/ppermute | solution.py:589
  106.1 3.0 %collective-permute-done.16.low = f32[2,64,128]{2,1,0:T(8,128)S(1)} collective-permute-done((f32[2,64,128]{2,1,0:T(8,128)S(1)}, f32[2,64,128]{2,1,0:T(8,128)S(1)}, u32[]{:S(2)}, u32[]{:S(2)}) %collective-permute-start.16) | collective-permute-done | bytes 65568 | tf_op jit(solution)/shard_map/ppermute | solution.py:589
  109.1 4.3 %finish.1 = f32[8,64,128]{2,1,0:T(8,128)} custom-call(s32[2]{0:T(128)S(1)} %pad_add_fusion.pos, f32[21,64,128]{2,1,0:T(8,128)S(1)} %get-tuple-element.40.base, f32[2,64,128]{2,1,0:T(8,128)S(1)} %collective-permute-done.16.low, f32[2,64,128]{2,1,0:T(8,128)S(1)} %solve_next.1.here, f32[2,64,128]{2,1,0:T(8,128)S(1)} %collective-permute-done.17.high, ...), custom_call_target="tpu_custom_call" | custom-call | tf_op jit(solution)/shard_map/finish/pallas_call | solution.py:571
  (22 shorter events, 0.3 us)
Async XLA Ops:
  0.0 1.0 copy-start
  1.1 18.6 %copy-start.1 = (f32[8,64,128]{2,1,0:T(8,128)S(1)}, f32[8,64,128]{2,1,0:T(8,128)}, u32[]{:S(2)}) copy-start(f32[8,64,128]{2,1,0:T(8,128)} %source.3) | copy-start | bytes 786436
  1.1 17.4 %collective-permute-start = (f32[7,64,128]{2,1,0:T(8,128)S(1)}, f32[7,64,128]{2,1,0:T(8,128)S(1)}, u32[]{:S(2)}, u32[]{:S(2)}) collective-permute-start(f32[7,64,128]{2,1,0:T(8,128)S(1)} %pad_maximum_fusion), channel_id=1, source_target_pairs={{0,8},{8,16},{16,24},{24,32},{32,40},{40,48},{48,56},{56,64},{64,7... | collective-permute-start | bytes 688136 | tf_op jit(solution)/shard_map/ppermute | solution.py:584
  5.1 14.6 %collective-permute-start.1 = (f32[7,64,128]{2,1,0:T(8,128)S(1)}, f32[7,64,128]{2,1,0:T(8,128)S(1)}, u32[]{:S(2)}, u32[]{:S(2)}) collective-permute-start(f32[7,64,128]{2,1,0:T(8,128)S(1)} %pad_maximum_fusion.1), channel_id=1, source_target_pairs={{8,0},{16,8},{24,16},{32,24},{40,32},{48,40},{56,48},{64,56},{72,6... | collective-permute-start | bytes 688136 | tf_op jit(solution)/shard_map/ppermute | solution.py:584
  19.7 4.9 %collective-permute-start.2 = (f32[16,8,128]{2,1,0:T(8,128)S(1)}, f32[16,8,128]{2,1,0:T(8,128)S(1)}, u32[]{:S(2)}, u32[]{:S(2)}) collective-permute-start(f32[16,8,128]{2,1,0:T(8,128)S(1)} %get-tuple-element.29), channel_id=1, source_target_pairs={{0,1},{1,2},{2,3},{3,4},{4,5},{5,6},{6,7},{7,0},{8,9},{9,10},{10,1... | collective-permute-start | bytes 196616 | tf_op jit(solution)/shard_map/ppermute | solution.py:589
  19.8 4.9 %collective-permute-start.3 = (f32[16,8,128]{2,1,0:T(8,128)S(1)}, f32[16,8,128]{2,1,0:T(8,128)S(1)}, u32[]{:S(2)}, u32[]{:S(2)}) collective-permute-start(f32[16,8,128]{2,1,0:T(8,128)S(1)} %get-tuple-element.30), channel_id=1, source_target_pairs={{0,7},{1,0},{2,1},{3,2},{4,3},{5,4},{6,5},{7,6},{8,15},{9,8},{10,9... | collective-permute-start | bytes 196616 | tf_op jit(solution)/shard_map/ppermute | solution.py:589
  27.0 8.8 %collective-permute-start.5 = (f32[5,32,128]{2,1,0:T(8,128)S(1)}, f32[5,32,128]{2,1,0:T(8,128)S(1)}, u32[]{:S(2)}, u32[]{:S(2)}) collective-permute-start(f32[5,32,128]{2,1,0:T(8,128)S(1)} %get-tuple-element.32), channel_id=1, source_target_pairs={{8,0},{16,8},{24,16},{32,24},{40,32},{48,40},{56,48},{64,56},{72,6... | collective-permute-start | bytes 245768 | tf_op jit(solution)/shard_map/ppermute | solution.py:584
  33.5 8.5 %collective-permute-start.4 = (f32[5,32,128]{2,1,0:T(8,128)S(1)}, f32[5,32,128]{2,1,0:T(8,128)S(1)}, u32[]{:S(2)}, u32[]{:S(2)}) collective-permute-start(f32[5,32,128]{2,1,0:T(8,128)S(1)} %get-tuple-element.31.here), channel_id=1, source_target_pairs={{0,8},{8,16},{16,24},{24,32},{32,40},{40,48},{48,56},{56,64},{64,7... | collective-permute-start | bytes 245768 | tf_op jit(solution)/shard_map/ppermute | solution.py:584
  42.1 5.4 %collective-permute-start.6 = (f32[14,16,128]{2,1,0:T(8,128)S(1)}, f32[14,16,128]{2,1,0:T(8,128)S(1)}, u32[]{:S(2)}, u32[]{:S(2)}) collective-permute-start(f32[14,16,128]{2,1,0:T(8,128)S(1)} %get-tuple-element.33), channel_id=1, source_target_pairs={{0,1},{1,2},{2,3},{3,4},{4,5},{5,6},{6,7},{7,0},{8,9},{9,10},{10,1... | collective-permute-start | bytes 344072 | tf_op jit(solution)/shard_map/ppermute | solution.py:589
  42.1 5.4 %collective-permute-start.7 = (f32[14,16,128]{2,1,0:T(8,128)S(1)}, f32[14,16,128]{2,1,0:T(8,128)S(1)}, u32[]{:S(2)}, u32[]{:S(2)}) collective-permute-start(f32[14,16,128]{2,1,0:T(8,128)S(1)} %get-tuple-element.34), channel_id=1, source_target_pairs={{0,7},{1,0},{2,1},{3,2},{4,3},{5,4},{6,5},{7,6},{8,15},{9,8},{10,9... | collective-permute-start | bytes 344072 | tf_op jit(solution)/shard_map/ppermute | solution.py:589
  49.4 5.9 %collective-permute-start.9 = (f32[2,32,128]{2,1,0:T(8,128)S(1)}, f32[2,32,128]{2,1,0:T(8,128)S(1)}, u32[]{:S(2)}, u32[]{:S(2)}) collective-permute-start(f32[2,32,128]{2,1,0:T(8,128)S(1)} %get-tuple-element.36), channel_id=1, source_target_pairs={{8,0},{16,8},{24,16},{32,24},{40,32},{48,40},{56,48},{64,56},{72,6... | collective-permute-start | bytes 98312 | tf_op jit(solution)/shard_map/ppermute | solution.py:584
  51.4 7.9 %collective-permute-start.8 = (f32[2,32,128]{2,1,0:T(8,128)S(1)}, f32[2,32,128]{2,1,0:T(8,128)S(1)}, u32[]{:S(2)}, u32[]{:S(2)}) collective-permute-start(f32[2,32,128]{2,1,0:T(8,128)S(1)} %get-tuple-element.35.here), channel_id=1, source_target_pairs={{0,8},{8,16},{16,24},{24,32},{32,40},{40,48},{48,56},{56,64},{64,7... | collective-permute-start | bytes 98312 | tf_op jit(solution)/shard_map/ppermute | solution.py:584
  82.6 9.4 %collective-permute-start.11 = (f32[64,2,128]{2,1,0:T(2,128)S(1)}, f32[64,2,128]{2,1,0:T(2,128)S(1)}, u32[]{:S(2)}, u32[]{:S(2)}) collective-permute-start(f32[64,2,128]{2,1,0:T(2,128)S(1)} %all_to_all.5), channel_id=1, source_target_pairs={{0,7},{1,0},{2,1},{3,2},{4,3},{5,4},{6,5},{7,6},{8,15},{9,8},{10,9... | collective-permute-start | bytes 196616 | tf_op jit(solution)/shard_map/ppermute | solution.py:589
  84.3 7.7 %collective-permute-start.10 = (f32[64,2,128]{2,1,0:T(2,128)S(1)}, f32[64,2,128]{2,1,0:T(2,128)S(1)}, u32[]{:S(2)}, u32[]{:S(2)}) collective-permute-start(f32[64,2,128]{2,1,0:T(2,128)S(1)} %all_to_all.5), channel_id=1, source_target_pairs={{0,1},{1,2},{2,3},{3,4},{4,5},{5,6},{6,7},{7,0},{8,9},{9,10},{10,1... | collective-permute-start | bytes 196616 | tf_op jit(solution)/shard_map/ppermute | solution.py:589
  84.3 7.7 %collective-permute-start.12 = (f32[32,128]{1,0:T(8,128)S(1)}, f32[32,128]{1,0:T(8,128)S(1)}, u32[]{:S(2)}, u32[]{:S(2)}) collective-permute-start(f32[32,128]{1,0:T(8,128)S(1)} %get-tuple-element.39), channel_id=1, source_target_pairs={{0,8},{8,16},{16,24},{24,32},{32,40},{40,48},{48,56},{56,64},{64,7... | collective-permute-start | bytes 49160 | tf_op jit(solution)/shard_map/ppermute | solution.py:584
  93.5 7.4 %collective-permute-start.14 = (f32[2,64,128]{2,1,0:T(8,128)S(1)}, f32[2,64,128]{2,1,0:T(8,128)S(1)}, u32[]{:S(2)}, u32[]{:S(2)}) collective-permute-start(f32[2,64,128]{2,1,0:T(8,128)S(1)} %get-tuple-element.41.here), channel_id=1, source_target_pairs={{0,7},{1,0},{2,1},{3,2},{4,3},{5,4},{6,5},{7,6},{8,15},{9,8},{10,9... | collective-permute-start | bytes 196616 | tf_op jit(solution)/shard_map/ppermute | solution.py:589
  95.3 5.6 %collective-permute-start.13 = (f32[2,64,128]{2,1,0:T(8,128)S(1)}, f32[2,64,128]{2,1,0:T(8,128)S(1)}, u32[]{:S(2)}, u32[]{:S(2)}) collective-permute-start(f32[2,64,128]{2,1,0:T(8,128)S(1)} %get-tuple-element.41.here), channel_id=1, source_target_pairs={{0,1},{1,2},{2,3},{3,4},{4,5},{5,6},{6,7},{7,0},{8,9},{9,10},{10,1... | collective-permute-start | bytes 196616 | tf_op jit(solution)/shard_map/ppermute | solution.py:589
  95.3 5.6 %collective-permute-start.15 = (f32[32,128]{1,0:T(8,128)S(1)}, f32[32,128]{1,0:T(8,128)S(1)}, u32[]{:S(2)}, u32[]{:S(2)}) collective-permute-start(f32[32,128]{1,0:T(8,128)S(1)} %get-tuple-element.43), channel_id=1, source_target_pairs={{8,0},{16,8},{24,16},{32,24},{40,32},{48,40},{56,48},{64,56},{72,6... | collective-permute-start | bytes 49160 | tf_op jit(solution)/shard_map/ppermute | solution.py:584
  102.4 3.7 %collective-permute-start.17 = (f32[2,64,128]{2,1,0:T(8,128)S(1)}, f32[2,64,128]{2,1,0:T(8,128)S(1)}, u32[]{:S(2)}, u32[]{:S(2)}) collective-permute-start(f32[2,64,128]{2,1,0:T(8,128)S(1)} %solve_next.1.here), channel_id=1, source_target_pairs={{0,7},{1,0},{2,1},{3,2},{4,3},{5,4},{6,5},{7,6},{8,15},{9,8},{10,9... | collective-permute-start | bytes 196616 | tf_op jit(solution)/shard_map/ppermute | solution.py:589
  104.2 4.9 %collective-permute-start.16 = (f32[2,64,128]{2,1,0:T(8,128)S(1)}, f32[2,64,128]{2,1,0:T(8,128)S(1)}, u32[]{:S(2)}, u32[]{:S(2)}) collective-permute-start(f32[2,64,128]{2,1,0:T(8,128)S(1)} %solve_next.1.here), channel_id=1, source_target_pairs={{0,1},{1,2},{2,3},{3,4},{4,5},{5,6},{6,7},{7,0},{8,9},{9,10},{10,1... | collective-permute-start | bytes 196616 | tf_op jit(solution)/shard_map/ppermute | solution.py:589

commit v5 on v3

--- a/solution.py
+++ b/solution.py
@@ -11,6 +11,7 @@
 COARSE_ITERS = 20
 LANES = 128
 ROW = 16
+LATE = 8
 SOLVE = (8, 16)
 
 
@@ -49,53 +50,39 @@
     return value + jnp.where(odd, roll(value, stride), roll(value, -stride))
 
 
-class View:
-    def __init__(self, ref, plane, row):
-        self.ref, self.plane, self.row = (ref, plane, row)
-
-    def __getitem__(self, index):
-        plane, rows, lanes = index
-        return self.ref[plane - self.plane, rows.start - self.row : rows.stop - self.row, lanes]
-
-
 class Level:
     def __init__(self, level, gx, gz, brick, cells, first_plane, refs, first_row=ROW):
         self.stride, self.scale, self.first_row = (2**level, 0.25**level, first_row)
         self.gx, self.gz, self.brick, self.cells, self.first_plane = (gx, gz, brick, cells, first_plane)
         self.half, self.fx, self.fz, self.left, self.right, self.diag, self.inverse = refs
 
-    def coefs(self, planes, row, count):
+    def coefs(self, planes, row, count, source, first):
         half, stride = (self.half, self.stride)
         lane = lanes_of(count)
+        in_left, in_right = (lane >= stride, lane < LANES - stride)
         here = rows_of(count) + (row - self.first_row + self.gz * self.brick[1])
-        first, last = (planes[0], planes[-1])
-        for p in planes:
-            self.fx[p, row : row + count, :] = half[p - 1, row : row + count, :] + half[p, row : row + count, :]
-        p = last + 1
-        self.fx[p, row : row + count, :] = half[p - 1, row : row + count, :] + half[p, row : row + count, :]
-        more = count + 1
-        for p in planes:
-            self.fz[p, row : row + more, :] = half[p, row - 1 : row - 1 + more, :] + half[p, row : row + more, :]
+        inside_rows = jnp.where((here >= 0) & (here < self.cells[1]), 1.0 / self.scale, 0.0)
         for p in planes:
             center = half[p, row : row + count, :]
-            face_left = center + jnp.where(lane >= stride, roll(center, stride), 0.0)
-            face_right = center + jnp.where(lane < LANES - stride, roll(center, -stride), 0.0)
-            diagonal = (
-                self.fx[p, row : row + count, :]
-                + self.fx[p + 1, row : row + count, :]
-                + self.fz[p, row : row + count, :]
-                + self.fz[p, row + 1 : row + 1 + count, :]
-                + face_left
-                + face_right
-            )
-            self.left[p, row : row + count, :] = jnp.where(lane >= stride, face_left, 0.0)
-            self.right[p, row : row + count, :] = jnp.where(lane < LANES - stride, face_right, 0.0)
+            before = center + half[p - 1, row : row + count, :]
+            after = center + half[p + 1, row : row + count, :]
+            low = center + half[p, row - 1 : row - 1 + count, :]
+            high = center + half[p, row + 1 : row + 1 + count, :]
+            left = center + jnp.where(in_left, roll(center, stride), 0.0)
+            right = center + jnp.where(in_right, roll(center, -stride), 0.0)
+            diagonal = ((before + after) + (low + high)) + (left + right)
+            plane = p - self.first_plane + self.gx * self.brick[0]
+            inside = jnp.where(jnp.logical_and(plane >= 0, plane < self.cells[0]), 1.0, 0.0)
+            inverse = (inside * inside_rows) * jnp.where(diagonal > 0.0, 1.0 / diagonal, 0.0)
+            self.fx[p, row : row + count, :] = before
+            self.fz[p, row : row + count, :] = low
+            self.fz[p, row + 1 : row + 1 + count, :] = high
+            self.left[p, row : row + count, :] = jnp.where(in_left, left, 0.0)
+            self.right[p, row : row + count, :] = jnp.where(in_right, right, 0.0)
             self.diag[p, row : row + count, :] = diagonal
-            plane = p - self.first_plane + self.gx * self.brick[0]
-            outside = jnp.where(jnp.logical_and(plane >= 0, plane < self.cells[0]), 0, 1 << 20)
-            index = here + outside
-            inside = (index >= 0) & (index < self.cells[1]) & (diagonal > 0.0)
-            self.inverse[p, row : row + count, :] = jnp.where(inside, 1.0 / (self.scale * diagonal), 0.0)
+            self.inverse[p, row : row + count, :] = inverse
+            first[p, row : row + count, :] = GAIN_FIRST * (inverse * source[p, row : row + count, :])
+        self.fx[planes[-1] + 1, row : row + count, :] = after
 
     def remainder(self, source, guess, p, row, count):
         center = guess[p, row : row + count, :]
@@ -121,12 +108,6 @@
             update = CARRY * start + GAIN * (self.inverse[p, row : row + count, :] * rest)
             out[p, row : row + count, :] = start + update
 
-    def first_down(self, source, first, planes, row, count):
-        for p in planes:
-            first[p, row : row + count, :] = GAIN_FIRST * (
-                self.inverse[p, row : row + count, :] * source[p, row : row + count, :]
-            )
-
     def restricted_remainder(self, source, guess, temp, planes, row, rows):
         parts = []
         for p in planes[::2]:
@@ -170,11 +151,6 @@
     return GAIN_FIRST * source * inverse
 
 
-def keep_window(out, window, first_plane, first_row):
-    planes, rows = out.shape[0:2]
-    out[...] = window[first_plane : first_plane + planes, first_row : first_row + rows, :]
-
-
 def cut(half_ref, planes, row, count):
     return [half_ref[p, row : row + count, :] for p in planes]
 
@@ -184,67 +160,81 @@
     zero = jnp.zeros((4, LANES), jnp.float32)
     for rows, out in ((slice(bz - 4, bz), to_high), (slice(0, 4), to_low)):
         out[0, 0:4, :] = zero
-        out[bx + 7, 0:4, :] = zero
+        out[bx + 5, 0:4, :] = zero
+        for p in range(2):
+            out[p + 1, 0:4, :] = low[p, rows, :]
+            out[p + bx + 3, 0:4, :] = high[p, rows, :]
         for p in range(3):
-            out[p + 1, 0:4, :] = low[p, rows, :]
-            out[p + bx + 4, 0:4, :] = high[p, rows, :]
-        for p in range(4):
-            out[p, 4:8, :] = low[p + 3, rows, :]
-            out[p + bx + 4, 4:8, :] = high[p + 3, rows, :]
+            out[p, 4:8, :] = low[p + 2, rows, :]
+            out[p + bx + 3, 4:8, :] = high[p + 2, rows, :]
         for p in range(bx):
-            out[p + 4, 0:4, :] = source[p, rows, :]
-            out[p + 4, 4:8, :] = cond[p, rows, :]
-
-
-def down_0(cells, pos, source, cond, low, high, z_low, z_high, kept_s, kept_h, kept_g, to_next, to_prev, win_s, win_h, guess, fx, fz, left, right, diag, inverse, first, temp, next_half):
+            out[p + 3, 0:4, :] = source[p, rows, :]
+            out[p + 3, 4:8, :] = cond[p, rows, :]
+
+
+def inner_0(cells, pos, source, cond, low, high, win_s, win_h, guess, fx, fz, left, right, diag, inverse, first, next_source, next_half, temp):
     gx, gz = (pos[0], pos[1])
     bx, bz = source.shape[0:2]
-    planes = bx + 8
+    planes, end = (bx + 6, ROW + bz)
     zero = jnp.zeros((8, LANES), jnp.float32)
-    end = ROW + bz
-    has_low, has_high = inside_z(gz, cells[1] // bz)
     for p in range(planes):
         for edge in (8, end, end + 8):
             win_s[p, edge : edge + 8, :] = zero
             win_h[p, edge : edge + 8, :] = zero
             guess[p, edge : edge + 8, :] = zero
             first[p, edge : edge + 8, :] = zero
+    for p in range(bx):
+        win_s[p + 3, ROW:end, :] = source[p, :, :]
+        win_h[p + 3, ROW:end, :] = 0.5 * cond[p, :, :]
+    for p in range(2):
+        win_s[p + 1, ROW:end, :] = low[p, :, :]
+        win_s[p + bx + 3, ROW:end, :] = high[p, :, :]
+    for p in range(3):
+        win_h[p, ROW:end, :] = 0.5 * low[p + 2, :, :]
+        win_h[p + bx + 3, ROW:end, :] = 0.5 * high[p + 2, :, :]
+    level = Level(0, gx, gz, (bx, bz), cells, 3, (win_h, fx, fz, left, right, diag, inverse))
+    level.coefs(range(1, planes - 1), ROW, bz, win_s, first)
+    level.second_down(win_s, first, guess, range(2, planes - 2), ROW, bz)
+    for p, value in enumerate(level.restricted_remainder(win_s, guess, temp, range(3, 3 + bx), ROW, bz)):
+        next_source[p, :, :] = value
+    for p, value in enumerate(restricted(win_h, temp, 1, range(1, planes - 1), ROW - 8, bz + 16)):
+        next_half[p, :, :] = value
+
+
+def outer_0(cells, pos, z_low, z_high, *refs):
+    win_s, win_h, guess, fx, fz, left, right, diag, inverse, first, next_source, next_half = refs[12:24]
+    to_next, to_prev, temp = refs[24:]
+    gx, gz = (pos[0], pos[1])
+    planes, bx, bz = (win_s.shape[0], win_s.shape[0] - 6, win_s.shape[1] - 32)
+    end = ROW + bz
+    has_low, has_high = inside_z(gz, cells[1] // bz)
+    for p in range(planes):
         win_s[p, ROW - 4 : ROW, :] = z_low[p, 0:4, :]
         win_s[p, end : end + 4, :] = z_high[p, 0:4, :]
         win_h[p, ROW - 4 : ROW, :] = (0.5 * has_low) * z_low[p, 4:8, :]
         win_h[p, end : end + 4, :] = (0.5 * has_high) * z_high[p, 4:8, :]
-    for p in range(bx):
-        win_s[p + 4, ROW:end, :] = source[p, :, :]
-        win_h[p + 4, ROW:end, :] = 0.5 * cond[p, :, :]
-    for p in range(3):
-        win_s[p + 1, ROW:end, :] = low[p, :, :]
-        win_s[p + bx + 4, ROW:end, :] = high[p, :, :]
-    for p in range(4):
-        win_h[p, ROW:end, :] = 0.5 * low[p + 3, :, :]
-        win_h[p + bx + 4, ROW:end, :] = 0.5 * high[p + 3, :, :]
-
-    level = Level(0, gx, gz, (bx, bz), cells, 4, (win_h, fx, fz, left, right, diag, inverse))
-    row, count = (ROW - 4, bz + 8)
-    level.coefs(range(1, planes - 1), row, count)
-    level.first_down(win_s, first, range(1, planes - 1), row, count)
-    level.second_down(win_s, first, guess, range(2, planes - 2), row, count)
-    sources = level.restricted_remainder(win_s, guess, temp, range(4, 4 + bx), ROW, bz)
-    halves = restricted(win_h, temp, 1, range(2, planes - 2), ROW - 8, bz + 16)
-    for p, value in enumerate(halves):
-        next_half[p, :, :] = value
+    level = Level(0, gx, gz, (bx, bz), cells, 3, (win_h, fx, fz, left, right, diag, inverse))
+    strips = ROW - 4, end - 4
+    for row in strips:
+        level.coefs(range(1, planes - 1), row, 8, win_s, first)
+    for row in strips:
+        level.second_down(win_s, first, guess, range(2, planes - 2), row, 8)
     own = bz // 2
+    for row, at in ((ROW, 0), (end - 8, own - 4)):
+        for p, value in enumerate(level.restricted_remainder(win_s, guess, temp, range(3, 3 + bx), row, 8)):
+            next_source[p, at : at + 4, :] = value
+        for p, value in enumerate(restricted(win_h, temp, 1, range(1, planes - 1), row - 8 if row == ROW else end, 8)):
+            at_half = 0 if row == ROW else own + 4
+            next_half[p, at_half : at_half + 4, :] = value
     odd = (lanes_of(own) & 1) == 1
-    padded = cut(next_half, range(bx // 2 + 2), 3, own + 2)
-    for p, value in enumerate(sources):
-        mixed = jnp.where(odd, padded[p + 1][1 : 1 + own], value)
+    for p in range(bx // 2):
+        mixed = jnp.where(odd, next_half[p + 1, 4 : 4 + own, :], next_source[p, :, :])
         to_next[p, :, :] = mixed
         to_prev[p, :, :] = mixed
-    end = bx // 2 - 1
-    to_next[end + 1, :, :] = first_iterate(sources[0], padded, 1, own, 1, 2)
-    to_prev[end + 1, :, :] = first_iterate(sources[end], padded, end + 1, own, 1, 2)
-    keep_window(kept_s, win_s, 3, 8)
-    keep_window(kept_h, win_h, 2, 8)
-    keep_window(kept_g, guess, 2, 8)
+    padded = cut(next_half, range(bx // 2 + 2), 3, own + 2)
+    last = bx // 2 - 1
+    to_next[last + 1, :, :] = first_iterate(next_source[0, :, :], padded, 1, own, 1, 2)
+    to_prev[last + 1, :, :] = first_iterate(next_source[last, :, :], padded, last + 1, own, 1, 2)
 
 
 def inside_z(gz, count):
@@ -260,54 +250,67 @@
         at += count
 
 
-def down_1(cells, pos, here, low, high, z_low, z_high, kept_s, kept_h, kept_g, to_next, to_prev, win_s, win_h, guess, fx, fz, left, right, diag, inverse, first, temp, next_source, next_half):
+def unpack_1(win_s, win_h, p, start, rows, mixed):
+    odd = (lanes_of(rows) & 1) == 1
+    win_s[p, start : start + rows, :] = jnp.where(odd, roll(mixed, 1), mixed)
+    win_h[p, start : start + rows, :] = jnp.where(odd, mixed, roll(mixed, -1))
+
+
+def inner_1(cells, pos, here, low, high, win_s, win_h, guess, fx, fz, left, right, diag, inverse, first, next_source, next_half, temp):
     gx, gz = (pos[0], pos[1])
     bx, bz = (here.shape[0] - 1, here.shape[1])
     planes, base = (3 * bx, 24)
     end = base + bz
     zero = jnp.zeros((8, LANES), jnp.float32)
-    has_low, has_high = inside_z(gz, cells[1] // bz)
-
-    def unpack(p, start, rows, mixed):
-        odd = (lanes_of(rows) & 1) == 1
-        win_s[p, start : start + rows, :] = jnp.where(odd, roll(mixed, 1), mixed)
-        win_h[p, start : start + rows, :] = jnp.where(odd, mixed, roll(mixed, -1))
-
-    edges = 0
     for b, part in enumerate((low, here, high)):
         for p in range(bx):
-            unpack(b * bx + p, base, bz, part[p, :, :])
-            unpack(b * bx + p, base - 16, 16, has_low * z_low[edges + p, :, :])
-            unpack(b * bx + p, end, 16, has_high * z_high[edges + p, :, :])
-        edges += bx
-        if b != 1:
-            q = 0 if b == 0 else planes - 1
-            first[q, base:end, :] = part[bx, :, :]
-            first[q, base - 16 : base, :] = has_low * z_low[edges, :, :]
-            first[q, end : end + 16, :] = has_high * z_high[edges, :, :]
-            edges += 1
+            unpack_1(win_s, win_h, b * bx + p, base, bz, part[p, :, :])
+    first[0, base:end, :] = low[bx, :, :]
+    first[planes - 1, base:end, :] = high[bx, :, :]
     for p in range(planes):
-        for ref in (win_s, win_h):
-            ref[p, 0:8, :] = zero
-            ref[p, end + 16 : end + 24, :] = zero
-        for ref in (first, guess):
-            ref[p, 8:16, :] = zero if 0 < p < planes - 1 or ref is guess else ref[p, 8:16, :]
-            ref[p, end + 8 : end + 16, :] = zero if 0 < p < planes - 1 or ref is guess else ref[p, end + 8 : end + 16, :]
-
+        for ref in (win_s, win_h, first, guess):
+            for row in (0, 8, 16, end, end + 8, end + 16):
+                ref[p, row : row + 8, :] = zero
     level = Level(1, gx, gz, (bx, bz), cells, bx, (win_h, fx, fz, left, right, diag, inverse), base)
-    row, count = (base - 12, bz + 24)
-    level.coefs(range(1, planes - 1), row, count)
-    level.first_down(win_s, first, range(1, planes - 1), row, count)
-    level.second_down(win_s, first, guess, range(1, planes - 1), row, count)
+    level.coefs(range(1, planes - 1), base, bz, win_s, first)
+    level.second_down(win_s, first, guess, range(1, planes - 1), base, bz)
+    next_source[...] = jnp.zeros(next_source.shape, jnp.float32)
     own = bz // 2
-    sources = level.restricted_remainder(win_s, guess, temp, range(bx - 2, 2 * bx + 2), row, count)
-    halves = restricted(win_h, temp, 2, range(planes), base - 16, bz + 32)
-    next_source[...] = jnp.zeros(next_source.shape, jnp.float32)
-    for p, value in enumerate(sources):
-        next_source[p + 1, 2 : 2 + count // 2, :] = value
-    for p, value in enumerate(halves):
-        next_half[p, :, :] = value
-    lane = lanes_of(own + 16) & 3
+    for p, value in enumerate(level.restricted_remainder(win_s, guess, temp, range(bx - 2, 2 * bx + 2), base, bz)):
+        next_source[p + 1, 8 : 8 + own, :] = value
+    for p, value in enumerate(restricted(win_h, temp, 2, range(planes), base, bz)):
+        next_half[p, 8 : 8 + own, :] = value
+
+
+def outer_1(cells, pos, z_low, z_high, *refs):
+    win_s, win_h, guess, fx, fz, left, right, diag, inverse, first, next_source, next_half = refs[12:24]
+    to_next, to_prev, temp = refs[24:]
+    gx, gz = (pos[0], pos[1])
+    planes, base = (win_s.shape[0], 24)
+    bx, bz = (planes // 3, win_s.shape[1] - 48)
+    end = base + bz
+    has_low, has_high = inside_z(gz, cells[1] // bz)
+    for start, ref, inside in ((base - 16, z_low, has_low), (end, z_high, has_high)):
+        for p in range(planes):
+            at = p if p < bx else p + 1
+            unpack_1(win_s, win_h, p, start, 16, inside * ref[at, :, :])
+        first[0, start : start + 16, :] = inside * ref[bx, :, :]
+        first[planes - 1, start : start + 16, :] = inside * ref[planes + 1, :, :]
+    level = Level(1, gx, gz, (bx, bz), cells, bx, (win_h, fx, fz, left, right, diag, inverse), base)
+    strips = base - 12, end - 4
+    for row in strips:
+        level.coefs(range(1, planes - 1), row, 16, win_s, first)
+    for row in strips:
+        level.second_down(win_s, first, guess, range(1, planes - 1), row, 16)
+    for row in strips:
+        at = (row - base + 16) // 2
+        for p, value in enumerate(level.restricted_remainder(win_s, guess, temp, range(bx - 2, 2 * bx + 2), row, 16)):
+            next_source[p + 1, at : at + 8, :] = value
+    for row in (base - 16, end):
+        at = (row - base + 16) // 2
+        for p, value in enumerate(restricted(win_h, temp, 2, range(planes), row, 16)):
+            next_half[p, at : at + 8, :] = value
+    lane = lanes_of(next_source.shape[1]) & 3
 
     def pair(p):
         mixed = jnp.where(lane == 0, next_source[p, :, :], next_half[p, :, :])
@@ -319,9 +322,6 @@
     to_next[1, :, :] = middle
     to_prev[0, :, :] = middle
     to_prev[1, :, :] = pair(4)
-    keep_window(kept_s, win_s, 2, base - 8)
-    keep_window(kept_h, win_h, 1, base - 8)
-    keep_window(kept_g, guess, 1, base - 8)
 
 
 def spread(mixed, which):
@@ -331,7 +331,7 @@
     return twice + roll(twice, 2)
 
 
-def down_2(cells, pos, prev, here, next_, kept_s, kept_h, kept_g, message, to_next, to_prev, win_s, win_h, guess, fx, fz, left, right, diag, inverse, first, temp):
+def down_2(cells, pos, prev, here, next_, guess0, win_s, guess, fx, fz, left, right, diag, inverse, message, to_next, to_prev, win_h, first, temp):
     gx, gz = (pos[0], pos[1])
     bx, bz = (2, prev.shape[1] - 16)
     own, planes = (4, 10)
@@ -349,18 +349,15 @@
             ref[p, end + 8 : end + 16, :] = zero
     level = Level(2, gx, gz, (bx, bz), cells, own, (win_h, fx, fz, left, right, diag, inverse))
     row, count = (ROW - 8, bz + 16)
-    level.coefs(range(own - 3, own + 5), row, count)
-    level.first_down(win_s, first, range(own - 3, own + 5), row, count)
+    level.coefs(range(own - 3, own + 5), row, count, win_s, first)
     level.second_down(win_s, first, guess, range(own - 2, own + 4), row, count)
-    keep_window(kept_s, win_s, 1, 8)
-    keep_window(kept_h, win_h, 0, 8)
-    keep_window(kept_g, guess, own, 8)
-    lane = lanes_of(count) & 3
     for out, begin in ((to_next, own - 2), (to_prev, own)):
-        mixed = guess[begin, row : row + count, :]
-        for p in range(1, 4):
-            mixed = jnp.where(lane == p, guess[begin + p, row : row + count, :], mixed)
-        out[...] = mixed
+        for p in range(4):
+            out[p, :, :] = guess[begin + p, row : row + count, :]
+        far = guess0.shape[0] - 5 if out is to_next else 4
+        for p in range(4, out.shape[0]):
+            begin0 = ROW + ((p - 4) & 1) * count
+            out[p, :, :] = guess0[far, begin0 : begin0 + count, :]
     sources = level.restricted_remainder(win_s, guess, temp, range(own, own + bx), ROW, bz)
     halves = restricted(win_h, temp, 4, range(own, own + bx), ROW, bz)
     rows = bz // 2
@@ -469,13 +466,10 @@
     level.leave(out)
 
 
-def finish(cells, pos, base, low, here, high, prev2, next2, s2, h2, g2, s1, h1, g1, s0, h0, g0, out, *scratch):
+def finish(cells, pos, base, low, here, high, prev2, next2, *refs):
     gx, gz = (pos[0], pos[1])
-    state, update3, coarse2, temp, start2, start1, start0 = scratch[:7]
-    shared, middle, update = (scratch[7:13], scratch[13], scratch[14])
-    s2, h2, g2 = (View(s2, 1, 8), View(h2, 0, 8), View(g2, 4, 8))
-    s1, h1, g1 = (View(s1, 2, 8), View(h1, 1, 8), View(g1, 1, 8))
-    s0, h0, g0 = (View(s0, 3, 8), View(h0, 2, 8), View(g0, 2, 8))
+    (s2, g2, *coefs2), (s1, g1, *coefs1), (s0, g0, *coefs0) = (refs[0:8], refs[8:16], refs[16:24])
+    out, state, update3, coarse2, temp, start2, start1, start0, middle, update = refs[24:]
     bz0 = out.shape[1]
     bz1, bz2 = (bz0 // 2, bz0 // 4)
     has_low, has_high = inside_z(gz, cells[0][1] // bz0)
@@ -509,12 +503,11 @@
             if q == 2:
                 guess = g2[p, row : row + count, :]
             else:
-                guess = spread((prev2 if q < 2 else next2)[4 : 4 + count, :], p if q < 2 else p - own - bx2)
+                guess = (prev2 if q < 2 else next2)[p if q < 2 else p - own - bx2, 4 : 4 + count, :]
             start[p, row : row + count, :] = guess + coarse2[q * rows : (q + 1) * rows, :]
-    level = Level(2, gx, gz, (bx2, bz2), cells[2], own, (h2,) + tuple(shared))
-    level.coefs(range(own - 3, own + 5), row, count)
-
-    bx1 = 4
+    level = Level(2, gx, gz, (bx2, bz2), cells[2], own, (None, *coefs2))
+
+    bx1, base1 = (4, 24)
 
     def to_level_1(p, value):
         q = 2 * (p - own) + 4
@@ -522,38 +515,43 @@
         temp[pl.ds(1, value.shape[0], stride=2), :] = value
         for r in (q, q + 1):
             if 1 <= r <= 10:
-                start1[r, ROW - 4 : ROW + bz1 + 4, :] = (
-                    g1[r, ROW - 4 : ROW + bz1 + 4, :] + temp[0 : bz1 + 8, :]
+                start1[r, base1 - 4 : base1 + bz1 + 4, :] = (
+                    g1[r, base1 - 4 : base1 + bz1 + 4, :] + temp[0 : bz1 + 8, :]
                 )
 
     for r in range(1, 11):
-        start1[r, 8:16, :] = zero
-        start1[r, ROW + bz1 : ROW + bz1 + 8, :] = zero
+        start1[r, base1 - 8 : base1, :] = zero
+        start1[r, base1 + bz1 : base1 + bz1 + 8, :] = zero
     level.up(s2, start, middle, update, to_level_1, range(own - 2, own + 4), row, count, ROW - 2, bz2 + 4)
-    level = Level(1, gx, gz, (bx1, bz1), cells[1], 4, (h1,) + tuple(shared))
-    row, count = (ROW - 4, bz1 + 8)
-    level.coefs(range(2, 10), row, count)
+    level = Level(1, gx, gz, (bx1, bz1), cells[1], 4, (None, *coefs1), base1)
+    row, count = (base1 - 4, bz1 + 8)
 
     bx0 = out.shape[0]
-    for r in range(2, 14):
+    for r in range(1, 13):
         start0[r, 8:16, :] = zero
         start0[r, ROW + bz0 : ROW + bz0 + 8, :] = zero
 
     def to_level_0(p, value):
-        q = 2 * (p - 4) + 4
+        q = 2 * (p - 4) + 3
         temp[pl.ds(0, value.shape[0], stride=2), :] = value
         temp[pl.ds(1, value.shape[0], stride=2), :] = value
         for r in (q, q + 1):
+            if r in (1, 12):
+                for part in range(2):
+                    begin = ROW + part * (bz0 // 2)
+                    start0[r, begin : begin + bz0 // 2, :] = (prev2 if r == 1 else next2)[4 + part, :, :] + temp[
+                        begin - ROW + 4 : begin - ROW + 4 + bz0 // 2, :
+                    ]
+                continue
             start0[r, ROW - 4 : ROW + bz0 + 4, :] = g0[r, ROW - 4 : ROW + bz0 + 4, :] + temp[0 : bz0 + 8, :]
 
-    level.up(s1, start1, middle, update, to_level_0, range(3, 9), row, count, ROW - 2, bz1 + 4)
-    level = Level(0, gx, gz, (bx0, bz0), cells[0], 4, (h0,) + tuple(shared))
-    level.coefs(range(3, 13), ROW - 4, bz0 + 8)
+    level.up(s1, start1, middle, update, to_level_0, range(3, 9), row, count, base1 - 2, bz1 + 4)
+    level = Level(0, gx, gz, (bx0, bz0), cells[0], 3, (None, *coefs0))
 
     def to_out(p, value):
-        out[p - 4, :, :] = value
-
-    level.up(s0, start0, middle, update, to_out, range(4, 12), ROW - 4, bz0 + 8, ROW, bz0)
+        out[p - 3, :, :] = value
+
+    level.up(s0, start0, middle, update, to_out, range(3, 11), ROW - 4, bz0 + 8, ROW, bz0)
 
 
 def f32(*shape):
@@ -564,9 +562,9 @@
     return pltpu.VMEM(shape, jnp.float32)
 
 
-def call(kernel, name, outs, scratches, *args):
+def call(kernel, name, outs, scratches, *args, aliases={}):
     smem = pl.BlockSpec(memory_space=pltpu.SMEM)
-    limit = 4 * 2**20 + sum(4 * math.prod(ref.shape) for ref in scratches)
+    limit = 4 * 2**20 + sum(4 * math.prod(ref.shape) for ref in [*scratches, *outs, *args])
     vmem = pl.BlockSpec(memory_space=pltpu.VMEM)
     return pl.pallas_call(
         kernel,
@@ -575,6 +573,7 @@
         in_specs=[smem if arg.dtype == jnp.int32 else vmem for arg in args],
         out_specs=[vmem] * len(outs),
         scratch_shapes=scratches,
+        input_output_aliases=aliases,
         compiler_params=pltpu.CompilerParams(vmem_limit_bytes=limit),
     )(*args)
 
@@ -594,27 +593,39 @@
     bx, bz = right_side.shape[0:2]
     cells = [(nx * bx >> level, nz * bz >> level) for level in range(4)]
     pos = jnp.stack([lax.axis_index("gx"), lax.axis_index("gz")]).astype(jnp.int32)
-    low = shift(jnp.concatenate([right_side[bx - 3 :], conductivity[bx - 4 :]]), "gx", 1)
-    high = shift(jnp.concatenate([right_side[:3], conductivity[:4]]), "gx", -1)
-    planes = bx + 8
+    for_next = jnp.concatenate([right_side[bx - 2 :], conductivity[bx - 3 :]])
+    for_prev = jnp.concatenate([right_side[:2], conductivity[:3]])
+    low, high = (shift(for_next, "gx", 1), shift(for_prev, "gx", -1))
+    planes = bx + 6
     to_high, to_low = call(
         edge_rows_0, "edge_rows_0", [f32(planes, 8, LANES)] * 2, [], right_side, conductivity, low, high
     )
     z_low, z_high = (turn(to_high, "gz", 1), turn(to_low, "gz", -1))
     window = (planes, bz + 32, LANES)
-    s0, h0, g0, for_next, for_prev = call(
-        functools.partial(down_0, cells[0]),
-        "down_0",
-        [f32(bx + 2, bz + 16, LANES)] + [f32(bx + 4, bz + 16, LANES)] * 2 + [f32(bx // 2 + 1, bz // 2, LANES)] * 2,
-        [scratch(*window)] * 10 + [scratch(bz + 16, LANES), scratch(bx // 2 + 2, bz // 2 + 8, LANES)],
+    half1 = (bx // 2 + 2, bz // 2 + 8, LANES)
+    arrays = call(
+        functools.partial(inner_0, cells[0]),
+        "inner_0",
+        [f32(*window)] * 10 + [f32(bx // 2, bz // 2, LANES), f32(*half1)],
+        [scratch(bz + 16, LANES)],
         pos,
         right_side,
         conductivity,
         low,
         high,
+    )
+    *arrays, for_next, for_prev = call(
+        functools.partial(outer_0, cells[0]),
+        "outer_0",
+        [f32(*array.shape) for array in arrays] + [f32(bx // 2 + 1, bz // 2, LANES)] * 2,
+        [scratch(16, LANES)],
+        pos,
         z_low,
         z_high,
-    )
+        *arrays,
+        aliases={i + 3: i for i in range(12)},
+    )
+    kept0 = (arrays[0], arrays[2], *arrays[3:9])
 
     bx, bz = (bx // 2, bz // 2)
     low, high = (shift(for_next, "gx", 1), shift(for_prev, "gx", -1))
@@ -623,33 +634,43 @@
     )
     z_low, z_high = (turn(to_high, "gz", 1), turn(to_low, "gz", -1))
     window = (3 * bx, bz + 48, LANES)
-    s1, h1, g1, for_next, for_prev = call(
-        functools.partial(down_1, cells[1]),
-        "down_1",
-        [f32(bx + 4, bz + 16, LANES)] + [f32(bx + 6, bz + 16, LANES)] * 2 + [f32(2, bz // 2 + 16, LANES)] * 2,
-        [scratch(*window)] * 10 + [scratch(bz + 32, LANES)] + [scratch(bx // 2 + 4, bz // 2 + 16, LANES)] * 2,
+    half2 = (bx // 2 + 4, bz // 2 + 16, LANES)
+    arrays1 = call(
+        functools.partial(inner_1, cells[1]),
+        "inner_1",
+        [f32(*window)] * 10 + [f32(*half2)] * 2,
+        [scratch(bz, LANES)],
         pos,
         for_next,
         low,
         high,
+    )
+    *arrays1, for_next, for_prev = call(
+        functools.partial(outer_1, cells[1]),
+        "outer_1",
+        [f32(*array.shape) for array in arrays1] + [f32(2, bz // 2 + 16, LANES)] * 2,
+        [scratch(16, LANES)],
+        pos,
         z_low,
         z_high,
-    )
+        *arrays1,
+        aliases={i + 3: i for i in range(12)},
+    )
+    kept1 = (arrays1[0], arrays1[2], *arrays1[3:9])
 
     bx, bz = (bx // 2, bz // 2)
     prev, next_ = (shift(for_next, "gx", 1), shift(for_prev, "gx", -1))
     window = (bx + 8, bz + 32, LANES)
-    s2, h2, g2, row3, for_next, for_prev = call(
+    *kept2, row3, for_next, for_prev = call(
         functools.partial(down_2, cells[2]),
         "down_2",
-        [f32(bx + 6, bz + 16, LANES), f32(bx + 8, bz + 16, LANES), f32(bx, bz + 16, LANES)]
-        + [f32(nx, 2, LANES)]
-        + [f32(bz + 16, LANES)] * 2,
-        [scratch(*window)] * 10 + [scratch(bz + 16, LANES)],
+        [f32(*window)] * 8 + [f32(nx, 2, LANES)] + [f32(LATE, bz + 16, LANES)] * 2,
+        [scratch(*window)] * 2 + [scratch(bz + 16, LANES)],
         pos,
         prev,
         for_next,
         next_,
+        arrays[2],
     )
 
     here = lax.all_to_all(row3, "gx", 0, 0, tiled=True)
@@ -675,13 +696,13 @@
     low, high = (turn(here, "gz", 1), turn(here, "gz", -1))
 
     bx, bz = right_side.shape[0:2]
-    window = (bx + 8, bz + 32, LANES)
+    window = (bx + 6, bz + 32, LANES)
     work = solving + [scratch(5 * (bz // 4 + 8), LANES), scratch(bz + 32, LANES)]
-    work += [scratch(bx // 4 + 8, bz // 4 + 32, LANES), scratch(bx // 2 + 8, bz // 2 + 32, LANES)]
-    work += [scratch(*window)] * 9
+    work += [scratch(bx // 4 + 8, bz // 4 + 32, LANES), scratch(bx // 2 + 8, bz // 2 + 48, LANES)]
+    work += [scratch(*window)] * 3
     (result,) = call(
         functools.partial(finish, cells), "finish", [f32(*right_side.shape)], work, pos, base, low, here, high,
-        prev2, next2, s2, h2, g2, s1, h1, g1, s0, h0, g0,
+        prev2, next2, *kept2, *kept1, *kept0,
     )
     return result
 

time: 112 us -> 106 us (0.946)
  waiting for transfers between devices: 30.5 us -> 22.3 us
  starting transfers between devices: 44.5 us -> 46.3 us
    ppermute x10, waiting for transfers between devices: 13.7 us -> 8.39 us  [turn(): lax.ppermute(array, axis, [(i, (i + by) % devices) for i in range(devices)])]
    ppermute x8, waiting for transfers between devices: 16.8 us -> 13.9 us  [shift(): lax.ppermute(array, axis, [(i, i + by) for i in range(devices) if 0 <= i...]
    ppermute x10, starting transfers between devices: 8.6 us -> 10.5 us  [turn(): lax.ppermute(array, axis, [(i, (i + by) % devices) for i in range(devices)])]
    pallas_call x8 -> x10, Pallas kernels: 12.8 us -> 13.4 us  [call(): pl.pallas_call(kernel, name=name, out_shape=outs, in_specs=[smem if arg.d...]
  transfers between devices with their start and end apart: 18 -> 18, of which waited for: 12 -> 9; matrix products, arithmetic and copies ran while one was open for 0% -> 0% of each run, Pallas kernels for 0% -> 6%
where the time goes in v5:
time: 106 us; the launch traced here: 105 us
  starting transfers between devices  46.3 us (44%)
  waiting for transfers between devices  22.3 us (21%)
  blocking collectives  21.9 us (21%)
  Pallas kernels  13.4 us (13%)
    ppermute x8, starting transfers between devices, shift(): lax.ppermute(array, axis, [(i, i + by) for i in range(devices) if 0 <= i...  35.8 us
    all_to_all x1, blocking collectives, on_device(): here = lax.all_to_all(row3, 'gx', 0, 0, tiled=True)  21.9 us
    ppermute x8, waiting for transfers between devices, shift(): lax.ppermute(array, axis, [(i, i + by) for i in range(devices) if 0 <= i...  13.9 us
    pallas_call x10, Pallas kernels, call(): pl.pallas_call(kernel, name=name, out_shape=outs, in_specs=[smem if arg.d...  13.4 us
    ppermute x10, starting transfers between devices, turn(): lax.ppermute(array, axis, [(i, (i + by) % devices) for i in range(devices)])  10.5 us
    ppermute x10, waiting for transfers between devices, turn(): lax.ppermute(array, axis, [(i, (i + by) % devices) for i in range(devices)])  8.39 us
  transfers between devices with their start and end apart: 18, of which 9 were waited for; matrix products, arithmetic and copies ran while one was open for 0% of the time, Pallas kernels for 6%

profile of v5, /device:TPU:6, one launch (start us, length us, event | category | flops | bytes accessed | tf_op | source)
XLA Modules:
  0.0 105.4 jit_solution(9123145361440077373)
XLA Ops:
  0.0 0.9 fusion
  1.1 4.0 %collective-permute-start = (f32[5,64,128]{2,1,0:T(8,128)S(1)}, f32[5,64,128]{2,1,0:T(8,128)S(1)}, u32[]{:S(2)}, u32[]{:S(2)}) collective-permute-start(f32[5,64,128]{2,1,0:T(8,128)S(1)} %pad_maximum_fusion), channel_id=1, source_target_pairs={{0,8},{8,16},{16,24},{24,32},{32,40},{40,48},{48,56},{56,64},{64,7... | collective-permute-start | bytes 491528 | tf_op jit(solution)/shard_map/ppermute | solution.py:583
  5.0 9.8 %collective-permute-start.1 = (f32[5,64,128]{2,1,0:T(8,128)S(1)}, f32[5,64,128]{2,1,0:T(8,128)S(1)}, u32[]{:S(2)}, u32[]{:S(2)}) collective-permute-start(f32[5,64,128]{2,1,0:T(8,128)S(1)} %pad_maximum_fusion.1), channel_id=1, source_target_pairs={{8,0},{16,8},{24,16},{32,24},{40,32},{48,40},{56,48},{64,56},{72,6... | collective-permute-start | bytes 491528 | tf_op jit(solution)/shard_map/ppermute | solution.py:583
  14.8 2.2 %collective-permute-done.low = f32[5,64,128]{2,1,0:T(8,128)S(1)} collective-permute-done((f32[5,64,128]{2,1,0:T(8,128)S(1)}, f32[5,64,128]{2,1,0:T(8,128)S(1)}, u32[]{:S(2)}, u32[]{:S(2)}) %collective-permute-start) | collective-permute-done | bytes 163872 | tf_op jit(solution)/shard_map/ppermute | solution.py:583
  17.1 1.2 %collective-permute-done.1.high = f32[5,64,128]{2,1,0:T(8,128)S(1)} collective-permute-done((f32[5,64,128]{2,1,0:T(8,128)S(1)}, f32[5,64,128]{2,1,0:T(8,128)S(1)}, u32[]{:S(2)}, u32[]{:S(2)}) %collective-permute-start.1) | collective-permute-done | bytes 163872 | tf_op jit(solution)/shard_map/ppermute | solution.py:583
  18.3 2.9 %collective-permute-start.3 = (f32[14,8,128]{2,1,0:T(8,128)S(1)}, f32[14,8,128]{2,1,0:T(8,128)S(1)}, u32[]{:S(2)}, u32[]{:S(2)}) collective-permute-start(f32[14,8,128]{2,1,0:T(8,128)S(1)} %get-tuple-element.69), channel_id=1, source_target_pairs={{0,7},{1,0},{2,1},{3,2},{4,3},{5,4},{6,5},{7,6},{8,15},{9,8},{10,9... | collective-permute-start | bytes 172040 | tf_op jit(solution)/shard_map/ppermute | solution.py:588
  21.3 1.9 %inner_0.1 = (f32[14,96,128]{2,1,0:T(8,128)S(1)}, f32[14,96,128]{2,1,0:T(8,128)S(1)}, f32[14,96,128]{2,1,0:T(8,128)S(1)}, f32[14,96,128]{2,1,0:T(8,128)S(1)}, f3...) custom-call(s32[2]{0:T(128)S(1)} %pad_add_fusion.pos, ...), custom_call_target="tpu_custom_call" | custom-call | tf_op jit(solution)/shard_map/inner_0/pallas_call | solution.py:569
  23.3 1.2 %outer_0.1 = (f32[14,96,128]{2,1,0:T(8,128)S(1)}, f32[14,96,128]{2,1,0:T(8,128)S(1)}, f32[14,96,128]{2,1,0:T(8,128)S(1)}, f32[14,96,128]{2,1,0:T(8,128)S(1)}, f3...) custom-call(s32[2]{0:T(128)S(1)} %pad_add_fusion.pos, ...), custom_call_target="tpu_custom_call", output_to_operand_aliasing={{0}: (3, {}), {1}: (4, {}), {2}: (5, {}), {3}: (6, {}), {4}... | custom-call | tf_op jit(solution)/shard_map/outer_0/pallas_call | solution.py:569
  24.5 6.5 %collective-permute-start.5 = (f32[5,32,128]{2,1,0:T(8,128)S(1)}, f32[5,32,128]{2,1,0:T(8,128)S(1)}, u32[]{:S(2)}, u32[]{:S(2)}) collective-permute-start(f32[5,32,128]{2,1,0:T(8,128)S(1)} %get-tuple-element.83), channel_id=1, source_target_pairs={{8,0},{16,8},{24,16},{32,24},{40,32},{48,40},{56,48},{64,56},{72,6... | collective-permute-start | bytes 245768 | tf_op jit(solution)/shard_map/ppermute | solution.py:583
  31.0 1.9 %collective-permute-start.4 = (f32[5,32,128]{2,1,0:T(8,128)S(1)}, f32[5,32,128]{2,1,0:T(8,128)S(1)}, u32[]{:S(2)}, u32[]{:S(2)}) collective-permute-start(f32[5,32,128]{2,1,0:T(8,128)S(1)} %get-tuple-element.82.here), channel_id=1, source_target_pairs={{0,8},{8,16},{16,24},{24,32},{32,40},{40,48},{48,56},{56,64},{64,7... | collective-permute-start | bytes 245768 | tf_op jit(solution)/shard_map/ppermute | solution.py:583
  32.9 0.2 collective-permute-done.5.high
  33.1 6.3 %collective-permute-done.4.low = f32[5,32,128]{2,1,0:T(8,128)S(1)} collective-permute-done((f32[5,32,128]{2,1,0:T(8,128)S(1)}, f32[5,32,128]{2,1,0:T(8,128)S(1)}, u32[]{:S(2)}, u32[]{:S(2)}) %collective-permute-start.4) | collective-permute-done | bytes 81952 | tf_op jit(solution)/shard_map/ppermute | solution.py:583
  39.5 2.9 %collective-permute-start.7 = (f32[14,16,128]{2,1,0:T(8,128)S(1)}, f32[14,16,128]{2,1,0:T(8,128)S(1)}, u32[]{:S(2)}, u32[]{:S(2)}) collective-permute-start(f32[14,16,128]{2,1,0:T(8,128)S(1)} %get-tuple-element.85), channel_id=1, source_target_pairs={{0,7},{1,0},{2,1},{3,2},{4,3},{5,4},{6,5},{7,6},{8,15},{9,8},{10,9... | collective-permute-start | bytes 344072 | tf_op jit(solution)/shard_map/ppermute | solution.py:588
  42.4 1.2 %inner_1.1 = (f32[12,80,128]{2,1,0:T(8,128)S(1)}, f32[12,80,128]{2,1,0:T(8,128)S(1)}, f32[12,80,128]{2,1,0:T(8,128)S(1)}, f32[12,80,128]{2,1,0:T(8,128)S(1)}, f3...) custom-call(s32[2]{0:T(128)S(1)} %pad_add_fusion.pos, ...), custom_call_target="tpu_custom_call" | custom-call | tf_op jit(solution)/shard_map/inner_1/pallas_call | solution.py:569
  43.7 1.2 %collective-permute-done.6.z_low = f32[14,16,128]{2,1,0:T(8,128)S(1)} collective-permute-done((f32[14,16,128]{2,1,0:T(8,128)S(1)}, f32[14,16,128]{2,1,0:T(8,128)S(1)}, u32[]{:S(2)}, u32[]{:S(2)}) %collective-permute-start.6) | collective-permute-done | bytes 114720 | tf_op jit(solution)/shard_map/ppermute | solution.py:588
  44.9 1.2 %outer_1.1 = (f32[12,80,128]{2,1,0:T(8,128)S(1)}, f32[12,80,128]{2,1,0:T(8,128)S(1)}, f32[12,80,128]{2,1,0:T(8,128)S(1)}, f32[12,80,128]{2,1,0:T(8,128)S(1)}, f3...) custom-call(s32[2]{0:T(128)S(1)} %pad_add_fusion.pos, ...), custom_call_target="tpu_custom_call", output_to_operand_aliasing={{0}: (3, {}), {1}: (4, {}), {2}: (5, {}), {3}: (6, {}), {4}... | custom-call | tf_op jit(solution)/shard_map/outer_1/pallas_call | solution.py:569
  46.1 1.9 %collective-permute-start.9 = (f32[2,32,128]{2,1,0:T(8,128)S(1)}, f32[2,32,128]{2,1,0:T(8,128)S(1)}, u32[]{:S(2)}, u32[]{:S(2)}) collective-permute-start(f32[2,32,128]{2,1,0:T(8,128)S(1)} %get-tuple-element.99), channel_id=1, source_target_pairs={{8,0},{16,8},{24,16},{32,24},{40,32},{48,40},{56,48},{64,56},{72,6... | collective-permute-start | bytes 98312 | tf_op jit(solution)/shard_map/ppermute | solution.py:583
  48.1 3.9 %collective-permute-start.8 = (f32[2,32,128]{2,1,0:T(8,128)S(1)}, f32[2,32,128]{2,1,0:T(8,128)S(1)}, u32[]{:S(2)}, u32[]{:S(2)}) collective-permute-start(f32[2,32,128]{2,1,0:T(8,128)S(1)} %get-tuple-element.98.here), channel_id=1, source_target_pairs={{0,8},{8,16},{16,24},{24,32},{32,40},{40,48},{48,56},{56,64},{64,7... | collective-permute-start | bytes 98312 | tf_op jit(solution)/shard_map/ppermute | solution.py:583
  52.0 4.0 %collective-permute-done.8.prev = f32[2,32,128]{2,1,0:T(8,128)S(1)} collective-permute-done((f32[2,32,128]{2,1,0:T(8,128)S(1)}, f32[2,32,128]{2,1,0:T(8,128)S(1)}, u32[]{:S(2)}, u32[]{:S(2)}) %collective-permute-start.8) | collective-permute-done | bytes 32800 | tf_op jit(solution)/shard_map/ppermute | solution.py:583
  56.0 1.4 %down_2.1 = (f32[10,48,128]{2,1,0:T(8,128)S(1)}, f32[10,48,128]{2,1,0:T(8,128)S(1)}, f32[10,48,128]{2,1,0:T(8,128)S(1)}, f32[10,48,128]{2,1,0:T(8,128)S(1)}, f32...) custom-call(s32[2]{0:T(128)S(1)} %pad_add_fusion.pos, ...), custom_call_target="tpu_custom_call" | custom-call | tf_op jit(solution)/shard_map/down_2/pallas_call | solution.py:569
  57.4 21.9 %all_to_all.5 = f32[64,2,128]{2,1,0:T(2,128)S(1)} all-to-all(f32[64,2,128]{2,1,0:T(2,128)S(1)} %get-tuple-element.101), channel_id=1, replica_groups=mesh['gx'=64,'gz'=8] {'gx'}, dimensions={0} | all-to-all | bytes 131072 | tf_op jit(solution)/shard_map/all_to_all | solution.py:676
  79.3 1.4 %collective-permute-start.11 = (f32[64,2,128]{2,1,0:T(2,128)S(1)}, f32[64,2,128]{2,1,0:T(2,128)S(1)}, u32[]{:S(2)}, u32[]{:S(2)}) collective-permute-start(f32[64,2,128]{2,1,0:T(2,128)S(1)} %all_to_all.5), channel_id=1, source_target_pairs={{0,7},{1,0},{2,1},{3,2},{4,3},{5,4},{6,5},{7,6},{8,15},{9,8},{10,9... | collective-permute-start | bytes 196616 | tf_op jit(solution)/shard_map/ppermute | solution.py:588
  80.7 2.6 %collective-permute-start.16 = (f32[8,32,128]{2,1,0:T(8,128)S(1)}, f32[8,32,128]{2,1,0:T(8,128)S(1)}, u32[]{:S(2)}, u32[]{:S(2)}) collective-permute-start(f32[8,32,128]{2,1,0:T(8,128)S(1)} %get-tuple-element.105), channel_id=1, source_target_pairs={{0,8},{8,16},{16,24},{24,32},{32,40},{40,48},{48,56},{56,64},{64,7... | collective-permute-start | bytes 393224 | tf_op jit(solution)/shard_map/ppermute | solution.py:583
  83.4 2.3 %collective-permute-done.10 = f32[64,2,128]{2,1,0:T(2,128)S(1)} collective-permute-done((f32[64,2,128]{2,1,0:T(2,128)S(1)}, f32[64,2,128]{2,1,0:T(2,128)S(1)}, u32[]{:S(2)}, u32[]{:S(2)}) %collective-permute-start.10) | collective-permute-done | bytes 65568 | tf_op jit(solution)/shard_map/ppermute | solution.py:588
  85.6 1.5 %solve_first.1 = (f32[21,64,128]{2,1,0:T(8,128)S(1)}, f32[2,64,128]{2,1,0:T(8,128)S(1)}) custom-call(s32[2]{0:T(128)S(1)} %pad_add_fusion.pos, f32[128,128]{1,0:T(8,128)S(1)} %bitcast.7, f32[128,128]{1,0:T(8,128)S(1)} %bitcast.5, f32[128,128]{1,0:T(8,128)S(1)} %bitcast.6), custom_call_target="tpu_custom_call" | custom-call | tf_op jit(solution)/shard_map/solve_first/pallas_call | solution.py:569
  87.2 0.4 collective-permute-start.13
  87.7 5.2 %collective-permute-start.17 = (f32[8,32,128]{2,1,0:T(8,128)S(1)}, f32[8,32,128]{2,1,0:T(8,128)S(1)}, u32[]{:S(2)}, u32[]{:S(2)}) collective-permute-start(f32[8,32,128]{2,1,0:T(8,128)S(1)} %get-tuple-element.107), channel_id=1, source_target_pairs={{8,0},{16,8},{24,16},{32,24},{40,32},{48,40},{56,48},{64,56},{72,6... | collective-permute-start | bytes 393224 | tf_op jit(solution)/shard_map/ppermute | solution.py:583
  92.9 1.5 %solve_next.1.here = f32[2,64,128]{2,1,0:T(8,128)S(1)} custom-call(s32[2]{0:T(128)S(1)} %pad_add_fusion.pos, f32[21,64,128]{2,1,0:T(8,128)S(1)} %get-tuple-element.102.base, f32[2,64,128]{2,1,0:T(8,128)S(1)} %collective-permute-done.12.low, f32[2,64,128]{2,1,0:T(8,128)S(1)} %get-tuple-element.103.here, f32[2,64,128]{2,1,0:T(8,128)S(1)} %collective-permute-done.13.high), custom_call_target="tpu_custom_call" | custom-call | tf_op jit(solution)/shard_map/solve_next/pallas_call | solution.py:569
  94.5 2.7 %collective-permute-start.15 = (f32[2,64,128]{2,1,0:T(8,128)S(1)}, f32[2,64,128]{2,1,0:T(8,128)S(1)}, u32[]{:S(2)}, u32[]{:S(2)}) collective-permute-start(f32[2,64,128]{2,1,0:T(8,128)S(1)} %solve_next.1.here), channel_id=1, source_target_pairs={{0,7},{1,0},{2,1},{3,2},{4,3},{5,4},{6,5},{7,6},{8,15},{9,8},{10,9... | collective-permute-start | bytes 196616 | tf_op jit(solution)/shard_map/ppermute | solution.py:588
  97.2 1.9 %collective-permute-done.15.high = f32[2,64,128]{2,1,0:T(8,128)S(1)} collective-permute-done((f32[2,64,128]{2,1,0:T(8,128)S(1)}, f32[2,64,128]{2,1,0:T(8,128)S(1)}, u32[]{:S(2)}, u32[]{:S(2)}) %collective-permute-start.15) | collective-permute-done | bytes 65568 | tf_op jit(solution)/shard_map/ppermute | solution.py:588
  99.1 3.0 %collective-permute-done.14.low = f32[2,64,128]{2,1,0:T(8,128)S(1)} collective-permute-done((f32[2,64,128]{2,1,0:T(8,128)S(1)}, f32[2,64,128]{2,1,0:T(8,128)S(1)}, u32[]{:S(2)}, u32[]{:S(2)}) %collective-permute-start.14) | collective-permute-done | bytes 65568 | tf_op jit(solution)/shard_map/ppermute | solution.py:588
  102.1 3.3 %finish.1 = f32[8,64,128]{2,1,0:T(8,128)} custom-call(s32[2]{0:T(128)S(1)} %pad_add_fusion.pos, f32[21,64,128]{2,1,0:T(8,128)S(1)} %get-tuple-element.102.base, f32[2,64,128]{2,1,0:T(8,128)S(1)} %collective-permute-done.14.low, f32[2,64,128]{2,1,0:T(8,128)S(1)} %solve_next.1.here, f32[2,64,128]{2,1,0:T(8,128)S(1)} %collective-permute-done.15.high, ...), custom_call_target="tpu_custom_call" | custom-call | tf_op jit(solution)/shard_map/finish/pallas_call | solution.py:569
  (24 shorter events, 0.4 us)
Async XLA Ops:
  0.0 1.0 copy-start
  1.0 17.2 %copy-start.1 = (f32[8,64,128]{2,1,0:T(8,128)S(1)}, f32[8,64,128]{2,1,0:T(8,128)}, u32[]{:S(2)}) copy-start(f32[8,64,128]{2,1,0:T(8,128)} %source.3) | copy-start | bytes 786436
  1.1 16.0 %collective-permute-start = (f32[5,64,128]{2,1,0:T(8,128)S(1)}, f32[5,64,128]{2,1,0:T(8,128)S(1)}, u32[]{:S(2)}, u32[]{:S(2)}) collective-permute-start(f32[5,64,128]{2,1,0:T(8,128)S(1)} %pad_maximum_fusion), channel_id=1, source_target_pairs={{0,8},{8,16},{16,24},{24,32},{32,40},{40,48},{48,56},{56,64},{64,7... | collective-permute-start | bytes 491528 | tf_op jit(solution)/shard_map/ppermute | solution.py:583
  5.0 13.2 %collective-permute-start.1 = (f32[5,64,128]{2,1,0:T(8,128)S(1)}, f32[5,64,128]{2,1,0:T(8,128)S(1)}, u32[]{:S(2)}, u32[]{:S(2)}) collective-permute-start(f32[5,64,128]{2,1,0:T(8,128)S(1)} %pad_maximum_fusion.1), channel_id=1, source_target_pairs={{8,0},{16,8},{24,16},{32,24},{40,32},{48,40},{56,48},{64,56},{72,6... | collective-permute-start | bytes 491528 | tf_op jit(solution)/shard_map/ppermute | solution.py:583
  18.3 5.0 %collective-permute-start.2 = (f32[14,8,128]{2,1,0:T(8,128)S(1)}, f32[14,8,128]{2,1,0:T(8,128)S(1)}, u32[]{:S(2)}, u32[]{:S(2)}) collective-permute-start(f32[14,8,128]{2,1,0:T(8,128)S(1)} %get-tuple-element.68), channel_id=1, source_target_pairs={{0,1},{1,2},{2,3},{3,4},{4,5},{5,6},{6,7},{7,0},{8,9},{9,10},{10,1... | collective-permute-start | bytes 172040 | tf_op jit(solution)/shard_map/ppermute | solution.py:588
  18.3 5.0 %collective-permute-start.3 = (f32[14,8,128]{2,1,0:T(8,128)S(1)}, f32[14,8,128]{2,1,0:T(8,128)S(1)}, u32[]{:S(2)}, u32[]{:S(2)}) collective-permute-start(f32[14,8,128]{2,1,0:T(8,128)S(1)} %get-tuple-element.69), channel_id=1, source_target_pairs={{0,7},{1,0},{2,1},{3,2},{4,3},{5,4},{6,5},{7,6},{8,15},{9,8},{10,9... | collective-permute-start | bytes 172040 | tf_op jit(solution)/shard_map/ppermute | solution.py:588
  24.5 8.6 %collective-permute-start.5 = (f32[5,32,128]{2,1,0:T(8,128)S(1)}, f32[5,32,128]{2,1,0:T(8,128)S(1)}, u32[]{:S(2)}, u32[]{:S(2)}) collective-permute-start(f32[5,32,128]{2,1,0:T(8,128)S(1)} %get-tuple-element.83), channel_id=1, source_target_pairs={{8,0},{16,8},{24,16},{32,24},{40,32},{48,40},{56,48},{64,56},{72,6... | collective-permute-start | bytes 245768 | tf_op jit(solution)/shard_map/ppermute | solution.py:583
  31.0 8.4 %collective-permute-start.4 = (f32[5,32,128]{2,1,0:T(8,128)S(1)}, f32[5,32,128]{2,1,0:T(8,128)S(1)}, u32[]{:S(2)}, u32[]{:S(2)}) collective-permute-start(f32[5,32,128]{2,1,0:T(8,128)S(1)} %get-tuple-element.82.here), channel_id=1, source_target_pairs={{0,8},{8,16},{16,24},{24,32},{32,40},{40,48},{48,56},{56,64},{64,7... | collective-permute-start | bytes 245768 | tf_op jit(solution)/shard_map/ppermute | solution.py:583
  39.5 5.4 %collective-permute-start.6 = (f32[14,16,128]{2,1,0:T(8,128)S(1)}, f32[14,16,128]{2,1,0:T(8,128)S(1)}, u32[]{:S(2)}, u32[]{:S(2)}) collective-permute-start(f32[14,16,128]{2,1,0:T(8,128)S(1)} %get-tuple-element.84), channel_id=1, source_target_pairs={{0,1},{1,2},{2,3},{3,4},{4,5},{5,6},{6,7},{7,0},{8,9},{9,10},{10,1... | collective-permute-start | bytes 344072 | tf_op jit(solution)/shard_map/ppermute | solution.py:588
  39.5 5.4 %collective-permute-start.7 = (f32[14,16,128]{2,1,0:T(8,128)S(1)}, f32[14,16,128]{2,1,0:T(8,128)S(1)}, u32[]{:S(2)}, u32[]{:S(2)}) collective-permute-start(f32[14,16,128]{2,1,0:T(8,128)S(1)} %get-tuple-element.85), channel_id=1, source_target_pairs={{0,7},{1,0},{2,1},{3,2},{4,3},{5,4},{6,5},{7,6},{8,15},{9,8},{10,9... | collective-permute-start | bytes 344072 | tf_op jit(solution)/shard_map/ppermute | solution.py:588
  46.1 5.9 %collective-permute-start.9 = (f32[2,32,128]{2,1,0:T(8,128)S(1)}, f32[2,32,128]{2,1,0:T(8,128)S(1)}, u32[]{:S(2)}, u32[]{:S(2)}) collective-permute-start(f32[2,32,128]{2,1,0:T(8,128)S(1)} %get-tuple-element.99), channel_id=1, source_target_pairs={{8,0},{16,8},{24,16},{32,24},{40,32},{48,40},{56,48},{64,56},{72,6... | collective-permute-start | bytes 98312 | tf_op jit(solution)/shard_map/ppermute | solution.py:583
  48.1 7.9 %collective-permute-start.8 = (f32[2,32,128]{2,1,0:T(8,128)S(1)}, f32[2,32,128]{2,1,0:T(8,128)S(1)}, u32[]{:S(2)}, u32[]{:S(2)}) collective-permute-start(f32[2,32,128]{2,1,0:T(8,128)S(1)} %get-tuple-element.98.here), channel_id=1, source_target_pairs={{0,8},{8,16},{16,24},{24,32},{32,40},{40,48},{48,56},{56,64},{64,7... | collective-permute-start | bytes 98312 | tf_op jit(solution)/shard_map/ppermute | solution.py:583
  79.3 4.0 %collective-permute-start.11 = (f32[64,2,128]{2,1,0:T(2,128)S(1)}, f32[64,2,128]{2,1,0:T(2,128)S(1)}, u32[]{:S(2)}, u32[]{:S(2)}) collective-permute-start(f32[64,2,128]{2,1,0:T(2,128)S(1)} %all_to_all.5), channel_id=1, source_target_pairs={{0,7},{1,0},{2,1},{3,2},{4,3},{5,4},{6,5},{7,6},{8,15},{9,8},{10,9... | collective-permute-start | bytes 196616 | tf_op jit(solution)/shard_map/ppermute | solution.py:588
  80.7 4.9 %collective-permute-start.10 = (f32[64,2,128]{2,1,0:T(2,128)S(1)}, f32[64,2,128]{2,1,0:T(2,128)S(1)}, u32[]{:S(2)}, u32[]{:S(2)}) collective-permute-start(f32[64,2,128]{2,1,0:T(2,128)S(1)} %all_to_all.5), channel_id=1, source_target_pairs={{0,1},{1,2},{2,3},{3,4},{4,5},{5,6},{6,7},{7,0},{8,9},{9,10},{10,1... | collective-permute-start | bytes 196616 | tf_op jit(solution)/shard_map/ppermute | solution.py:588
  80.7 16.4 %collective-permute-start.16 = (f32[8,32,128]{2,1,0:T(8,128)S(1)}, f32[8,32,128]{2,1,0:T(8,128)S(1)}, u32[]{:S(2)}, u32[]{:S(2)}) collective-permute-start(f32[8,32,128]{2,1,0:T(8,128)S(1)} %get-tuple-element.105), channel_id=1, source_target_pairs={{0,8},{8,16},{16,24},{24,32},{32,40},{40,48},{48,56},{56,64},{64,7... | collective-permute-start | bytes 393224 | tf_op jit(solution)/shard_map/ppermute | solution.py:583
  87.2 5.8 %collective-permute-start.13 = (f32[2,64,128]{2,1,0:T(8,128)S(1)}, f32[2,64,128]{2,1,0:T(8,128)S(1)}, u32[]{:S(2)}, u32[]{:S(2)}) collective-permute-start(f32[2,64,128]{2,1,0:T(8,128)S(1)} %get-tuple-element.103.here), channel_id=1, source_target_pairs={{0,7},{1,0},{2,1},{3,2},{4,3},{5,4},{6,5},{7,6},{8,15},{9,8},{10,9... | collective-permute-start | bytes 196616 | tf_op jit(solution)/shard_map/ppermute | solution.py:588
  87.6 5.3 %collective-permute-start.12 = (f32[2,64,128]{2,1,0:T(8,128)S(1)}, f32[2,64,128]{2,1,0:T(8,128)S(1)}, u32[]{:S(2)}, u32[]{:S(2)}) collective-permute-start(f32[2,64,128]{2,1,0:T(8,128)S(1)} %get-tuple-element.103.here), channel_id=1, source_target_pairs={{0,1},{1,2},{2,3},{3,4},{4,5},{5,6},{6,7},{7,0},{8,9},{9,10},{10,1... | collective-permute-start | bytes 196616 | tf_op jit(solution)/shard_map/ppermute | solution.py:588
  87.7 14.4 %collective-permute-start.17 = (f32[8,32,128]{2,1,0:T(8,128)S(1)}, f32[8,32,128]{2,1,0:T(8,128)S(1)}, u32[]{:S(2)}, u32[]{:S(2)}) collective-permute-start(f32[8,32,128]{2,1,0:T(8,128)S(1)} %get-tuple-element.107), channel_id=1, source_target_pairs={{8,0},{16,8},{24,16},{32,24},{40,32},{48,40},{56,48},{64,56},{72,6... | collective-permute-start | bytes 393224 | tf_op jit(solution)/shard_map/ppermute | solution.py:583
  94.5 4.6 %collective-permute-start.15 = (f32[2,64,128]{2,1,0:T(8,128)S(1)}, f32[2,64,128]{2,1,0:T(8,128)S(1)}, u32[]{:S(2)}, u32[]{:S(2)}) collective-permute-start(f32[2,64,128]{2,1,0:T(8,128)S(1)} %solve_next.1.here), channel_id=1, source_target_pairs={{0,7},{1,0},{2,1},{3,2},{4,3},{5,4},{6,5},{7,6},{8,15},{9,8},{10,9... | collective-permute-start | bytes 196616 | tf_op jit(solution)/shard_map/ppermute | solution.py:588
  97.1 4.9 %collective-permute-start.14 = (f32[2,64,128]{2,1,0:T(8,128)S(1)}, f32[2,64,128]{2,1,0:T(8,128)S(1)}, u32[]{:S(2)}, u32[]{:S(2)}) collective-permute-start(f32[2,64,128]{2,1,0:T(8,128)S(1)} %solve_next.1.here), channel_id=1, source_target_pairs={{0,1},{1,2},{2,3},{3,4},{4,5},{5,6},{6,7},{7,0},{8,9},{9,10},{10,1... | collective-permute-start | bytes 196616 | tf_op jit(solution)/shard_map/ppermute | solution.py:588

commit v6 on v5

--- a/solution.py
+++ b/solution.py
@@ -172,8 +172,8 @@
             out[p + 3, 4:8, :] = cond[p, rows, :]
 
 
-def inner_0(cells, pos, source, cond, low, high, win_s, win_h, guess, fx, fz, left, right, diag, inverse, first, next_source, next_half, temp):
-    gx, gz = (pos[0], pos[1])
+def inner_0(cells, source, cond, low, high, win_s, win_h, guess, fx, fz, left, right, diag, inverse, first, next_source, next_half, temp):
+    gx, gz = (lax.axis_index("gx"), lax.axis_index("gz"))
     bx, bz = source.shape[0:2]
     planes, end = (bx + 6, ROW + bz)
     zero = jnp.zeros((8, LANES), jnp.float32)
@@ -201,10 +201,10 @@
         next_half[p, :, :] = value
 
 
-def outer_0(cells, pos, z_low, z_high, *refs):
+def outer_0(cells, z_low, z_high, *refs):
     win_s, win_h, guess, fx, fz, left, right, diag, inverse, first, next_source, next_half = refs[12:24]
     to_next, to_prev, temp = refs[24:]
-    gx, gz = (pos[0], pos[1])
+    gx, gz = (lax.axis_index("gx"), lax.axis_index("gz"))
     planes, bx, bz = (win_s.shape[0], win_s.shape[0] - 6, win_s.shape[1] - 32)
     end = ROW + bz
     has_low, has_high = inside_z(gz, cells[1] // bz)
@@ -227,27 +227,28 @@
             at_half = 0 if row == ROW else own + 4
             next_half[p, at_half : at_half + 4, :] = value
     odd = (lanes_of(own) & 1) == 1
+    padded = cut(next_half, range(bx // 2 + 2), 3, own + 2)
+    last = bx // 2 - 1
     for p in range(bx // 2):
-        mixed = jnp.where(odd, next_half[p + 1, 4 : 4 + own, :], next_source[p, :, :])
+        mixed = jnp.where(odd, padded[p + 1][1 : 1 + own], next_source[p, :, :])
         to_next[p, :, :] = mixed
         to_prev[p, :, :] = mixed
-    padded = cut(next_half, range(bx // 2 + 2), 3, own + 2)
-    last = bx // 2 - 1
-    to_next[last + 1, :, :] = first_iterate(next_source[0, :, :], padded, 1, own, 1, 2)
-    to_prev[last + 1, :, :] = first_iterate(next_source[last, :, :], padded, last + 1, own, 1, 2)
+    for p, out in ((0, to_next), (last, to_prev)):
+        iterate = first_iterate(next_source[p, :, :], padded, p + 1, own, 1, 2)
+        out[p, :, :] = jnp.where(odd, padded[p + 1][1 : 1 + own], iterate)
 
 
 def inside_z(gz, count):
     return (jnp.where(gz > 0, 1.0, 0.0), jnp.where(gz < count - 1, 1.0, 0.0))
 
 
-def edge_rows_1(low, here, high, to_high, to_low):
-    at = 0
-    for part, count in ((low, low.shape[0]), (here, here.shape[0] - 1), (high, high.shape[0])):
-        rows = part.shape[1]
-        to_high[at : at + count, :, :] = part[0:count, rows - 16 : rows, :]
-        to_low[at : at + count, :, :] = part[0:count, 0:16, :]
-        at += count
+def edge_rows_1(low, to_next, to_prev, high, to_high, to_low):
+    bx, rows = low.shape[0:2]
+    own = [to_prev] * (bx - 1) + [to_next]
+    planes = [(low, p) for p in range(bx)] + list(zip(own, range(bx))) + [(high, p) for p in range(bx)]
+    for at, (part, p) in enumerate(planes):
+        to_high[at, :, :] = part[p, rows - 16 : rows, :]
+        to_low[at, :, :] = part[p, 0:16, :]
 
 
 def unpack_1(win_s, win_h, p, start, rows, mixed):
@@ -256,17 +257,19 @@
     win_h[p, start : start + rows, :] = jnp.where(odd, mixed, roll(mixed, -1))
 
 
-def inner_1(cells, pos, here, low, high, win_s, win_h, guess, fx, fz, left, right, diag, inverse, first, next_source, next_half, temp):
-    gx, gz = (pos[0], pos[1])
-    bx, bz = (here.shape[0] - 1, here.shape[1])
+def inner_1(cells, source, half, low, high, win_s, win_h, guess, fx, fz, left, right, diag, inverse, first, next_source, next_half, temp):
+    gx, gz = (lax.axis_index("gx"), lax.axis_index("gz"))
+    bx, bz = source.shape[0:2]
     planes, base = (3 * bx, 24)
     end = base + bz
     zero = jnp.zeros((8, LANES), jnp.float32)
-    for b, part in enumerate((low, here, high)):
-        for p in range(bx):
-            unpack_1(win_s, win_h, b * bx + p, base, bz, part[p, :, :])
-    first[0, base:end, :] = low[bx, :, :]
-    first[planes - 1, base:end, :] = high[bx, :, :]
+    for p in range(bx):
+        unpack_1(win_s, win_h, p, base, bz, low[p, :, :])
+        unpack_1(win_s, win_h, 2 * bx + p, base, bz, high[p, :, :])
+        win_s[bx + p, base:end, :] = source[p, :, :]
+        win_h[bx + p, base:end, :] = half[p + 1, 4 : 4 + bz, :]
+    for p in (0, planes - 1):
+        first[p, base:end, :] = win_s[p, base:end, :]
     for p in range(planes):
         for ref in (win_s, win_h, first, guess):
             for row in (0, 8, 16, end, end + 8, end + 16):
@@ -282,20 +285,19 @@
         next_half[p, 8 : 8 + own, :] = value
 
 
-def outer_1(cells, pos, z_low, z_high, *refs):
+def outer_1(cells, z_low, z_high, *refs):
     win_s, win_h, guess, fx, fz, left, right, diag, inverse, first, next_source, next_half = refs[12:24]
     to_next, to_prev, temp = refs[24:]
-    gx, gz = (pos[0], pos[1])
+    gx, gz = (lax.axis_index("gx"), lax.axis_index("gz"))
     planes, base = (win_s.shape[0], 24)
     bx, bz = (planes // 3, win_s.shape[1] - 48)
     end = base + bz
     has_low, has_high = inside_z(gz, cells[1] // bz)
     for start, ref, inside in ((base - 16, z_low, has_low), (end, z_high, has_high)):
         for p in range(planes):
-            at = p if p < bx else p + 1
-            unpack_1(win_s, win_h, p, start, 16, inside * ref[at, :, :])
-        first[0, start : start + 16, :] = inside * ref[bx, :, :]
-        first[planes - 1, start : start + 16, :] = inside * ref[planes + 1, :, :]
+            unpack_1(win_s, win_h, p, start, 16, inside * ref[p, :, :])
+        for p in (0, planes - 1):
+            first[p, start : start + 16, :] = win_s[p, start : start + 16, :]
     level = Level(1, gx, gz, (bx, bz), cells, bx, (win_h, fx, fz, left, right, diag, inverse), base)
     strips = base - 12, end - 4
     for row in strips:
@@ -331,8 +333,8 @@
     return twice + roll(twice, 2)
 
 
-def down_2(cells, pos, prev, here, next_, guess0, win_s, guess, fx, fz, left, right, diag, inverse, message, to_next, to_prev, win_h, first, temp):
-    gx, gz = (pos[0], pos[1])
+def down_2(cells, prev, here, next_, guess0, win_s, guess, fx, fz, left, right, diag, inverse, message, to_next, to_prev, win_h, first, temp):
+    gx, gz = (lax.axis_index("gx"), lax.axis_index("gz"))
     bx, bz = (2, prev.shape[1] - 16)
     own, planes = (4, 10)
     end = ROW + bz
@@ -365,9 +367,10 @@
     lane = lax.broadcasted_iota(jnp.int32, (LANES, LANES), 1)
     pick = jnp.where(((cell >> 3) == (lane & 15)) & ((cell & 7) == 0), 1.0, 0.0)
     keep = (lanes_of(rows) >> 4) == rows_of(rows)
-    for at, value in enumerate((sources[0], halves[0])):
-        dense = jnp.dot(value, pick, precision=lax.Precision.HIGHEST, preferred_element_type=jnp.float32)
-        dense = jnp.sum(jnp.where(keep, dense, 0.0), axis=0, keepdims=True)
+    both = jnp.concatenate([sources[0], halves[0]])
+    both = jnp.dot(both, pick, precision=lax.Precision.HIGHEST, preferred_element_type=jnp.float32)
+    for at in range(2):
+        dense = jnp.sum(jnp.where(keep, both[at * rows : (at + 1) * rows], 0.0), axis=0, keepdims=True)
         for device in range(message.shape[0]):
             message[device, at : at + 1, :] = dense
 
@@ -428,14 +431,16 @@
             self.state[self.now, b, 8 : self.planes + 8, :] = flags[b] * parts[b][0, :, :]
             self.update[b, :, :] = flags[b] * parts[b][1, :, :]
 
-    def steps(self, which):
+    def steps(self, which, keep):
         for index in which:
+            blocks = range(3) if keep or index < which[-1] else (1,)
             carry, gain = self.weights[index]
             old, new = (self.now, 1 - self.now)
             for x in range(0, self.planes, 8):
                 centers = [self.state[old, b, x + 8 : x + 16, :] for b in range(3)]
                 before, after = self.beside_z(centers)
-                for b, center in enumerate(centers):
+                for b in blocks:
+                    center = centers[b]
                     face = [self.base[7 * b + k, x : x + 8, :] for k in range(7)]
                     beside = face[0] * self.state[old, b, x + 7 : x + 15, :] + face[1] * self.state[old, b, x + 9 : x + 17, :]
                     beside = beside + (face[2] * before[b] + face[3] * after[b])
@@ -450,24 +455,24 @@
         out[1, :, :] = self.update[1, :, :]
 
 
-def solve_first(count, pos, low, here, high, base, out, half, state, update):
-    has_low, has_high = inside_z(pos[1], count)
+def solve_first(count, low, here, high, base, out, half, state, update):
+    has_low, has_high = inside_z(lax.axis_index("gz"), count)
     level = Coarsest(base, state, update)
     level.start((low, here, high), half, (has_low, 1.0, has_high))
-    level.steps(range(1, SOLVE[0]))
+    level.steps(range(1, SOLVE[0]), False)
     level.leave(out)
 
 
-def solve_next(count, pos, base, low, here, high, out, state, update):
-    has_low, has_high = inside_z(pos[1], count)
+def solve_next(count, base, low, here, high, out, state, update):
+    has_low, has_high = inside_z(lax.axis_index("gz"), count)
     level = Coarsest(base, state, update)
     level.resume((low, here, high), (has_low, 1.0, has_high))
-    level.steps(range(SOLVE[0], SOLVE[1]))
+    level.steps(range(SOLVE[0], SOLVE[1]), False)
     level.leave(out)
 
 
-def finish(cells, pos, base, low, here, high, prev2, next2, *refs):
-    gx, gz = (pos[0], pos[1])
+def finish(cells, base, low, here, high, prev2, next2, *refs):
+    gx, gz = (lax.axis_index("gx"), lax.axis_index("gz"))
     (s2, g2, *coefs2), (s1, g1, *coefs1), (s0, g0, *coefs0) = (refs[0:8], refs[8:16], refs[16:24])
     out, state, update3, coarse2, temp, start2, start1, start0, middle, update = refs[24:]
     bz0 = out.shape[1]
@@ -475,7 +480,7 @@
     has_low, has_high = inside_z(gz, cells[0][1] // bz0)
     level = Coarsest(base, state, update3)
     level.resume((low, here, high), (has_low, 1.0, has_high))
-    level.steps(range(SOLVE[1], COARSE_ITERS))
+    level.steps(range(SOLVE[1], COARSE_ITERS), True)
     last = level.now
 
     bx2 = 2
@@ -563,14 +568,13 @@
 
 
 def call(kernel, name, outs, scratches, *args, aliases={}):
-    smem = pl.BlockSpec(memory_space=pltpu.SMEM)
     limit = 4 * 2**20 + sum(4 * math.prod(ref.shape) for ref in [*scratches, *outs, *args])
     vmem = pl.BlockSpec(memory_space=pltpu.VMEM)
     return pl.pallas_call(
         kernel,
         name=name,
         out_shape=outs,
-        in_specs=[smem if arg.dtype == jnp.int32 else vmem for arg in args],
+        in_specs=[vmem] * len(args),
         out_specs=[vmem] * len(outs),
         scratch_shapes=scratches,
         input_output_aliases=aliases,
@@ -592,7 +596,6 @@
     nx, nz = (lax.axis_size("gx"), lax.axis_size("gz"))
     bx, bz = right_side.shape[0:2]
     cells = [(nx * bx >> level, nz * bz >> level) for level in range(4)]
-    pos = jnp.stack([lax.axis_index("gx"), lax.axis_index("gz")]).astype(jnp.int32)
     for_next = jnp.concatenate([right_side[bx - 2 :], conductivity[bx - 3 :]])
     for_prev = jnp.concatenate([right_side[:2], conductivity[:3]])
     low, high = (shift(for_next, "gx", 1), shift(for_prev, "gx", -1))
@@ -608,7 +611,6 @@
         "inner_0",
         [f32(*window)] * 10 + [f32(bx // 2, bz // 2, LANES), f32(*half1)],
         [scratch(bz + 16, LANES)],
-        pos,
         right_side,
         conductivity,
         low,
@@ -617,20 +619,19 @@
     *arrays, for_next, for_prev = call(
         functools.partial(outer_0, cells[0]),
         "outer_0",
-        [f32(*array.shape) for array in arrays] + [f32(bx // 2 + 1, bz // 2, LANES)] * 2,
+        [f32(*array.shape) for array in arrays] + [f32(bx // 2, bz // 2, LANES)] * 2,
         [scratch(16, LANES)],
-        pos,
         z_low,
         z_high,
         *arrays,
-        aliases={i + 3: i for i in range(12)},
+        aliases={i + 2: i for i in range(12)},
     )
     kept0 = (arrays[0], arrays[2], *arrays[3:9])
 
     bx, bz = (bx // 2, bz // 2)
     low, high = (shift(for_next, "gx", 1), shift(for_prev, "gx", -1))
     to_high, to_low = call(
-        edge_rows_1, "edge_rows_1", [f32(3 * bx + 2, 16, LANES)] * 2, [], low, for_next, high
+        edge_rows_1, "edge_rows_1", [f32(3 * bx, 16, LANES)] * 2, [], low, for_next, for_prev, high
     )
     z_low, z_high = (turn(to_high, "gz", 1), turn(to_low, "gz", -1))
     window = (3 * bx, bz + 48, LANES)
@@ -640,8 +641,8 @@
         "inner_1",
         [f32(*window)] * 10 + [f32(*half2)] * 2,
         [scratch(bz, LANES)],
-        pos,
-        for_next,
+        arrays[10],
+        arrays[11],
         low,
         high,
     )
@@ -650,11 +651,10 @@
         "outer_1",
         [f32(*array.shape) for array in arrays1] + [f32(2, bz // 2 + 16, LANES)] * 2,
         [scratch(16, LANES)],
-        pos,
         z_low,
         z_high,
         *arrays1,
-        aliases={i + 3: i for i in range(12)},
+        aliases={i + 2: i for i in range(12)},
     )
     kept1 = (arrays1[0], arrays1[2], *arrays1[3:9])
 
@@ -666,7 +666,6 @@
         "down_2",
         [f32(*window)] * 8 + [f32(nx, 2, LANES)] + [f32(LATE, bz + 16, LANES)] * 2,
         [scratch(*window)] * 2 + [scratch(bz + 16, LANES)],
-        pos,
         prev,
         for_next,
         next_,
@@ -684,14 +683,13 @@
         "solve_first",
         [f32(21, nx, LANES), f32(2, nx, LANES)],
         [scratch(3, nx + 16, LANES)] + solving,
-        pos,
         *blocks,
     )
     low, high = (turn(here, "gz", 1), turn(here, "gz", -1))
     for_prev, _ = lax.optimization_barrier((for_prev, here))
     next2 = shift(for_prev, "gx", -1)
     (here,) = call(
-        functools.partial(solve_next, nz), "solve_next", [f32(2, nx, LANES)], solving, pos, base, low, here, high
+        functools.partial(solve_next, nz), "solve_next", [f32(2, nx, LANES)], solving, base, low, here, high
     )
     low, high = (turn(here, "gz", 1), turn(here, "gz", -1))
 
@@ -701,7 +699,7 @@
     work += [scratch(bx // 4 + 8, bz // 4 + 32, LANES), scratch(bx // 2 + 8, bz // 2 + 48, LANES)]
     work += [scratch(*window)] * 3
     (result,) = call(
-        functools.partial(finish, cells), "finish", [f32(*right_side.shape)], work, pos, base, low, here, high,
+        functools.partial(finish, cells), "finish", [f32(*right_side.shape)], work, base, low, here, high,
         prev2, next2, *kept2, *kept1, *kept0,
     )
     return result

time: 106 us -> 102 us (0.962)
  Pallas kernels: 13.4 us -> 9.07 us
  starting transfers between devices: 46.3 us -> 48.8 us
  waiting for transfers between devices: 22.3 us -> 20.9 us
    pallas_call x10, Pallas kernels: 13.4 us -> 9.07 us  [call(): pl.pallas_call(kernel, name=name, out_shape=outs, in_specs=[vmem] * len(a...]
    ppermute x8, waiting for transfers between devices: 13.9 us -> 11.4 us  [shift(): lax.ppermute(array, axis, [(i, i + by) for i in range(devices) if 0 <= i...]
    ppermute x8, starting transfers between devices: 35.8 us -> 38.1 us  [shift(): lax.ppermute(array, axis, [(i, i + by) for i in range(devices) if 0 <= i...]
    ppermute x10, waiting for transfers between devices: 8.39 us -> 9.54 us  [turn(): lax.ppermute(array, axis, [(i, (i + by) % devices) for i in range(devices)])]
  transfers between devices with their start and end apart: 18 -> 18, of which waited for: 9 -> 10; matrix products, arithmetic and copies ran while one was open for 0% -> 0% of each run, Pallas kernels for 6% -> 4%
where the time goes in v6:
time: 102 us
  starting transfers between devices  48.8 us (48%)
  blocking collectives  22 us (22%)
  waiting for transfers between devices  20.9 us (20%)
  Pallas kernels  9.07 us (9%)
  local copies, waits for them, and re-layouts  1.03 us (1%)
    ppermute x8, starting transfers between devices, shift(): lax.ppermute(array, axis, [(i, i + by) for i in range(devices) if 0 <= i...  38.1 us
    all_to_all x1, blocking collectives, on_device(): here = lax.all_to_all(row3, 'gx', 0, 0, tiled=True)  22 us
    ppermute x8, waiting for transfers between devices, shift(): lax.ppermute(array, axis, [(i, i + by) for i in range(devices) if 0 <= i...  11.4 us
    ppermute x10, starting transfers between devices, turn(): lax.ppermute(array, axis, [(i, (i + by) % devices) for i in range(devices)])  10.6 us
    ppermute x10, waiting for transfers between devices, turn(): lax.ppermute(array, axis, [(i, (i + by) % devices) for i in range(devices)])  9.54 us
    pallas_call x10, Pallas kernels, call(): pl.pallas_call(kernel, name=name, out_shape=outs, in_specs=[vmem] * len(a...  9.07 us
  transfers between devices with their start and end apart: 18, of which 10 were waited for; matrix products, arithmetic and copies ran while one was open for 0% of the time, Pallas kernels for 4%

profile of v6, /device:TPU:6, one launch (start us, length us, event | category | flops | bytes accessed | tf_op | source)
XLA Modules:
  0.0 102.0 jit_solution(5245825189550706951)
XLA Ops:
  0.0 0.9 fusion
  1.1 4.0 %collective-permute-start = (f32[5,64,128]{2,1,0:T(8,128)S(1)}, f32[5,64,128]{2,1,0:T(8,128)S(1)}, u32[]{:S(2)}, u32[]{:S(2)}) collective-permute-start(f32[5,64,128]{2,1,0:T(8,128)S(1)} %pad_maximum_fusion), channel_id=1, source_target_pairs={{0,8},{8,16},{16,24},{24,32},{32,40},{40,48},{48,56},{56,64},{64,7... | collective-permute-start | bytes 491528 | tf_op jit(solution)/shard_map/ppermute | solution.py:587
  5.0 9.8 %collective-permute-start.1 = (f32[5,64,128]{2,1,0:T(8,128)S(1)}, f32[5,64,128]{2,1,0:T(8,128)S(1)}, u32[]{:S(2)}, u32[]{:S(2)}) collective-permute-start(f32[5,64,128]{2,1,0:T(8,128)S(1)} %pad_maximum_fusion.1), channel_id=1, source_target_pairs={{8,0},{16,8},{24,16},{32,24},{40,32},{48,40},{56,48},{64,56},{72,6... | collective-permute-start | bytes 491528 | tf_op jit(solution)/shard_map/ppermute | solution.py:587
  14.8 2.2 %collective-permute-done.low = f32[5,64,128]{2,1,0:T(8,128)S(1)} collective-permute-done((f32[5,64,128]{2,1,0:T(8,128)S(1)}, f32[5,64,128]{2,1,0:T(8,128)S(1)}, u32[]{:S(2)}, u32[]{:S(2)}) %collective-permute-start) | collective-permute-done | bytes 163872 | tf_op jit(solution)/shard_map/ppermute | solution.py:587
  17.1 1.2 %collective-permute-done.1.high = f32[5,64,128]{2,1,0:T(8,128)S(1)} collective-permute-done((f32[5,64,128]{2,1,0:T(8,128)S(1)}, f32[5,64,128]{2,1,0:T(8,128)S(1)}, u32[]{:S(2)}, u32[]{:S(2)}) %collective-permute-start.1) | collective-permute-done | bytes 163872 | tf_op jit(solution)/shard_map/ppermute | solution.py:587
  18.3 2.9 %collective-permute-start.3 = (f32[14,8,128]{2,1,0:T(8,128)S(1)}, f32[14,8,128]{2,1,0:T(8,128)S(1)}, u32[]{:S(2)}, u32[]{:S(2)}) collective-permute-start(f32[14,8,128]{2,1,0:T(8,128)S(1)} %get-tuple-element.71), channel_id=1, source_target_pairs={{0,7},{1,0},{2,1},{3,2},{4,3},{5,4},{6,5},{7,6},{8,15},{9,8},{10,9... | collective-permute-start | bytes 172040 | tf_op jit(solution)/shard_map/ppermute | solution.py:592
  21.3 1.4 %inner_0.1 = (f32[14,96,128]{2,1,0:T(8,128)S(1)}, f32[14,96,128]{2,1,0:T(8,128)S(1)}, f32[14,96,128]{2,1,0:T(8,128)S(1)}, f32[14,96,128]{2,1,0:T(8,128)S(1)}, f3...) custom-call(f32[8,64,128]{2,1,0:T(8,128)S(1)} %copy-done.1, ...), custom_call_target="tpu_custom_call" | custom-call | tf_op jit(solution)/shard_map/inner_0/pallas_call | solution.py:573
  22.6 0.5 collective-permute-done.2.z_low
  23.1 0.6 outer_0.1
  23.8 1.9 %collective-permute-start.4 = (f32[4,32,128]{2,1,0:T(8,128)S(1)}, f32[4,32,128]{2,1,0:T(8,128)S(1)}, u32[]{:S(2)}, u32[]{:S(2)}) collective-permute-start(f32[4,32,128]{2,1,0:T(8,128)S(1)} %get-tuple-element.84.to_next), channel_id=1, source_target_pairs={{0,8},{8,16},{16,24},{24,32},{32,40},{40,48},{48,56},{56,64},{64,7... | collective-permute-start | bytes 196616 | tf_op jit(solution)/shard_map/ppermute | solution.py:587
  25.7 6.5 %collective-permute-start.5 = (f32[4,32,128]{2,1,0:T(8,128)S(1)}, f32[4,32,128]{2,1,0:T(8,128)S(1)}, u32[]{:S(2)}, u32[]{:S(2)}) collective-permute-start(f32[4,32,128]{2,1,0:T(8,128)S(1)} %get-tuple-element.85.to_prev), channel_id=1, source_target_pairs={{8,0},{16,8},{24,16},{32,24},{40,32},{48,40},{56,48},{64,56},{72,6... | collective-permute-start | bytes 196616 | tf_op jit(solution)/shard_map/ppermute | solution.py:587
  32.2 0.8 collective-permute-done.4.low
  33.0 1.2 %collective-permute-done.5.high = f32[4,32,128]{2,1,0:T(8,128)S(1)} collective-permute-done((f32[4,32,128]{2,1,0:T(8,128)S(1)}, f32[4,32,128]{2,1,0:T(8,128)S(1)}, u32[]{:S(2)}, u32[]{:S(2)}) %collective-permute-start.5) | collective-permute-done | bytes 65568 | tf_op jit(solution)/shard_map/ppermute | solution.py:587
  34.2 2.9 %collective-permute-start.7 = (f32[12,16,128]{2,1,0:T(8,128)S(1)}, f32[12,16,128]{2,1,0:T(8,128)S(1)}, u32[]{:S(2)}, u32[]{:S(2)}) collective-permute-start(f32[12,16,128]{2,1,0:T(8,128)S(1)} %get-tuple-element.87), channel_id=1, source_target_pairs={{0,7},{1,0},{2,1},{3,2},{4,3},{5,4},{6,5},{7,6},{8,15},{9,8},{10,9... | collective-permute-start | bytes 294920 | tf_op jit(solution)/shard_map/ppermute | solution.py:592
  37.2 0.7 inner_1.1
  37.8 1.6 %collective-permute-done.6.z_low = f32[12,16,128]{2,1,0:T(8,128)S(1)} collective-permute-done((f32[12,16,128]{2,1,0:T(8,128)S(1)}, f32[12,16,128]{2,1,0:T(8,128)S(1)}, u32[]{:S(2)}, u32[]{:S(2)}) %collective-permute-start.6) | collective-permute-done | bytes 98336 | tf_op jit(solution)/shard_map/ppermute | solution.py:592
  39.5 0.7 outer_1.1
  40.1 6.5 %collective-permute-start.9 = (f32[2,32,128]{2,1,0:T(8,128)S(1)}, f32[2,32,128]{2,1,0:T(8,128)S(1)}, u32[]{:S(2)}, u32[]{:S(2)}) collective-permute-start(f32[2,32,128]{2,1,0:T(8,128)S(1)} %get-tuple-element.103), channel_id=1, source_target_pairs={{8,0},{16,8},{24,16},{32,24},{40,32},{48,40},{56,48},{64,56},{72,6... | collective-permute-start | bytes 98312 | tf_op jit(solution)/shard_map/ppermute | solution.py:587
  46.6 1.9 %collective-permute-start.8 = (f32[2,32,128]{2,1,0:T(8,128)S(1)}, f32[2,32,128]{2,1,0:T(8,128)S(1)}, u32[]{:S(2)}, u32[]{:S(2)}) collective-permute-start(f32[2,32,128]{2,1,0:T(8,128)S(1)} %get-tuple-element.102.here), channel_id=1, source_target_pairs={{0,8},{8,16},{16,24},{24,32},{32,40},{40,48},{48,56},{56,64},{64,7... | collective-permute-start | bytes 98312 | tf_op jit(solution)/shard_map/ppermute | solution.py:587
  48.6 6.0 %collective-permute-done.8.prev = f32[2,32,128]{2,1,0:T(8,128)S(1)} collective-permute-done((f32[2,32,128]{2,1,0:T(8,128)S(1)}, f32[2,32,128]{2,1,0:T(8,128)S(1)}, u32[]{:S(2)}, u32[]{:S(2)}) %collective-permute-start.8) | collective-permute-done | bytes 32800 | tf_op jit(solution)/shard_map/ppermute | solution.py:587
  54.6 0.9 down_2.1
  55.4 22.0 %all_to_all.5 = f32[64,2,128]{2,1,0:T(2,128)S(1)} all-to-all(f32[64,2,128]{2,1,0:T(2,128)S(1)} %get-tuple-element.105), channel_id=1, replica_groups=mesh['gx'=64,'gz'=8] {'gx'}, dimensions={0} | all-to-all | bytes 131072 | tf_op jit(solution)/shard_map/all_to_all | solution.py:675
  77.5 1.5 %collective-permute-start.11 = (f32[64,2,128]{2,1,0:T(2,128)S(1)}, f32[64,2,128]{2,1,0:T(2,128)S(1)}, u32[]{:S(2)}, u32[]{:S(2)}) collective-permute-start(f32[64,2,128]{2,1,0:T(2,128)S(1)} %all_to_all.5), channel_id=1, source_target_pairs={{0,7},{1,0},{2,1},{3,2},{4,3},{5,4},{6,5},{7,6},{8,15},{9,8},{10,9... | collective-permute-start | bytes 196616 | tf_op jit(solution)/shard_map/ppermute | solution.py:592
  79.0 2.3 %collective-permute-start.16 = (f32[8,32,128]{2,1,0:T(8,128)S(1)}, f32[8,32,128]{2,1,0:T(8,128)S(1)}, u32[]{:S(2)}, u32[]{:S(2)}) collective-permute-start(f32[8,32,128]{2,1,0:T(8,128)S(1)} %get-tuple-element.109), channel_id=1, source_target_pairs={{0,8},{8,16},{16,24},{24,32},{32,40},{40,48},{48,56},{56,64},{64,7... | collective-permute-start | bytes 393224 | tf_op jit(solution)/shard_map/ppermute | solution.py:587
  81.3 2.6 %collective-permute-done.10 = f32[64,2,128]{2,1,0:T(2,128)S(1)} collective-permute-done((f32[64,2,128]{2,1,0:T(2,128)S(1)}, f32[64,2,128]{2,1,0:T(2,128)S(1)}, u32[]{:S(2)}, u32[]{:S(2)}) %collective-permute-start.10) | collective-permute-done | bytes 65568 | tf_op jit(solution)/shard_map/ppermute | solution.py:592
  83.9 1.0 solve_first.1
  85.4 5.2 %collective-permute-start.17 = (f32[8,32,128]{2,1,0:T(8,128)S(1)}, f32[8,32,128]{2,1,0:T(8,128)S(1)}, u32[]{:S(2)}, u32[]{:S(2)}) collective-permute-start(f32[8,32,128]{2,1,0:T(8,128)S(1)} %get-tuple-element.111), channel_id=1, source_target_pairs={{8,0},{16,8},{24,16},{32,24},{40,32},{48,40},{56,48},{64,56},{72,6... | collective-permute-start | bytes 393224 | tf_op jit(solution)/shard_map/ppermute | solution.py:587
  90.7 1.0 solve_next.1.here
  91.6 2.7 %collective-permute-start.15 = (f32[2,64,128]{2,1,0:T(8,128)S(1)}, f32[2,64,128]{2,1,0:T(8,128)S(1)}, u32[]{:S(2)}, u32[]{:S(2)}) collective-permute-start(f32[2,64,128]{2,1,0:T(8,128)S(1)} %solve_next.1.here), channel_id=1, source_target_pairs={{0,7},{1,0},{2,1},{3,2},{4,3},{5,4},{6,5},{7,6},{8,15},{9,8},{10,9... | collective-permute-start | bytes 196616 | tf_op jit(solution)/shard_map/ppermute | solution.py:592
  94.3 1.9 %collective-permute-done.15.high = f32[2,64,128]{2,1,0:T(8,128)S(1)} collective-permute-done((f32[2,64,128]{2,1,0:T(8,128)S(1)}, f32[2,64,128]{2,1,0:T(8,128)S(1)}, u32[]{:S(2)}, u32[]{:S(2)}) %collective-permute-start.15) | collective-permute-done | bytes 65568 | tf_op jit(solution)/shard_map/ppermute | solution.py:592
  96.2 3.0 %collective-permute-done.14.low = f32[2,64,128]{2,1,0:T(8,128)S(1)} collective-permute-done((f32[2,64,128]{2,1,0:T(8,128)S(1)}, f32[2,64,128]{2,1,0:T(8,128)S(1)}, u32[]{:S(2)}, u32[]{:S(2)}) %collective-permute-start.14) | collective-permute-done | bytes 65568 | tf_op jit(solution)/shard_map/ppermute | solution.py:592
  99.2 2.8 %finish.1 = f32[8,64,128]{2,1,0:T(8,128)} custom-call(f32[21,64,128]{2,1,0:T(8,128)S(1)} %get-tuple-element.106.base, f32[2,64,128]{2,1,0:T(8,128)S(1)} %collective-permute-done.14.low, f32[2,64,128]{2,1,0:T(8,128)S(1)} %solve_next.1.here, f32[2,64,128]{2,1,0:T(8,128)S(1)} %collective-permute-done.15.high, f32[8,32,128]{2,1,0:T(8,128)S(1)} %collective-permute-done.16.prev2, ...), custom_call_target="tpu_custom_call" | custom-call | tf_op jit(solution)/shard_map/finish/pallas_call | solution.py:573
  (23 shorter events, 0.8 us)
Async XLA Ops:
  0.0 1.0 copy-start
  1.0 17.2 %copy-start.1 = (f32[8,64,128]{2,1,0:T(8,128)S(1)}, f32[8,64,128]{2,1,0:T(8,128)}, u32[]{:S(2)}) copy-start(f32[8,64,128]{2,1,0:T(8,128)} %source.3) | copy-start | bytes 786436
  1.1 16.0 %collective-permute-start = (f32[5,64,128]{2,1,0:T(8,128)S(1)}, f32[5,64,128]{2,1,0:T(8,128)S(1)}, u32[]{:S(2)}, u32[]{:S(2)}) collective-permute-start(f32[5,64,128]{2,1,0:T(8,128)S(1)} %pad_maximum_fusion), channel_id=1, source_target_pairs={{0,8},{8,16},{16,24},{24,32},{32,40},{40,48},{48,56},{56,64},{64,7... | collective-permute-start | bytes 491528 | tf_op jit(solution)/shard_map/ppermute | solution.py:587
  5.0 13.2 %collective-permute-start.1 = (f32[5,64,128]{2,1,0:T(8,128)S(1)}, f32[5,64,128]{2,1,0:T(8,128)S(1)}, u32[]{:S(2)}, u32[]{:S(2)}) collective-permute-start(f32[5,64,128]{2,1,0:T(8,128)S(1)} %pad_maximum_fusion.1), channel_id=1, source_target_pairs={{8,0},{16,8},{24,16},{32,24},{40,32},{48,40},{56,48},{64,56},{72,6... | collective-permute-start | bytes 491528 | tf_op jit(solution)/shard_map/ppermute | solution.py:587
  18.3 4.8 %collective-permute-start.2 = (f32[14,8,128]{2,1,0:T(8,128)S(1)}, f32[14,8,128]{2,1,0:T(8,128)S(1)}, u32[]{:S(2)}, u32[]{:S(2)}) collective-permute-start(f32[14,8,128]{2,1,0:T(8,128)S(1)} %get-tuple-element.70), channel_id=1, source_target_pairs={{0,1},{1,2},{2,3},{3,4},{4,5},{5,6},{6,7},{7,0},{8,9},{9,10},{10,1... | collective-permute-start | bytes 172040 | tf_op jit(solution)/shard_map/ppermute | solution.py:592
  18.3 4.8 %collective-permute-start.3 = (f32[14,8,128]{2,1,0:T(8,128)S(1)}, f32[14,8,128]{2,1,0:T(8,128)S(1)}, u32[]{:S(2)}, u32[]{:S(2)}) collective-permute-start(f32[14,8,128]{2,1,0:T(8,128)S(1)} %get-tuple-element.71), channel_id=1, source_target_pairs={{0,7},{1,0},{2,1},{3,2},{4,3},{5,4},{6,5},{7,6},{8,15},{9,8},{10,9... | collective-permute-start | bytes 172040 | tf_op jit(solution)/shard_map/ppermute | solution.py:592
  23.8 9.2 %collective-permute-start.4 = (f32[4,32,128]{2,1,0:T(8,128)S(1)}, f32[4,32,128]{2,1,0:T(8,128)S(1)}, u32[]{:S(2)}, u32[]{:S(2)}) collective-permute-start(f32[4,32,128]{2,1,0:T(8,128)S(1)} %get-tuple-element.84.to_next), channel_id=1, source_target_pairs={{0,8},{8,16},{16,24},{24,32},{32,40},{40,48},{48,56},{56,64},{64,7... | collective-permute-start | bytes 196616 | tf_op jit(solution)/shard_map/ppermute | solution.py:587
  25.7 8.5 %collective-permute-start.5 = (f32[4,32,128]{2,1,0:T(8,128)S(1)}, f32[4,32,128]{2,1,0:T(8,128)S(1)}, u32[]{:S(2)}, u32[]{:S(2)}) collective-permute-start(f32[4,32,128]{2,1,0:T(8,128)S(1)} %get-tuple-element.85.to_prev), channel_id=1, source_target_pairs={{8,0},{16,8},{24,16},{32,24},{40,32},{48,40},{56,48},{64,56},{72,6... | collective-permute-start | bytes 196616 | tf_op jit(solution)/shard_map/ppermute | solution.py:587
  34.2 5.3 %collective-permute-start.6 = (f32[12,16,128]{2,1,0:T(8,128)S(1)}, f32[12,16,128]{2,1,0:T(8,128)S(1)}, u32[]{:S(2)}, u32[]{:S(2)}) collective-permute-start(f32[12,16,128]{2,1,0:T(8,128)S(1)} %get-tuple-element.86), channel_id=1, source_target_pairs={{0,1},{1,2},{2,3},{3,4},{4,5},{5,6},{6,7},{7,0},{8,9},{9,10},{10,1... | collective-permute-start | bytes 294920 | tf_op jit(solution)/shard_map/ppermute | solution.py:592
  34.2 5.2 %collective-permute-start.7 = (f32[12,16,128]{2,1,0:T(8,128)S(1)}, f32[12,16,128]{2,1,0:T(8,128)S(1)}, u32[]{:S(2)}, u32[]{:S(2)}) collective-permute-start(f32[12,16,128]{2,1,0:T(8,128)S(1)} %get-tuple-element.87), channel_id=1, source_target_pairs={{0,7},{1,0},{2,1},{3,2},{4,3},{5,4},{6,5},{7,6},{8,15},{9,8},{10,9... | collective-permute-start | bytes 294920 | tf_op jit(solution)/shard_map/ppermute | solution.py:592
  40.1 8.4 %collective-permute-start.9 = (f32[2,32,128]{2,1,0:T(8,128)S(1)}, f32[2,32,128]{2,1,0:T(8,128)S(1)}, u32[]{:S(2)}, u32[]{:S(2)}) collective-permute-start(f32[2,32,128]{2,1,0:T(8,128)S(1)} %get-tuple-element.103), channel_id=1, source_target_pairs={{8,0},{16,8},{24,16},{32,24},{40,32},{48,40},{56,48},{64,56},{72,6... | collective-permute-start | bytes 98312 | tf_op jit(solution)/shard_map/ppermute | solution.py:587
  46.6 7.9 %collective-permute-start.8 = (f32[2,32,128]{2,1,0:T(8,128)S(1)}, f32[2,32,128]{2,1,0:T(8,128)S(1)}, u32[]{:S(2)}, u32[]{:S(2)}) collective-permute-start(f32[2,32,128]{2,1,0:T(8,128)S(1)} %get-tuple-element.102.here), channel_id=1, source_target_pairs={{0,8},{8,16},{16,24},{24,32},{32,40},{40,48},{48,56},{56,64},{64,7... | collective-permute-start | bytes 98312 | tf_op jit(solution)/shard_map/ppermute | solution.py:587
  77.5 3.9 %collective-permute-start.11 = (f32[64,2,128]{2,1,0:T(2,128)S(1)}, f32[64,2,128]{2,1,0:T(2,128)S(1)}, u32[]{:S(2)}, u32[]{:S(2)}) collective-permute-start(f32[64,2,128]{2,1,0:T(2,128)S(1)} %all_to_all.5), channel_id=1, source_target_pairs={{0,7},{1,0},{2,1},{3,2},{4,3},{5,4},{6,5},{7,6},{8,15},{9,8},{10,9... | collective-permute-start | bytes 196616 | tf_op jit(solution)/shard_map/ppermute | solution.py:592
  79.0 4.9 %collective-permute-start.10 = (f32[64,2,128]{2,1,0:T(2,128)S(1)}, f32[64,2,128]{2,1,0:T(2,128)S(1)}, u32[]{:S(2)}, u32[]{:S(2)}) collective-permute-start(f32[64,2,128]{2,1,0:T(2,128)S(1)} %all_to_all.5), channel_id=1, source_target_pairs={{0,1},{1,2},{2,3},{3,4},{4,5},{5,6},{6,7},{7,0},{8,9},{9,10},{10,1... | collective-permute-start | bytes 196616 | tf_op jit(solution)/shard_map/ppermute | solution.py:592
  79.0 15.3 %collective-permute-start.16 = (f32[8,32,128]{2,1,0:T(8,128)S(1)}, f32[8,32,128]{2,1,0:T(8,128)S(1)}, u32[]{:S(2)}, u32[]{:S(2)}) collective-permute-start(f32[8,32,128]{2,1,0:T(8,128)S(1)} %get-tuple-element.109), channel_id=1, source_target_pairs={{0,8},{8,16},{16,24},{24,32},{32,40},{40,48},{48,56},{56,64},{64,7... | collective-permute-start | bytes 393224 | tf_op jit(solution)/shard_map/ppermute | solution.py:587
  84.9 5.8 %collective-permute-start.13 = (f32[2,64,128]{2,1,0:T(8,128)S(1)}, f32[2,64,128]{2,1,0:T(8,128)S(1)}, u32[]{:S(2)}, u32[]{:S(2)}) collective-permute-start(f32[2,64,128]{2,1,0:T(8,128)S(1)} %get-tuple-element.107.here), channel_id=1, source_target_pairs={{0,7},{1,0},{2,1},{3,2},{4,3},{5,4},{6,5},{7,6},{8,15},{9,8},{10,9... | collective-permute-start | bytes 196616 | tf_op jit(solution)/shard_map/ppermute | solution.py:592
  85.0 5.6 %collective-permute-start.12 = (f32[2,64,128]{2,1,0:T(8,128)S(1)}, f32[2,64,128]{2,1,0:T(8,128)S(1)}, u32[]{:S(2)}, u32[]{:S(2)}) collective-permute-start(f32[2,64,128]{2,1,0:T(8,128)S(1)} %get-tuple-element.107.here), channel_id=1, source_target_pairs={{0,1},{1,2},{2,3},{3,4},{4,5},{5,6},{6,7},{7,0},{8,9},{9,10},{10,1... | collective-permute-start | bytes 196616 | tf_op jit(solution)/shard_map/ppermute | solution.py:592
  85.4 13.8 %collective-permute-start.17 = (f32[8,32,128]{2,1,0:T(8,128)S(1)}, f32[8,32,128]{2,1,0:T(8,128)S(1)}, u32[]{:S(2)}, u32[]{:S(2)}) collective-permute-start(f32[8,32,128]{2,1,0:T(8,128)S(1)} %get-tuple-element.111), channel_id=1, source_target_pairs={{8,0},{16,8},{24,16},{32,24},{40,32},{48,40},{56,48},{64,56},{72,6... | collective-permute-start | bytes 393224 | tf_op jit(solution)/shard_map/ppermute | solution.py:587
  91.6 4.6 %collective-permute-start.15 = (f32[2,64,128]{2,1,0:T(8,128)S(1)}, f32[2,64,128]{2,1,0:T(8,128)S(1)}, u32[]{:S(2)}, u32[]{:S(2)}) collective-permute-start(f32[2,64,128]{2,1,0:T(8,128)S(1)} %solve_next.1.here), channel_id=1, source_target_pairs={{0,7},{1,0},{2,1},{3,2},{4,3},{5,4},{6,5},{7,6},{8,15},{9,8},{10,9... | collective-permute-start | bytes 196616 | tf_op jit(solution)/shard_map/ppermute | solution.py:592
  94.3 4.9 %collective-permute-start.14 = (f32[2,64,128]{2,1,0:T(8,128)S(1)}, f32[2,64,128]{2,1,0:T(8,128)S(1)}, u32[]{:S(2)}, u32[]{:S(2)}) collective-permute-start(f32[2,64,128]{2,1,0:T(8,128)S(1)} %solve_next.1.here), channel_id=1, source_target_pairs={{0,1},{1,2},{2,3},{3,4},{4,5},{5,6},{6,7},{7,0},{8,9},{9,10},{10,1... | collective-permute-start | bytes 196616 | tf_op jit(solution)/shard_map/ppermute | solution.py:592

commit v7 on v6

--- a/solution.py
+++ b/solution.py
@@ -11,7 +11,9 @@
 COARSE_ITERS = 20
 LANES = 128
 ROW = 16
-LATE = 8
+EDGE = 13
+LATE = 3
+WIDTHS = ((22, 48), (14, 32), (6, 16))
 SOLVE = (8, 16)
 
 
@@ -155,21 +157,33 @@
     return [half_ref[p, row : row + count, :] for p in planes]
 
 
+def edge_spec_0(bx):
+    spec, at = ([], 0)
+    for p in range(bx + 6):
+        away = max(3 - p, p - bx - 2, 0)
+        spec.append((p, at, 3 - away, 4 - away))
+        at += 7 - 2 * away
+    return spec, at
+
+
 def edge_rows_0(source, cond, low, high, to_high, to_low):
     bx, bz = source.shape[0:2]
-    zero = jnp.zeros((4, LANES), jnp.float32)
-    for rows, out in ((slice(bz - 4, bz), to_high), (slice(0, 4), to_low)):
-        out[0, 0:4, :] = zero
-        out[bx + 5, 0:4, :] = zero
-        for p in range(2):
-            out[p + 1, 0:4, :] = low[p, rows, :]
-            out[p + bx + 3, 0:4, :] = high[p, rows, :]
-        for p in range(3):
-            out[p, 4:8, :] = low[p + 2, rows, :]
-            out[p + bx + 3, 4:8, :] = high[p + 2, rows, :]
-        for p in range(bx):
-            out[p + 3, 0:4, :] = source[p, rows, :]
-            out[p + 3, 4:8, :] = cond[p, rows, :]
+    spec, length = edge_spec_0(bx)
+    for p, at, few, many in spec:
+        if p < 3:
+            (part, q), (other, r) = ((low, p - 1), (low, p + 2))
+        elif p < bx + 3:
+            (part, q), (other, r) = ((source, p - 3), (cond, p - 3))
+        else:
+            (part, q), (other, r) = ((high, p - bx - 3), (high, p - bx - 1))
+        if few:
+            to_high[at : at + few, :] = part[q, bz - few : bz, :]
+            to_low[at : at + few, :] = part[q, 0:few, :]
+        to_high[at + few : at + few + many, :] = other[r, bz - many : bz, :]
+        to_low[at + few : at + few + many, :] = other[r, 0:many, :]
+    rest = to_high.shape[0] - length
+    for out in (to_high, to_low):
+        out[length : length + rest, :] = jnp.zeros((rest, LANES), jnp.float32)
 
 
 def inner_0(cells, source, cond, low, high, win_s, win_h, guess, fx, fz, left, right, diag, inverse, first, next_source, next_half, temp):
@@ -208,11 +222,12 @@
     planes, bx, bz = (win_s.shape[0], win_s.shape[0] - 6, win_s.shape[1] - 32)
     end = ROW + bz
     has_low, has_high = inside_z(gz, cells[1] // bz)
-    for p in range(planes):
-        win_s[p, ROW - 4 : ROW, :] = z_low[p, 0:4, :]
-        win_s[p, end : end + 4, :] = z_high[p, 0:4, :]
-        win_h[p, ROW - 4 : ROW, :] = (0.5 * has_low) * z_low[p, 4:8, :]
-        win_h[p, end : end + 4, :] = (0.5 * has_high) * z_high[p, 4:8, :]
+    for p, at, few, many in edge_spec_0(bx)[0]:
+        if few:
+            win_s[p, ROW - few : ROW, :] = z_low[at : at + few, :]
+            win_s[p, end : end + few, :] = z_high[at : at + few, :]
+        win_h[p, ROW - many : ROW, :] = (0.5 * has_low) * z_low[at + few : at + few + many, :]
+        win_h[p, end : end + many, :] = (0.5 * has_high) * z_high[at + few : at + few + many, :]
     level = Level(0, gx, gz, (bx, bz), cells, 3, (win_h, fx, fz, left, right, diag, inverse))
     strips = ROW - 4, end - 4
     for row in strips:
@@ -247,8 +262,11 @@
     own = [to_prev] * (bx - 1) + [to_next]
     planes = [(low, p) for p in range(bx)] + list(zip(own, range(bx))) + [(high, p) for p in range(bx)]
     for at, (part, p) in enumerate(planes):
-        to_high[at, :, :] = part[p, rows - 16 : rows, :]
-        to_low[at, :, :] = part[p, 0:16, :]
+        to_high[EDGE * at : EDGE * (at + 1), :] = part[p, rows - EDGE : rows, :]
+        to_low[EDGE * at : EDGE * (at + 1), :] = part[p, 0:EDGE, :]
+    used, whole = (EDGE * len(planes), to_high.shape[0])
+    for out in (to_high, to_low):
+        out[used:whole, :] = jnp.zeros((whole - used, LANES), jnp.float32)
 
 
 def unpack_1(win_s, win_h, p, start, rows, mixed):
@@ -293,11 +311,11 @@
     bx, bz = (planes // 3, win_s.shape[1] - 48)
     end = base + bz
     has_low, has_high = inside_z(gz, cells[1] // bz)
-    for start, ref, inside in ((base - 16, z_low, has_low), (end, z_high, has_high)):
+    for start, ref, inside in ((base - EDGE, z_low, has_low), (end, z_high, has_high)):
         for p in range(planes):
-            unpack_1(win_s, win_h, p, start, 16, inside * ref[p, :, :])
+            unpack_1(win_s, win_h, p, start, EDGE, inside * ref[EDGE * p : EDGE * (p + 1), :])
         for p in (0, planes - 1):
-            first[p, start : start + 16, :] = win_s[p, start : start + 16, :]
+            first[p, start : start + EDGE, :] = win_s[p, start : start + EDGE, :]
     level = Level(1, gx, gz, (bx, bz), cells, bx, (win_h, fx, fz, left, right, diag, inverse), base)
     strips = base - 12, end - 4
     for row in strips:
@@ -353,12 +371,15 @@
     row, count = (ROW - 8, bz + 16)
     level.coefs(range(own - 3, own + 5), row, count, win_s, first)
     level.second_down(win_s, first, guess, range(own - 2, own + 4), row, count)
+    lane = lanes_of(count) & 3
     for out, begin in ((to_next, own - 2), (to_prev, own)):
-        for p in range(4):
-            out[p, :, :] = guess[begin + p, row : row + count, :]
+        mixed = guess[begin, row : row + count, :]
+        for p in range(1, 4):
+            mixed = jnp.where(lane == p, guess[begin + p, row : row + count, :], mixed)
+        out[0, :, :] = mixed
         far = guess0.shape[0] - 5 if out is to_next else 4
-        for p in range(4, out.shape[0]):
-            begin0 = ROW + ((p - 4) & 1) * count
+        for p in range(1, LATE):
+            begin0 = ROW + (p - 1) * count
             out[p, :, :] = guess0[far, begin0 : begin0 + count, :]
     sources = level.restricted_remainder(win_s, guess, temp, range(own, own + bx), ROW, bz)
     halves = restricted(win_h, temp, 4, range(own, own + bx), ROW, bz)
@@ -373,6 +394,12 @@
         dense = jnp.sum(jnp.where(keep, both[at * rows : (at + 1) * rows], 0.0), axis=0, keepdims=True)
         for device in range(message.shape[0]):
             message[device, at : at + 1, :] = dense
+
+
+def part_of_x(which, planes):
+    before, width = WIDTHS[which]
+    width = min(width, planes)
+    return (jnp.clip(lax.axis_index("gx") - before, 0, planes - width), width)
 
 
 class Coarsest:
@@ -450,25 +477,39 @@
                     self.state[new, b, x + 8 : x + 16, :] = center + change
             self.now = new
 
-    def leave(self, out):
-        out[0, :, :] = self.state[self.now, 1, 8 : self.planes + 8, :]
-        out[1, :, :] = self.update[1, :, :]
-
-
-def solve_first(count, low, here, high, base, out, half, state, update):
+    def leave(self, out, skip):
+        count = out.shape[1]
+        out[0, :, :] = self.state[self.now, 1, pl.ds(skip + 8, count), :]
+        out[1, :, :] = self.update[1, pl.ds(skip, count), :]
+
+
+def window_3(planes, whole, out):
+    first, width = part_of_x(0, planes)
+    out[...] = whole[pl.ds(2 * first, 2 * width), :]
+
+
+def narrow(planes, base, second, third):
+    first = part_of_x(0, planes)[0]
+    for which, out in ((1, second), (2, third)):
+        begin, width = part_of_x(which, planes)
+        for k in range(base.shape[0]):
+            out[k, :, :] = base[k, pl.ds(begin - first, width), :]
+
+
+def solve_first(count, planes, low, here, high, base, out, half, state, update):
     has_low, has_high = inside_z(lax.axis_index("gz"), count)
     level = Coarsest(base, state, update)
     level.start((low, here, high), half, (has_low, 1.0, has_high))
     level.steps(range(1, SOLVE[0]), False)
-    level.leave(out)
-
-
-def solve_next(count, base, low, here, high, out, state, update):
+    level.leave(out, part_of_x(1, planes)[0] - part_of_x(0, planes)[0])
+
+
+def solve_next(count, planes, base, low, here, high, out, state, update):
     has_low, has_high = inside_z(lax.axis_index("gz"), count)
     level = Coarsest(base, state, update)
     level.resume((low, here, high), (has_low, 1.0, has_high))
     level.steps(range(SOLVE[0], SOLVE[1]), False)
-    level.leave(out)
+    level.leave(out, part_of_x(2, planes)[0] - part_of_x(1, planes)[0])
 
 
 def finish(cells, base, low, here, high, prev2, next2, *refs):
@@ -490,7 +531,8 @@
     pick = jnp.where((cell & 15) == (lane >> 3), 1.0, 0.0)
     z3 = (rows_of(rows) >> 1) - 2
     keep = (lanes_of(rows) >> 4) == (z3 & 7)
-    columns = [state[last, b, pl.ds(gx + 6, 8), :] for b in range(3)]
+    local = gx - part_of_x(2, cells[3][0])[0]
+    columns = [state[last, b, pl.ds(local + 6, 8), :] for b in range(3)]
     for q in range(5):
         picked = [column[q : q + 1, :] for column in columns]
         wide = jnp.where(z3 < 0, picked[0], jnp.where(z3 < 8, picked[1], picked[2]))
@@ -508,7 +550,7 @@
             if q == 2:
                 guess = g2[p, row : row + count, :]
             else:
-                guess = (prev2 if q < 2 else next2)[p if q < 2 else p - own - bx2, 4 : 4 + count, :]
+                guess = spread((prev2 if q < 2 else next2)[0, 4 : 4 + count, :], p if q < 2 else p - own - bx2)
             start[p, row : row + count, :] = guess + coarse2[q * rows : (q + 1) * rows, :]
     level = Level(2, gx, gz, (bx2, bz2), cells[2], own, (None, *coefs2))
 
@@ -544,7 +586,7 @@
             if r in (1, 12):
                 for part in range(2):
                     begin = ROW + part * (bz0 // 2)
-                    start0[r, begin : begin + bz0 // 2, :] = (prev2 if r == 1 else next2)[4 + part, :, :] + temp[
+                    start0[r, begin : begin + bz0 // 2, :] = (prev2 if r == 1 else next2)[1 + part, :, :] + temp[
                         begin - ROW + 4 : begin - ROW + 4 + bz0 // 2, :
                     ]
                 continue
@@ -601,7 +643,7 @@
     low, high = (shift(for_next, "gx", 1), shift(for_prev, "gx", -1))
     planes = bx + 6
     to_high, to_low = call(
-        edge_rows_0, "edge_rows_0", [f32(planes, 8, LANES)] * 2, [], right_side, conductivity, low, high
+        edge_rows_0, "edge_rows_0", [f32(-(-edge_spec_0(bx)[1] // 8) * 8, LANES)] * 2, [], right_side, conductivity, low, high
     )
     z_low, z_high = (turn(to_high, "gz", 1), turn(to_low, "gz", -1))
     window = (planes, bz + 32, LANES)
@@ -631,7 +673,7 @@
     bx, bz = (bx // 2, bz // 2)
     low, high = (shift(for_next, "gx", 1), shift(for_prev, "gx", -1))
     to_high, to_low = call(
-        edge_rows_1, "edge_rows_1", [f32(3 * bx, 16, LANES)] * 2, [], low, for_next, for_prev, high
+        edge_rows_1, "edge_rows_1", [f32(-(-3 * bx * EDGE // 8) * 8, LANES)] * 2, [], low, for_next, for_prev, high
     )
     z_low, z_high = (turn(to_high, "gz", 1), turn(to_low, "gz", -1))
     window = (3 * bx, bz + 48, LANES)
@@ -672,34 +714,47 @@
         arrays[2],
     )
 
-    here = lax.all_to_all(row3, "gx", 0, 0, tiled=True)
-    low, high = (turn(here, "gz", 1), turn(here, "gz", -1))
-    blocks = [part.reshape(2 * nx, LANES) for part in (low, here, high)]
-    solving = [scratch(2, 3, nx + 16, LANES), scratch(3, nx, LANES)]
+    here = lax.all_to_all(row3, "gx", 0, 0, tiled=True).reshape(2 * nx, LANES)
+    widths = [part_of_x(which, nx)[1] for which in range(3)]
     for_next, _ = lax.optimization_barrier((for_next, here))
     prev2 = shift(for_next, "gx", 1)
+    (here,) = call(functools.partial(window_3, nx), "window_3", [f32(2 * widths[0], LANES)], [], here)
+    low, high = (turn(here, "gz", 1), turn(here, "gz", -1))
+    solving = [[scratch(2, 3, width + 16, LANES), scratch(3, width, LANES)] for width in widths]
     base, here = call(
-        functools.partial(solve_first, nz),
+        functools.partial(solve_first, nz, nx),
         "solve_first",
-        [f32(21, nx, LANES), f32(2, nx, LANES)],
-        [scratch(3, nx + 16, LANES)] + solving,
-        *blocks,
+        [f32(21, widths[0], LANES), f32(2, widths[1], LANES)],
+        [scratch(3, widths[0] + 16, LANES)] + solving[0],
+        low,
+        here,
+        high,
     )
     low, high = (turn(here, "gz", 1), turn(here, "gz", -1))
     for_prev, _ = lax.optimization_barrier((for_prev, here))
     next2 = shift(for_prev, "gx", -1)
+    base2, base3 = call(
+        functools.partial(narrow, nx), "narrow", [f32(21, width, LANES) for width in widths[1:]], [], base
+    )
     (here,) = call(
-        functools.partial(solve_next, nz), "solve_next", [f32(2, nx, LANES)], solving, base, low, here, high
+        functools.partial(solve_next, nz, nx),
+        "solve_next",
+        [f32(2, widths[2], LANES)],
+        solving[1],
+        base2,
+        low,
+        here,
+        high,
     )
     low, high = (turn(here, "gz", 1), turn(here, "gz", -1))
 
     bx, bz = right_side.shape[0:2]
     window = (bx + 6, bz + 32, LANES)
-    work = solving + [scratch(5 * (bz // 4 + 8), LANES), scratch(bz + 32, LANES)]
+    work = solving[2] + [scratch(5 * (bz // 4 + 8), LANES), scratch(bz + 32, LANES)]
     work += [scratch(bx // 4 + 8, bz // 4 + 32, LANES), scratch(bx // 2 + 8, bz // 2 + 48, LANES)]
     work += [scratch(*window)] * 3
     (result,) = call(
-        functools.partial(finish, cells), "finish", [f32(*right_side.shape)], work, base, low, here, high,
+        functools.partial(finish, cells), "finish", [f32(*right_side.shape)], work, base3, low, here, high,
         prev2, next2, *kept2, *kept1, *kept0,
     )
     return result

time: 102 us -> 101 us (level)
  waiting for transfers between devices: 20.9 us -> 19.8 us
    ppermute x10, waiting for transfers between devices: 9.54 us -> 8.37 us  [turn(): lax.ppermute(array, axis, [(i, (i + by) % devices) for i in range(devices)])]
    pallas_call x10 -> x12, Pallas kernels: 9.07 us -> 9.02 us  [call(): pl.pallas_call(kernel, name=name, out_shape=outs, in_specs=[vmem] * len(a...]
where the time goes in v7:
time: 101 us
  starting transfers between devices  48.9 us (48%)
  blocking collectives  22 us (22%)
  waiting for transfers between devices  19.8 us (20%)
  Pallas kernels  9.02 us (9%)
  local copies, waits for them, and re-layouts  1.03 us (1%)
    ppermute x8, starting transfers between devices, shift(): lax.ppermute(array, axis, [(i, i + by) for i in range(devices) if 0 <= i...  38.3 us
    all_to_all x1, blocking collectives, on_device(): here = lax.all_to_all(row3, 'gx', 0, 0, tiled=True).reshape(2 * nx, LANES)  22 us
    ppermute x8, waiting for transfers between devices, shift(): lax.ppermute(array, axis, [(i, i + by) for i in range(devices) if 0 <= i...  11.4 us
    ppermute x10, starting transfers between devices, turn(): lax.ppermute(array, axis, [(i, (i + by) % devices) for i in range(devices)])  10.6 us
    pallas_call x12, Pallas kernels, call(): pl.pallas_call(kernel, name=name, out_shape=outs, in_specs=[vmem] * len(a...  9.02 us
    ppermute x10, waiting for transfers between devices, turn(): lax.ppermute(array, axis, [(i, (i + by) % devices) for i in range(devices)])  8.37 us
  transfers between devices with their start and end apart: 18, of which 10 were waited for; matrix products, arithmetic and copies ran while one was open for 0% of the time, Pallas kernels for 4%

profile of v7, /device:TPU:6, one launch (start us, length us, event | category | flops | bytes accessed | tf_op | source)
XLA Modules:
  0.0 101.0 jit_solution(15273042678221923930)
XLA Ops:
  0.0 0.9 fusion
  1.1 4.0 %collective-permute-start = (f32[5,64,128]{2,1,0:T(8,128)S(1)}, f32[5,64,128]{2,1,0:T(8,128)S(1)}, u32[]{:S(2)}, u32[]{:S(2)}) collective-permute-start(f32[5,64,128]{2,1,0:T(8,128)S(1)} %pad_maximum_fusion), channel_id=1, source_target_pairs={{0,8},{8,16},{16,24},{24,32},{32,40},{40,48},{48,56},{56,64},{64,7... | collective-permute-start | bytes 491528 | tf_op jit(solution)/shard_map/ppermute | solution.py:629
  5.0 9.8 %collective-permute-start.1 = (f32[5,64,128]{2,1,0:T(8,128)S(1)}, f32[5,64,128]{2,1,0:T(8,128)S(1)}, u32[]{:S(2)}, u32[]{:S(2)}) collective-permute-start(f32[5,64,128]{2,1,0:T(8,128)S(1)} %pad_maximum_fusion.1), channel_id=1, source_target_pairs={{8,0},{16,8},{24,16},{32,24},{40,32},{48,40},{56,48},{64,56},{72,6... | collective-permute-start | bytes 491528 | tf_op jit(solution)/shard_map/ppermute | solution.py:629
  14.8 2.2 %collective-permute-done.low = f32[5,64,128]{2,1,0:T(8,128)S(1)} collective-permute-done((f32[5,64,128]{2,1,0:T(8,128)S(1)}, f32[5,64,128]{2,1,0:T(8,128)S(1)}, u32[]{:S(2)}, u32[]{:S(2)}) %collective-permute-start) | collective-permute-done | bytes 163872 | tf_op jit(solution)/shard_map/ppermute | solution.py:629
  17.1 1.2 %collective-permute-done.1.high = f32[5,64,128]{2,1,0:T(8,128)S(1)} collective-permute-done((f32[5,64,128]{2,1,0:T(8,128)S(1)}, f32[5,64,128]{2,1,0:T(8,128)S(1)}, u32[]{:S(2)}, u32[]{:S(2)}) %collective-permute-start.1) | collective-permute-done | bytes 163872 | tf_op jit(solution)/shard_map/ppermute | solution.py:629
  18.3 2.9 %collective-permute-start.3 = (f32[80,128]{1,0:T(8,128)S(1)}, f32[80,128]{1,0:T(8,128)S(1)}, u32[]{:S(2)}, u32[]{:S(2)}) collective-permute-start(f32[80,128]{1,0:T(8,128)S(1)} %get-tuple-element.73), channel_id=1, source_target_pairs={{0,7},{1,0},{2,1},{3,2},{4,3},{5,4},{6,5},{7,6},{8,15},{9,8},{10,9... | collective-permute-start | bytes 122888 | tf_op jit(solution)/shard_map/ppermute | solution.py:634
  21.3 1.5 %inner_0.1 = (f32[14,96,128]{2,1,0:T(8,128)S(1)}, f32[14,96,128]{2,1,0:T(8,128)S(1)}, f32[14,96,128]{2,1,0:T(8,128)S(1)}, f32[14,96,128]{2,1,0:T(8,128)S(1)}, f3...) custom-call(f32[8,64,128]{2,1,0:T(8,128)S(1)} %copy-done.1, ...), custom_call_target="tpu_custom_call" | custom-call | tf_op jit(solution)/shard_map/inner_0/pallas_call | solution.py:615
  22.9 0.6 outer_0.1
  23.6 1.9 %collective-permute-start.4 = (f32[4,32,128]{2,1,0:T(8,128)S(1)}, f32[4,32,128]{2,1,0:T(8,128)S(1)}, u32[]{:S(2)}, u32[]{:S(2)}) collective-permute-start(f32[4,32,128]{2,1,0:T(8,128)S(1)} %get-tuple-element.86.to_next), channel_id=1, source_target_pairs={{0,8},{8,16},{16,24},{24,32},{32,40},{40,48},{48,56},{56,64},{64,7... | collective-permute-start | bytes 196616 | tf_op jit(solution)/shard_map/ppermute | solution.py:629
  25.5 6.5 %collective-permute-start.5 = (f32[4,32,128]{2,1,0:T(8,128)S(1)}, f32[4,32,128]{2,1,0:T(8,128)S(1)}, u32[]{:S(2)}, u32[]{:S(2)}) collective-permute-start(f32[4,32,128]{2,1,0:T(8,128)S(1)} %get-tuple-element.87.to_prev), channel_id=1, source_target_pairs={{8,0},{16,8},{24,16},{32,24},{40,32},{48,40},{56,48},{64,56},{72,6... | collective-permute-start | bytes 196616 | tf_op jit(solution)/shard_map/ppermute | solution.py:629
  32.0 0.8 collective-permute-done.4.low
  32.8 1.2 %collective-permute-done.5.high = f32[4,32,128]{2,1,0:T(8,128)S(1)} collective-permute-done((f32[4,32,128]{2,1,0:T(8,128)S(1)}, f32[4,32,128]{2,1,0:T(8,128)S(1)}, u32[]{:S(2)}, u32[]{:S(2)}) %collective-permute-start.5) | collective-permute-done | bytes 65568 | tf_op jit(solution)/shard_map/ppermute | solution.py:629
  34.0 2.9 %collective-permute-start.7 = (f32[160,128]{1,0:T(8,128)S(1)}, f32[160,128]{1,0:T(8,128)S(1)}, u32[]{:S(2)}, u32[]{:S(2)}) collective-permute-start(f32[160,128]{1,0:T(8,128)S(1)} %get-tuple-element.89), channel_id=1, source_target_pairs={{0,7},{1,0},{2,1},{3,2},{4,3},{5,4},{6,5},{7,6},{8,15},{9,8},{10,9... | collective-permute-start | bytes 245768 | tf_op jit(solution)/shard_map/ppermute | solution.py:634
  37.0 0.7 inner_1.1
  37.6 1.4 %collective-permute-done.6.z_low = f32[160,128]{1,0:T(8,128)S(1)} collective-permute-done((f32[160,128]{1,0:T(8,128)S(1)}, f32[160,128]{1,0:T(8,128)S(1)}, u32[]{:S(2)}, u32[]{:S(2)}) %collective-permute-start.6) | collective-permute-done | bytes 81952 | tf_op jit(solution)/shard_map/ppermute | solution.py:634
  39.1 0.7 outer_1.1
  39.8 6.5 %collective-permute-start.9 = (f32[2,32,128]{2,1,0:T(8,128)S(1)}, f32[2,32,128]{2,1,0:T(8,128)S(1)}, u32[]{:S(2)}, u32[]{:S(2)}) collective-permute-start(f32[2,32,128]{2,1,0:T(8,128)S(1)} %get-tuple-element.105), channel_id=1, source_target_pairs={{8,0},{16,8},{24,16},{32,24},{40,32},{48,40},{56,48},{64,56},{72,6... | collective-permute-start | bytes 98312 | tf_op jit(solution)/shard_map/ppermute | solution.py:629
  46.3 1.9 %collective-permute-start.8 = (f32[2,32,128]{2,1,0:T(8,128)S(1)}, f32[2,32,128]{2,1,0:T(8,128)S(1)}, u32[]{:S(2)}, u32[]{:S(2)}) collective-permute-start(f32[2,32,128]{2,1,0:T(8,128)S(1)} %get-tuple-element.104.here), channel_id=1, source_target_pairs={{0,8},{8,16},{16,24},{24,32},{32,40},{40,48},{48,56},{56,64},{64,7... | collective-permute-start | bytes 98312 | tf_op jit(solution)/shard_map/ppermute | solution.py:629
  48.2 6.0 %collective-permute-done.8.prev = f32[2,32,128]{2,1,0:T(8,128)S(1)} collective-permute-done((f32[2,32,128]{2,1,0:T(8,128)S(1)}, f32[2,32,128]{2,1,0:T(8,128)S(1)}, u32[]{:S(2)}, u32[]{:S(2)}) %collective-permute-start.8) | collective-permute-done | bytes 32800 | tf_op jit(solution)/shard_map/ppermute | solution.py:629
  54.2 0.8 down_2.1
  55.1 22.0 %all_to_all.5 = f32[64,2,128]{2,1,0:T(2,128)S(1)} all-to-all(f32[64,2,128]{2,1,0:T(2,128)S(1)} %get-tuple-element.107), channel_id=1, replica_groups=mesh['gx'=64,'gz'=8] {'gx'}, dimensions={0} | all-to-all | bytes 131072 | tf_op jit(solution)/shard_map/all_to_all | solution.py:717
  77.1 1.5 %collective-permute-start.11 = (f32[96,128]{1,0:T(8,128)S(1)}, f32[96,128]{1,0:T(8,128)S(1)}, u32[]{:S(2)}, u32[]{:S(2)}) collective-permute-start(f32[96,128]{1,0:T(8,128)S(1)} %window_3.1.here), channel_id=1, source_target_pairs={{0,7},{1,0},{2,1},{3,2},{4,3},{5,4},{6,5},{7,6},{8,15},{9,8},{10,9... | collective-permute-start | bytes 147464 | tf_op jit(solution)/shard_map/ppermute | solution.py:634
  78.6 2.3 %collective-permute-start.16 = (f32[3,32,128]{2,1,0:T(8,128)S(1)}, f32[3,32,128]{2,1,0:T(8,128)S(1)}, u32[]{:S(2)}, u32[]{:S(2)}) collective-permute-start(f32[3,32,128]{2,1,0:T(8,128)S(1)} %get-tuple-element.113), channel_id=1, source_target_pairs={{0,8},{8,16},{16,24},{24,32},{32,40},{40,48},{48,56},{56,64},{64,7... | collective-permute-start | bytes 147464 | tf_op jit(solution)/shard_map/ppermute | solution.py:629
  81.0 2.4 %collective-permute-done.10.low = f32[96,128]{1,0:T(8,128)S(1)} collective-permute-done((f32[96,128]{1,0:T(8,128)S(1)}, f32[96,128]{1,0:T(8,128)S(1)}, u32[]{:S(2)}, u32[]{:S(2)}) %collective-permute-start.10) | collective-permute-done | bytes 49184 | tf_op jit(solution)/shard_map/ppermute | solution.py:634
  83.3 0.9 solve_first.1
  84.2 0.3 collective-permute-start.13
  84.8 5.4 %collective-permute-start.17 = (f32[3,32,128]{2,1,0:T(8,128)S(1)}, f32[3,32,128]{2,1,0:T(8,128)S(1)}, u32[]{:S(2)}, u32[]{:S(2)}) collective-permute-start(f32[3,32,128]{2,1,0:T(8,128)S(1)} %get-tuple-element.115), channel_id=1, source_target_pairs={{8,0},{16,8},{24,16},{32,24},{40,32},{48,40},{56,48},{64,56},{72,6... | collective-permute-start | bytes 147464 | tf_op jit(solution)/shard_map/ppermute | solution.py:629
  90.2 0.9 solve_next.1.here
  91.1 2.7 %collective-permute-start.15 = (f32[2,16,128]{2,1,0:T(8,128)S(1)}, f32[2,16,128]{2,1,0:T(8,128)S(1)}, u32[]{:S(2)}, u32[]{:S(2)}) collective-permute-start(f32[2,16,128]{2,1,0:T(8,128)S(1)} %solve_next.1.here), channel_id=1, source_target_pairs={{0,7},{1,0},{2,1},{3,2},{4,3},{5,4},{6,5},{7,6},{8,15},{9,8},{10,9... | collective-permute-start | bytes 49160 | tf_op jit(solution)/shard_map/ppermute | solution.py:634
  93.8 1.4 %collective-permute-done.15.high = f32[2,16,128]{2,1,0:T(8,128)S(1)} collective-permute-done((f32[2,16,128]{2,1,0:T(8,128)S(1)}, f32[2,16,128]{2,1,0:T(8,128)S(1)}, u32[]{:S(2)}, u32[]{:S(2)}) %collective-permute-start.15) | collective-permute-done | bytes 16416 | tf_op jit(solution)/shard_map/ppermute | solution.py:634
  95.2 2.9 %collective-permute-done.14.low = f32[2,16,128]{2,1,0:T(8,128)S(1)} collective-permute-done((f32[2,16,128]{2,1,0:T(8,128)S(1)}, f32[2,16,128]{2,1,0:T(8,128)S(1)}, u32[]{:S(2)}, u32[]{:S(2)}) %collective-permute-start.14) | collective-permute-done | bytes 16416 | tf_op jit(solution)/shard_map/ppermute | solution.py:634
  98.2 2.8 %finish.1 = f32[8,64,128]{2,1,0:T(8,128)} custom-call(f32[21,16,128]{2,1,0:T(8,128)S(1)} %get-tuple-element.109.base, f32[2,16,128]{2,1,0:T(8,128)S(1)} %collective-permute-done.14.low, f32[2,16,128]{2,1,0:T(8,128)S(1)} %solve_next.1.here, f32[2,16,128]{2,1,0:T(8,128)S(1)} %collective-permute-done.15.high, f32[3,32,128]{2,1,0:T(8,128)S(1)} %collective-permute-done.16.prev2, ...), custom_call_target="tpu_custom_call" | custom-call | tf_op jit(solution)/shard_map/finish/pallas_call | solution.py:615
  (25 shorter events, 0.7 us)
Async XLA Ops:
  0.0 1.0 %copy-start = (f32[8,64,128]{2,1,0:T(8,128)S(1)}, f32[8,64,128]{2,1,0:T(8,128)}, u32[]{:S(2)}) copy-start(f32[8,64,128]{2,1,0:T(8,128)} %cond.3) | copy-start | bytes 786436
  1.0 17.2 %copy-start.1 = (f32[8,64,128]{2,1,0:T(8,128)S(1)}, f32[8,64,128]{2,1,0:T(8,128)}, u32[]{:S(2)}) copy-start(f32[8,64,128]{2,1,0:T(8,128)} %source.3) | copy-start | bytes 786436
  1.1 16.0 %collective-permute-start = (f32[5,64,128]{2,1,0:T(8,128)S(1)}, f32[5,64,128]{2,1,0:T(8,128)S(1)}, u32[]{:S(2)}, u32[]{:S(2)}) collective-permute-start(f32[5,64,128]{2,1,0:T(8,128)S(1)} %pad_maximum_fusion), channel_id=1, source_target_pairs={{0,8},{8,16},{16,24},{24,32},{32,40},{40,48},{48,56},{56,64},{64,7... | collective-permute-start | bytes 491528 | tf_op jit(solution)/shard_map/ppermute | solution.py:629
  5.0 13.2 %collective-permute-start.1 = (f32[5,64,128]{2,1,0:T(8,128)S(1)}, f32[5,64,128]{2,1,0:T(8,128)S(1)}, u32[]{:S(2)}, u32[]{:S(2)}) collective-permute-start(f32[5,64,128]{2,1,0:T(8,128)S(1)} %pad_maximum_fusion.1), channel_id=1, source_target_pairs={{8,0},{16,8},{24,16},{32,24},{40,32},{48,40},{56,48},{64,56},{72,6... | collective-permute-start | bytes 491528 | tf_op jit(solution)/shard_map/ppermute | solution.py:629
  18.3 4.7 %collective-permute-start.2 = (f32[80,128]{1,0:T(8,128)S(1)}, f32[80,128]{1,0:T(8,128)S(1)}, u32[]{:S(2)}, u32[]{:S(2)}) collective-permute-start(f32[80,128]{1,0:T(8,128)S(1)} %get-tuple-element.72), channel_id=1, source_target_pairs={{0,1},{1,2},{2,3},{3,4},{4,5},{5,6},{6,7},{7,0},{8,9},{9,10},{10,1... | collective-permute-start | bytes 122888 | tf_op jit(solution)/shard_map/ppermute | solution.py:634
  18.3 4.6 %collective-permute-start.3 = (f32[80,128]{1,0:T(8,128)S(1)}, f32[80,128]{1,0:T(8,128)S(1)}, u32[]{:S(2)}, u32[]{:S(2)}) collective-permute-start(f32[80,128]{1,0:T(8,128)S(1)} %get-tuple-element.73), channel_id=1, source_target_pairs={{0,7},{1,0},{2,1},{3,2},{4,3},{5,4},{6,5},{7,6},{8,15},{9,8},{10,9... | collective-permute-start | bytes 122888 | tf_op jit(solution)/shard_map/ppermute | solution.py:634
  23.6 9.2 %collective-permute-start.4 = (f32[4,32,128]{2,1,0:T(8,128)S(1)}, f32[4,32,128]{2,1,0:T(8,128)S(1)}, u32[]{:S(2)}, u32[]{:S(2)}) collective-permute-start(f32[4,32,128]{2,1,0:T(8,128)S(1)} %get-tuple-element.86.to_next), channel_id=1, source_target_pairs={{0,8},{8,16},{16,24},{24,32},{32,40},{40,48},{48,56},{56,64},{64,7... | collective-permute-start | bytes 196616 | tf_op jit(solution)/shard_map/ppermute | solution.py:629
  25.5 8.5 %collective-permute-start.5 = (f32[4,32,128]{2,1,0:T(8,128)S(1)}, f32[4,32,128]{2,1,0:T(8,128)S(1)}, u32[]{:S(2)}, u32[]{:S(2)}) collective-permute-start(f32[4,32,128]{2,1,0:T(8,128)S(1)} %get-tuple-element.87.to_prev), channel_id=1, source_target_pairs={{8,0},{16,8},{24,16},{32,24},{40,32},{48,40},{56,48},{64,56},{72,6... | collective-permute-start | bytes 196616 | tf_op jit(solution)/shard_map/ppermute | solution.py:629
  34.0 5.1 %collective-permute-start.6 = (f32[160,128]{1,0:T(8,128)S(1)}, f32[160,128]{1,0:T(8,128)S(1)}, u32[]{:S(2)}, u32[]{:S(2)}) collective-permute-start(f32[160,128]{1,0:T(8,128)S(1)} %get-tuple-element.88), channel_id=1, source_target_pairs={{0,1},{1,2},{2,3},{3,4},{4,5},{5,6},{6,7},{7,0},{8,9},{9,10},{10,1... | collective-permute-start | bytes 245768 | tf_op jit(solution)/shard_map/ppermute | solution.py:634
  34.0 5.1 %collective-permute-start.7 = (f32[160,128]{1,0:T(8,128)S(1)}, f32[160,128]{1,0:T(8,128)S(1)}, u32[]{:S(2)}, u32[]{:S(2)}) collective-permute-start(f32[160,128]{1,0:T(8,128)S(1)} %get-tuple-element.89), channel_id=1, source_target_pairs={{0,7},{1,0},{2,1},{3,2},{4,3},{5,4},{6,5},{7,6},{8,15},{9,8},{10,9... | collective-permute-start | bytes 245768 | tf_op jit(solution)/shard_map/ppermute | solution.py:634
  39.8 8.4 %collective-permute-start.9 = (f32[2,32,128]{2,1,0:T(8,128)S(1)}, f32[2,32,128]{2,1,0:T(8,128)S(1)}, u32[]{:S(2)}, u32[]{:S(2)}) collective-permute-start(f32[2,32,128]{2,1,0:T(8,128)S(1)} %get-tuple-element.105), channel_id=1, source_target_pairs={{8,0},{16,8},{24,16},{32,24},{40,32},{48,40},{56,48},{64,56},{72,6... | collective-permute-start | bytes 98312 | tf_op jit(solution)/shard_map/ppermute | solution.py:629
  46.3 7.9 %collective-permute-start.8 = (f32[2,32,128]{2,1,0:T(8,128)S(1)}, f32[2,32,128]{2,1,0:T(8,128)S(1)}, u32[]{:S(2)}, u32[]{:S(2)}) collective-permute-start(f32[2,32,128]{2,1,0:T(8,128)S(1)} %get-tuple-element.104.here), channel_id=1, source_target_pairs={{0,8},{8,16},{16,24},{24,32},{32,40},{40,48},{48,56},{56,64},{64,7... | collective-permute-start | bytes 98312 | tf_op jit(solution)/shard_map/ppermute | solution.py:629
  77.1 3.9 %collective-permute-start.11 = (f32[96,128]{1,0:T(8,128)S(1)}, f32[96,128]{1,0:T(8,128)S(1)}, u32[]{:S(2)}, u32[]{:S(2)}) collective-permute-start(f32[96,128]{1,0:T(8,128)S(1)} %window_3.1.here), channel_id=1, source_target_pairs={{0,7},{1,0},{2,1},{3,2},{4,3},{5,4},{6,5},{7,6},{8,15},{9,8},{10,9... | collective-permute-start | bytes 147464 | tf_op jit(solution)/shard_map/ppermute | solution.py:634
  78.6 4.7 %collective-permute-start.10 = (f32[96,128]{1,0:T(8,128)S(1)}, f32[96,128]{1,0:T(8,128)S(1)}, u32[]{:S(2)}, u32[]{:S(2)}) collective-permute-start(f32[96,128]{1,0:T(8,128)S(1)} %window_3.1.here), channel_id=1, source_target_pairs={{0,1},{1,2},{2,3},{3,4},{4,5},{5,6},{6,7},{7,0},{8,9},{9,10},{10,1... | collective-permute-start | bytes 147464 | tf_op jit(solution)/shard_map/ppermute | solution.py:634
  78.6 15.2 %collective-permute-start.16 = (f32[3,32,128]{2,1,0:T(8,128)S(1)}, f32[3,32,128]{2,1,0:T(8,128)S(1)}, u32[]{:S(2)}, u32[]{:S(2)}) collective-permute-start(f32[3,32,128]{2,1,0:T(8,128)S(1)} %get-tuple-element.113), channel_id=1, source_target_pairs={{0,8},{8,16},{16,24},{24,32},{32,40},{40,48},{48,56},{56,64},{64,7... | collective-permute-start | bytes 147464 | tf_op jit(solution)/shard_map/ppermute | solution.py:629
  84.2 6.0 %collective-permute-start.13 = (f32[2,32,128]{2,1,0:T(8,128)S(1)}, f32[2,32,128]{2,1,0:T(8,128)S(1)}, u32[]{:S(2)}, u32[]{:S(2)}) collective-permute-start(f32[2,32,128]{2,1,0:T(8,128)S(1)} %get-tuple-element.111.here), channel_id=1, source_target_pairs={{0,7},{1,0},{2,1},{3,2},{4,3},{5,4},{6,5},{7,6},{8,15},{9,8},{10,9... | collective-permute-start | bytes 98312 | tf_op jit(solution)/shard_map/ppermute | solution.py:634
  84.6 5.7 %collective-permute-start.12 = (f32[2,32,128]{2,1,0:T(8,128)S(1)}, f32[2,32,128]{2,1,0:T(8,128)S(1)}, u32[]{:S(2)}, u32[]{:S(2)}) collective-permute-start(f32[2,32,128]{2,1,0:T(8,128)S(1)} %get-tuple-element.111.here), channel_id=1, source_target_pairs={{0,1},{1,2},{2,3},{3,4},{4,5},{5,6},{6,7},{7,0},{8,9},{9,10},{10,1... | collective-permute-start | bytes 98312 | tf_op jit(solution)/shard_map/ppermute | solution.py:634
  84.8 13.4 %collective-permute-start.17 = (f32[3,32,128]{2,1,0:T(8,128)S(1)}, f32[3,32,128]{2,1,0:T(8,128)S(1)}, u32[]{:S(2)}, u32[]{:S(2)}) collective-permute-start(f32[3,32,128]{2,1,0:T(8,128)S(1)} %get-tuple-element.115), channel_id=1, source_target_pairs={{8,0},{16,8},{24,16},{32,24},{40,32},{48,40},{56,48},{64,56},{72,6... | collective-permute-start | bytes 147464 | tf_op jit(solution)/shard_map/ppermute | solution.py:629
  91.1 4.1 %collective-permute-start.15 = (f32[2,16,128]{2,1,0:T(8,128)S(1)}, f32[2,16,128]{2,1,0:T(8,128)S(1)}, u32[]{:S(2)}, u32[]{:S(2)}) collective-permute-start(f32[2,16,128]{2,1,0:T(8,128)S(1)} %solve_next.1.here), channel_id=1, source_target_pairs={{0,7},{1,0},{2,1},{3,2},{4,3},{5,4},{6,5},{7,6},{8,15},{9,8},{10,9... | collective-permute-start | bytes 49160 | tf_op jit(solution)/shard_map/ppermute | solution.py:634
  93.8 4.4 %collective-permute-start.14 = (f32[2,16,128]{2,1,0:T(8,128)S(1)}, f32[2,16,128]{2,1,0:T(8,128)S(1)}, u32[]{:S(2)}, u32[]{:S(2)}) collective-permute-start(f32[2,16,128]{2,1,0:T(8,128)S(1)} %solve_next.1.here), channel_id=1, source_target_pairs={{0,1},{1,2},{2,3},{3,4},{4,5},{5,6},{6,7},{7,0},{8,9},{9,10},{10,1... | collective-permute-start | bytes 49160 | tf_op jit(solution)/shard_map/ppermute | solution.py:634

commit v8 on v7

--- a/solution.py
+++ b/solution.py
@@ -515,7 +515,7 @@
 def finish(cells, base, low, here, high, prev2, next2, *refs):
     gx, gz = (lax.axis_index("gx"), lax.axis_index("gz"))
     (s2, g2, *coefs2), (s1, g1, *coefs1), (s0, g0, *coefs0) = (refs[0:8], refs[8:16], refs[16:24])
-    out, state, update3, coarse2, temp, start2, start1, start0, middle, update = refs[24:]
+    out, state, update3, coarse2, temp, start2, start1, start0, middle, update, result, sent = refs[24:]
     bz0 = out.shape[1]
     bz1, bz2 = (bz0 // 2, bz0 // 4)
     has_low, has_high = inside_z(gz, cells[0][1] // bz0)
@@ -595,10 +595,15 @@
     level.up(s1, start1, middle, update, to_level_0, range(3, 9), row, count, base1 - 2, bz1 + 4)
     level = Level(0, gx, gz, (bx0, bz0), cells[0], 3, (None, *coefs0))
 
+    copies = [pltpu.make_async_copy(result.at[p], out.at[p], sent.at[p]) for p in range(bx0)]
+
     def to_out(p, value):
-        out[p - 3, :, :] = value
+        result[p - 3, :, :] = value
+        copies[p - 3].start()
 
     level.up(s0, start0, middle, update, to_out, range(3, 11), ROW - 4, bz0 + 8, ROW, bz0)
+    for copy in copies:
+        copy.wait()
 
 
 def f32(*shape):
@@ -609,7 +614,7 @@
     return pltpu.VMEM(shape, jnp.float32)
 
 
-def call(kernel, name, outs, scratches, *args, aliases={}):
+def call(kernel, name, outs, scratches, *args, aliases={}, space=pltpu.VMEM, semaphores=()):
     limit = 4 * 2**20 + sum(4 * math.prod(ref.shape) for ref in [*scratches, *outs, *args])
     vmem = pl.BlockSpec(memory_space=pltpu.VMEM)
     return pl.pallas_call(
@@ -617,8 +622,8 @@
         name=name,
         out_shape=outs,
         in_specs=[vmem] * len(args),
-        out_specs=[vmem] * len(outs),
-        scratch_shapes=scratches,
+        out_specs=[pl.BlockSpec(memory_space=space)] * len(outs),
+        scratch_shapes=[*scratches, *semaphores],
         input_output_aliases=aliases,
         compiler_params=pltpu.CompilerParams(vmem_limit_bytes=limit),
     )(*args)
@@ -752,10 +757,10 @@
     window = (bx + 6, bz + 32, LANES)
     work = solving[2] + [scratch(5 * (bz // 4 + 8), LANES), scratch(bz + 32, LANES)]
     work += [scratch(bx // 4 + 8, bz // 4 + 32, LANES), scratch(bx // 2 + 8, bz // 2 + 48, LANES)]
-    work += [scratch(*window)] * 3
+    work += [scratch(*window)] * 3 + [scratch(*right_side.shape)]
     (result,) = call(
         functools.partial(finish, cells), "finish", [f32(*right_side.shape)], work, base3, low, here, high,
-        prev2, next2, *kept2, *kept1, *kept0,
+        prev2, next2, *kept2, *kept1, *kept0, space=pl.ANY, semaphores=[pltpu.SemaphoreType.DMA((bx,))],
     )
     return result
 

time: 101 us -> 101 us (level)
  no operation moved by 1% of the time
where the time goes in v8:
time: 101 us
  starting transfers between devices  48.9 us (48%)
  blocking collectives  22 us (22%)
  waiting for transfers between devices  19.8 us (20%)
  Pallas kernels  8.95 us (9%)
  local copies, waits for them, and re-layouts  1.03 us (1%)
    ppermute x8, starting transfers between devices, shift(): lax.ppermute(array, axis, [(i, i + by) for i in range(devices) if 0 <= i...  38.3 us
    all_to_all x1, blocking collectives, on_device(): here = lax.all_to_all(row3, 'gx', 0, 0, tiled=True).reshape(2 * nx, LANES)  22 us
    ppermute x8, waiting for transfers between devices, shift(): lax.ppermute(array, axis, [(i, i + by) for i in range(devices) if 0 <= i...  11.4 us
    ppermute x10, starting transfers between devices, turn(): lax.ppermute(array, axis, [(i, (i + by) % devices) for i in range(devices)])  10.6 us
    pallas_call x12, Pallas kernels, call(): pl.pallas_call(kernel, name=name, out_shape=outs, in_specs=[vmem] * len(a...  8.95 us
    ppermute x10, waiting for transfers between devices, turn(): lax.ppermute(array, axis, [(i, (i + by) % devices) for i in range(devices)])  8.4 us
  transfers between devices with their start and end apart: 18, of which 10 were waited for; matrix products, arithmetic and copies ran while one was open for 0% of the time, Pallas kernels for 4%

profile of v8, /device:TPU:6, one launch (start us, length us, event | category | flops | bytes accessed | tf_op | source)
XLA Modules:
  0.0 101.0 jit_solution(3985774748962297894)
XLA Ops:
  0.0 0.9 fusion
  1.1 4.0 %collective-permute-start = (f32[5,64,128]{2,1,0:T(8,128)S(1)}, f32[5,64,128]{2,1,0:T(8,128)S(1)}, u32[]{:S(2)}, u32[]{:S(2)}) collective-permute-start(f32[5,64,128]{2,1,0:T(8,128)S(1)} %pad_maximum_fusion), channel_id=1, source_target_pairs={{0,8},{8,16},{16,24},{24,32},{32,40},{40,48},{48,56},{56,64},{64,7... | collective-permute-start | bytes 491528 | tf_op jit(solution)/shard_map/ppermute | solution.py:634
  5.0 9.8 %collective-permute-start.1 = (f32[5,64,128]{2,1,0:T(8,128)S(1)}, f32[5,64,128]{2,1,0:T(8,128)S(1)}, u32[]{:S(2)}, u32[]{:S(2)}) collective-permute-start(f32[5,64,128]{2,1,0:T(8,128)S(1)} %pad_maximum_fusion.1), channel_id=1, source_target_pairs={{8,0},{16,8},{24,16},{32,24},{40,32},{48,40},{56,48},{64,56},{72,6... | collective-permute-start | bytes 491528 | tf_op jit(solution)/shard_map/ppermute | solution.py:634
  14.8 2.2 %collective-permute-done.low = f32[5,64,128]{2,1,0:T(8,128)S(1)} collective-permute-done((f32[5,64,128]{2,1,0:T(8,128)S(1)}, f32[5,64,128]{2,1,0:T(8,128)S(1)}, u32[]{:S(2)}, u32[]{:S(2)}) %collective-permute-start) | collective-permute-done | bytes 163872 | tf_op jit(solution)/shard_map/ppermute | solution.py:634
  17.1 1.2 %collective-permute-done.1.high = f32[5,64,128]{2,1,0:T(8,128)S(1)} collective-permute-done((f32[5,64,128]{2,1,0:T(8,128)S(1)}, f32[5,64,128]{2,1,0:T(8,128)S(1)}, u32[]{:S(2)}, u32[]{:S(2)}) %collective-permute-start.1) | collective-permute-done | bytes 163872 | tf_op jit(solution)/shard_map/ppermute | solution.py:634
  18.3 2.9 %collective-permute-start.3 = (f32[80,128]{1,0:T(8,128)S(1)}, f32[80,128]{1,0:T(8,128)S(1)}, u32[]{:S(2)}, u32[]{:S(2)}) collective-permute-start(f32[80,128]{1,0:T(8,128)S(1)} %get-tuple-element.73), channel_id=1, source_target_pairs={{0,7},{1,0},{2,1},{3,2},{4,3},{5,4},{6,5},{7,6},{8,15},{9,8},{10,9... | collective-permute-start | bytes 122888 | tf_op jit(solution)/shard_map/ppermute | solution.py:639
  21.3 1.5 %inner_0.1 = (f32[14,96,128]{2,1,0:T(8,128)S(1)}, f32[14,96,128]{2,1,0:T(8,128)S(1)}, f32[14,96,128]{2,1,0:T(8,128)S(1)}, f32[14,96,128]{2,1,0:T(8,128)S(1)}, f3...) custom-call(f32[8,64,128]{2,1,0:T(8,128)S(1)} %copy-done.1, ...), custom_call_target="tpu_custom_call" | custom-call | tf_op jit(solution)/shard_map/inner_0/pallas_call | solution.py:620
  22.9 0.6 outer_0.1
  23.6 1.9 %collective-permute-start.4 = (f32[4,32,128]{2,1,0:T(8,128)S(1)}, f32[4,32,128]{2,1,0:T(8,128)S(1)}, u32[]{:S(2)}, u32[]{:S(2)}) collective-permute-start(f32[4,32,128]{2,1,0:T(8,128)S(1)} %get-tuple-element.86.to_next), channel_id=1, source_target_pairs={{0,8},{8,16},{16,24},{24,32},{32,40},{40,48},{48,56},{56,64},{64,7... | collective-permute-start | bytes 196616 | tf_op jit(solution)/shard_map/ppermute | solution.py:634
  25.5 6.5 %collective-permute-start.5 = (f32[4,32,128]{2,1,0:T(8,128)S(1)}, f32[4,32,128]{2,1,0:T(8,128)S(1)}, u32[]{:S(2)}, u32[]{:S(2)}) collective-permute-start(f32[4,32,128]{2,1,0:T(8,128)S(1)} %get-tuple-element.87.to_prev), channel_id=1, source_target_pairs={{8,0},{16,8},{24,16},{32,24},{40,32},{48,40},{56,48},{64,56},{72,6... | collective-permute-start | bytes 196616 | tf_op jit(solution)/shard_map/ppermute | solution.py:634
  32.0 0.8 collective-permute-done.4.low
  32.8 1.2 %collective-permute-done.5.high = f32[4,32,128]{2,1,0:T(8,128)S(1)} collective-permute-done((f32[4,32,128]{2,1,0:T(8,128)S(1)}, f32[4,32,128]{2,1,0:T(8,128)S(1)}, u32[]{:S(2)}, u32[]{:S(2)}) %collective-permute-start.5) | collective-permute-done | bytes 65568 | tf_op jit(solution)/shard_map/ppermute | solution.py:634
  34.0 2.9 %collective-permute-start.7 = (f32[160,128]{1,0:T(8,128)S(1)}, f32[160,128]{1,0:T(8,128)S(1)}, u32[]{:S(2)}, u32[]{:S(2)}) collective-permute-start(f32[160,128]{1,0:T(8,128)S(1)} %get-tuple-element.89), channel_id=1, source_target_pairs={{0,7},{1,0},{2,1},{3,2},{4,3},{5,4},{6,5},{7,6},{8,15},{9,8},{10,9... | collective-permute-start | bytes 245768 | tf_op jit(solution)/shard_map/ppermute | solution.py:639
  37.0 0.7 inner_1.1
  37.6 1.4 %collective-permute-done.6.z_low = f32[160,128]{1,0:T(8,128)S(1)} collective-permute-done((f32[160,128]{1,0:T(8,128)S(1)}, f32[160,128]{1,0:T(8,128)S(1)}, u32[]{:S(2)}, u32[]{:S(2)}) %collective-permute-start.6) | collective-permute-done | bytes 81952 | tf_op jit(solution)/shard_map/ppermute | solution.py:639
  39.1 0.7 outer_1.1
  39.8 6.5 %collective-permute-start.9 = (f32[2,32,128]{2,1,0:T(8,128)S(1)}, f32[2,32,128]{2,1,0:T(8,128)S(1)}, u32[]{:S(2)}, u32[]{:S(2)}) collective-permute-start(f32[2,32,128]{2,1,0:T(8,128)S(1)} %get-tuple-element.105), channel_id=1, source_target_pairs={{8,0},{16,8},{24,16},{32,24},{40,32},{48,40},{56,48},{64,56},{72,6... | collective-permute-start | bytes 98312 | tf_op jit(solution)/shard_map/ppermute | solution.py:634
  46.3 1.9 %collective-permute-start.8 = (f32[2,32,128]{2,1,0:T(8,128)S(1)}, f32[2,32,128]{2,1,0:T(8,128)S(1)}, u32[]{:S(2)}, u32[]{:S(2)}) collective-permute-start(f32[2,32,128]{2,1,0:T(8,128)S(1)} %get-tuple-element.104.here), channel_id=1, source_target_pairs={{0,8},{8,16},{16,24},{24,32},{32,40},{40,48},{48,56},{56,64},{64,7... | collective-permute-start | bytes 98312 | tf_op jit(solution)/shard_map/ppermute | solution.py:634
  48.2 6.0 %collective-permute-done.8.prev = f32[2,32,128]{2,1,0:T(8,128)S(1)} collective-permute-done((f32[2,32,128]{2,1,0:T(8,128)S(1)}, f32[2,32,128]{2,1,0:T(8,128)S(1)}, u32[]{:S(2)}, u32[]{:S(2)}) %collective-permute-start.8) | collective-permute-done | bytes 32800 | tf_op jit(solution)/shard_map/ppermute | solution.py:634
  54.2 0.8 down_2.1
  55.1 22.0 %all_to_all.5 = f32[64,2,128]{2,1,0:T(2,128)S(1)} all-to-all(f32[64,2,128]{2,1,0:T(2,128)S(1)} %get-tuple-element.107), channel_id=1, replica_groups=mesh['gx'=64,'gz'=8] {'gx'}, dimensions={0} | all-to-all | bytes 131072 | tf_op jit(solution)/shard_map/all_to_all | solution.py:722
  77.1 1.5 %collective-permute-start.11 = (f32[96,128]{1,0:T(8,128)S(1)}, f32[96,128]{1,0:T(8,128)S(1)}, u32[]{:S(2)}, u32[]{:S(2)}) collective-permute-start(f32[96,128]{1,0:T(8,128)S(1)} %window_3.1.here), channel_id=1, source_target_pairs={{0,7},{1,0},{2,1},{3,2},{4,3},{5,4},{6,5},{7,6},{8,15},{9,8},{10,9... | collective-permute-start | bytes 147464 | tf_op jit(solution)/shard_map/ppermute | solution.py:639
  78.6 2.3 %collective-permute-start.16 = (f32[3,32,128]{2,1,0:T(8,128)S(1)}, f32[3,32,128]{2,1,0:T(8,128)S(1)}, u32[]{:S(2)}, u32[]{:S(2)}) collective-permute-start(f32[3,32,128]{2,1,0:T(8,128)S(1)} %get-tuple-element.113), channel_id=1, source_target_pairs={{0,8},{8,16},{16,24},{24,32},{32,40},{40,48},{48,56},{56,64},{64,7... | collective-permute-start | bytes 147464 | tf_op jit(solution)/shard_map/ppermute | solution.py:634
  80.9 2.4 %collective-permute-done.10.low = f32[96,128]{1,0:T(8,128)S(1)} collective-permute-done((f32[96,128]{1,0:T(8,128)S(1)}, f32[96,128]{1,0:T(8,128)S(1)}, u32[]{:S(2)}, u32[]{:S(2)}) %collective-permute-start.10) | collective-permute-done | bytes 49184 | tf_op jit(solution)/shard_map/ppermute | solution.py:639
  83.3 0.9 solve_first.1
  84.2 0.3 collective-permute-start.13
  84.7 5.4 %collective-permute-start.17 = (f32[3,32,128]{2,1,0:T(8,128)S(1)}, f32[3,32,128]{2,1,0:T(8,128)S(1)}, u32[]{:S(2)}, u32[]{:S(2)}) collective-permute-start(f32[3,32,128]{2,1,0:T(8,128)S(1)} %get-tuple-element.115), channel_id=1, source_target_pairs={{8,0},{16,8},{24,16},{32,24},{40,32},{48,40},{56,48},{64,56},{72,6... | collective-permute-start | bytes 147464 | tf_op jit(solution)/shard_map/ppermute | solution.py:634
  90.2 0.9 solve_next.1.here
  91.1 2.7 %collective-permute-start.15 = (f32[2,16,128]{2,1,0:T(8,128)S(1)}, f32[2,16,128]{2,1,0:T(8,128)S(1)}, u32[]{:S(2)}, u32[]{:S(2)}) collective-permute-start(f32[2,16,128]{2,1,0:T(8,128)S(1)} %solve_next.1.here), channel_id=1, source_target_pairs={{0,7},{1,0},{2,1},{3,2},{4,3},{5,4},{6,5},{7,6},{8,15},{9,8},{10,9... | collective-permute-start | bytes 49160 | tf_op jit(solution)/shard_map/ppermute | solution.py:639
  93.8 1.4 %collective-permute-done.15.high = f32[2,16,128]{2,1,0:T(8,128)S(1)} collective-permute-done((f32[2,16,128]{2,1,0:T(8,128)S(1)}, f32[2,16,128]{2,1,0:T(8,128)S(1)}, u32[]{:S(2)}, u32[]{:S(2)}) %collective-permute-start.15) | collective-permute-done | bytes 16416 | tf_op jit(solution)/shard_map/ppermute | solution.py:639
  95.2 2.9 %collective-permute-done.14.low = f32[2,16,128]{2,1,0:T(8,128)S(1)} collective-permute-done((f32[2,16,128]{2,1,0:T(8,128)S(1)}, f32[2,16,128]{2,1,0:T(8,128)S(1)}, u32[]{:S(2)}, u32[]{:S(2)}) %collective-permute-start.14) | collective-permute-done | bytes 16416 | tf_op jit(solution)/shard_map/ppermute | solution.py:639
  98.2 2.8 %finish.1 = f32[8,64,128]{2,1,0:T(8,128)} custom-call(f32[21,16,128]{2,1,0:T(8,128)S(1)} %get-tuple-element.109.base, f32[2,16,128]{2,1,0:T(8,128)S(1)} %collective-permute-done.14.low, f32[2,16,128]{2,1,0:T(8,128)S(1)} %solve_next.1.here, f32[2,16,128]{2,1,0:T(8,128)S(1)} %collective-permute-done.15.high, f32[3,32,128]{2,1,0:T(8,128)S(1)} %collective-permute-done.16.prev2, ...), custom_call_target="tpu_custom_call" | custom-call | tf_op jit(solution)/shard_map/finish/pallas_call | solution.py:620
  (25 shorter events, 0.7 us)
Async XLA Ops:
  0.0 1.0 %copy-start = (f32[8,64,128]{2,1,0:T(8,128)S(1)}, f32[8,64,128]{2,1,0:T(8,128)}, u32[]{:S(2)}) copy-start(f32[8,64,128]{2,1,0:T(8,128)} %cond.3) | copy-start | bytes 786436
  1.0 17.2 %copy-start.1 = (f32[8,64,128]{2,1,0:T(8,128)S(1)}, f32[8,64,128]{2,1,0:T(8,128)}, u32[]{:S(2)}) copy-start(f32[8,64,128]{2,1,0:T(8,128)} %source.3) | copy-start | bytes 786436
  1.1 16.0 %collective-permute-start = (f32[5,64,128]{2,1,0:T(8,128)S(1)}, f32[5,64,128]{2,1,0:T(8,128)S(1)}, u32[]{:S(2)}, u32[]{:S(2)}) collective-permute-start(f32[5,64,128]{2,1,0:T(8,128)S(1)} %pad_maximum_fusion), channel_id=1, source_target_pairs={{0,8},{8,16},{16,24},{24,32},{32,40},{40,48},{48,56},{56,64},{64,7... | collective-permute-start | bytes 491528 | tf_op jit(solution)/shard_map/ppermute | solution.py:634
  5.0 13.2 %collective-permute-start.1 = (f32[5,64,128]{2,1,0:T(8,128)S(1)}, f32[5,64,128]{2,1,0:T(8,128)S(1)}, u32[]{:S(2)}, u32[]{:S(2)}) collective-permute-start(f32[5,64,128]{2,1,0:T(8,128)S(1)} %pad_maximum_fusion.1), channel_id=1, source_target_pairs={{8,0},{16,8},{24,16},{32,24},{40,32},{48,40},{56,48},{64,56},{72,6... | collective-permute-start | bytes 491528 | tf_op jit(solution)/shard_map/ppermute | solution.py:634
  18.3 4.7 %collective-permute-start.2 = (f32[80,128]{1,0:T(8,128)S(1)}, f32[80,128]{1,0:T(8,128)S(1)}, u32[]{:S(2)}, u32[]{:S(2)}) collective-permute-start(f32[80,128]{1,0:T(8,128)S(1)} %get-tuple-element.72), channel_id=1, source_target_pairs={{0,1},{1,2},{2,3},{3,4},{4,5},{5,6},{6,7},{7,0},{8,9},{9,10},{10,1... | collective-permute-start | bytes 122888 | tf_op jit(solution)/shard_map/ppermute | solution.py:639
  18.3 4.6 %collective-permute-start.3 = (f32[80,128]{1,0:T(8,128)S(1)}, f32[80,128]{1,0:T(8,128)S(1)}, u32[]{:S(2)}, u32[]{:S(2)}) collective-permute-start(f32[80,128]{1,0:T(8,128)S(1)} %get-tuple-element.73), channel_id=1, source_target_pairs={{0,7},{1,0},{2,1},{3,2},{4,3},{5,4},{6,5},{7,6},{8,15},{9,8},{10,9... | collective-permute-start | bytes 122888 | tf_op jit(solution)/shard_map/ppermute | solution.py:639
  23.6 9.2 %collective-permute-start.4 = (f32[4,32,128]{2,1,0:T(8,128)S(1)}, f32[4,32,128]{2,1,0:T(8,128)S(1)}, u32[]{:S(2)}, u32[]{:S(2)}) collective-permute-start(f32[4,32,128]{2,1,0:T(8,128)S(1)} %get-tuple-element.86.to_next), channel_id=1, source_target_pairs={{0,8},{8,16},{16,24},{24,32},{32,40},{40,48},{48,56},{56,64},{64,7... | collective-permute-start | bytes 196616 | tf_op jit(solution)/shard_map/ppermute | solution.py:634
  25.5 8.5 %collective-permute-start.5 = (f32[4,32,128]{2,1,0:T(8,128)S(1)}, f32[4,32,128]{2,1,0:T(8,128)S(1)}, u32[]{:S(2)}, u32[]{:S(2)}) collective-permute-start(f32[4,32,128]{2,1,0:T(8,128)S(1)} %get-tuple-element.87.to_prev), channel_id=1, source_target_pairs={{8,0},{16,8},{24,16},{32,24},{40,32},{48,40},{56,48},{64,56},{72,6... | collective-permute-start | bytes 196616 | tf_op jit(solution)/shard_map/ppermute | solution.py:634
  34.0 5.1 %collective-permute-start.6 = (f32[160,128]{1,0:T(8,128)S(1)}, f32[160,128]{1,0:T(8,128)S(1)}, u32[]{:S(2)}, u32[]{:S(2)}) collective-permute-start(f32[160,128]{1,0:T(8,128)S(1)} %get-tuple-element.88), channel_id=1, source_target_pairs={{0,1},{1,2},{2,3},{3,4},{4,5},{5,6},{6,7},{7,0},{8,9},{9,10},{10,1... | collective-permute-start | bytes 245768 | tf_op jit(solution)/shard_map/ppermute | solution.py:639
  34.0 5.1 %collective-permute-start.7 = (f32[160,128]{1,0:T(8,128)S(1)}, f32[160,128]{1,0:T(8,128)S(1)}, u32[]{:S(2)}, u32[]{:S(2)}) collective-permute-start(f32[160,128]{1,0:T(8,128)S(1)} %get-tuple-element.89), channel_id=1, source_target_pairs={{0,7},{1,0},{2,1},{3,2},{4,3},{5,4},{6,5},{7,6},{8,15},{9,8},{10,9... | collective-permute-start | bytes 245768 | tf_op jit(solution)/shard_map/ppermute | solution.py:639
  39.8 8.4 %collective-permute-start.9 = (f32[2,32,128]{2,1,0:T(8,128)S(1)}, f32[2,32,128]{2,1,0:T(8,128)S(1)}, u32[]{:S(2)}, u32[]{:S(2)}) collective-permute-start(f32[2,32,128]{2,1,0:T(8,128)S(1)} %get-tuple-element.105), channel_id=1, source_target_pairs={{8,0},{16,8},{24,16},{32,24},{40,32},{48,40},{56,48},{64,56},{72,6... | collective-permute-start | bytes 98312 | tf_op jit(solution)/shard_map/ppermute | solution.py:634
  46.3 7.9 %collective-permute-start.8 = (f32[2,32,128]{2,1,0:T(8,128)S(1)}, f32[2,32,128]{2,1,0:T(8,128)S(1)}, u32[]{:S(2)}, u32[]{:S(2)}) collective-permute-start(f32[2,32,128]{2,1,0:T(8,128)S(1)} %get-tuple-element.104.here), channel_id=1, source_target_pairs={{0,8},{8,16},{16,24},{24,32},{32,40},{40,48},{48,56},{56,64},{64,7... | collective-permute-start | bytes 98312 | tf_op jit(solution)/shard_map/ppermute | solution.py:634
  77.1 3.9 %collective-permute-start.11 = (f32[96,128]{1,0:T(8,128)S(1)}, f32[96,128]{1,0:T(8,128)S(1)}, u32[]{:S(2)}, u32[]{:S(2)}) collective-permute-start(f32[96,128]{1,0:T(8,128)S(1)} %window_3.1.here), channel_id=1, source_target_pairs={{0,7},{1,0},{2,1},{3,2},{4,3},{5,4},{6,5},{7,6},{8,15},{9,8},{10,9... | collective-permute-start | bytes 147464 | tf_op jit(solution)/shard_map/ppermute | solution.py:639
  78.6 4.7 %collective-permute-start.10 = (f32[96,128]{1,0:T(8,128)S(1)}, f32[96,128]{1,0:T(8,128)S(1)}, u32[]{:S(2)}, u32[]{:S(2)}) collective-permute-start(f32[96,128]{1,0:T(8,128)S(1)} %window_3.1.here), channel_id=1, source_target_pairs={{0,1},{1,2},{2,3},{3,4},{4,5},{5,6},{6,7},{7,0},{8,9},{9,10},{10,1... | collective-permute-start | bytes 147464 | tf_op jit(solution)/shard_map/ppermute | solution.py:639
  78.6 15.2 %collective-permute-start.16 = (f32[3,32,128]{2,1,0:T(8,128)S(1)}, f32[3,32,128]{2,1,0:T(8,128)S(1)}, u32[]{:S(2)}, u32[]{:S(2)}) collective-permute-start(f32[3,32,128]{2,1,0:T(8,128)S(1)} %get-tuple-element.113), channel_id=1, source_target_pairs={{0,8},{8,16},{16,24},{24,32},{32,40},{40,48},{48,56},{56,64},{64,7... | collective-permute-start | bytes 147464 | tf_op jit(solution)/shard_map/ppermute | solution.py:634
  84.2 6.0 %collective-permute-start.13 = (f32[2,32,128]{2,1,0:T(8,128)S(1)}, f32[2,32,128]{2,1,0:T(8,128)S(1)}, u32[]{:S(2)}, u32[]{:S(2)}) collective-permute-start(f32[2,32,128]{2,1,0:T(8,128)S(1)} %get-tuple-element.111.here), channel_id=1, source_target_pairs={{0,7},{1,0},{2,1},{3,2},{4,3},{5,4},{6,5},{7,6},{8,15},{9,8},{10,9... | collective-permute-start | bytes 98312 | tf_op jit(solution)/shard_map/ppermute | solution.py:639
  84.5 5.7 %collective-permute-start.12 = (f32[2,32,128]{2,1,0:T(8,128)S(1)}, f32[2,32,128]{2,1,0:T(8,128)S(1)}, u32[]{:S(2)}, u32[]{:S(2)}) collective-permute-start(f32[2,32,128]{2,1,0:T(8,128)S(1)} %get-tuple-element.111.here), channel_id=1, source_target_pairs={{0,1},{1,2},{2,3},{3,4},{4,5},{5,6},{6,7},{7,0},{8,9},{9,10},{10,1... | collective-permute-start | bytes 98312 | tf_op jit(solution)/shard_map/ppermute | solution.py:639
  84.7 13.4 %collective-permute-start.17 = (f32[3,32,128]{2,1,0:T(8,128)S(1)}, f32[3,32,128]{2,1,0:T(8,128)S(1)}, u32[]{:S(2)}, u32[]{:S(2)}) collective-permute-start(f32[3,32,128]{2,1,0:T(8,128)S(1)} %get-tuple-element.115), channel_id=1, source_target_pairs={{8,0},{16,8},{24,16},{32,24},{40,32},{48,40},{56,48},{64,56},{72,6... | collective-permute-start | bytes 147464 | tf_op jit(solution)/shard_map/ppermute | solution.py:634
  91.1 4.1 %collective-permute-start.15 = (f32[2,16,128]{2,1,0:T(8,128)S(1)}, f32[2,16,128]{2,1,0:T(8,128)S(1)}, u32[]{:S(2)}, u32[]{:S(2)}) collective-permute-start(f32[2,16,128]{2,1,0:T(8,128)S(1)} %solve_next.1.here), channel_id=1, source_target_pairs={{0,7},{1,0},{2,1},{3,2},{4,3},{5,4},{6,5},{7,6},{8,15},{9,8},{10,9... | collective-permute-start | bytes 49160 | tf_op jit(solution)/shard_map/ppermute | solution.py:639
  93.8 4.4 %collective-permute-start.14 = (f32[2,16,128]{2,1,0:T(8,128)S(1)}, f32[2,16,128]{2,1,0:T(8,128)S(1)}, u32[]{:S(2)}, u32[]{:S(2)}) collective-permute-start(f32[2,16,128]{2,1,0:T(8,128)S(1)} %solve_next.1.here), channel_id=1, source_target_pairs={{0,1},{1,2},{2,3},{3,4},{4,5},{5,6},{6,7},{7,0},{8,9},{9,10},{10,1... | collective-permute-start | bytes 49160 | tf_op jit(solution)/shard_map/ppermute | solution.py:639
